TPU v7x, 512 devices: a whole 4x8x8 slice. The times are simulated.
512 devices in a mesh: context: 64 (over y_hi, x, z), dp: 8 (over y_lo, core).
Axes of the slice: x: 4, y: 8 (y_hi: 2, y_lo: 4; y = y_hi * 4 + y_lo), z: 8, core: 2. Of those that a mesh axis runs over, the one named last changes fastest.
Arguments:
- features: bfloat16 [4096, 3, 4096], P('context', None, 'dp'), may hold values from -6 to 6
- feat_weight: float32 [3, 3, 4096], P(None, None, 'dp'), may hold values from -30 to 30
- skip: float32 [4096], P('dp'), may hold values from -3 to 3
- residues: float32 [16, 4096], P(None, 'dp'), may hold values from -1.5 to 1.5
- rates: float32 [16, 4096], P(None, 'dp'), may hold values from 9.9e-06 to 0.0301
- norm_gain: float32 [4096], P('dp'), may hold values from 0.1 to 1.9
- attn_in: bfloat16 [4096, 3, 4096], P('context', None, 'dp'), may hold values from -8 to 8
Outputs:
- hyena_out: bfloat16 [4096, 4096], P('context', 'dp')
- attn_out: bfloat16 [4096, 4096], P('context', 'dp')
All inputs are finite; a program needn't handle non-finite values.
Results may differ from a plain program's by a relative error of at most 0.012.
The roundings to bfloat16 on the way count: a program that leaves them out, or rounds other values in their place, can miss the bound.
Values may be sent and summed in bfloat16 or wider, within the bound.
No kernel may reach another device: no remote copies, remote signals or barrier semaphores. Data moves between devices by JAX's collectives and lax.ppermute only.
A program may use at most 64 MiB of HBM per device.

v0:
```python
import math

import jax
import jax.numpy as jnp
from jax import lax
from jax.sharding import PartitionSpec as P

DH = 4096
HEAD = 128
FEAT = 3


rope_base = 1000000.0
floor_neg = -1e30


def shifted(value, axis, steps):
    count = lax.axis_size(axis)
    initial, last = (max(0, -steps), min(count, count - steps))
    return lax.ppermute(value, axis, [(source, source + steps) for source in range(initial, last)])


def rotary(tensor, position):
    halfway = tensor.shape[-1] // 2
    inverse = jnp.exp(
        jnp.arange(halfway, dtype=jnp.float32) * (-2.0 * math.log(rope_base) / tensor.shape[-1])
    )
    angle = position[:, None] * inverse[None, :]
    cosine = jnp.cos(angle)[:, None, :]
    sine = jnp.sin(angle)[:, None, :]
    first_half = tensor[..., :halfway]
    second_half = tensor[..., halfway:]
    return jnp.concatenate(
        [first_half * cosine - second_half * sine, second_half * cosine + first_half * sine], -1
    )


def angles(numerator, modulus):
    return 2.0 * math.pi / modulus * (numerator % modulus).astype(jnp.float32)


def contract(form, table, operand):
    return jnp.einsum(form, table, operand, precision=lax.Precision.HIGHEST)


def spectrum(residues, rates, frequency, seq_len):
    phase_angle = math.pi / seq_len * frequency.astype(jnp.float32)[..., None]
    parity = (1 - 2 * (frequency % 2)).astype(jnp.float32)[..., None]
    sine_phase = jnp.sin(phase_angle)
    half_sine = jnp.sin(0.5 * phase_angle)
    real_part = jnp.zeros(frequency.shape + (residues.shape[1],), jnp.float32)
    imag_part = jnp.zeros(frequency.shape + (residues.shape[1],), jnp.float32)
    for mode_index in range(residues.shape[0]):
        mode_rate = rates[mode_index]
        decay_factor = jnp.exp(-mode_rate)
        weight = residues[mode_index] * jnp.sqrt(-jnp.expm1(-2.0 * mode_rate))
        numerator = 1.0 - jnp.exp(-mode_rate * seq_len) * parity
        real_den = -jnp.expm1(-mode_rate) + 2.0 * decay_factor * half_sine * half_sine
        imag_den = decay_factor * sine_phase
        factor = weight * numerator / (real_den * real_den + imag_den * imag_den)
        real_part = real_part + factor * real_den
        imag_part = imag_part - factor * imag_den
    return (real_part, imag_part)


def section_tables(span):
    freq_one = 2 * span
    section_angle = angles(jnp.arange(freq_one)[:, None] * jnp.arange(span)[None, :], freq_one)
    return (jnp.cos(section_angle), jnp.sin(section_angle))


def local_convolve(signal, residues, rates, span):
    tokens = signal.shape[2]
    seq_len = tokens * span
    freq_one = 2 * span
    section_cosine, section_sine = section_tables(span)
    real_a = contract("kc,qcsd->qksd", section_cosine, signal)
    imag_a = -contract("kc,qcsd->qksd", section_sine, signal)
    positions = jnp.arange(tokens)
    low_freq = jnp.arange(freq_one)
    twist_angle = angles(low_freq[:, None] * positions[None, :], 2 * seq_len)[..., None]
    twist_cos = jnp.cos(twist_angle)
    twist_sin = jnp.sin(twist_angle)
    turned_r = real_a * twist_cos + imag_a * twist_sin
    turned_i = imag_a * twist_cos - real_a * twist_sin
    wave_angle = angles(positions[:, None] * positions[None, :], tokens)
    wave_cos = jnp.cos(wave_angle)
    wave_sin = jnp.sin(wave_angle)
    spec_r = contract("ms,qksd->qkmd", wave_cos, turned_r) + contract(
        "ms,qksd->qkmd", wave_sin, turned_i
    )
    spec_i = contract("ms,qksd->qkmd", wave_cos, turned_i) - contract(
        "ms,qksd->qkmd", wave_sin, turned_r
    )
    filt_r, filt_i = spectrum(
        residues, rates, low_freq[:, None] + freq_one * positions[None, :], seq_len
    )
    prod_r = spec_r * filt_r - spec_i * filt_i
    prod_i = spec_r * filt_i + spec_i * filt_r
    back_r = contract("ms,qkmd->qksd", wave_cos, prod_r) - contract(
        "ms,qkmd->qksd", wave_sin, prod_i
    )
    back_i = contract("ms,qkmd->qksd", wave_cos, prod_i) + contract(
        "ms,qkmd->qksd", wave_sin, prod_r
    )
    final_r = back_r * twist_cos - back_i * twist_sin
    final_i = back_i * twist_cos + back_r * twist_sin
    return (
        contract("kc,qksd->qcsd", section_cosine, final_r)
        - contract("kc,qksd->qcsd", section_sine, final_i)
    ) * (1.0 / (2 * seq_len))


def channel_major(product, residues, rates, device_index, groups, span):
    tokens, channels = product.shape
    devices = groups * span
    narrow = channels // devices
    moved = lax.all_to_all(product, "context", split_axis=1, concat_axis=0, tiled=True)
    signal = moved.astype(jnp.float32).reshape(groups, span, tokens, narrow)
    own_residues = lax.dynamic_slice_in_dim(residues, device_index * narrow, narrow, 1)
    own_rates = lax.dynamic_slice_in_dim(rates, device_index * narrow, narrow, 1)
    result = local_convolve(signal, own_residues, own_rates, span)
    return lax.all_to_all(
        result.reshape(devices * tokens, narrow).astype(jnp.bfloat16),
        "context",
        split_axis=0,
        concat_axis=1,
        tiled=True,
    ).astype(jnp.float32)


def attend(running, queries, block, allowed):
    row_max, row_total, accum = running
    scores = jnp.einsum(
        "phd,khd->hpk", queries, block[:, 0], preferred_element_type=jnp.float32
    ) * (1.0 / math.sqrt(HEAD))
    scores = jnp.where(allowed[None], scores, floor_neg)
    new_max = jnp.maximum(row_max, jnp.max(scores, -1))
    rescale = jnp.exp(row_max - new_max)
    weights = jnp.exp(scores - new_max[..., None])
    row_total = row_total * rescale + jnp.sum(weights, -1)
    accum = accum * rescale[..., None] + jnp.einsum(
        "hpk,khd->hpd",
        weights.astype(jnp.bfloat16),
        block[:, 1],
        preferred_element_type=jnp.float32,
    )
    return (new_max, row_total, accum)


def local(features, feat_weight, skip, residues, rates, norm_gain, attn_in):
    tokens = features.shape[0]
    devices = lax.axis_size("context")
    groups = devices // devices
    device_index = lax.axis_index("context")
    local_pos = device_index % devices
    rim_rows = shifted(features[tokens - (FEAT - 1) :], "context", 1)
    rim_rows = jnp.where(local_pos > 0, rim_rows, jnp.zeros_like(rim_rows))
    extended = jnp.concatenate([rim_rows, features], 0).astype(jnp.float32)
    featured = sum(
        (
            feat_weight[offset] * extended[FEAT - 1 - offset : FEAT - 1 - offset + tokens]
            for offset in range(FEAT)
        )
    )
    query_gate = featured[:, 0]
    product = (featured[:, 1] * featured[:, 2]).astype(jnp.bfloat16)
    product_wide = lax.optimization_barrier(product).astype(jnp.float32)
    convolved = channel_major(product, residues, rates, device_index, groups, devices)
    convolved = convolved + skip * product_wide
    gated_rows = query_gate * convolved
    squares = lax.psum(jnp.sum(gated_rows * gated_rows, -1), "dp")
    hyena_out = (gated_rows * lax.rsqrt(squares[:, None] / DH + 1e-06) * norm_gain).astype(
        jnp.bfloat16
    )
    heads_local = attn_in.shape[2] // HEAD
    raw_attn = attn_in.astype(jnp.float32).reshape(tokens, 3, heads_local, HEAD)
    positions = (local_pos * tokens + jnp.arange(tokens)).astype(jnp.float32)
    queries = rotary(raw_attn[:, 0], positions).astype(jnp.bfloat16)
    keys_rot = rotary(raw_attn[:, 1], positions).astype(jnp.bfloat16)
    packed = jnp.stack([keys_rot, attn_in[:, 2].reshape(tokens, heads_local, HEAD)], 1)
    running = (
        jnp.full((heads_local, tokens), floor_neg, jnp.float32),
        jnp.zeros((heads_local, tokens), jnp.float32),
        jnp.zeros((heads_local, tokens, HEAD), jnp.float32),
    )
    diagonal = jnp.arange(tokens)[None, :] <= jnp.arange(tokens)[:, None]
    running = attend(running, queries, packed, diagonal)

    def cycle_turn(turn_index, carry):
        state, moving = carry
        moving = shifted(moving, "context", 1)
        allowed = jnp.full((1, tokens), local_pos >= turn_index)
        return (attend(state, queries, moving, allowed), moving)

    running, _ = lax.fori_loop(1, devices, cycle_turn, (running, packed))
    row_max, row_total, accum = running
    attn_out = (
        (accum / row_total[..., None])
        .transpose(1, 0, 2)
        .reshape(tokens, heads_local * HEAD)
        .astype(jnp.bfloat16)
    )
    return (hyena_out, attn_out)


def solution(mesh):
    return jax.shard_map(
        local,
        mesh=mesh,
        in_specs=(
            P("context", None, "dp"),
            P(None, None, "dp"),
            P("dp"),
            P(None, "dp"),
            P(None, "dp"),
            P("dp"),
            P("context", None, "dp"),
        ),
        out_specs=(P("context", "dp"), P("context", "dp")),
        check_vma=False,
    )
```

profile of v0, /device:TPU:1, one launch (start us, length us, event | category | flops | bytes accessed | tf_op | source)
XLA Modules:
  0.0 1076.1 jit_solution(15036168925668273650)
XLA Ops:
  10.6 633.3 %while.19 = (s32[]{:T(128)}, f32[4,64]{1,0:T(4,128)S(1)}, f32[4,64]{1,0:T(4,128)S(1)}, f32[4,64,128]{2,1,0:T(8,128)S(1)}, bf16[64,2,4,128]{3,0,2,1:T(8,128)(2,1)...) while((s32[]{:T(128)}, f32[4,64]{1,0:T(4,128)S(1)}, f32[4,64]{1,0:T(4,128)S(1)}, ...), condition=%wide.region_7.8_spmd, body=%wide.region_4.7_spmd.sunk | while | flops 8569347 | bytes 1525895 | solution.py:196
  69.2 5.5 collective-permute-start
  131.4 5.5 collective-permute-start
  148.2 5.9 collective-permute-start
  156.5 6.2 collective-permute-start
  173.1 5.9 collective-permute-start
  181.4 6.5 collective-permute-start
  206.3 6.2 collective-permute-start
  215.0 6.2 collective-permute-start
  223.7 6.2 collective-permute-start
  233.6 6.2 collective-permute-start
  242.6 5.7 collective-permute-start
  250.7 6.4 collective-permute-start
  259.6 5.6 collective-permute-start
  267.6 5.6 collective-permute-start
  275.7 5.6 collective-permute-start
  283.8 6.2 collective-permute-start
  292.4 5.9 collective-permute-start
  301.5 6.2 collective-permute-start
  311.2 6.4 collective-permute-start
  320.0 5.5 collective-permute-start
  328.0 5.8 collective-permute-start
  336.3 6.4 collective-permute-start
  352.9 6.2 collective-permute-start
  361.6 6.2 collective-permute-start
  370.3 7.5 collective-permute-start
  380.2 14.4 %collective-permute-start = (bf16[64,2,4,128]{3,0,2,1:T(8,128)(2,1)S(1)}, bf16[64,2,4,128]{3,0,2,1:T(8,128)(2,1)S(1)}, u32[]{:S(2)}, u32[]{:S(2)}) collective-permute-start(bf16[64,2,4,128]{3,0,2,1:T(8,128)(2,1)S(1)} %get-tuple-element.428), channel_id=1, source_target_pairs={{0,8},{8,16},{16,24},{24,32},{32,40},{40,48},{48,56},{56,64},{64,7... | collective-permute-start | bytes 393224 | tf_op jit(solution)/shard_map/while/body/eval_jaxpr/ppermute | solution.py:20
  397.0 10.8 %collective-permute-start = (bf16[64,2,4,128]{3,0,2,1:T(8,128)(2,1)S(1)}, bf16[64,2,4,128]{3,0,2,1:T(8,128)(2,1)S(1)}, u32[]{:S(2)}, u32[]{:S(2)}) collective-permute-start(bf16[64,2,4,128]{3,0,2,1:T(8,128)(2,1)S(1)} %get-tuple-element.428), channel_id=1, source_target_pairs={{0,8},{8,16},{16,24},{24,32},{32,40},{40,48},{48,56},{56,64},{64,7... | collective-permute-start | bytes 393224 | tf_op jit(solution)/shard_map/while/body/eval_jaxpr/ppermute | solution.py:20
  410.3 12.8 %collective-permute-start = (bf16[64,2,4,128]{3,0,2,1:T(8,128)(2,1)S(1)}, bf16[64,2,4,128]{3,0,2,1:T(8,128)(2,1)S(1)}, u32[]{:S(2)}, u32[]{:S(2)}) collective-permute-start(bf16[64,2,4,128]{3,0,2,1:T(8,128)(2,1)S(1)} %get-tuple-element.428), channel_id=1, source_target_pairs={{0,8},{8,16},{16,24},{24,32},{32,40},{40,48},{48,56},{56,64},{64,7... | collective-permute-start | bytes 393224 | tf_op jit(solution)/shard_map/while/body/eval_jaxpr/ppermute | solution.py:20
  425.5 10.3 collective-permute-start
  438.9 12.9 %collective-permute-start = (bf16[64,2,4,128]{3,0,2,1:T(8,128)(2,1)S(1)}, bf16[64,2,4,128]{3,0,2,1:T(8,128)(2,1)S(1)}, u32[]{:S(2)}, u32[]{:S(2)}) collective-permute-start(bf16[64,2,4,128]{3,0,2,1:T(8,128)(2,1)S(1)} %get-tuple-element.428), channel_id=1, source_target_pairs={{0,8},{8,16},{16,24},{24,32},{32,40},{40,48},{48,56},{56,64},{64,7... | collective-permute-start | bytes 393224 | tf_op jit(solution)/shard_map/while/body/eval_jaxpr/ppermute | solution.py:20
  454.5 12.0 %collective-permute-start = (bf16[64,2,4,128]{3,0,2,1:T(8,128)(2,1)S(1)}, bf16[64,2,4,128]{3,0,2,1:T(8,128)(2,1)S(1)}, u32[]{:S(2)}, u32[]{:S(2)}) collective-permute-start(bf16[64,2,4,128]{3,0,2,1:T(8,128)(2,1)S(1)} %get-tuple-element.428), channel_id=1, source_target_pairs={{0,8},{8,16},{16,24},{24,32},{32,40},{40,48},{48,56},{56,64},{64,7... | collective-permute-start | bytes 393224 | tf_op jit(solution)/shard_map/while/body/eval_jaxpr/ppermute | solution.py:20
  469.0 12.0 %collective-permute-start = (bf16[64,2,4,128]{3,0,2,1:T(8,128)(2,1)S(1)}, bf16[64,2,4,128]{3,0,2,1:T(8,128)(2,1)S(1)}, u32[]{:S(2)}, u32[]{:S(2)}) collective-permute-start(bf16[64,2,4,128]{3,0,2,1:T(8,128)(2,1)S(1)} %get-tuple-element.428), channel_id=1, source_target_pairs={{0,8},{8,16},{16,24},{24,32},{32,40},{40,48},{48,56},{56,64},{64,7... | collective-permute-start | bytes 393224 | tf_op jit(solution)/shard_map/while/body/eval_jaxpr/ppermute | solution.py:20
  483.5 11.5 %collective-permute-start = (bf16[64,2,4,128]{3,0,2,1:T(8,128)(2,1)S(1)}, bf16[64,2,4,128]{3,0,2,1:T(8,128)(2,1)S(1)}, u32[]{:S(2)}, u32[]{:S(2)}) collective-permute-start(bf16[64,2,4,128]{3,0,2,1:T(8,128)(2,1)S(1)} %get-tuple-element.428), channel_id=1, source_target_pairs={{0,8},{8,16},{16,24},{24,32},{32,40},{40,48},{48,56},{56,64},{64,7... | collective-permute-start | bytes 393224 | tf_op jit(solution)/shard_map/while/body/eval_jaxpr/ppermute | solution.py:20
  497.4 12.2 %collective-permute-start = (bf16[64,2,4,128]{3,0,2,1:T(8,128)(2,1)S(1)}, bf16[64,2,4,128]{3,0,2,1:T(8,128)(2,1)S(1)}, u32[]{:S(2)}, u32[]{:S(2)}) collective-permute-start(bf16[64,2,4,128]{3,0,2,1:T(8,128)(2,1)S(1)} %get-tuple-element.428), channel_id=1, source_target_pairs={{0,8},{8,16},{16,24},{24,32},{32,40},{40,48},{48,56},{56,64},{64,7... | collective-permute-start | bytes 393224 | tf_op jit(solution)/shard_map/while/body/eval_jaxpr/ppermute | solution.py:20
  512.0 11.8 %collective-permute-start = (bf16[64,2,4,128]{3,0,2,1:T(8,128)(2,1)S(1)}, bf16[64,2,4,128]{3,0,2,1:T(8,128)(2,1)S(1)}, u32[]{:S(2)}, u32[]{:S(2)}) collective-permute-start(bf16[64,2,4,128]{3,0,2,1:T(8,128)(2,1)S(1)} %get-tuple-element.428), channel_id=1, source_target_pairs={{0,8},{8,16},{16,24},{24,32},{32,40},{40,48},{48,56},{56,64},{64,7... | collective-permute-start | bytes 393224 | tf_op jit(solution)/shard_map/while/body/eval_jaxpr/ppermute | solution.py:20
  526.3 12.2 %collective-permute-start = (bf16[64,2,4,128]{3,0,2,1:T(8,128)(2,1)S(1)}, bf16[64,2,4,128]{3,0,2,1:T(8,128)(2,1)S(1)}, u32[]{:S(2)}, u32[]{:S(2)}) collective-permute-start(bf16[64,2,4,128]{3,0,2,1:T(8,128)(2,1)S(1)} %get-tuple-element.428), channel_id=1, source_target_pairs={{0,8},{8,16},{16,24},{24,32},{32,40},{40,48},{48,56},{56,64},{64,7... | collective-permute-start | bytes 393224 | tf_op jit(solution)/shard_map/while/body/eval_jaxpr/ppermute | solution.py:20
  540.9 11.6 %collective-permute-start = (bf16[64,2,4,128]{3,0,2,1:T(8,128)(2,1)S(1)}, bf16[64,2,4,128]{3,0,2,1:T(8,128)(2,1)S(1)}, u32[]{:S(2)}, u32[]{:S(2)}) collective-permute-start(bf16[64,2,4,128]{3,0,2,1:T(8,128)(2,1)S(1)} %get-tuple-element.428), channel_id=1, source_target_pairs={{0,8},{8,16},{16,24},{24,32},{32,40},{40,48},{48,56},{56,64},{64,7... | collective-permute-start | bytes 393224 | tf_op jit(solution)/shard_map/while/body/eval_jaxpr/ppermute | solution.py:20
  555.0 11.9 %collective-permute-start = (bf16[64,2,4,128]{3,0,2,1:T(8,128)(2,1)S(1)}, bf16[64,2,4,128]{3,0,2,1:T(8,128)(2,1)S(1)}, u32[]{:S(2)}, u32[]{:S(2)}) collective-permute-start(bf16[64,2,4,128]{3,0,2,1:T(8,128)(2,1)S(1)} %get-tuple-element.428), channel_id=1, source_target_pairs={{0,8},{8,16},{16,24},{24,32},{32,40},{40,48},{48,56},{56,64},{64,7... | collective-permute-start | bytes 393224 | tf_op jit(solution)/shard_map/while/body/eval_jaxpr/ppermute | solution.py:20
  569.4 11.9 %collective-permute-start = (bf16[64,2,4,128]{3,0,2,1:T(8,128)(2,1)S(1)}, bf16[64,2,4,128]{3,0,2,1:T(8,128)(2,1)S(1)}, u32[]{:S(2)}, u32[]{:S(2)}) collective-permute-start(bf16[64,2,4,128]{3,0,2,1:T(8,128)(2,1)S(1)} %get-tuple-element.428), channel_id=1, source_target_pairs={{0,8},{8,16},{16,24},{24,32},{32,40},{40,48},{48,56},{56,64},{64,7... | collective-permute-start | bytes 393224 | tf_op jit(solution)/shard_map/while/body/eval_jaxpr/ppermute | solution.py:20
  583.8 12.2 %collective-permute-start = (bf16[64,2,4,128]{3,0,2,1:T(8,128)(2,1)S(1)}, bf16[64,2,4,128]{3,0,2,1:T(8,128)(2,1)S(1)}, u32[]{:S(2)}, u32[]{:S(2)}) collective-permute-start(bf16[64,2,4,128]{3,0,2,1:T(8,128)(2,1)S(1)} %get-tuple-element.428), channel_id=1, source_target_pairs={{0,8},{8,16},{16,24},{24,32},{32,40},{40,48},{48,56},{56,64},{64,7... | collective-permute-start | bytes 393224 | tf_op jit(solution)/shard_map/while/body/eval_jaxpr/ppermute | solution.py:20
  598.4 11.7 %collective-permute-start = (bf16[64,2,4,128]{3,0,2,1:T(8,128)(2,1)S(1)}, bf16[64,2,4,128]{3,0,2,1:T(8,128)(2,1)S(1)}, u32[]{:S(2)}, u32[]{:S(2)}) collective-permute-start(bf16[64,2,4,128]{3,0,2,1:T(8,128)(2,1)S(1)} %get-tuple-element.428), channel_id=1, source_target_pairs={{0,8},{8,16},{16,24},{24,32},{32,40},{40,48},{48,56},{56,64},{64,7... | collective-permute-start | bytes 393224 | tf_op jit(solution)/shard_map/while/body/eval_jaxpr/ppermute | solution.py:20
  612.7 12.0 %collective-permute-start = (bf16[64,2,4,128]{3,0,2,1:T(8,128)(2,1)S(1)}, bf16[64,2,4,128]{3,0,2,1:T(8,128)(2,1)S(1)}, u32[]{:S(2)}, u32[]{:S(2)}) collective-permute-start(bf16[64,2,4,128]{3,0,2,1:T(8,128)(2,1)S(1)} %get-tuple-element.428), channel_id=1, source_target_pairs={{0,8},{8,16},{16,24},{24,32},{32,40},{40,48},{48,56},{56,64},{64,7... | collective-permute-start | bytes 393224 | tf_op jit(solution)/shard_map/while/body/eval_jaxpr/ppermute | solution.py:20
  628.0 12.7 %collective-permute-start = (bf16[64,2,4,128]{3,0,2,1:T(8,128)(2,1)S(1)}, bf16[64,2,4,128]{3,0,2,1:T(8,128)(2,1)S(1)}, u32[]{:S(2)}, u32[]{:S(2)}) collective-permute-start(bf16[64,2,4,128]{3,0,2,1:T(8,128)(2,1)S(1)} %get-tuple-element.428), channel_id=1, source_target_pairs={{0,8},{8,16},{16,24},{24,32},{32,40},{40,48},{48,56},{56,64},{64,7... | collective-permute-start | bytes 393224 | tf_op jit(solution)/shard_map/while/body/eval_jaxpr/ppermute | solution.py:20
  647.4 292.1 %all-to-all-start = ((bf16[64,2,256]{2,1,0:T(2,128)(2,1)}), bf16[64,2,256]{2,1,0:T(2,128)(2,1)S(1)}, u32[]{:S(2)}, u32[]{:S(2)}) async-start(bf16[64,2,256]{2,1,0:T(2,128)(2,1)} %reshape.1797), calls=%async_computation | async-start | bytes 131072 | tf_op jit(solution)/shard_map/all_to_all | solution.py:118
  939.6 12.9 %all-to-all-done = bf16[64,2,256]{2,1,0:T(2,128)(2,1)S(1)} async-done(((bf16[64,2,256]{2,1,0:T(2,128)(2,1)}), bf16[64,2,256]{2,1,0:T(2,128)(2,1)S(1)}, u32[]{:S(2)}, u32[]{:S(2)}) %all-to-all-start) | async-done | bytes 65568 | tf_op jit(solution)/shard_map/all_to_all | solution.py:118
  967.2 13.2 %all-to-all-done.1 = bf16[64,2,256]{2,1,0:T(2,128)(2,1)S(1)} async-done(((bf16[64,2,256]{2,1,0:T(2,128)(2,1)}), bf16[64,2,256]{2,1,0:T(2,128)(2,1)S(1)}, u32[]{:S(2)}, u32[]{:S(2)}) %all-to-all-start.1) | async-done | bytes 65568 | tf_op jit(solution)/shard_map/all_to_all | solution.py:123
  980.8 94.4 %psum.7 = f32[64]{0:T(128)S(1)} all-reduce(f32[64]{0:T(128)S(1)} %multiply_reduce_fusion), channel_id=1, replica_groups=mesh['context'=64,'dp'=8] {'dp'}, use_global_device_ids=true, to_apply=%region_1.2 | all-reduce | flops 64 | bytes 512 | tf_op jit(solution)/shard_map/psum | solution.py:172
  (609 shorter events, 289.9 us)
Async XLA Ops:
  1.7 643.4 %collective-permute-start.1 = (bf16[2,3,512]{0,2,1:T(8,128)(2,1)S(1)}, bf16[2,3,512]{0,2,1:T(8,128)(2,1)S(1)}, u32[]{:S(2)}, u32[]{:S(2)}) collective-permute-start(bf16[2,3,512]{0,2,1:T(8,128)(2,1)S(1)} %copy.69), channel_id=1, source_target_pairs={{0,8},{8,16},{16,24},{24,32},{32,40},{40,48},{48,56},{56,64},{64,7... | collective-permute-start | bytes 18440 | tf_op jit(solution)/shard_map/ppermute | solution.py:20
  60.9 7.7 collective-permute-start
  69.2 8.3 collective-permute-start
  123.1 7.7 collective-permute-start
  131.4 8.3 collective-permute-start
  140.2 7.5 collective-permute-start
  148.2 7.8 collective-permute-start
  156.5 8.1 collective-permute-start
  173.1 7.8 collective-permute-start
  181.4 8.5 collective-permute-start
  206.3 8.2 collective-permute-start
  215.0 8.2 collective-permute-start
  223.7 9.4 collective-permute-start
  233.6 8.5 collective-permute-start
  242.6 7.6 collective-permute-start
  250.7 8.3 collective-permute-start
  259.6 7.5 collective-permute-start
  267.6 7.5 collective-permute-start
  275.7 7.5 collective-permute-start
  283.8 8.2 collective-permute-start
  292.4 8.5 collective-permute-start
  301.5 9.2 collective-permute-start
  311.2 8.3 collective-permute-start
  328.0 7.7 collective-permute-start
  336.3 8.3 collective-permute-start
  352.9 8.2 collective-permute-start
  361.6 8.2 collective-permute-start
  370.3 9.4 collective-permute-start
  380.2 16.3 %collective-permute-start = (bf16[64,2,4,128]{3,0,2,1:T(8,128)(2,1)S(1)}, bf16[64,2,4,128]{3,0,2,1:T(8,128)(2,1)S(1)}, u32[]{:S(2)}, u32[]{:S(2)}) collective-permute-start(bf16[64,2,4,128]{3,0,2,1:T(8,128)(2,1)S(1)} %get-tuple-element.428), channel_id=1, source_target_pairs={{0,8},{8,16},{16,24},{24,32},{32,40},{40,48},{48,56},{56,64},{64,7... | collective-permute-start | bytes 393224 | tf_op jit(solution)/shard_map/while/body/eval_jaxpr/ppermute | solution.py:20
  397.0 12.7 %collective-permute-start = (bf16[64,2,4,128]{3,0,2,1:T(8,128)(2,1)S(1)}, bf16[64,2,4,128]{3,0,2,1:T(8,128)(2,1)S(1)}, u32[]{:S(2)}, u32[]{:S(2)}) collective-permute-start(bf16[64,2,4,128]{3,0,2,1:T(8,128)(2,1)S(1)} %get-tuple-element.428), channel_id=1, source_target_pairs={{0,8},{8,16},{16,24},{24,32},{32,40},{40,48},{48,56},{56,64},{64,7... | collective-permute-start | bytes 393224 | tf_op jit(solution)/shard_map/while/body/eval_jaxpr/ppermute | solution.py:20
  410.3 14.7 %collective-permute-start = (bf16[64,2,4,128]{3,0,2,1:T(8,128)(2,1)S(1)}, bf16[64,2,4,128]{3,0,2,1:T(8,128)(2,1)S(1)}, u32[]{:S(2)}, u32[]{:S(2)}) collective-permute-start(bf16[64,2,4,128]{3,0,2,1:T(8,128)(2,1)S(1)} %get-tuple-element.428), channel_id=1, source_target_pairs={{0,8},{8,16},{16,24},{24,32},{32,40},{40,48},{48,56},{56,64},{64,7... | collective-permute-start | bytes 393224 | tf_op jit(solution)/shard_map/while/body/eval_jaxpr/ppermute | solution.py:20
  425.5 12.8 %collective-permute-start = (bf16[64,2,4,128]{3,0,2,1:T(8,128)(2,1)S(1)}, bf16[64,2,4,128]{3,0,2,1:T(8,128)(2,1)S(1)}, u32[]{:S(2)}, u32[]{:S(2)}) collective-permute-start(bf16[64,2,4,128]{3,0,2,1:T(8,128)(2,1)S(1)} %get-tuple-element.428), channel_id=1, source_target_pairs={{0,8},{8,16},{16,24},{24,32},{32,40},{40,48},{48,56},{56,64},{64,7... | collective-permute-start | bytes 393224 | tf_op jit(solution)/shard_map/while/body/eval_jaxpr/ppermute | solution.py:20
  438.9 15.1 %collective-permute-start = (bf16[64,2,4,128]{3,0,2,1:T(8,128)(2,1)S(1)}, bf16[64,2,4,128]{3,0,2,1:T(8,128)(2,1)S(1)}, u32[]{:S(2)}, u32[]{:S(2)}) collective-permute-start(bf16[64,2,4,128]{3,0,2,1:T(8,128)(2,1)S(1)} %get-tuple-element.428), channel_id=1, source_target_pairs={{0,8},{8,16},{16,24},{24,32},{32,40},{40,48},{48,56},{56,64},{64,7... | collective-permute-start | bytes 393224 | tf_op jit(solution)/shard_map/while/body/eval_jaxpr/ppermute | solution.py:20
  454.5 13.9 %collective-permute-start = (bf16[64,2,4,128]{3,0,2,1:T(8,128)(2,1)S(1)}, bf16[64,2,4,128]{3,0,2,1:T(8,128)(2,1)S(1)}, u32[]{:S(2)}, u32[]{:S(2)}) collective-permute-start(bf16[64,2,4,128]{3,0,2,1:T(8,128)(2,1)S(1)} %get-tuple-element.428), channel_id=1, source_target_pairs={{0,8},{8,16},{16,24},{24,32},{32,40},{40,48},{48,56},{56,64},{64,7... | collective-permute-start | bytes 393224 | tf_op jit(solution)/shard_map/while/body/eval_jaxpr/ppermute | solution.py:20
  469.0 14.0 %collective-permute-start = (bf16[64,2,4,128]{3,0,2,1:T(8,128)(2,1)S(1)}, bf16[64,2,4,128]{3,0,2,1:T(8,128)(2,1)S(1)}, u32[]{:S(2)}, u32[]{:S(2)}) collective-permute-start(bf16[64,2,4,128]{3,0,2,1:T(8,128)(2,1)S(1)} %get-tuple-element.428), channel_id=1, source_target_pairs={{0,8},{8,16},{16,24},{24,32},{32,40},{40,48},{48,56},{56,64},{64,7... | collective-permute-start | bytes 393224 | tf_op jit(solution)/shard_map/while/body/eval_jaxpr/ppermute | solution.py:20
  483.5 13.4 %collective-permute-start = (bf16[64,2,4,128]{3,0,2,1:T(8,128)(2,1)S(1)}, bf16[64,2,4,128]{3,0,2,1:T(8,128)(2,1)S(1)}, u32[]{:S(2)}, u32[]{:S(2)}) collective-permute-start(bf16[64,2,4,128]{3,0,2,1:T(8,128)(2,1)S(1)} %get-tuple-element.428), channel_id=1, source_target_pairs={{0,8},{8,16},{16,24},{24,32},{32,40},{40,48},{48,56},{56,64},{64,7... | collective-permute-start | bytes 393224 | tf_op jit(solution)/shard_map/while/body/eval_jaxpr/ppermute | solution.py:20
  497.4 14.1 %collective-permute-start = (bf16[64,2,4,128]{3,0,2,1:T(8,128)(2,1)S(1)}, bf16[64,2,4,128]{3,0,2,1:T(8,128)(2,1)S(1)}, u32[]{:S(2)}, u32[]{:S(2)}) collective-permute-start(bf16[64,2,4,128]{3,0,2,1:T(8,128)(2,1)S(1)} %get-tuple-element.428), channel_id=1, source_target_pairs={{0,8},{8,16},{16,24},{24,32},{32,40},{40,48},{48,56},{56,64},{64,7... | collective-permute-start | bytes 393224 | tf_op jit(solution)/shard_map/while/body/eval_jaxpr/ppermute | solution.py:20
  512.0 13.7 %collective-permute-start = (bf16[64,2,4,128]{3,0,2,1:T(8,128)(2,1)S(1)}, bf16[64,2,4,128]{3,0,2,1:T(8,128)(2,1)S(1)}, u32[]{:S(2)}, u32[]{:S(2)}) collective-permute-start(bf16[64,2,4,128]{3,0,2,1:T(8,128)(2,1)S(1)} %get-tuple-element.428), channel_id=1, source_target_pairs={{0,8},{8,16},{16,24},{24,32},{32,40},{40,48},{48,56},{56,64},{64,7... | collective-permute-start | bytes 393224 | tf_op jit(solution)/shard_map/while/body/eval_jaxpr/ppermute | solution.py:20
  526.3 14.1 %collective-permute-start = (bf16[64,2,4,128]{3,0,2,1:T(8,128)(2,1)S(1)}, bf16[64,2,4,128]{3,0,2,1:T(8,128)(2,1)S(1)}, u32[]{:S(2)}, u32[]{:S(2)}) collective-permute-start(bf16[64,2,4,128]{3,0,2,1:T(8,128)(2,1)S(1)} %get-tuple-element.428), channel_id=1, source_target_pairs={{0,8},{8,16},{16,24},{24,32},{32,40},{40,48},{48,56},{56,64},{64,7... | collective-permute-start | bytes 393224 | tf_op jit(solution)/shard_map/while/body/eval_jaxpr/ppermute | solution.py:20
  540.9 13.5 %collective-permute-start = (bf16[64,2,4,128]{3,0,2,1:T(8,128)(2,1)S(1)}, bf16[64,2,4,128]{3,0,2,1:T(8,128)(2,1)S(1)}, u32[]{:S(2)}, u32[]{:S(2)}) collective-permute-start(bf16[64,2,4,128]{3,0,2,1:T(8,128)(2,1)S(1)} %get-tuple-element.428), channel_id=1, source_target_pairs={{0,8},{8,16},{16,24},{24,32},{32,40},{40,48},{48,56},{56,64},{64,7... | collective-permute-start | bytes 393224 | tf_op jit(solution)/shard_map/while/body/eval_jaxpr/ppermute | solution.py:20
  555.0 13.9 %collective-permute-start = (bf16[64,2,4,128]{3,0,2,1:T(8,128)(2,1)S(1)}, bf16[64,2,4,128]{3,0,2,1:T(8,128)(2,1)S(1)}, u32[]{:S(2)}, u32[]{:S(2)}) collective-permute-start(bf16[64,2,4,128]{3,0,2,1:T(8,128)(2,1)S(1)} %get-tuple-element.428), channel_id=1, source_target_pairs={{0,8},{8,16},{16,24},{24,32},{32,40},{40,48},{48,56},{56,64},{64,7... | collective-permute-start | bytes 393224 | tf_op jit(solution)/shard_map/while/body/eval_jaxpr/ppermute | solution.py:20
  569.4 13.9 %collective-permute-start = (bf16[64,2,4,128]{3,0,2,1:T(8,128)(2,1)S(1)}, bf16[64,2,4,128]{3,0,2,1:T(8,128)(2,1)S(1)}, u32[]{:S(2)}, u32[]{:S(2)}) collective-permute-start(bf16[64,2,4,128]{3,0,2,1:T(8,128)(2,1)S(1)} %get-tuple-element.428), channel_id=1, source_target_pairs={{0,8},{8,16},{16,24},{24,32},{32,40},{40,48},{48,56},{56,64},{64,7... | collective-permute-start | bytes 393224 | tf_op jit(solution)/shard_map/while/body/eval_jaxpr/ppermute | solution.py:20
  583.8 14.1 %collective-permute-start = (bf16[64,2,4,128]{3,0,2,1:T(8,128)(2,1)S(1)}, bf16[64,2,4,128]{3,0,2,1:T(8,128)(2,1)S(1)}, u32[]{:S(2)}, u32[]{:S(2)}) collective-permute-start(bf16[64,2,4,128]{3,0,2,1:T(8,128)(2,1)S(1)} %get-tuple-element.428), channel_id=1, source_target_pairs={{0,8},{8,16},{16,24},{24,32},{32,40},{40,48},{48,56},{56,64},{64,7... | collective-permute-start | bytes 393224 | tf_op jit(solution)/shard_map/while/body/eval_jaxpr/ppermute | solution.py:20
  598.4 13.7 %collective-permute-start = (bf16[64,2,4,128]{3,0,2,1:T(8,128)(2,1)S(1)}, bf16[64,2,4,128]{3,0,2,1:T(8,128)(2,1)S(1)}, u32[]{:S(2)}, u32[]{:S(2)}) collective-permute-start(bf16[64,2,4,128]{3,0,2,1:T(8,128)(2,1)S(1)} %get-tuple-element.428), channel_id=1, source_target_pairs={{0,8},{8,16},{16,24},{24,32},{32,40},{40,48},{48,56},{56,64},{64,7... | collective-permute-start | bytes 393224 | tf_op jit(solution)/shard_map/while/body/eval_jaxpr/ppermute | solution.py:20
  612.7 14.8 %collective-permute-start = (bf16[64,2,4,128]{3,0,2,1:T(8,128)(2,1)S(1)}, bf16[64,2,4,128]{3,0,2,1:T(8,128)(2,1)S(1)}, u32[]{:S(2)}, u32[]{:S(2)}) collective-permute-start(bf16[64,2,4,128]{3,0,2,1:T(8,128)(2,1)S(1)} %get-tuple-element.428), channel_id=1, source_target_pairs={{0,8},{8,16},{16,24},{24,32},{32,40},{40,48},{48,56},{56,64},{64,7... | collective-permute-start | bytes 393224 | tf_op jit(solution)/shard_map/while/body/eval_jaxpr/ppermute | solution.py:20
  628.0 15.4 %collective-permute-start = (bf16[64,2,4,128]{3,0,2,1:T(8,128)(2,1)S(1)}, bf16[64,2,4,128]{3,0,2,1:T(8,128)(2,1)S(1)}, u32[]{:S(2)}, u32[]{:S(2)}) collective-permute-start(bf16[64,2,4,128]{3,0,2,1:T(8,128)(2,1)S(1)} %get-tuple-element.428), channel_id=1, source_target_pairs={{0,8},{8,16},{16,24},{24,32},{32,40},{40,48},{48,56},{56,64},{64,7... | collective-permute-start | bytes 393224 | tf_op jit(solution)/shard_map/while/body/eval_jaxpr/ppermute | solution.py:20
  647.4 305.2 %all-to-all-start = ((bf16[64,2,256]{2,1,0:T(2,128)(2,1)}), bf16[64,2,256]{2,1,0:T(2,128)(2,1)S(1)}, u32[]{:S(2)}, u32[]{:S(2)}) async-start(bf16[64,2,256]{2,1,0:T(2,128)(2,1)} %reshape.1797), calls=%async_computation | async-start | bytes 131072 | tf_op jit(solution)/shard_map/all_to_all | solution.py:118
  962.6 17.9 %all-to-all-start.1 = ((bf16[64,2,256]{2,1,0:T(2,128)(2,1)}), bf16[64,2,256]{2,1,0:T(2,128)(2,1)S(1)}, u32[]{:S(2)}, u32[]{:S(2)}) async-start(bf16[64,2,256]{2,1,0:T(2,128)(2,1)} %reshape.1799), calls=%async_computation.1 | async-start | bytes 131072 | tf_op jit(solution)/shard_map/all_to_all | solution.py:123
  (23 other events, 239.8 us)
where the time goes:
time: 1080 us
  starting transfers between devices  770 us (71%)
  waiting for transfers between devices  157 us (15%)
  blocking collectives  94.4 us (9%)
  matrix products  34.9 us (3%)
    ppermute x64, starting transfers between devices, shifted(): lax.ppermute(value, axis, [(source, source + steps) for source in range(i...  473 us
    all_to_all x1, starting transfers between devices, channel_major(): lax.all_to_all(product, 'context', split_axis=1, concat_axis=0, tiled=True)  292 us
    ppermute x64, waiting for transfers between devices, shifted(): lax.ppermute(value, axis, [(source, source + steps) for source in range(i...  130 us
    psum x1, blocking collectives, local(): squares = lax.psum(jnp.sum(gated_rows * gated_rows, -1), 'dp')  94.4 us
  transfers between devices with their start and end apart: 66, of which 65 were waited for; matrix products, arithmetic and copies ran while one was open for 3% of the time, Pallas kernels for 0%

commit v1 on v0

v1 whole, which is shorter than its diff:
```python
import functools
import itertools
import math

import jax
import jax.numpy as jnp
from jax import lax
from jax.experimental import pallas as pl
from jax.experimental.pallas import tpu as pltpu
from jax.sharding import PartitionSpec as P

DH = 4096
HEAD = 128
HEADS_DEV = 4
FEAT = 3
MODES = 16
TOK = 64
CH = 512
ROPE_BASE = 1000000.0
NEG = -1e30
BF = jnp.bfloat16
F32 = jnp.float32

DIGITS = {"y": (2, 32), "x": (4, 8), "z2": (2, 4), "w": (4, 1)}


def groups_over(*free):
    fixed = [d for d in DIGITS if d not in free]

    def places(names):
        return [
            sum(v * DIGITS[d][1] for v, d in zip(values, names))
            for values in itertools.product(*[range(DIGITS[d][0]) for d in names])
        ]

    return [[base + step for step in places(free)] for base in places(fixed)]


Q_GROUPS = groups_over("x", "w")
KV_GROUPS = groups_over("x", "z2")
STATE_GROUPS = groups_over("y", "w")

VMEM = pl.BlockSpec(memory_space=pltpu.VMEM)
SMEM = pl.BlockSpec(memory_space=pltpu.SMEM)


def call(kernel, outs, specs, flops, scratch=()):
    return pl.pallas_call(
        kernel,
        out_shape=[jax.ShapeDtypeStruct(s, d) for s, d in outs],
        in_specs=specs,
        out_specs=[VMEM] * len(outs),
        scratch_shapes=list(scratch),
        compiler_params=pltpu.CompilerParams(vmem_limit_bytes=40 * 1024 * 1024),
        cost_estimate=pl.CostEstimate(flops=flops, bytes_accessed=1000, transcendentals=0),
    )


def digits(index):
    return [(index // step) % size for size, step in DIGITS.values()]


def split2(value):
    high = value.astype(BF)
    return high, (value - high.astype(F32)).astype(BF)


def rotate_kernel(attn_ref, cos_ref, sin_ref, q_ref, kv_ref):
    cosine, sine = cos_ref[...], sin_ref[...]
    for g in range(2):
        x = attn_ref[g].astype(F32)
        for h in range(HEADS_DEV):
            part = x[:, h * HEAD : (h + 1) * HEAD]
            turned = (part * cosine + pltpu.roll(part, HEAD // 2, 1) * sine).astype(BF)
            if g == 0:
                for w in range(4):
                    q_ref[h * 4 + w] = turned
            else:
                kv_ref[h, :TOK, :] = turned
    for h in range(HEADS_DEV):
        kv_ref[h, TOK:, :] = attn_ref[2, :, h * HEAD : (h + 1) * HEAD]


def state_kernel(feat_ref, rim_ref, weight_ref, rates_ref, kv_ref, sent_ref, gate_ref, prod_ref):
    groups = []
    for g in range(3):
        x = jnp.concatenate([rim_ref[g], feat_ref[g].astype(F32)], 0)
        total = weight_ref[0, g : g + 1, :] * x[8 : 8 + TOK]
        for o in range(1, FEAT):
            total = total + weight_ref[o, g : g + 1, :] * x[8 - o : 8 - o + TOK]
        groups.append(total)
    gate_ref[...] = groups[0]
    product = (groups[1] * groups[2]).astype(BF).astype(F32)
    prod_ref[...] = product
    back = (TOK - 1 - lax.broadcasted_iota(jnp.int32, (TOK, 128), 0)).astype(F32)
    for part in range(CH // 128):
        lanes = slice(part * 128, (part + 1) * 128)
        u = product[:, lanes]
        rows = [
            jnp.sum(jnp.exp(-rates_ref[n : n + 1, lanes] * back) * u, 0, keepdims=True)
            for n in range(MODES)
        ]
        high, low = split2(jnp.concatenate(rows, 0))
        for peer in range(8):
            sent_ref[peer, 128 + part * 16 : 144 + part * 16, :] = high
            sent_ref[peer, 192 + part * 16 : 208 + part * 16, :] = low
    for x in range(4):
        for z2 in range(2):
            sent_ref[x * 2 + z2, :128, :] = kv_ref[x]


def near_kernel(prod_ref, coeff_ref, rates_ref, skip_ref, out_ref, padded, impulse):
    padded[:TOK, :] = jnp.zeros((TOK, CH), F32)
    padded[TOK:, :] = prod_ref[...]
    ahead = lax.broadcasted_iota(jnp.int32, (TOK, 128), 0).astype(F32)
    for part in range(CH // 128):
        lanes = slice(part * 128, (part + 1) * 128)
        total = jnp.zeros((TOK, 128), F32)
        for n in range(MODES):
            rate = rates_ref[n : n + 1, lanes]
            total = total + coeff_ref[n : n + 1, lanes] * jnp.exp(-rate * ahead)
        impulse[:, lanes] = total
        y = skip_ref[:, lanes] * prod_ref[:, lanes]
        for t in range(TOK):
            y = y + impulse[t : t + 1, lanes] * padded[TOK - t : 2 * TOK - t, lanes]
        out_ref[:, lanes] = y


def message_kernel(place_ref, got_ref, rates_ref, out_ref):
    y, x, z2, w = digits(place_ref[0])
    for part in range(CH // 128):
        lanes = slice(part * 128, (part + 1) * 128)
        decay = rates_ref[:, lanes] * (-float(TOK))
        states = [
            got_ref[i, 128 + part * 16 : 144 + part * 16, :].astype(F32)
            + got_ref[i, 192 + part * 16 : 208 + part * 16, :].astype(F32)
            for i in range(8)
        ]
        for j in range(8):
            target = (j // 4) * 32 + x * 8 + z2 * 4 + j % 4
            total = jnp.zeros((MODES, 128), F32)
            for i in range(8):
                source = y * 32 + (i // 2) * 8 + (i % 2) * 4 + w
                steps = target - source - 1
                keep = jnp.where(steps >= 0, 1.0, 0.0).astype(F32)
                far = jnp.maximum(steps, 0).astype(F32)
                total = total + (jnp.exp(decay * far) * keep) * states[i]
            out_ref[j, :, lanes] = total


def far_kernel(got_ref, coeff_ref, rates_ref, near_ref, gate_ref, gated_ref, square_ref):
    ahead = (lax.broadcasted_iota(jnp.int32, (TOK, 128), 0) + 1).astype(F32)
    squares = jnp.zeros((TOK, 128), F32)
    for part in range(CH // 128):
        lanes = slice(part * 128, (part + 1) * 128)
        state = got_ref[0, :, lanes]
        for j in range(1, 8):
            state = state + got_ref[j, :, lanes]
        y = near_ref[:, lanes]
        for n in range(MODES):
            rate = rates_ref[n : n + 1, lanes]
            y = y + jnp.exp(-rate * ahead) * (coeff_ref[n : n + 1, lanes] * state[n : n + 1, :])
        gated = gate_ref[:, lanes] * y
        gated_ref[:, lanes] = gated
        squares = squares + gated * gated
    total = jnp.broadcast_to(jnp.sum(squares, 1, keepdims=True), (TOK, 128))
    total = jnp.concatenate([total, jnp.zeros((TOK, 128), F32)], 0)
    square_ref[...] = jnp.transpose(total)[:8, :]


def norm_kernel(square_ref, gated_ref, gain_ref, out_ref):
    total = jnp.sum(square_ref[...], 0, keepdims=True)
    total = jnp.transpose(jnp.broadcast_to(total, (128, 128)))[:TOK, :]
    factor = lax.rsqrt(total * (1.0 / DH) + 1e-06)
    for part in range(CH // 128):
        lanes = slice(part * 128, (part + 1) * 128)
        out_ref[:, lanes] = (gated_ref[:, lanes] * factor * gain_ref[:, lanes]).astype(BF)


def attend_kernel(place_ref, q_ref, own_ref, other_ref, out_ref):
    y, _, z2, w = digits(place_ref[0])
    scale = 1.0 / math.sqrt(HEAD)
    wide = 256
    keys = jnp.concatenate(
        [own_ref[:, :TOK, :].reshape(8 * TOK, HEAD), other_ref[:, :TOK, :].reshape(8 * TOK, HEAD)], 0
    )
    values = jnp.concatenate(
        [own_ref[:, TOK:128, :].reshape(8 * TOK, HEAD), other_ref[:, TOK:, :].reshape(8 * TOK, HEAD)], 0
    )
    row = lax.broadcasted_iota(jnp.int32, (16 * TOK, 1), 0)
    block = row // TOK
    key_place = ((block // 2) % 4) * 8 + (block % 2) * 4 + w
    key_pos = key_place * TOK + row % TOK
    far_off = jnp.where(y == 1, -1, 1 << 20)
    key_pos = jnp.where(block < 8, key_pos, far_off)
    for tile in range(16 * TOK // wide):
        blocks = wide // TOK
        query = q_ref[tile * blocks : (tile + 1) * blocks].reshape(wide, HEAD)
        lane = lax.broadcasted_iota(jnp.int32, (1, wide), 1) + tile * wide
        q_block = lane // TOK
        q_pos = ((q_block // 4) * 8 + z2 * 4 + q_block % 4) * TOK + lane % TOK
        scores = lax.dot_general(
            keys, query, (((1,), (1,)), ((), ())), preferred_element_type=F32
        ) * scale
        scores = jnp.where(key_pos <= q_pos, scores, NEG)
        top = jnp.max(scores, 0, keepdims=True)
        weights = jnp.exp(scores - top)
        total = jnp.sum(weights, 0, keepdims=True)
        mixed = lax.dot_general(
            values, weights.astype(BF), (((0,), (0,)), ((), ())), preferred_element_type=F32
        ) / total
        mixed = jnp.transpose(mixed).astype(BF)
        level = top + jnp.log(total)
        high = level.astype(BF).astype(F32)
        rest = level - high
        middle = rest.astype(BF).astype(F32)
        last = rest - middle
        for b in range(blocks):
            place = tile * blocks + b
            out_ref[place, :TOK, :] = mixed[b * TOK : (b + 1) * TOK]
            lanes = slice((b // 2) * 128, (b // 2) * 128 + 128)
            which = lax.broadcasted_iota(jnp.int32, (16, 128), 0)
            stats = jnp.where(
                which == 0,
                high[:, lanes],
                jnp.where(which == 1, middle[:, lanes], jnp.where(which == 2, last[:, lanes], 0.0)),
            )
            out_ref[place, TOK:, :] = stats.astype(BF)


def merge_kernel(place_ref, got_ref, out_ref):
    odd = place_ref[0] % 2
    levels = jnp.concatenate(
        [jnp.sum(got_ref[k, TOK : TOK + 16, :].astype(F32), 0, keepdims=True) for k in range(16)], 0
    )
    levels = jnp.where(odd == 1, pltpu.roll(levels, TOK, 1), levels)
    weights = []
    for h in range(HEADS_DEV):
        part = levels[h * 4 : (h + 1) * 4]
        part = jnp.exp(part - jnp.max(part, 0, keepdims=True))
        weights.append(part / jnp.sum(part, 0, keepdims=True))
    weights = jnp.concatenate(weights + [jnp.zeros((112, 128), F32)], 0)
    weights = jnp.transpose(weights)[:TOK, :]
    for h in range(HEADS_DEV):
        total = jnp.zeros((TOK, HEAD), F32)
        for k in range(4):
            place = h * 4 + k
            total = total + weights[:, place : place + 1] * got_ref[place, :TOK, :].astype(F32)
        out_ref[:, h * HEAD : (h + 1) * HEAD] = total.astype(BF)


def exchange(value, groups):
    return lax.all_to_all(value, "context", 0, 0, axis_index_groups=groups, tiled=True)


def local(features, feat_weight, skip, residues, rates, norm_gain, attn_in):
    index = lax.axis_index("context")
    devices = lax.axis_size("context")
    place = index.astype(jnp.int32)[None]
    features = jnp.transpose(features, (1, 0, 2))
    attn_in = jnp.transpose(attn_in, (1, 0, 2))
    rim = lax.ppermute(
        features[:, TOK - (FEAT - 1) :], "context", [(s, s + 1) for s in range(devices - 1)]
    )

    coeff = residues * jnp.sqrt(-jnp.expm1(-2.0 * rates))
    inverse = jnp.exp(
        jnp.arange(HEAD // 2, dtype=F32) * (-2.0 * math.log(ROPE_BASE) / HEAD)
    )
    positions = (index * TOK + jnp.arange(TOK)).astype(F32)
    angle = positions[:, None] * inverse[None, :]
    cosine, sine = jnp.cos(angle), jnp.sin(angle)
    cosine = jnp.concatenate([cosine, cosine], 1)
    sine = jnp.concatenate([-sine, sine], 1)

    queries, pairs = call(
        rotate_kernel,
        [((16, TOK, HEAD), BF), ((HEADS_DEV, 2 * TOK, HEAD), BF)],
        [VMEM] * 3,
        1000000000,
    )(attn_in, cosine, sine)
    queries = exchange(queries, Q_GROUPS)

    rim = jnp.pad(rim.astype(F32), ((0, 0), (6, 0), (0, 0)))
    sent, gate, product = call(
        state_kernel,
        [((8, 256, HEAD), BF), ((TOK, CH), F32), ((TOK, CH), F32)],
        [VMEM] * 5,
        2000000000,
    )(features, rim, feat_weight, rates, pairs)
    queries, sent = lax.optimization_barrier((queries, sent))
    got = exchange(sent, KV_GROUPS)

    (near,) = call(
        near_kernel,
        [((TOK, CH), F32)],
        [VMEM] * 4,
        2000000000,
        [pltpu.VMEM((2 * TOK, CH), F32), pltpu.VMEM((TOK, CH), F32)],
    )(product, coeff, rates, skip[None, :])

    other = lax.ppermute(
        got[:, :128], "context", [(s, s + devices // 2) for s in range(devices // 2)]
    )
    (messages,) = call(
        message_kernel, [((8, MODES, CH), F32)], [SMEM, VMEM, VMEM], 1000000000
    )(place, got, rates)
    arrived = exchange(messages, STATE_GROUPS)

    gated, squares = call(
        far_kernel,
        [((TOK, CH), F32), ((8, 128), F32)],
        [VMEM] * 5,
        1000000000,
    )(arrived, coeff, rates, near, gate)
    squares = lax.all_to_all(squares, "dp", 0, 0, tiled=True)
    (hyena_out,) = call(norm_kernel, [((TOK, CH), BF)], [VMEM] * 3, 100000000)(
        squares, gated, norm_gain[None, :]
    )

    (partial,) = call(
        attend_kernel,
        [((16, TOK + 16, HEAD), BF)],
        [SMEM, VMEM, VMEM, VMEM],
        4000000000,
    )(place, queries, got, other)
    partial = exchange(partial, Q_GROUPS)
    (attn_out,) = call(merge_kernel, [((TOK, CH), BF)], [SMEM, VMEM], 1000000000)(place, partial)
    return (hyena_out, attn_out)


def solution(mesh):
    return jax.shard_map(
        local,
        mesh=mesh,
        in_specs=(
            P("context", None, "dp"),
            P(None, None, "dp"),
            P("dp"),
            P(None, "dp"),
            P(None, "dp"),
            P("dp"),
            P("context", None, "dp"),
        ),
        out_specs=(P("context", "dp"), P("context", "dp")),
        check_vma=False,
    )
```

time: 1080 us -> 101 us (0.09)
  starting transfers between devices: 770 us -> 48.4 us
  waiting for transfers between devices: 157 us -> 18.8 us
  blocking collectives: 94.4 us -> 18.9 us
  matrix products: 34.9 us -> 0 us
    ppermute x64 -> x2, starting transfers between devices: 473 us -> 10.5 us  [the longest x1 7.28 us: local(): lax.ppermute(got[:, :128], 'context', [(s, s + devices // 2) for s in ran...]
    all_to_all x2 -> x4, starting transfers between devices: 297 us -> 37.8 us  [the longest x3 31.3 us: exchange(): lax.all_to_all(value, 'context', 0, 0, axis_index_groups=groups, tiled=True)]
    ppermute x64 -> x2, waiting for transfers between devices: 130 us -> 0.81 us  [the longest x1 0.81 us: local(): lax.ppermute(features[:, TOK - (FEAT - 1):], 'context', [(s, s + 1) for s...]
    psum x1 -> x0, blocking collectives: 94.4 us -> none  [local(): squares = lax.psum(jnp.sum(gated_rows * gated_rows, -1), 'dp')]
    dot_general x140 -> x0, matrix products: 34.9 us -> none  [the longest x64 14.8 us: attend(): jnp.einsum('hpk,khd->hpd', weights.astype(jnp.bfloat16), block[:, 1], pre...]
    all_to_all x0 -> x1, blocking collectives: none -> 18.9 us  [exchange(): lax.all_to_all(value, 'context', 0, 0, axis_index_groups=groups, tiled=True)]
    all_to_all x2 -> x4, waiting for transfers between devices: 26.1 us -> 18 us  [the longest x3 17.1 us: exchange(): lax.all_to_all(value, 'context', 0, 0, axis_index_groups=groups, tiled=True)]
  transfers between devices with their start and end apart: 66 -> 6, of which waited for: 65 -> 5; matrix products, arithmetic and copies ran while one was open for 3% -> 0% of each run, Pallas kernels for 0% -> 8%
where the time goes in v1:
time: 101 us; the launch traced here: 99.2 us
  starting transfers between devices  48.4 us (48%)
  blocking collectives  18.9 us (19%)
  waiting for transfers between devices  18.8 us (19%)
  Pallas kernels  10.5 us (10%)
  local copies, waits for them, and re-layouts  1.32 us (1%)
    all_to_all x3, starting transfers between devices, exchange(): lax.all_to_all(value, 'context', 0, 0, axis_index_groups=groups, tiled=True)  31.3 us
    all_to_all x1, blocking collectives, exchange(): lax.all_to_all(value, 'context', 0, 0, axis_index_groups=groups, tiled=True)  18.9 us
    all_to_all x3, waiting for transfers between devices, exchange(): lax.all_to_all(value, 'context', 0, 0, axis_index_groups=groups, tiled=True)  17.1 us
    ppermute x1, starting transfers between devices, local(): lax.ppermute(got[:, :128], 'context', [(s, s + devices // 2) for s in ran...  7.28 us
    all_to_all x1, starting transfers between devices, local(): squares = lax.all_to_all(squares, 'dp', 0, 0, tiled=True)  6.5 us
    pallas_call x1, Pallas kernels, local(): call(attend_kernel, [((16, TOK + 16, HEAD), BF)], [SMEM, VMEM, VMEM, VMEM...  3.82 us
    ppermute x1, starting transfers between devices, local(): lax.ppermute(features[:, TOK - (FEAT - 1):], 'context', [(s, s + 1) for s...  3.27 us
  transfers between devices with their start and end apart: 6, of which 5 were waited for; matrix products, arithmetic and copies ran while one was open for 0% of the time, Pallas kernels for 8%

profile of v1, /device:TPU:1, one launch (start us, length us, event | category | flops | bytes accessed | tf_op | source)
XLA Modules:
  0.0 99.2 jit_solution(4689110076256881989)
XLA Ops:
  0.6 0.0 copy-start.2
  0.7 0.2 fusion
  0.9 0.1 pad_maximum_fusion
  1.0 0.6 copy-done.2
  1.6 0.8 shard_map.86
  2.3 0.0 copy-start.1
  2.3 10.5 %all-to-all-start = ((bf16[16,64,128]{2,1,0:T(8,128)(2,1)}), bf16[16,64,128]{2,1,0:T(8,128)(2,1)S(1)}, u32[]{:S(2)}, u32[]{:S(2)}) async-start(bf16[16,64,128]{2,1,0:T(8,128)(2,1)} %get-tuple-element.11), calls=%async_computation | async-start | bytes 524288 | tf_op jit(solution)/shard_map/all_to_all | solution.py:253
  12.9 0.0 copy-done.1
  12.9 0.0 copy-start
  12.9 0.0 copy-start.3
  12.9 3.3 %collective-permute-start = (bf16[3,2,512]{2,1,0:T(2,128)(2,1)S(1)}, bf16[3,2,512]{2,1,0:T(2,128)(2,1)S(1)}, u32[]{:S(2)}, u32[]{:S(2)}) collective-permute-start(bf16[3,2,512]{2,1,0:T(2,128)(2,1)S(1)} %slice.8), channel_id=1, source_target_pairs={{0,8},{8,16},{16,24},{24,32},{32,40},{40,48},{48,56},{56,64},{64,7... | collective-permute-start | bytes 18440 | tf_op jit(solution)/shard_map/ppermute | solution.py:262
  16.2 0.8 collective-permute-done
  17.0 0.0 copy-done
  17.0 0.0 copy-done.3
  17.0 0.6 shard_map.87
  17.6 4.9 %all-to-all-done.q_ref = bf16[16,64,128]{2,1,0:T(8,128)(2,1)S(1)} async-done(((bf16[16,64,128]{2,1,0:T(8,128)(2,1)}), bf16[16,64,128]{2,1,0:T(8,128)(2,1)S(1)}, u32[]{:S(2)}, u32[]{:S(2)}) %all-to-all-start) | async-done | bytes 262176 | tf_op jit(solution)/shard_map/all_to_all | solution.py:253
  22.6 18.9 %all_to_all.31.got_ref.own_ref = bf16[8,256,128]{2,1,0:T(8,128)(2,1)S(1)} all-to-all(bf16[8,256,128]{2,1,0:T(8,128)(2,1)S(1)} %get-tuple-element.14), channel_id=1, replica_groups={{0,32,64,96,128,160,192,224},{8,40,72,104,136,168,200,232},{16,48,80,11..., dimensions={0} | all-to-all | bytes 1048576 | tf_op jit(solution)/shard_map/all_to_all | solution.py:253
  41.5 1.2 %shard_map.88 = f32[8,16,512]{2,1,0:T(8,128)} custom-call(s32[1]{0:T(128)} %bitcast.place_ref, bf16[8,256,128]{2,1,0:T(8,128)(2,1)S(1)} %all_to_all.31.got_ref.own_ref, f32[16,512]{1,0:T(8,128)S(1)} %copy-done), custom_call_target="tpu_custom_call" | custom-call | flops 1000000000 | bytes 1000 | tf_op jit(solution)/shard_map/pallas_call | solution.py:305
  42.7 0.0 copy-start.6
  42.7 17.3 %all-to-all-start.2 = ((f32[8,16,512]{2,1,0:T(8,128)}), f32[8,16,512]{2,1,0:T(8,128)S(1)}, u32[]{:S(2)}, u32[]{:S(2)}) async-start(f32[8,16,512]{2,1,0:T(8,128)} %shard_map.88), calls=%async_computation.2 | async-start | bytes 524288 | tf_op jit(solution)/shard_map/all_to_all | solution.py:253
  60.0 0.0 copy-done.6
  60.0 0.0 copy-start.4
  60.1 7.3 %collective-permute-start.1 = (bf16[8,128,128]{2,1,0:T(8,128)(2,1)S(1)}, bf16[8,128,128]{2,1,0:T(8,128)(2,1)S(1)}, u32[]{:S(2)}, u32[]{:S(2)}) collective-permute-start(bf16[8,128,128]{2,1,0:T(8,128)(2,1)S(1)} %slice.9), channel_id=1, source_target_pairs={{0,256},{8,264},{16,272},{24,280},{32,288},{40,296},{48,304},{56,3... | collective-permute-start | bytes 786440 | tf_op jit(solution)/shard_map/ppermute | solution.py:302
  67.3 0.0 copy-done.4
  67.4 1.2 %shard_map.89.near_ref = f32[64,512]{1,0:T(8,128)S(1)} custom-call(f32[64,512]{1,0:T(8,128)S(1)} %get-tuple-element.15.prod_ref, f32[16,512]{1,0:T(8,128)S(1)} %sqrt_multiply_fusion.coeff_ref, f32[16,512]{1,0:T(8,128)S(1)} %copy-done, f32[1,512]{1,0:T(1,128)S(1)} %bitcast.13), custom_call_target="tpu_custom_call" | custom-call | flops 2000000000 | bytes 1000 | tf_op jit(solution)/shard_map/pallas_call | solution.py:294
  68.6 2.3 %all-to-all-done.2.got_ref = f32[8,16,512]{2,1,0:T(8,128)S(1)} async-done(((f32[8,16,512]{2,1,0:T(8,128)}), f32[8,16,512]{2,1,0:T(8,128)S(1)}, u32[]{:S(2)}, u32[]{:S(2)}) %all-to-all-start.2) | async-done | bytes 262176 | tf_op jit(solution)/shard_map/all_to_all | solution.py:253
  70.9 1.1 %shard_map.90 = (f32[64,512]{1,0:T(8,128)S(1)}, f32[8,128]{1,0:T(8,128)}) custom-call(f32[8,16,512]{2,1,0:T(8,128)S(1)} %all-to-all-done.2.got_ref, f32[16,512]{1,0:T(8,128)S(1)} %sqrt_multiply_fusion.coeff_ref, f32[16,512]{1,0:T(8,128)S(1)} %copy-done, f32[64,512]{1,0:T(8,128)S(1)} %shard_map.89.near_ref, f32[64,512]{1,0:T(8,128)S(1)} %get-tuple-element.16.gate_ref), custom_call_target="tpu_custom_call" | custom-call | flops 1000000000 | bytes 1000 | tf_op jit(solution)/shard_map/pallas_call | solution.py:310
  72.0 6.5 %all-to-all-start.3 = ((f32[8,1,128]{2,1,0:T(1,128)}), f32[8,1,128]{2,1,0:T(1,128)S(1)}, u32[]{:S(2)}, u32[]{:S(2)}) async-start(f32[8,1,128]{2,1,0:T(1,128)} %bitcast.5), calls=%async_computation.3 | async-start | bytes 8192 | tf_op jit(solution)/shard_map/all_to_all | solution.py:316
  78.5 0.0 collective-permute-done.1.other_ref
  78.5 3.8 %shard_map.92 = bf16[16,80,128]{2,1,0:T(8,128)(2,1)} custom-call(s32[1]{0:T(128)} %bitcast.place_ref, bf16[16,64,128]{2,1,0:T(8,128)(2,1)S(1)} %all-to-all-done.q_ref, bf16[8,256,128]{2,1,0:T(8,128)(2,1)S(1)} %all_to_all.31.got_ref.own_ref, bf16[8,128,128]{2,1,0:T(8,128)(2,1)S(1)} %collective-permute-done.1.other_ref), custom_call_target="tpu_custom_call" | custom-call | flops 4000000000 | bytes 1000 | tf_op jit(solution)/shard_map/pallas_call | solution.py:321
  82.3 1.0 all-to-all-done.3
  83.3 3.5 %all-to-all-start.4 = ((bf16[16,80,128]{2,1,0:T(8,128)(2,1)}), bf16[16,80,128]{2,1,0:T(8,128)(2,1)S(1)}, u32[]{:S(2)}, u32[]{:S(2)}) async-start(bf16[16,80,128]{2,1,0:T(8,128)(2,1)} %shard_map.92), calls=%async_computation.4 | async-start | bytes 655360 | tf_op jit(solution)/shard_map/all_to_all | solution.py:253
  86.8 0.0 copy-start.5
  86.8 0.7 copy-done.5
  87.5 0.7 shard_map.91
  88.2 9.8 %all-to-all-done.4.got_ref = bf16[16,80,128]{2,1,0:T(8,128)(2,1)S(1)} async-done(((bf16[16,80,128]{2,1,0:T(8,128)(2,1)}), bf16[16,80,128]{2,1,0:T(8,128)(2,1)S(1)}, u32[]{:S(2)}, u32[]{:S(2)}) %all-to-all-start.4) | async-done | bytes 327712 | tf_op jit(solution)/shard_map/all_to_all | solution.py:253
  98.1 1.1 %shard_map.93 = bf16[64,512]{1,0:T(8,128)(2,1)} custom-call(s32[1]{0:T(128)} %bitcast.place_ref, bf16[16,80,128]{2,1,0:T(8,128)(2,1)S(1)} %all-to-all-done.4.got_ref), custom_call_target="tpu_custom_call" | custom-call | flops 1000000000 | bytes 1000 | tf_op jit(solution)/shard_map/pallas_call | solution.py:328
  (6 shorter events, 0.1 us)
Async XLA Ops:
  0.6 0.9 copy-start.2
  2.3 10.5 %copy-start.1 = (bf16[64,3,512]{2,0,1:T(8,128)(2,1)S(1)}, bf16[64,3,512]{2,0,1:T(8,128)(2,1)}, u32[]{:S(2)}) copy-start(bf16[64,3,512]{2,0,1:T(8,128)(2,1)} %param.7) | copy-start | bytes 589828
  2.3 20.2 %all-to-all-start = ((bf16[16,64,128]{2,1,0:T(8,128)(2,1)}), bf16[16,64,128]{2,1,0:T(8,128)(2,1)S(1)}, u32[]{:S(2)}, u32[]{:S(2)}) async-start(bf16[16,64,128]{2,1,0:T(8,128)(2,1)} %get-tuple-element.11), calls=%async_computation | async-start | bytes 524288 | tf_op jit(solution)/shard_map/all_to_all | solution.py:253
  12.9 4.1 %copy-start = (f32[16,512]{1,0:T(8,128)S(1)}, f32[16,512]{1,0:T(8,128)}, u32[]{:S(2)}) copy-start(f32[16,512]{1,0:T(8,128)} %rates_ref.7) | copy-start | bytes 98308
  12.9 4.1 %copy-start.3 = (f32[3,3,512]{2,1,0:T(4,128)S(1)}, f32[3,3,512]{2,1,0:T(4,128)}, u32[]{:S(2)}) copy-start(f32[3,3,512]{2,1,0:T(4,128)} %weight_ref.1) | copy-start | bytes 55300
  12.9 4.1 %collective-permute-start = (bf16[3,2,512]{2,1,0:T(2,128)(2,1)S(1)}, bf16[3,2,512]{2,1,0:T(2,128)(2,1)S(1)}, u32[]{:S(2)}, u32[]{:S(2)}) collective-permute-start(bf16[3,2,512]{2,1,0:T(2,128)(2,1)S(1)} %slice.8), channel_id=1, source_target_pairs={{0,8},{8,16},{16,24},{24,32},{32,40},{40,48},{48,56},{56,64},{64,7... | collective-permute-start | bytes 18440 | tf_op jit(solution)/shard_map/ppermute | solution.py:262
  42.7 17.3 %copy-start.6 = (f32[16,512]{1,0:T(8,128)S(1)}, f32[16,512]{1,0:T(8,128)}, u32[]{:S(2)}) copy-start(f32[16,512]{1,0:T(8,128)} %param.10) | copy-start | bytes 98308
  42.7 28.2 %all-to-all-start.2 = ((f32[8,16,512]{2,1,0:T(8,128)}), f32[8,16,512]{2,1,0:T(8,128)S(1)}, u32[]{:S(2)}, u32[]{:S(2)}) async-start(f32[8,16,512]{2,1,0:T(8,128)} %shard_map.88), calls=%async_computation.2 | async-start | bytes 524288 | tf_op jit(solution)/shard_map/all_to_all | solution.py:253
  60.0 7.3 %copy-start.4 = (f32[512]{0:T(512)S(1)}, f32[512]{0:T(512)}, u32[]{:S(2)}) copy-start(f32[512]{0:T(512)} %param.9) | copy-start | bytes 6148
  60.1 18.4 %collective-permute-start.1 = (bf16[8,128,128]{2,1,0:T(8,128)(2,1)S(1)}, bf16[8,128,128]{2,1,0:T(8,128)(2,1)S(1)}, u32[]{:S(2)}, u32[]{:S(2)}) collective-permute-start(bf16[8,128,128]{2,1,0:T(8,128)(2,1)S(1)} %slice.9), channel_id=1, source_target_pairs={{0,256},{8,264},{16,272},{24,280},{32,288},{40,296},{48,304},{56,3... | collective-permute-start | bytes 786440 | tf_op jit(solution)/shard_map/ppermute | solution.py:302
  72.0 11.3 %all-to-all-start.3 = ((f32[8,1,128]{2,1,0:T(1,128)}), f32[8,1,128]{2,1,0:T(1,128)S(1)}, u32[]{:S(2)}, u32[]{:S(2)}) async-start(f32[8,1,128]{2,1,0:T(1,128)} %bitcast.5), calls=%async_computation.3 | async-start | bytes 8192 | tf_op jit(solution)/shard_map/all_to_all | solution.py:316
  83.3 14.8 %all-to-all-start.4 = ((bf16[16,80,128]{2,1,0:T(8,128)(2,1)}), bf16[16,80,128]{2,1,0:T(8,128)(2,1)S(1)}, u32[]{:S(2)}, u32[]{:S(2)}) async-start(bf16[16,80,128]{2,1,0:T(8,128)(2,1)} %shard_map.92), calls=%async_computation.4 | async-start | bytes 655360 | tf_op jit(solution)/shard_map/all_to_all | solution.py:253
  86.8 0.7 copy-start.5

commit v2 on v1

--- a/solution.py
+++ b/solution.py
@@ -58,11 +58,6 @@
 
 def digits(index):
     return [(index // step) % size for size, step in DIGITS.values()]
-
-
-def split2(value):
-    high = value.astype(BF)
-    return high, (value - high.astype(F32)).astype(BF)
 
 
 def rotate_kernel(attn_ref, cos_ref, sin_ref, q_ref, kv_ref):
@@ -100,10 +95,9 @@
             jnp.sum(jnp.exp(-rates_ref[n : n + 1, lanes] * back) * u, 0, keepdims=True)
             for n in range(MODES)
         ]
-        high, low = split2(jnp.concatenate(rows, 0))
+        state = jnp.concatenate(rows, 0).astype(BF)
         for peer in range(8):
-            sent_ref[peer, 128 + part * 16 : 144 + part * 16, :] = high
-            sent_ref[peer, 192 + part * 16 : 208 + part * 16, :] = low
+            sent_ref[peer, 128 + part * 16 : 144 + part * 16, :] = state
     for x in range(4):
         for z2 in range(2):
             sent_ref[x * 2 + z2, :128, :] = kv_ref[x]
@@ -132,9 +126,7 @@
         lanes = slice(part * 128, (part + 1) * 128)
         decay = rates_ref[:, lanes] * (-float(TOK))
         states = [
-            got_ref[i, 128 + part * 16 : 144 + part * 16, :].astype(F32)
-            + got_ref[i, 192 + part * 16 : 208 + part * 16, :].astype(F32)
-            for i in range(8)
+            got_ref[i, 128 + part * 16 : 144 + part * 16, :].astype(F32) for i in range(8)
         ]
         for j in range(8):
             target = (j // 4) * 32 + x * 8 + z2 * 4 + j % 4
@@ -145,7 +137,7 @@
                 keep = jnp.where(steps >= 0, 1.0, 0.0).astype(F32)
                 far = jnp.maximum(steps, 0).astype(F32)
                 total = total + (jnp.exp(decay * far) * keep) * states[i]
-            out_ref[j, :, lanes] = total
+            out_ref[j, :, lanes] = total.astype(BF)
 
 
 def far_kernel(got_ref, coeff_ref, rates_ref, near_ref, gate_ref, gated_ref, square_ref):
@@ -153,9 +145,9 @@
     squares = jnp.zeros((TOK, 128), F32)
     for part in range(CH // 128):
         lanes = slice(part * 128, (part + 1) * 128)
-        state = got_ref[0, :, lanes]
+        state = got_ref[0, :, lanes].astype(F32)
         for j in range(1, 8):
-            state = state + got_ref[j, :, lanes]
+            state = state + got_ref[j, :, lanes].astype(F32)
         y = near_ref[:, lanes]
         for n in range(MODES):
             rate = rates_ref[n : n + 1, lanes]
@@ -284,12 +276,20 @@
     rim = jnp.pad(rim.astype(F32), ((0, 0), (6, 0), (0, 0)))
     sent, gate, product = call(
         state_kernel,
-        [((8, 256, HEAD), BF), ((TOK, CH), F32), ((TOK, CH), F32)],
+        [((8, 192, HEAD), BF), ((TOK, CH), F32), ((TOK, CH), F32)],
         [VMEM] * 5,
         2000000000,
     )(features, rim, feat_weight, rates, pairs)
     queries, sent = lax.optimization_barrier((queries, sent))
     got = exchange(sent, KV_GROUPS)
+
+    other = lax.ppermute(
+        got[:, :128], "context", [(s, s + devices // 2) for s in range(devices // 2)]
+    )
+    (messages,) = call(
+        message_kernel, [((8, MODES, CH), BF)], [SMEM, VMEM, VMEM], 1000000000
+    )(place, got, rates)
+    arrived = exchange(messages, STATE_GROUPS)
 
     (near,) = call(
         near_kernel,
@@ -298,34 +298,26 @@
         2000000000,
         [pltpu.VMEM((2 * TOK, CH), F32), pltpu.VMEM((TOK, CH), F32)],
     )(product, coeff, rates, skip[None, :])
-
-    other = lax.ppermute(
-        got[:, :128], "context", [(s, s + devices // 2) for s in range(devices // 2)]
-    )
-    (messages,) = call(
-        message_kernel, [((8, MODES, CH), F32)], [SMEM, VMEM, VMEM], 1000000000
-    )(place, got, rates)
-    arrived = exchange(messages, STATE_GROUPS)
-
+    (partial,) = call(
+        attend_kernel,
+        [((16, TOK + 16, HEAD), BF)],
+        [SMEM, VMEM, VMEM, VMEM],
+        30000000000,
+    )(place, queries, got, other)
+    partial, arrived = lax.optimization_barrier((partial, arrived))
+    partial = exchange(partial, Q_GROUPS)
     gated, squares = call(
         far_kernel,
         [((TOK, CH), F32), ((8, 128), F32)],
         [VMEM] * 5,
         1000000000,
     )(arrived, coeff, rates, near, gate)
+    squares, partial = lax.optimization_barrier((squares, partial))
     squares = lax.all_to_all(squares, "dp", 0, 0, tiled=True)
+    (attn_out,) = call(merge_kernel, [((TOK, CH), BF)], [SMEM, VMEM], 1000000000)(place, partial)
     (hyena_out,) = call(norm_kernel, [((TOK, CH), BF)], [VMEM] * 3, 100000000)(
         squares, gated, norm_gain[None, :]
     )
-
-    (partial,) = call(
-        attend_kernel,
-        [((16, TOK + 16, HEAD), BF)],
-        [SMEM, VMEM, VMEM, VMEM],
-        4000000000,
-    )(place, queries, got, other)
-    partial = exchange(partial, Q_GROUPS)
-    (attn_out,) = call(merge_kernel, [((TOK, CH), BF)], [SMEM, VMEM], 1000000000)(place, partial)
     return (hyena_out, attn_out)
 
 

time: 101 us -> 97.5 us (0.965); the launches traced: 99.2 us -> 96.9 us
  starting transfers between devices: 48.4 us -> 41.7 us
  waiting for transfers between devices: 18.8 us -> 23.2 us
    all_to_all x3, starting transfers between devices: 31.3 us -> 23.7 us  [exchange(): lax.all_to_all(value, 'context', 0, 0, axis_index_groups=groups, tiled=True)]
    all_to_all x1, waiting for transfers between devices: 0.96 us -> 3.73 us  [local(): squares = lax.all_to_all(squares, 'dp', 0, 0, tiled=True)]
    all_to_all x3, waiting for transfers between devices: 17.1 us -> 18.6 us  [exchange(): lax.all_to_all(value, 'context', 0, 0, axis_index_groups=groups, tiled=True)]
  transfers between devices with their start and end apart: 6 -> 6, of which waited for: 5 -> 5; matrix products, arithmetic and copies ran while one was open for 0% -> 0% of each run, Pallas kernels for 8% -> 9%
where the time goes in v2:
time: 97.5 us; the launch traced here: 96.9 us
  starting transfers between devices  41.7 us (43%)
  waiting for transfers between devices  23.2 us (24%)
  blocking collectives  18.3 us (19%)
  Pallas kernels  10.5 us (11%)
  local copies, waits for them, and re-layouts  2 us (2%)
    all_to_all x3, starting transfers between devices, exchange(): lax.all_to_all(value, 'context', 0, 0, axis_index_groups=groups, tiled=True)  23.7 us
    all_to_all x3, waiting for transfers between devices, exchange(): lax.all_to_all(value, 'context', 0, 0, axis_index_groups=groups, tiled=True)  18.6 us
    all_to_all x1, blocking collectives, exchange(): lax.all_to_all(value, 'context', 0, 0, axis_index_groups=groups, tiled=True)  18.3 us
    ppermute x1, starting transfers between devices, local(): lax.ppermute(got[:, :128], 'context', [(s, s + devices // 2) for s in ran...  7.46 us
    all_to_all x1, starting transfers between devices, local(): squares = lax.all_to_all(squares, 'dp', 0, 0, tiled=True)  7.27 us
    pallas_call x1, Pallas kernels, local(): call(attend_kernel, [((16, TOK + 16, HEAD), BF)], [SMEM, VMEM, VMEM, VMEM...  3.82 us
    all_to_all x1, waiting for transfers between devices, local(): squares = lax.all_to_all(squares, 'dp', 0, 0, tiled=True)  3.73 us
    ppermute x1, starting transfers between devices, local(): lax.ppermute(features[:, TOK - (FEAT - 1):], 'context', [(s, s + 1) for s...  3.27 us
  transfers between devices with their start and end apart: 6, of which 5 were waited for; matrix products, arithmetic and copies ran while one was open for 0% of the time, Pallas kernels for 9%

profile of v2, /device:TPU:1, one launch (start us, length us, event | category | flops | bytes accessed | tf_op | source)
XLA Modules:
  0.0 96.9 jit_solution(4667672507787161051)
XLA Ops:
  0.6 0.0 copy-start.2
  0.7 0.2 fusion
  0.9 0.1 pad_maximum_fusion
  1.0 0.6 copy-done.2
  1.6 0.8 shard_map.86
  2.3 0.0 copy-start.1
  2.3 10.5 %all-to-all-start = ((bf16[16,64,128]{2,1,0:T(8,128)(2,1)}), bf16[16,64,128]{2,1,0:T(8,128)(2,1)S(1)}, u32[]{:S(2)}, u32[]{:S(2)}) async-start(bf16[16,64,128]{2,1,0:T(8,128)(2,1)} %get-tuple-element.15), calls=%async_computation | async-start | bytes 524288 | tf_op jit(solution)/shard_map/all_to_all | solution.py:245
  12.9 0.0 copy-done.1
  12.9 0.0 copy-start
  12.9 0.0 copy-start.3
  12.9 3.3 %collective-permute-start = (bf16[3,2,512]{2,1,0:T(2,128)(2,1)S(1)}, bf16[3,2,512]{2,1,0:T(2,128)(2,1)S(1)}, u32[]{:S(2)}, u32[]{:S(2)}) collective-permute-start(bf16[3,2,512]{2,1,0:T(2,128)(2,1)S(1)} %slice.8), channel_id=1, source_target_pairs={{0,8},{8,16},{16,24},{24,32},{32,40},{40,48},{48,56},{56,64},{64,7... | collective-permute-start | bytes 18440 | tf_op jit(solution)/shard_map/ppermute | solution.py:254
  16.2 0.8 collective-permute-done
  17.0 0.0 copy-done
  17.0 0.0 copy-done.3
  17.0 0.6 shard_map.87
  17.6 4.9 %all-to-all-done.q_ref = bf16[16,64,128]{2,1,0:T(8,128)(2,1)S(1)} async-done(((bf16[16,64,128]{2,1,0:T(8,128)(2,1)}), bf16[16,64,128]{2,1,0:T(8,128)(2,1)S(1)}, u32[]{:S(2)}, u32[]{:S(2)}) %all-to-all-start) | async-done | bytes 262176 | tf_op jit(solution)/shard_map/all_to_all | solution.py:245
  22.6 18.3 %all_to_all.31.own_ref.got_ref = bf16[8,192,128]{2,1,0:T(8,128)(2,1)S(1)} all-to-all(bf16[8,192,128]{2,1,0:T(8,128)(2,1)S(1)} %get-tuple-element.19), channel_id=1, replica_groups={{0,32,64,96,128,160,192,224},{8,40,72,104,136,168,200,232},{16,48,80,11..., dimensions={0} | all-to-all | bytes 786432 | tf_op jit(solution)/shard_map/all_to_all | solution.py:245
  40.9 7.5 %collective-permute-start.1 = (bf16[8,128,128]{2,1,0:T(8,128)(2,1)S(1)}, bf16[8,128,128]{2,1,0:T(8,128)(2,1)S(1)}, u32[]{:S(2)}, u32[]{:S(2)}) collective-permute-start(bf16[8,128,128]{2,1,0:T(8,128)(2,1)S(1)} %slice.9), channel_id=1, source_target_pairs={{0,256},{8,264},{16,272},{24,280},{32,288},{40,296},{48,304},{56,3... | collective-permute-start | bytes 786440 | tf_op jit(solution)/shard_map/ppermute | solution.py:286
  48.4 1.2 %shard_map.89 = bf16[8,16,512]{2,1,0:T(8,128)(2,1)} custom-call(s32[1]{0:T(128)} %bitcast.place_ref, bf16[8,192,128]{2,1,0:T(8,128)(2,1)S(1)} %all_to_all.31.own_ref.got_ref, f32[16,512]{1,0:T(8,128)S(1)} %copy-done), custom_call_target="tpu_custom_call" | custom-call | flops 1000000000 | bytes 1000 | tf_op jit(solution)/shard_map/pallas_call | solution.py:289
  49.6 9.7 %all-to-all-start.2 = ((bf16[8,16,512]{2,1,0:T(8,128)(2,1)}), bf16[8,16,512]{2,1,0:T(8,128)(2,1)S(1)}, u32[]{:S(2)}, u32[]{:S(2)}) async-start(bf16[8,16,512]{2,1,0:T(8,128)(2,1)} %shard_map.89), calls=%async_computation.2 | async-start | bytes 262144 | tf_op jit(solution)/shard_map/all_to_all | solution.py:245
  59.2 0.0 collective-permute-done.1.other_ref
  59.2 3.8 %shard_map.88 = bf16[16,80,128]{2,1,0:T(8,128)(2,1)} custom-call(s32[1]{0:T(128)} %bitcast.place_ref, bf16[16,64,128]{2,1,0:T(8,128)(2,1)S(1)} %all-to-all-done.q_ref, bf16[8,192,128]{2,1,0:T(8,128)(2,1)S(1)} %all_to_all.31.own_ref.got_ref, bf16[8,128,128]{2,1,0:T(8,128)(2,1)S(1)} %collective-permute-done.1.other_ref), custom_call_target="tpu_custom_call" | custom-call | flops 30000001024 | bytes 1000 | tf_op jit(solution)/shard_map/pallas_call | solution.py:301
  63.1 0.0 copy-start.6
  63.1 6.0 %all-to-all-done.2.got_ref = bf16[8,16,512]{2,1,0:T(8,128)(2,1)S(1)} async-done(((bf16[8,16,512]{2,1,0:T(8,128)(2,1)}), bf16[8,16,512]{2,1,0:T(8,128)(2,1)S(1)}, u32[]{:S(2)}, u32[]{:S(2)}) %all-to-all-start.2) | async-done | bytes 131104 | tf_op jit(solution)/shard_map/all_to_all | solution.py:245
  69.1 3.5 %all-to-all-start.3 = ((bf16[16,80,128]{2,1,0:T(8,128)(2,1)}), bf16[16,80,128]{2,1,0:T(8,128)(2,1)S(1)}, u32[]{:S(2)}, u32[]{:S(2)}) async-start(bf16[16,80,128]{2,1,0:T(8,128)(2,1)} %shard_map.88), calls=%async_computation.3 | async-start | bytes 655360 | tf_op jit(solution)/shard_map/all_to_all | solution.py:245
  72.7 0.0 copy-done.6
  72.7 0.0 copy-start.4
  72.7 0.7 copy-done.4
  73.4 1.2 %shard_map.90.near_ref = f32[64,512]{1,0:T(8,128)S(1)} custom-call(f32[64,512]{1,0:T(8,128)S(1)} %get-tuple-element.21.prod_ref, f32[16,512]{1,0:T(8,128)S(1)} %sqrt_multiply_fusion.coeff_ref, f32[16,512]{1,0:T(8,128)S(1)} %copy-done, f32[1,512]{1,0:T(1,128)S(1)} %bitcast.13), custom_call_target="tpu_custom_call" | custom-call | flops 2000000000 | bytes 1000 | tf_op jit(solution)/shard_map/pallas_call | solution.py:294
  74.6 1.1 %shard_map.91 = (f32[64,512]{1,0:T(8,128)S(1)}, f32[8,128]{1,0:T(8,128)}) custom-call(bf16[8,16,512]{2,1,0:T(8,128)(2,1)S(1)} %all-to-all-done.2.got_ref, f32[16,512]{1,0:T(8,128)S(1)} %sqrt_multiply_fusion.coeff_ref, f32[16,512]{1,0:T(8,128)S(1)} %copy-done, f32[64,512]{1,0:T(8,128)S(1)} %shard_map.90.near_ref, f32[64,512]{1,0:T(8,128)S(1)} %get-tuple-element.22.gate_ref), custom_call_target="tpu_custom_call" | custom-call | flops 1000000000 | bytes 1000 | tf_op jit(solution)/shard_map/pallas_call | solution.py:309
  75.7 7.7 %all-to-all-done.3.got_ref = bf16[16,80,128]{2,1,0:T(8,128)(2,1)S(1)} async-done(((bf16[16,80,128]{2,1,0:T(8,128)(2,1)}), bf16[16,80,128]{2,1,0:T(8,128)(2,1)S(1)}, u32[]{:S(2)}, u32[]{:S(2)}) %all-to-all-start.3) | async-done | bytes 327712 | tf_op jit(solution)/shard_map/all_to_all | solution.py:245
  83.4 7.3 %all-to-all-start.4 = ((f32[8,1,128]{2,1,0:T(1,128)}), f32[8,1,128]{2,1,0:T(1,128)S(1)}, u32[]{:S(2)}, u32[]{:S(2)}) async-start(f32[8,1,128]{2,1,0:T(1,128)} %bitcast.5), calls=%async_computation.4 | async-start | bytes 8192 | tf_op jit(solution)/shard_map/all_to_all | solution.py:316
  90.7 1.1 %shard_map.93 = bf16[64,512]{1,0:T(8,128)(2,1)} custom-call(s32[1]{0:T(128)} %bitcast.place_ref, bf16[16,80,128]{2,1,0:T(8,128)(2,1)S(1)} %all-to-all-done.3.got_ref), custom_call_target="tpu_custom_call" | custom-call | flops 1000000000 | bytes 1000 | tf_op jit(solution)/shard_map/pallas_call | solution.py:317
  91.7 3.7 %all-to-all-done.4 = f32[8,1,128]{2,1,0:T(1,128)S(1)} async-done(((f32[8,1,128]{2,1,0:T(1,128)}), f32[8,1,128]{2,1,0:T(1,128)S(1)}, u32[]{:S(2)}, u32[]{:S(2)}) %all-to-all-start.4) | async-done | bytes 4128 | tf_op jit(solution)/shard_map/all_to_all | solution.py:316
  95.4 0.0 copy-start.5
  95.4 0.7 copy-done.5
  96.1 0.7 shard_map.92
  (6 shorter events, 0.1 us)
Async XLA Ops:
  0.6 0.9 copy-start.2
  2.3 10.5 %copy-start.1 = (bf16[64,3,512]{2,0,1:T(8,128)(2,1)S(1)}, bf16[64,3,512]{2,0,1:T(8,128)(2,1)}, u32[]{:S(2)}) copy-start(bf16[64,3,512]{2,0,1:T(8,128)(2,1)} %param.7) | copy-start | bytes 589828
  2.3 20.2 %all-to-all-start = ((bf16[16,64,128]{2,1,0:T(8,128)(2,1)}), bf16[16,64,128]{2,1,0:T(8,128)(2,1)S(1)}, u32[]{:S(2)}, u32[]{:S(2)}) async-start(bf16[16,64,128]{2,1,0:T(8,128)(2,1)} %get-tuple-element.15), calls=%async_computation | async-start | bytes 524288 | tf_op jit(solution)/shard_map/all_to_all | solution.py:245
  12.9 4.1 %copy-start = (f32[16,512]{1,0:T(8,128)S(1)}, f32[16,512]{1,0:T(8,128)}, u32[]{:S(2)}) copy-start(f32[16,512]{1,0:T(8,128)} %rates_ref.7) | copy-start | bytes 98308
  12.9 4.1 %copy-start.3 = (f32[3,3,512]{2,1,0:T(4,128)S(1)}, f32[3,3,512]{2,1,0:T(4,128)}, u32[]{:S(2)}) copy-start(f32[3,3,512]{2,1,0:T(4,128)} %weight_ref.1) | copy-start | bytes 55300
  12.9 4.1 %collective-permute-start = (bf16[3,2,512]{2,1,0:T(2,128)(2,1)S(1)}, bf16[3,2,512]{2,1,0:T(2,128)(2,1)S(1)}, u32[]{:S(2)}, u32[]{:S(2)}) collective-permute-start(bf16[3,2,512]{2,1,0:T(2,128)(2,1)S(1)} %slice.8), channel_id=1, source_target_pairs={{0,8},{8,16},{16,24},{24,32},{32,40},{40,48},{48,56},{56,64},{64,7... | collective-permute-start | bytes 18440 | tf_op jit(solution)/shard_map/ppermute | solution.py:254
  40.9 18.3 %collective-permute-start.1 = (bf16[8,128,128]{2,1,0:T(8,128)(2,1)S(1)}, bf16[8,128,128]{2,1,0:T(8,128)(2,1)S(1)}, u32[]{:S(2)}, u32[]{:S(2)}) collective-permute-start(bf16[8,128,128]{2,1,0:T(8,128)(2,1)S(1)} %slice.9), channel_id=1, source_target_pairs={{0,256},{8,264},{16,272},{24,280},{32,288},{40,296},{48,304},{56,3... | collective-permute-start | bytes 786440 | tf_op jit(solution)/shard_map/ppermute | solution.py:286
  49.6 19.5 %all-to-all-start.2 = ((bf16[8,16,512]{2,1,0:T(8,128)(2,1)}), bf16[8,16,512]{2,1,0:T(8,128)(2,1)S(1)}, u32[]{:S(2)}, u32[]{:S(2)}) async-start(bf16[8,16,512]{2,1,0:T(8,128)(2,1)} %shard_map.89), calls=%async_computation.2 | async-start | bytes 262144 | tf_op jit(solution)/shard_map/all_to_all | solution.py:245
  63.1 9.6 %copy-start.6 = (f32[16,512]{1,0:T(8,128)S(1)}, f32[16,512]{1,0:T(8,128)}, u32[]{:S(2)}) copy-start(f32[16,512]{1,0:T(8,128)} %param.10) | copy-start | bytes 98308
  69.1 14.3 %all-to-all-start.3 = ((bf16[16,80,128]{2,1,0:T(8,128)(2,1)}), bf16[16,80,128]{2,1,0:T(8,128)(2,1)S(1)}, u32[]{:S(2)}, u32[]{:S(2)}) async-start(bf16[16,80,128]{2,1,0:T(8,128)(2,1)} %shard_map.88), calls=%async_computation.3 | async-start | bytes 655360 | tf_op jit(solution)/shard_map/all_to_all | solution.py:245
  72.7 0.7 copy-start.4
  83.4 12.1 %all-to-all-start.4 = ((f32[8,1,128]{2,1,0:T(1,128)}), f32[8,1,128]{2,1,0:T(1,128)S(1)}, u32[]{:S(2)}, u32[]{:S(2)}) async-start(f32[8,1,128]{2,1,0:T(1,128)} %bitcast.5), calls=%async_computation.4 | async-start | bytes 8192 | tf_op jit(solution)/shard_map/all_to_all | solution.py:316
  95.4 0.7 copy-start.5

commit v3 on v2

--- a/solution.py
+++ b/solution.py
@@ -18,6 +18,8 @@
 CH = 512
 ROPE_BASE = 1000000.0
 NEG = -1e30
+WIDE = 256
+BLOCKS = WIDE // TOK
 BF = jnp.bfloat16
 F32 = jnp.float32
 
@@ -140,7 +142,7 @@
             out_ref[j, :, lanes] = total.astype(BF)
 
 
-def far_kernel(got_ref, coeff_ref, rates_ref, near_ref, gate_ref, gated_ref, square_ref):
+def far_kernel(got_ref, coeff_ref, rates_ref, near_ref, gate_ref, gain_ref, gained_ref, square_ref):
     ahead = (lax.broadcasted_iota(jnp.int32, (TOK, 128), 0) + 1).astype(F32)
     squares = jnp.zeros((TOK, 128), F32)
     for part in range(CH // 128):
@@ -153,69 +155,86 @@
             rate = rates_ref[n : n + 1, lanes]
             y = y + jnp.exp(-rate * ahead) * (coeff_ref[n : n + 1, lanes] * state[n : n + 1, :])
         gated = gate_ref[:, lanes] * y
-        gated_ref[:, lanes] = gated
+        gained_ref[:, lanes] = gated * gain_ref[:, lanes]
         squares = squares + gated * gated
     total = jnp.broadcast_to(jnp.sum(squares, 1, keepdims=True), (TOK, 128))
     total = jnp.concatenate([total, jnp.zeros((TOK, 128), F32)], 0)
     square_ref[...] = jnp.transpose(total)[:8, :]
 
 
-def norm_kernel(square_ref, gated_ref, gain_ref, out_ref):
+def norm_kernel(square_ref, gained_ref, out_ref):
     total = jnp.sum(square_ref[...], 0, keepdims=True)
     total = jnp.transpose(jnp.broadcast_to(total, (128, 128)))[:TOK, :]
     factor = lax.rsqrt(total * (1.0 / DH) + 1e-06)
     for part in range(CH // 128):
         lanes = slice(part * 128, (part + 1) * 128)
-        out_ref[:, lanes] = (gated_ref[:, lanes] * factor * gain_ref[:, lanes]).astype(BF)
-
-
-def attend_kernel(place_ref, q_ref, own_ref, other_ref, out_ref):
-    y, _, z2, w = digits(place_ref[0])
-    scale = 1.0 / math.sqrt(HEAD)
-    wide = 256
-    keys = jnp.concatenate(
-        [own_ref[:, :TOK, :].reshape(8 * TOK, HEAD), other_ref[:, :TOK, :].reshape(8 * TOK, HEAD)], 0
-    )
-    values = jnp.concatenate(
-        [own_ref[:, TOK:128, :].reshape(8 * TOK, HEAD), other_ref[:, TOK:, :].reshape(8 * TOK, HEAD)], 0
-    )
-    row = lax.broadcasted_iota(jnp.int32, (16 * TOK, 1), 0)
+        out_ref[:, lanes] = (gained_ref[:, lanes] * factor).astype(BF)
+
+
+def attend(keys, values, query, mask):
+    scores = lax.dot_general(
+        keys, query, (((1,), (1,)), ((), ())), preferred_element_type=F32
+    ) * (1.0 / math.sqrt(HEAD))
+    scores = mask(scores)
+    top = jnp.max(scores, 0, keepdims=True)
+    weights = jnp.exp(scores - top)
+    total = jnp.sum(weights, 0, keepdims=True)
+    mixed = lax.dot_general(
+        values, weights.astype(BF), (((0,), (0,)), ((), ())), preferred_element_type=F32
+    )
+    return top, total, mixed
+
+
+def near_attend_kernel(place_ref, q_ref, own_ref, mixed_ref, stats_ref):
+    _, _, z2, w = digits(place_ref[0])
+    keys = own_ref[:, :TOK, :].reshape(8 * TOK, HEAD)
+    values = own_ref[:, TOK:128, :].reshape(8 * TOK, HEAD)
+    row = lax.broadcasted_iota(jnp.int32, (8 * TOK, 1), 0)
     block = row // TOK
-    key_place = ((block // 2) % 4) * 8 + (block % 2) * 4 + w
-    key_pos = key_place * TOK + row % TOK
-    far_off = jnp.where(y == 1, -1, 1 << 20)
-    key_pos = jnp.where(block < 8, key_pos, far_off)
-    for tile in range(16 * TOK // wide):
-        blocks = wide // TOK
-        query = q_ref[tile * blocks : (tile + 1) * blocks].reshape(wide, HEAD)
-        lane = lax.broadcasted_iota(jnp.int32, (1, wide), 1) + tile * wide
+    key_pos = ((block // 2) * 8 + (block % 2) * 4 + w) * TOK + row % TOK
+    for tile in range(16 * TOK // WIDE):
+        query = q_ref[tile * BLOCKS : (tile + 1) * BLOCKS].reshape(WIDE, HEAD)
+        lane = lax.broadcasted_iota(jnp.int32, (1, WIDE), 1) + tile * WIDE
         q_block = lane // TOK
         q_pos = ((q_block // 4) * 8 + z2 * 4 + q_block % 4) * TOK + lane % TOK
-        scores = lax.dot_general(
-            keys, query, (((1,), (1,)), ((), ())), preferred_element_type=F32
-        ) * scale
-        scores = jnp.where(key_pos <= q_pos, scores, NEG)
-        top = jnp.max(scores, 0, keepdims=True)
-        weights = jnp.exp(scores - top)
-        total = jnp.sum(weights, 0, keepdims=True)
-        mixed = lax.dot_general(
-            values, weights.astype(BF), (((0,), (0,)), ((), ())), preferred_element_type=F32
-        ) / total
+        top, total, mixed = attend(
+            keys, values, query, lambda s: jnp.where(key_pos <= q_pos, s, NEG)
+        )
+        lanes = slice(tile * WIDE, (tile + 1) * WIDE)
+        mixed_ref[:, lanes] = mixed
+        stats_ref[0:1, lanes] = top
+        stats_ref[1:2, lanes] = total
+
+
+def far_attend_kernel(place_ref, q_ref, other_ref, mixed_ref, stats_ref, out_ref):
+    bias = jnp.where(digits(place_ref[0])[0] == 1, 0.0, NEG).astype(F32)
+    keys = other_ref[:, :TOK, :].reshape(8 * TOK, HEAD)
+    values = other_ref[:, TOK:, :].reshape(8 * TOK, HEAD)
+    which = lax.broadcasted_iota(jnp.int32, (16, 128), 0)
+    for tile in range(16 * TOK // WIDE):
+        lanes = slice(tile * WIDE, (tile + 1) * WIDE)
+        query = q_ref[tile * BLOCKS : (tile + 1) * BLOCKS].reshape(WIDE, HEAD)
+        top_b, total_b, mixed_b = attend(keys, values, query, lambda s: s + bias)
+        top_a, total_a = stats_ref[0:1, lanes], stats_ref[1:2, lanes]
+        top = jnp.maximum(top_a, top_b)
+        scale_a, scale_b = jnp.exp(top_a - top), jnp.exp(top_b - top)
+        total = total_a * scale_a + total_b * scale_b
+        inverse = 1.0 / total
+        mixed = mixed_ref[:, lanes] * (scale_a * inverse) + mixed_b * (scale_b * inverse)
         mixed = jnp.transpose(mixed).astype(BF)
         level = top + jnp.log(total)
         high = level.astype(BF).astype(F32)
         rest = level - high
         middle = rest.astype(BF).astype(F32)
         last = rest - middle
-        for b in range(blocks):
-            place = tile * blocks + b
+        for b in range(BLOCKS):
+            place = tile * BLOCKS + b
             out_ref[place, :TOK, :] = mixed[b * TOK : (b + 1) * TOK]
-            lanes = slice((b // 2) * 128, (b // 2) * 128 + 128)
-            which = lax.broadcasted_iota(jnp.int32, (16, 128), 0)
+            part = slice((b // 2) * 128, (b // 2) * 128 + 128)
             stats = jnp.where(
                 which == 0,
-                high[:, lanes],
-                jnp.where(which == 1, middle[:, lanes], jnp.where(which == 2, last[:, lanes], 0.0)),
+                high[:, part],
+                jnp.where(which == 1, middle[:, part], jnp.where(which == 2, last[:, part], 0.0)),
             )
             out_ref[place, TOK:, :] = stats.astype(BF)
 
@@ -283,14 +302,6 @@
     queries, sent = lax.optimization_barrier((queries, sent))
     got = exchange(sent, KV_GROUPS)
 
-    other = lax.ppermute(
-        got[:, :128], "context", [(s, s + devices // 2) for s in range(devices // 2)]
-    )
-    (messages,) = call(
-        message_kernel, [((8, MODES, CH), BF)], [SMEM, VMEM, VMEM], 1000000000
-    )(place, got, rates)
-    arrived = exchange(messages, STATE_GROUPS)
-
     (near,) = call(
         near_kernel,
         [((TOK, CH), F32)],
@@ -298,26 +309,37 @@
         2000000000,
         [pltpu.VMEM((2 * TOK, CH), F32), pltpu.VMEM((TOK, CH), F32)],
     )(product, coeff, rates, skip[None, :])
-    (partial,) = call(
-        attend_kernel,
-        [((16, TOK + 16, HEAD), BF)],
-        [SMEM, VMEM, VMEM, VMEM],
-        30000000000,
-    )(place, queries, got, other)
-    partial, arrived = lax.optimization_barrier((partial, arrived))
-    partial = exchange(partial, Q_GROUPS)
-    gated, squares = call(
+    near, got = lax.optimization_barrier((near, got))
+    other = lax.ppermute(
+        got[:, :128], "context", [(s, s + devices // 2) for s in range(devices // 2)]
+    )
+    (messages,) = call(
+        message_kernel, [((8, MODES, CH), BF)], [SMEM, VMEM, VMEM], 1000000000
+    )(place, got, rates)
+    arrived = exchange(messages, STATE_GROUPS)
+
+    mixed, stats = call(
+        near_attend_kernel,
+        [((HEAD, 16 * TOK), F32), ((8, 16 * TOK), F32)],
+        [SMEM, VMEM, VMEM],
+        2000000000,
+    )(place, queries, got)
+    gained, squares = call(
         far_kernel,
         [((TOK, CH), F32), ((8, 128), F32)],
-        [VMEM] * 5,
+        [VMEM] * 6,
         1000000000,
-    )(arrived, coeff, rates, near, gate)
-    squares, partial = lax.optimization_barrier((squares, partial))
+    )(arrived, coeff, rates, near, gate, norm_gain[None, :])
     squares = lax.all_to_all(squares, "dp", 0, 0, tiled=True)
+    (partial,) = call(
+        far_attend_kernel,
+        [((16, TOK + 16, HEAD), BF)],
+        [SMEM, VMEM, VMEM, VMEM, VMEM],
+        2000000000,
+    )(place, queries, other, mixed, stats)
+    partial = exchange(partial, Q_GROUPS)
+    (hyena_out,) = call(norm_kernel, [((TOK, CH), BF)], [VMEM] * 2, 100000000)(squares, gained)
     (attn_out,) = call(merge_kernel, [((TOK, CH), BF)], [SMEM, VMEM], 1000000000)(place, partial)
-    (hyena_out,) = call(norm_kernel, [((TOK, CH), BF)], [VMEM] * 3, 100000000)(
-        squares, gated, norm_gain[None, :]
-    )
     return (hyena_out, attn_out)
 
 

time: 97.5 us -> 95.8 us (0.983)
  blocking collectives: 18.3 us -> 0 us
  starting transfers between devices: 41.7 us -> 53.1 us
  waiting for transfers between devices: 23.2 us -> 27.4 us
  Pallas kernels: 10.5 us -> 11.7 us
    all_to_all x1 -> x0, blocking collectives: 18.3 us -> none  [exchange(): lax.all_to_all(value, 'context', 0, 0, axis_index_groups=groups, tiled=True)]
    all_to_all x3 -> x4, starting transfers between devices: 23.7 us -> 37.1 us  [exchange(): lax.all_to_all(value, 'context', 0, 0, axis_index_groups=groups, tiled=True)]
    all_to_all x3 -> x4, waiting for transfers between devices: 18.6 us -> 24.3 us  [exchange(): lax.all_to_all(value, 'context', 0, 0, axis_index_groups=groups, tiled=True)]
    all_to_all x1, starting transfers between devices: 7.27 us -> 5.48 us  [local(): squares = lax.all_to_all(squares, 'dp', 0, 0, tiled=True)]
    all_to_all x1, waiting for transfers between devices: 3.73 us -> 2.24 us  [local(): squares = lax.all_to_all(squares, 'dp', 0, 0, tiled=True)]
    pallas_call x3 -> x4, Pallas kernels: 5.69 us -> 6.24 us  [the longest x1 2.57 us: local(): call(far_attend_kernel, [((16, TOK + 16, HEAD), BF)], [SMEM, VMEM, VMEM,...]
  transfers between devices with their start and end apart: 6 -> 7, of which waited for: 5 -> 6; matrix products, arithmetic and copies ran while one was open for 0% -> 0% of each run, Pallas kernels for 9% -> 9%
where the time goes in v3:
time: 95.8 us; the launch traced here: 94.7 us
  starting transfers between devices  53.1 us (55%)
  waiting for transfers between devices  27.4 us (29%)
  Pallas kernels  11.7 us (12%)
  local copies, waits for them, and re-layouts  1.35 us (1%)
    all_to_all x4, starting transfers between devices, exchange(): lax.all_to_all(value, 'context', 0, 0, axis_index_groups=groups, tiled=True)  37.1 us
    all_to_all x4, waiting for transfers between devices, exchange(): lax.all_to_all(value, 'context', 0, 0, axis_index_groups=groups, tiled=True)  24.3 us
    ppermute x1, starting transfers between devices, local(): lax.ppermute(got[:, :128], 'context', [(s, s + devices // 2) for s in ran...  7.29 us
    all_to_all x1, starting transfers between devices, local(): squares = lax.all_to_all(squares, 'dp', 0, 0, tiled=True)  5.48 us
    ppermute x1, starting transfers between devices, local(): lax.ppermute(features[:, TOK - (FEAT - 1):], 'context', [(s, s + 1) for s...  3.27 us
    pallas_call x1, Pallas kernels, local(): call(far_attend_kernel, [((16, TOK + 16, HEAD), BF)], [SMEM, VMEM, VMEM,...  2.57 us
    all_to_all x1, waiting for transfers between devices, local(): squares = lax.all_to_all(squares, 'dp', 0, 0, tiled=True)  2.24 us
  transfers between devices with their start and end apart: 7, of which 6 were waited for; matrix products, arithmetic and copies ran while one was open for 0% of the time, Pallas kernels for 9%

profile of v3, /device:TPU:1, one launch (start us, length us, event | category | flops | bytes accessed | tf_op | source)
XLA Modules:
  0.0 94.7 jit_solution(17358675510796038573)
XLA Ops:
  0.6 0.0 copy-start.2
  0.7 0.2 fusion
  0.9 0.1 pad_maximum_fusion
  1.0 0.6 copy-done.2
  1.6 0.8 shard_map.86
  2.4 0.0 copy-start.1
  2.4 10.5 %all-to-all-start = ((bf16[16,64,128]{2,1,0:T(8,128)(2,1)}), bf16[16,64,128]{2,1,0:T(8,128)(2,1)S(1)}, u32[]{:S(2)}, u32[]{:S(2)}) async-start(bf16[16,64,128]{2,1,0:T(8,128)(2,1)} %get-tuple-element.17), calls=%async_computation | async-start | bytes 524288 | tf_op jit(solution)/shard_map/all_to_all | solution.py:264
  12.9 0.0 copy-done.1
  12.9 0.0 copy-start
  12.9 0.0 copy-start.3
  12.9 3.3 %collective-permute-start = (bf16[3,2,512]{2,1,0:T(2,128)(2,1)S(1)}, bf16[3,2,512]{2,1,0:T(2,128)(2,1)S(1)}, u32[]{:S(2)}, u32[]{:S(2)}) collective-permute-start(bf16[3,2,512]{2,1,0:T(2,128)(2,1)S(1)} %slice.8), channel_id=1, source_target_pairs={{0,8},{8,16},{16,24},{24,32},{32,40},{40,48},{48,56},{56,64},{64,7... | collective-permute-start | bytes 18440 | tf_op jit(solution)/shard_map/ppermute | solution.py:273
  16.2 0.8 collective-permute-done
  17.0 0.0 copy-done
  17.0 0.0 copy-done.3
  17.0 1.3 %shard_map.87 = (bf16[8,192,128]{2,1,0:T(8,128)(2,1)}, f32[64,512]{1,0:T(8,128)S(1)}, f32[64,512]{1,0:T(8,128)S(1)}) custom-call(bf16[3,64,512]{2,1,0:T(8,128)(2,1)S(1)} %bitcast.11, f32[3,8,512]{2,1,0:T(8,128)S(1)} %pad_convert_fusion.rim_ref, f32[3,3,512]{2,1,0:T(4,128)S(1)} %copy-done.3, f32[16,512]{1,0:T(8,128)S(1)} %copy-done, ...), custom_call_target="tpu_custom_call" | custom-call | flops 2000000000 | bytes 1000 | tf_op jit(solution)/shard_map/pallas_call | solution.py:296
  18.3 4.2 %all-to-all-done.q_ref = bf16[16,64,128]{2,1,0:T(8,128)(2,1)S(1)} async-done(((bf16[16,64,128]{2,1,0:T(8,128)(2,1)}), bf16[16,64,128]{2,1,0:T(8,128)(2,1)S(1)}, u32[]{:S(2)}, u32[]{:S(2)}) %all-to-all-start) | async-done | bytes 262176 | tf_op jit(solution)/shard_map/all_to_all | solution.py:264
  22.6 0.0 copy-start.6
  22.6 7.7 %all-to-all-start.1 = ((bf16[8,192,128]{2,1,0:T(8,128)(2,1)}), bf16[8,192,128]{2,1,0:T(8,128)(2,1)S(1)}, u32[]{:S(2)}, u32[]{:S(2)}) async-start(bf16[8,192,128]{2,1,0:T(8,128)(2,1)} %get-tuple-element.19), calls=%async_computation.1 | async-start | bytes 786432 | tf_op jit(solution)/shard_map/all_to_all | solution.py:264
  30.3 0.0 copy-done.6
  30.3 0.0 copy-start.4
  30.4 0.7 copy-done.4
  31.0 1.2 %shard_map.88.near_ref = f32[64,512]{1,0:T(8,128)S(1)} custom-call(f32[64,512]{1,0:T(8,128)S(1)} %get-tuple-element.16.prod_ref, f32[16,512]{1,0:T(8,128)S(1)} %sqrt_multiply_fusion.coeff_ref, f32[16,512]{1,0:T(8,128)S(1)} %copy-done, f32[1,512]{1,0:T(1,128)S(1)} %bitcast.13), custom_call_target="tpu_custom_call" | custom-call | flops 2000000000 | bytes 1000 | tf_op jit(solution)/shard_map/pallas_call | solution.py:305
  32.2 8.9 %all-to-all-done.1.got_ref.own_ref = bf16[8,192,128]{2,1,0:T(8,128)(2,1)S(1)} async-done(((bf16[8,192,128]{2,1,0:T(8,128)(2,1)}), bf16[8,192,128]{2,1,0:T(8,128)(2,1)S(1)}, u32[]{:S(2)}, u32[]{:S(2)}) %all-to-all-start.1) | async-done | bytes 393248 | tf_op jit(solution)/shard_map/all_to_all | solution.py:264
  41.1 1.2 %shard_map.89 = bf16[8,16,512]{2,1,0:T(8,128)(2,1)} custom-call(s32[1]{0:T(128)} %bitcast.place_ref, bf16[8,192,128]{2,1,0:T(8,128)(2,1)S(1)} %all-to-all-done.1.got_ref.own_ref, f32[16,512]{1,0:T(8,128)S(1)} %copy-done), custom_call_target="tpu_custom_call" | custom-call | flops 1000000000 | bytes 1000 | tf_op jit(solution)/shard_map/pallas_call | solution.py:316
  42.3 14.6 %all-to-all-start.2 = ((bf16[8,16,512]{2,1,0:T(8,128)(2,1)}), bf16[8,16,512]{2,1,0:T(8,128)(2,1)S(1)}, u32[]{:S(2)}, u32[]{:S(2)}) async-start(bf16[8,16,512]{2,1,0:T(8,128)(2,1)} %shard_map.89), calls=%async_computation.2 | async-start | bytes 262144 | tf_op jit(solution)/shard_map/all_to_all | solution.py:264
  56.9 7.3 %collective-permute-start.1 = (bf16[8,128,128]{2,1,0:T(8,128)(2,1)S(1)}, bf16[8,128,128]{2,1,0:T(8,128)(2,1)S(1)}, u32[]{:S(2)}, u32[]{:S(2)}) collective-permute-start(bf16[8,128,128]{2,1,0:T(8,128)(2,1)S(1)} %slice.7), channel_id=1, source_target_pairs={{0,256},{8,264},{16,272},{24,280},{32,288},{40,296},{48,304},{56,3... | collective-permute-start | bytes 786440 | tf_op jit(solution)/shard_map/ppermute | solution.py:313
  64.2 1.8 %shard_map.92 = (f32[128,1024]{1,0:T(8,128)S(1)}, f32[8,1024]{1,0:T(8,128)S(1)}) custom-call(s32[1]{0:T(128)} %bitcast.place_ref, bf16[16,64,128]{2,1,0:T(8,128)(2,1)S(1)} %all-to-all-done.q_ref, bf16[8,192,128]{2,1,0:T(8,128)(2,1)S(1)} %all-to-all-done.1.got_ref.own_ref), custom_call_target="tpu_custom_call" | custom-call | flops 2000000000 | bytes 1000 | tf_op jit(solution)/shard_map/pallas_call | solution.py:321
  66.1 0.0 copy-start.5
  66.1 0.6 all-to-all-done.2.got_ref
  66.7 0.0 copy-done.5
  66.7 1.1 %shard_map.90 = (f32[64,512]{1,0:T(8,128)S(1)}, f32[8,128]{1,0:T(8,128)}) custom-call(bf16[8,16,512]{2,1,0:T(8,128)(2,1)S(1)} %all-to-all-done.2.got_ref, f32[16,512]{1,0:T(8,128)S(1)} %sqrt_multiply_fusion.coeff_ref, f32[16,512]{1,0:T(8,128)S(1)} %copy-done, f32[64,512]{1,0:T(8,128)S(1)} %shard_map.88.near_ref, f32[64,512]{1,0:T(8,128)S(1)} %get-tuple-element.22.gate_ref, ...), custom_call_target="tpu_custom_call" | custom-call | flops 1000000000 | bytes 1000 | tf_op jit(solution)/shard_map/pallas_call | solution.py:327
  67.9 5.5 %all-to-all-start.3 = ((f32[8,1,128]{2,1,0:T(1,128)}), f32[8,1,128]{2,1,0:T(1,128)S(1)}, u32[]{:S(2)}, u32[]{:S(2)}) async-start(f32[8,1,128]{2,1,0:T(1,128)} %bitcast.6), calls=%async_computation.3 | async-start | bytes 8192 | tf_op jit(solution)/shard_map/all_to_all | solution.py:333
  73.4 0.0 collective-permute-done.1.other_ref
  73.4 2.6 %shard_map.93 = bf16[16,80,128]{2,1,0:T(8,128)(2,1)} custom-call(s32[1]{0:T(128)} %bitcast.place_ref, bf16[16,64,128]{2,1,0:T(8,128)(2,1)S(1)} %all-to-all-done.q_ref, bf16[8,128,128]{2,1,0:T(8,128)(2,1)S(1)} %collective-permute-done.1.other_ref, f32[128,1024]{1,0:T(8,128)S(1)} %get-tuple-element.26.mixed_ref, f32[8,1024]{1,0:T(8,128)S(1)} %get-tuple-element.27.stats_ref), custom_call_target="tpu_custom_call" | custom-call | flops 2000000000 | bytes 1000 | tf_op jit(solution)/shard_map/pallas_call | solution.py:334
  75.9 2.2 %all-to-all-done.3 = f32[8,1,128]{2,1,0:T(1,128)S(1)} async-done(((f32[8,1,128]{2,1,0:T(1,128)}), f32[8,1,128]{2,1,0:T(1,128)S(1)}, u32[]{:S(2)}, u32[]{:S(2)}) %all-to-all-start.3) | async-done | bytes 4128 | tf_op jit(solution)/shard_map/all_to_all | solution.py:333
  78.2 4.2 %all-to-all-start.4 = ((bf16[16,80,128]{2,1,0:T(8,128)(2,1)}), bf16[16,80,128]{2,1,0:T(8,128)(2,1)S(1)}, u32[]{:S(2)}, u32[]{:S(2)}) async-start(bf16[16,80,128]{2,1,0:T(8,128)(2,1)} %shard_map.93), calls=%async_computation.4 | async-start | bytes 655360 | tf_op jit(solution)/shard_map/all_to_all | solution.py:264
  82.4 0.7 shard_map.91
  83.1 10.5 %all-to-all-done.4.got_ref = bf16[16,80,128]{2,1,0:T(8,128)(2,1)S(1)} async-done(((bf16[16,80,128]{2,1,0:T(8,128)(2,1)}), bf16[16,80,128]{2,1,0:T(8,128)(2,1)S(1)}, u32[]{:S(2)}, u32[]{:S(2)}) %all-to-all-start.4) | async-done | bytes 327712 | tf_op jit(solution)/shard_map/all_to_all | solution.py:264
  93.6 1.1 %shard_map.94 = bf16[64,512]{1,0:T(8,128)(2,1)} custom-call(s32[1]{0:T(128)} %bitcast.place_ref, bf16[16,80,128]{2,1,0:T(8,128)(2,1)S(1)} %all-to-all-done.4.got_ref), custom_call_target="tpu_custom_call" | custom-call | flops 1000000000 | bytes 1000 | tf_op jit(solution)/shard_map/pallas_call | solution.py:342
  (6 shorter events, 0.1 us)
Async XLA Ops:
  0.6 0.9 copy-start.2
  2.4 10.5 %copy-start.1 = (bf16[64,3,512]{2,0,1:T(8,128)(2,1)S(1)}, bf16[64,3,512]{2,0,1:T(8,128)(2,1)}, u32[]{:S(2)}) copy-start(bf16[64,3,512]{2,0,1:T(8,128)(2,1)} %param.7) | copy-start | bytes 589828
  2.4 20.2 %all-to-all-start = ((bf16[16,64,128]{2,1,0:T(8,128)(2,1)}), bf16[16,64,128]{2,1,0:T(8,128)(2,1)S(1)}, u32[]{:S(2)}, u32[]{:S(2)}) async-start(bf16[16,64,128]{2,1,0:T(8,128)(2,1)} %get-tuple-element.17), calls=%async_computation | async-start | bytes 524288 | tf_op jit(solution)/shard_map/all_to_all | solution.py:264
  12.9 4.1 %copy-start = (f32[16,512]{1,0:T(8,128)S(1)}, f32[16,512]{1,0:T(8,128)}, u32[]{:S(2)}) copy-start(f32[16,512]{1,0:T(8,128)} %rates_ref.7) | copy-start | bytes 98308
  12.9 4.1 %copy-start.3 = (f32[3,3,512]{2,1,0:T(4,128)S(1)}, f32[3,3,512]{2,1,0:T(4,128)}, u32[]{:S(2)}) copy-start(f32[3,3,512]{2,1,0:T(4,128)} %weight_ref.1) | copy-start | bytes 55300
  12.9 4.1 %collective-permute-start = (bf16[3,2,512]{2,1,0:T(2,128)(2,1)S(1)}, bf16[3,2,512]{2,1,0:T(2,128)(2,1)S(1)}, u32[]{:S(2)}, u32[]{:S(2)}) collective-permute-start(bf16[3,2,512]{2,1,0:T(2,128)(2,1)S(1)} %slice.8), channel_id=1, source_target_pairs={{0,8},{8,16},{16,24},{24,32},{32,40},{40,48},{48,56},{56,64},{64,7... | collective-permute-start | bytes 18440 | tf_op jit(solution)/shard_map/ppermute | solution.py:273
  22.6 7.7 %copy-start.6 = (f32[16,512]{1,0:T(8,128)S(1)}, f32[16,512]{1,0:T(8,128)}, u32[]{:S(2)}) copy-start(f32[16,512]{1,0:T(8,128)} %param.10) | copy-start | bytes 98308
  22.6 18.6 %all-to-all-start.1 = ((bf16[8,192,128]{2,1,0:T(8,128)(2,1)}), bf16[8,192,128]{2,1,0:T(8,128)(2,1)S(1)}, u32[]{:S(2)}, u32[]{:S(2)}) async-start(bf16[8,192,128]{2,1,0:T(8,128)(2,1)} %get-tuple-element.19), calls=%async_computation.1 | async-start | bytes 786432 | tf_op jit(solution)/shard_map/all_to_all | solution.py:264
  30.3 0.7 copy-start.4
  42.3 24.4 %all-to-all-start.2 = ((bf16[8,16,512]{2,1,0:T(8,128)(2,1)}), bf16[8,16,512]{2,1,0:T(8,128)(2,1)S(1)}, u32[]{:S(2)}, u32[]{:S(2)}) async-start(bf16[8,16,512]{2,1,0:T(8,128)(2,1)} %shard_map.89), calls=%async_computation.2 | async-start | bytes 262144 | tf_op jit(solution)/shard_map/all_to_all | solution.py:264
  56.9 16.4 %collective-permute-start.1 = (bf16[8,128,128]{2,1,0:T(8,128)(2,1)S(1)}, bf16[8,128,128]{2,1,0:T(8,128)(2,1)S(1)}, u32[]{:S(2)}, u32[]{:S(2)}) collective-permute-start(bf16[8,128,128]{2,1,0:T(8,128)(2,1)S(1)} %slice.7), channel_id=1, source_target_pairs={{0,256},{8,264},{16,272},{24,280},{32,288},{40,296},{48,304},{56,3... | collective-permute-start | bytes 786440 | tf_op jit(solution)/shard_map/ppermute | solution.py:313
  66.1 0.7 copy-start.5
  67.9 10.3 %all-to-all-start.3 = ((f32[8,1,128]{2,1,0:T(1,128)}), f32[8,1,128]{2,1,0:T(1,128)S(1)}, u32[]{:S(2)}, u32[]{:S(2)}) async-start(f32[8,1,128]{2,1,0:T(1,128)} %bitcast.6), calls=%async_computation.3 | async-start | bytes 8192 | tf_op jit(solution)/shard_map/all_to_all | solution.py:333
  78.2 15.5 %all-to-all-start.4 = ((bf16[16,80,128]{2,1,0:T(8,128)(2,1)}), bf16[16,80,128]{2,1,0:T(8,128)(2,1)S(1)}, u32[]{:S(2)}, u32[]{:S(2)}) async-start(bf16[16,80,128]{2,1,0:T(8,128)(2,1)} %shard_map.93), calls=%async_computation.4 | async-start | bytes 655360 | tf_op jit(solution)/shard_map/all_to_all | solution.py:264

commit v4 on v3

--- a/solution.py
+++ b/solution.py
@@ -53,13 +53,23 @@
         in_specs=specs,
         out_specs=[VMEM] * len(outs),
         scratch_shapes=list(scratch),
-        compiler_params=pltpu.CompilerParams(vmem_limit_bytes=40 * 1024 * 1024),
+        compiler_params=pltpu.CompilerParams(vmem_limit_bytes=16 * 1024 * 1024),
         cost_estimate=pl.CostEstimate(flops=flops, bytes_accessed=1000, transcendentals=0),
     )
 
 
 def digits(index):
     return [(index // step) % size for size, step in DIGITS.values()]
+
+
+def expand(rates, weights, start):
+    ahead = (lax.broadcasted_iota(jnp.int32, (8, 128), 0) + start).astype(F32)
+    bases = [jnp.exp(-rates[n : n + 1, :] * ahead) for n in range(MODES)]
+    tiles = []
+    for a in range(8):
+        scaled = weights * jnp.exp(rates * (-8.0 * a))
+        tiles.append(sum(bases[n] * scaled[n : n + 1, :] for n in range(MODES)))
+    return tiles
 
 
 def rotate_kernel(attn_ref, cos_ref, sin_ref, q_ref, kv_ref):
@@ -89,14 +99,17 @@
     gate_ref[...] = groups[0]
     product = (groups[1] * groups[2]).astype(BF).astype(F32)
     prod_ref[...] = product
-    back = (TOK - 1 - lax.broadcasted_iota(jnp.int32, (TOK, 128), 0)).astype(F32)
-    for part in range(CH // 128):
-        lanes = slice(part * 128, (part + 1) * 128)
-        u = product[:, lanes]
-        rows = [
-            jnp.sum(jnp.exp(-rates_ref[n : n + 1, lanes] * back) * u, 0, keepdims=True)
-            for n in range(MODES)
-        ]
+    back = (7 - lax.broadcasted_iota(jnp.int32, (8, 128), 0)).astype(F32)
+    for part in range(CH // 128):
+        lanes = slice(part * 128, (part + 1) * 128)
+        step = jnp.exp(-8.0 * rates_ref[:, lanes])
+        rows = []
+        for n in range(MODES):
+            total = product[:8, lanes]
+            for a in range(1, 8):
+                total = total * step[n : n + 1, :] + product[8 * a : 8 * a + 8, lanes]
+            total = total * jnp.exp(-rates_ref[n : n + 1, lanes] * back)
+            rows.append(jnp.sum(total, 0, keepdims=True))
         state = jnp.concatenate(rows, 0).astype(BF)
         for peer in range(8):
             sent_ref[peer, 128 + part * 16 : 144 + part * 16, :] = state
@@ -108,14 +121,11 @@
 def near_kernel(prod_ref, coeff_ref, rates_ref, skip_ref, out_ref, padded, impulse):
     padded[:TOK, :] = jnp.zeros((TOK, CH), F32)
     padded[TOK:, :] = prod_ref[...]
-    ahead = lax.broadcasted_iota(jnp.int32, (TOK, 128), 0).astype(F32)
-    for part in range(CH // 128):
-        lanes = slice(part * 128, (part + 1) * 128)
-        total = jnp.zeros((TOK, 128), F32)
-        for n in range(MODES):
-            rate = rates_ref[n : n + 1, lanes]
-            total = total + coeff_ref[n : n + 1, lanes] * jnp.exp(-rate * ahead)
-        impulse[:, lanes] = total
+    for part in range(CH // 128):
+        lanes = slice(part * 128, (part + 1) * 128)
+        rows = expand(rates_ref[:, lanes], coeff_ref[:, lanes], 0)
+        for a in range(8):
+            impulse[8 * a : 8 * a + 8, lanes] = rows[a]
         y = skip_ref[:, lanes] * prod_ref[:, lanes]
         for t in range(TOK):
             y = y + impulse[t : t + 1, lanes] * padded[TOK - t : 2 * TOK - t, lanes]
@@ -124,37 +134,39 @@
 
 def message_kernel(place_ref, got_ref, rates_ref, out_ref):
     y, x, z2, w = digits(place_ref[0])
+    gaps = [8 * (x - i // 2) + 4 * (z2 - i % 2) for i in range(8)]
     for part in range(CH // 128):
         lanes = slice(part * 128, (part + 1) * 128)
         decay = rates_ref[:, lanes] * (-float(TOK))
-        states = [
-            got_ref[i, 128 + part * 16 : 144 + part * 16, :].astype(F32) for i in range(8)
-        ]
-        for j in range(8):
-            target = (j // 4) * 32 + x * 8 + z2 * 4 + j % 4
-            total = jnp.zeros((MODES, 128), F32)
-            for i in range(8):
-                source = y * 32 + (i // 2) * 8 + (i % 2) * 4 + w
-                steps = target - source - 1
-                keep = jnp.where(steps >= 0, 1.0, 0.0).astype(F32)
-                far = jnp.maximum(steps, 0).astype(F32)
-                total = total + (jnp.exp(decay * far) * keep) * states[i]
-            out_ref[j, :, lanes] = total.astype(BF)
+
+        def faded(steps):
+            return jnp.exp(decay * jnp.maximum(steps, 0).astype(F32))
+
+        before = jnp.zeros((MODES, 128), F32)
+        whole = jnp.zeros((MODES, 128), F32)
+        own = jnp.zeros((MODES, 128), F32)
+        for i, gap in enumerate(gaps):
+            state = got_ref[i, 128 + part * 16 : 144 + part * 16, :].astype(F32)
+            before = before + jnp.where(gap > 0, 1.0, 0.0).astype(F32) * faded(gap - 4) * state
+            own = own + jnp.where(gap == 0, 1.0, 0.0).astype(F32) * state
+            whole = whole + faded(gap + 28) * state
+        for other in range(4):
+            reach = faded(other - w + 3)
+            same = reach * before + jnp.where(other > w, 1.0, 0.0).astype(F32) * faded(other - w - 1) * own
+            cross = reach * whole
+            out_ref[other, :, lanes] = jnp.where(y == 0, same, 0.0).astype(BF)
+            out_ref[4 + other, :, lanes] = jnp.where(y == 0, cross, same).astype(BF)
 
 
 def far_kernel(got_ref, coeff_ref, rates_ref, near_ref, gate_ref, gain_ref, gained_ref, square_ref):
-    ahead = (lax.broadcasted_iota(jnp.int32, (TOK, 128), 0) + 1).astype(F32)
     squares = jnp.zeros((TOK, 128), F32)
     for part in range(CH // 128):
         lanes = slice(part * 128, (part + 1) * 128)
         state = got_ref[0, :, lanes].astype(F32)
         for j in range(1, 8):
             state = state + got_ref[j, :, lanes].astype(F32)
-        y = near_ref[:, lanes]
-        for n in range(MODES):
-            rate = rates_ref[n : n + 1, lanes]
-            y = y + jnp.exp(-rate * ahead) * (coeff_ref[n : n + 1, lanes] * state[n : n + 1, :])
-        gated = gate_ref[:, lanes] * y
+        tiles = expand(rates_ref[:, lanes], coeff_ref[:, lanes] * state, 1)
+        gated = gate_ref[:, lanes] * (near_ref[:, lanes] + jnp.concatenate(tiles, 0))
         gained_ref[:, lanes] = gated * gain_ref[:, lanes]
         squares = squares + gated * gated
     total = jnp.broadcast_to(jnp.sum(squares, 1, keepdims=True), (TOK, 128))
@@ -241,9 +253,7 @@
 
 def merge_kernel(place_ref, got_ref, out_ref):
     odd = place_ref[0] % 2
-    levels = jnp.concatenate(
-        [jnp.sum(got_ref[k, TOK : TOK + 16, :].astype(F32), 0, keepdims=True) for k in range(16)], 0
-    )
+    levels = jnp.sum(got_ref[:, TOK:, :].astype(F32), 1)
     levels = jnp.where(odd == 1, pltpu.roll(levels, TOK, 1), levels)
     weights = []
     for h in range(HEADS_DEV):
@@ -297,11 +307,12 @@
         state_kernel,
         [((8, 192, HEAD), BF), ((TOK, CH), F32), ((TOK, CH), F32)],
         [VMEM] * 5,
-        2000000000,
+        20000000000,
     )(features, rim, feat_weight, rates, pairs)
-    queries, sent = lax.optimization_barrier((queries, sent))
+    queries, sent, coeff = lax.optimization_barrier((queries, sent, coeff))
     got = exchange(sent, KV_GROUPS)
 
+    product, got = lax.optimization_barrier((product, got))
     (near,) = call(
         near_kernel,
         [((TOK, CH), F32)],
@@ -309,7 +320,6 @@
         2000000000,
         [pltpu.VMEM((2 * TOK, CH), F32), pltpu.VMEM((TOK, CH), F32)],
     )(product, coeff, rates, skip[None, :])
-    near, got = lax.optimization_barrier((near, got))
     other = lax.ppermute(
         got[:, :128], "context", [(s, s + devices // 2) for s in range(devices // 2)]
     )
@@ -322,7 +332,7 @@
         near_attend_kernel,
         [((HEAD, 16 * TOK), F32), ((8, 16 * TOK), F32)],
         [SMEM, VMEM, VMEM],
-        2000000000,
+        200000000,
     )(place, queries, got)
     gained, squares = call(
         far_kernel,
@@ -335,7 +345,7 @@
         far_attend_kernel,
         [((16, TOK + 16, HEAD), BF)],
         [SMEM, VMEM, VMEM, VMEM, VMEM],
-        2000000000,
+        20000000000,
     )(place, queries, other, mixed, stats)
     partial = exchange(partial, Q_GROUPS)
     (hyena_out,) = call(norm_kernel, [((TOK, CH), BF)], [VMEM] * 2, 100000000)(squares, gained)

time: 95.8 us -> 98 us (1.023)
  blocking collectives: 0 us -> 15.3 us
  waiting for transfers between devices: 27.4 us -> 21.3 us
  starting transfers between devices: 53.1 us -> 47.1 us
  Pallas kernels: 11.7 us -> 10.4 us
    all_to_all x0 -> x1, blocking collectives: none -> 15.3 us  [exchange(): lax.all_to_all(value, 'context', 0, 0, axis_index_groups=groups, tiled=True)]
    all_to_all x4 -> x3, starting transfers between devices: 37.1 us -> 29.6 us  [exchange(): lax.all_to_all(value, 'context', 0, 0, axis_index_groups=groups, tiled=True)]
    all_to_all x4 -> x3, waiting for transfers between devices: 24.3 us -> 19 us  [exchange(): lax.all_to_all(value, 'context', 0, 0, axis_index_groups=groups, tiled=True)]
    ppermute x1, starting transfers between devices: 3.27 us -> 4.83 us  [local(): lax.ppermute(features[:, TOK - (FEAT - 1):], 'context', [(s, s + 1) for s...]
  transfers between devices with their start and end apart: 7 -> 6, of which waited for: 6 -> 3; matrix products, arithmetic and copies ran while one was open for 0% -> 0% of each run, Pallas kernels for 9% -> 9%
where the time goes in v4:
time: 98 us; the launch traced here: 97.4 us
  starting transfers between devices  47.1 us (48%)
  waiting for transfers between devices  21.3 us (22%)
  blocking collectives  15.3 us (16%)
  Pallas kernels  10.4 us (11%)
  local copies, waits for them, and re-layouts  2.19 us (2%)
    all_to_all x3, starting transfers between devices, exchange(): lax.all_to_all(value, 'context', 0, 0, axis_index_groups=groups, tiled=True)  29.6 us
    all_to_all x3, waiting for transfers between devices, exchange(): lax.all_to_all(value, 'context', 0, 0, axis_index_groups=groups, tiled=True)  19 us
    all_to_all x1, blocking collectives, exchange(): lax.all_to_all(value, 'context', 0, 0, axis_index_groups=groups, tiled=True)  15.3 us
    ppermute x1, starting transfers between devices, local(): lax.ppermute(got[:, :128], 'context', [(s, s + devices // 2) for s in ran...  7.29 us
    all_to_all x1, starting transfers between devices, local(): squares = lax.all_to_all(squares, 'dp', 0, 0, tiled=True)  5.31 us
    ppermute x1, starting transfers between devices, local(): lax.ppermute(features[:, TOK - (FEAT - 1):], 'context', [(s, s + 1) for s...  4.83 us
    pallas_call x1, Pallas kernels, local(): call(far_attend_kernel, [((16, TOK + 16, HEAD), BF)], [SMEM, VMEM, VMEM,...  2.57 us
    all_to_all x1, waiting for transfers between devices, local(): squares = lax.all_to_all(squares, 'dp', 0, 0, tiled=True)  2.25 us
  transfers between devices with their start and end apart: 6, of which 3 were waited for; matrix products, arithmetic and copies ran while one was open for 0% of the time, Pallas kernels for 9%

profile of v4, /device:TPU:1, one launch (start us, length us, event | category | flops | bytes accessed | tf_op | source)
XLA Modules:
  0.0 97.4 jit_solution(14169052113793432944)
XLA Ops:
  0.6 0.0 copy-start.2
  0.6 0.8 slice.8
  1.4 4.8 %collective-permute-start = (bf16[3,2,512]{2,1,0:T(2,128)(2,1)S(1)}, bf16[3,2,512]{2,1,0:T(2,128)(2,1)S(1)}, u32[]{:S(2)}, u32[]{:S(2)}) collective-permute-start(bf16[3,2,512]{2,1,0:T(2,128)(2,1)S(1)} %slice.8), channel_id=1, source_target_pairs={{0,8},{8,16},{16,24},{24,32},{32,40},{40,48},{48,56},{56,64},{64,7... | collective-permute-start | bytes 18440 | tf_op jit(solution)/shard_map/ppermute | solution.py:283
  6.3 0.2 fusion
  6.5 0.1 pad_maximum_fusion
  6.6 0.0 copy-done.2
  6.6 0.8 shard_map.86
  7.4 0.0 copy-start
  7.4 0.0 copy-start.6
  7.4 0.0 copy-start.1
  7.4 10.9 %all-to-all-start = ((bf16[16,64,128]{2,1,0:T(8,128)(2,1)}), bf16[16,64,128]{2,1,0:T(8,128)(2,1)S(1)}, u32[]{:S(2)}, u32[]{:S(2)}) async-start(bf16[16,64,128]{2,1,0:T(8,128)(2,1)} %get-tuple-element.18), calls=%async_computation | async-start | bytes 524288 | tf_op jit(solution)/shard_map/all_to_all | solution.py:274
  18.3 0.0 copy-done
  18.3 0.0 copy-done.6
  18.4 0.0 copy-start.3
  18.4 0.0 collective-permute-done
  18.4 0.0 copy-done.1
  18.4 0.7 copy-done.3
  19.1 0.4 shard_map.87
  19.5 8.5 %all-to-all-done.q_ref = bf16[16,64,128]{2,1,0:T(8,128)(2,1)S(1)} async-done(((bf16[16,64,128]{2,1,0:T(8,128)(2,1)}), bf16[16,64,128]{2,1,0:T(8,128)(2,1)S(1)}, u32[]{:S(2)}, u32[]{:S(2)}) %all-to-all-start) | async-done | bytes 262176 | tf_op jit(solution)/shard_map/all_to_all | solution.py:274
  28.0 15.3 %all_to_all.31.got_ref.own_ref = bf16[8,192,128]{2,1,0:T(8,128)(2,1)S(1)} all-to-all(bf16[8,192,128]{2,1,0:T(8,128)(2,1)S(1)} %get-tuple-element.20), channel_id=1, replica_groups={{0,32,64,96,128,160,192,224},{8,40,72,104,136,168,200,232},{16,48,80,11..., dimensions={0} | all-to-all | bytes 786432 | tf_op jit(solution)/shard_map/all_to_all | solution.py:274
  43.3 0.9 shard_map.88
  44.2 13.8 %all-to-all-start.2 = ((bf16[8,16,512]{2,1,0:T(8,128)(2,1)}), bf16[8,16,512]{2,1,0:T(8,128)(2,1)S(1)}, u32[]{:S(2)}, u32[]{:S(2)}) async-start(bf16[8,16,512]{2,1,0:T(8,128)(2,1)} %shard_map.88), calls=%async_computation.2 | async-start | bytes 262144 | tf_op jit(solution)/shard_map/all_to_all | solution.py:274
  58.0 0.0 copy-start.4
  58.0 7.3 %collective-permute-start.1 = (bf16[8,128,128]{2,1,0:T(8,128)(2,1)S(1)}, bf16[8,128,128]{2,1,0:T(8,128)(2,1)S(1)}, u32[]{:S(2)}, u32[]{:S(2)}) collective-permute-start(bf16[8,128,128]{2,1,0:T(8,128)(2,1)S(1)} %slice.7), channel_id=1, source_target_pairs={{0,256},{8,264},{16,272},{24,280},{32,288},{40,296},{48,304},{56,3... | collective-permute-start | bytes 786440 | tf_op jit(solution)/shard_map/ppermute | solution.py:323
  65.3 1.8 %shard_map.92 = (f32[128,1024]{1,0:T(8,128)S(1)}, f32[8,1024]{1,0:T(8,128)S(1)}) custom-call(s32[1]{0:T(128)} %bitcast.place_ref, bf16[16,64,128]{2,1,0:T(8,128)(2,1)S(1)} %all-to-all-done.q_ref, bf16[8,192,128]{2,1,0:T(8,128)(2,1)S(1)} %all_to_all.31.got_ref.own_ref), custom_call_target="tpu_custom_call" | custom-call | flops 200000000 | bytes 1000 | tf_op jit(solution)/shard_map/pallas_call | solution.py:331
  67.1 0.0 copy-done.4
  67.1 1.1 %shard_map.89.near_ref = f32[64,512]{1,0:T(8,128)S(1)} custom-call(f32[64,512]{1,0:T(8,128)S(1)} %get-tuple-element.23.prod_ref, f32[16,512]{1,0:T(8,128)S(1)} %sqrt_multiply_fusion.coeff_ref, f32[16,512]{1,0:T(8,128)S(1)} %copy-done, f32[1,512]{1,0:T(1,128)S(1)} %bitcast.13), custom_call_target="tpu_custom_call" | custom-call | flops 2000000000 | bytes 1000 | tf_op jit(solution)/shard_map/pallas_call | solution.py:316
  68.2 0.0 copy-start.5
  68.2 0.0 all-to-all-done.2.got_ref
  68.3 0.7 copy-done.5
  68.9 1.0 %shard_map.90 = (f32[64,512]{1,0:T(8,128)S(1)}, f32[8,128]{1,0:T(8,128)}) custom-call(bf16[8,16,512]{2,1,0:T(8,128)(2,1)S(1)} %all-to-all-done.2.got_ref, f32[16,512]{1,0:T(8,128)S(1)} %sqrt_multiply_fusion.coeff_ref, f32[16,512]{1,0:T(8,128)S(1)} %copy-done, f32[64,512]{1,0:T(8,128)S(1)} %shard_map.89.near_ref, f32[64,512]{1,0:T(8,128)S(1)} %get-tuple-element.24.gate_ref, ...), custom_call_target="tpu_custom_call" | custom-call | flops 1000000000 | bytes 1000 | tf_op jit(solution)/shard_map/pallas_call | solution.py:337
  70.0 5.3 %all-to-all-start.3 = ((f32[8,1,128]{2,1,0:T(1,128)}), f32[8,1,128]{2,1,0:T(1,128)S(1)}, u32[]{:S(2)}, u32[]{:S(2)}) async-start(f32[8,1,128]{2,1,0:T(1,128)} %bitcast.6), calls=%async_computation.3 | async-start | bytes 8192 | tf_op jit(solution)/shard_map/all_to_all | solution.py:343
  75.3 0.0 collective-permute-done.1.other_ref
  75.3 2.6 %shard_map.93 = bf16[16,80,128]{2,1,0:T(8,128)(2,1)} custom-call(s32[1]{0:T(128)} %bitcast.place_ref, bf16[16,64,128]{2,1,0:T(8,128)(2,1)S(1)} %all-to-all-done.q_ref, bf16[8,128,128]{2,1,0:T(8,128)(2,1)S(1)} %collective-permute-done.1.other_ref, f32[128,1024]{1,0:T(8,128)S(1)} %get-tuple-element.28.mixed_ref, f32[8,1024]{1,0:T(8,128)S(1)} %get-tuple-element.29.stats_ref), custom_call_target="tpu_custom_call" | custom-call | flops 20000000000 | bytes 1000 | tf_op jit(solution)/shard_map/pallas_call | solution.py:344
  77.8 2.2 %all-to-all-done.3 = f32[8,1,128]{2,1,0:T(1,128)S(1)} async-done(((f32[8,1,128]{2,1,0:T(1,128)}), f32[8,1,128]{2,1,0:T(1,128)S(1)}, u32[]{:S(2)}, u32[]{:S(2)}) %all-to-all-start.3) | async-done | bytes 4128 | tf_op jit(solution)/shard_map/all_to_all | solution.py:343
  80.1 5.0 %all-to-all-start.4 = ((bf16[16,80,128]{2,1,0:T(8,128)(2,1)}), bf16[16,80,128]{2,1,0:T(8,128)(2,1)S(1)}, u32[]{:S(2)}, u32[]{:S(2)}) async-start(bf16[16,80,128]{2,1,0:T(8,128)(2,1)} %shard_map.93), calls=%async_computation.4 | async-start | bytes 655360 | tf_op jit(solution)/shard_map/all_to_all | solution.py:274
  85.1 0.7 shard_map.91
  85.8 10.5 %all-to-all-done.4.got_ref = bf16[16,80,128]{2,1,0:T(8,128)(2,1)S(1)} async-done(((bf16[16,80,128]{2,1,0:T(8,128)(2,1)}), bf16[16,80,128]{2,1,0:T(8,128)(2,1)S(1)}, u32[]{:S(2)}, u32[]{:S(2)}) %all-to-all-start.4) | async-done | bytes 327712 | tf_op jit(solution)/shard_map/all_to_all | solution.py:274
  96.3 1.1 %shard_map.94 = bf16[64,512]{1,0:T(8,128)(2,1)} custom-call(s32[1]{0:T(128)} %bitcast.place_ref, bf16[16,80,128]{2,1,0:T(8,128)(2,1)S(1)} %all-to-all-done.4.got_ref), custom_call_target="tpu_custom_call" | custom-call | flops 1000000000 | bytes 1000 | tf_op jit(solution)/shard_map/pallas_call | solution.py:352
  (5 shorter events, 0.1 us)
Async XLA Ops:
  0.6 6.0 %copy-start.2 = (bf16[64,3,512]{2,0,1:T(8,128)(2,1)S(1)}, bf16[64,3,512]{2,0,1:T(8,128)(2,1)}, u32[]{:S(2)}) copy-start(bf16[64,3,512]{2,0,1:T(8,128)(2,1)} %param.13) | copy-start | bytes 589828
  1.4 16.9 %collective-permute-start = (bf16[3,2,512]{2,1,0:T(2,128)(2,1)S(1)}, bf16[3,2,512]{2,1,0:T(2,128)(2,1)S(1)}, u32[]{:S(2)}, u32[]{:S(2)}) collective-permute-start(bf16[3,2,512]{2,1,0:T(2,128)(2,1)S(1)} %slice.8), channel_id=1, source_target_pairs={{0,8},{8,16},{16,24},{24,32},{32,40},{40,48},{48,56},{56,64},{64,7... | collective-permute-start | bytes 18440 | tf_op jit(solution)/shard_map/ppermute | solution.py:283
  7.4 10.9 %copy-start = (f32[16,512]{1,0:T(8,128)S(1)}, f32[16,512]{1,0:T(8,128)}, u32[]{:S(2)}) copy-start(f32[16,512]{1,0:T(8,128)} %rates_ref.7) | copy-start | bytes 98308
  7.4 10.9 %copy-start.6 = (f32[16,512]{1,0:T(8,128)S(1)}, f32[16,512]{1,0:T(8,128)}, u32[]{:S(2)}) copy-start(f32[16,512]{1,0:T(8,128)} %param.10) | copy-start | bytes 98308
  7.4 11.0 %copy-start.1 = (bf16[64,3,512]{2,0,1:T(8,128)(2,1)S(1)}, bf16[64,3,512]{2,0,1:T(8,128)(2,1)}, u32[]{:S(2)}) copy-start(bf16[64,3,512]{2,0,1:T(8,128)(2,1)} %param.7) | copy-start | bytes 589828
  7.4 20.6 %all-to-all-start = ((bf16[16,64,128]{2,1,0:T(8,128)(2,1)}), bf16[16,64,128]{2,1,0:T(8,128)(2,1)S(1)}, u32[]{:S(2)}, u32[]{:S(2)}) async-start(bf16[16,64,128]{2,1,0:T(8,128)(2,1)} %get-tuple-element.18), calls=%async_computation | async-start | bytes 524288 | tf_op jit(solution)/shard_map/all_to_all | solution.py:274
  18.4 0.7 copy-start.3
  44.2 24.1 %all-to-all-start.2 = ((bf16[8,16,512]{2,1,0:T(8,128)(2,1)}), bf16[8,16,512]{2,1,0:T(8,128)(2,1)S(1)}, u32[]{:S(2)}, u32[]{:S(2)}) async-start(bf16[8,16,512]{2,1,0:T(8,128)(2,1)} %shard_map.88), calls=%async_computation.2 | async-start | bytes 262144 | tf_op jit(solution)/shard_map/all_to_all | solution.py:274
  58.0 9.1 %copy-start.4 = (f32[512]{0:T(512)S(1)}, f32[512]{0:T(512)}, u32[]{:S(2)}) copy-start(f32[512]{0:T(512)} %param.9) | copy-start | bytes 6148
  58.0 17.3 %collective-permute-start.1 = (bf16[8,128,128]{2,1,0:T(8,128)(2,1)S(1)}, bf16[8,128,128]{2,1,0:T(8,128)(2,1)S(1)}, u32[]{:S(2)}, u32[]{:S(2)}) collective-permute-start(bf16[8,128,128]{2,1,0:T(8,128)(2,1)S(1)} %slice.7), channel_id=1, source_target_pairs={{0,256},{8,264},{16,272},{24,280},{32,288},{40,296},{48,304},{56,3... | collective-permute-start | bytes 786440 | tf_op jit(solution)/shard_map/ppermute | solution.py:323
  68.2 0.7 copy-start.5
  70.0 10.1 %all-to-all-start.3 = ((f32[8,1,128]{2,1,0:T(1,128)}), f32[8,1,128]{2,1,0:T(1,128)S(1)}, u32[]{:S(2)}, u32[]{:S(2)}) async-start(f32[8,1,128]{2,1,0:T(1,128)} %bitcast.6), calls=%async_computation.3 | async-start | bytes 8192 | tf_op jit(solution)/shard_map/all_to_all | solution.py:343
  80.1 16.3 %all-to-all-start.4 = ((bf16[16,80,128]{2,1,0:T(8,128)(2,1)}), bf16[16,80,128]{2,1,0:T(8,128)(2,1)S(1)}, u32[]{:S(2)}, u32[]{:S(2)}) async-start(bf16[16,80,128]{2,1,0:T(8,128)(2,1)} %shard_map.93), calls=%async_computation.4 | async-start | bytes 655360 | tf_op jit(solution)/shard_map/all_to_all | solution.py:274

commit v5 on v4

--- a/solution.py
+++ b/solution.py
@@ -40,7 +40,6 @@
 
 Q_GROUPS = groups_over("x", "w")
 KV_GROUPS = groups_over("x", "z2")
-STATE_GROUPS = groups_over("y", "w")
 
 VMEM = pl.BlockSpec(memory_space=pltpu.VMEM)
 SMEM = pl.BlockSpec(memory_space=pltpu.SMEM)
@@ -132,39 +131,41 @@
         out_ref[:, lanes] = y
 
 
-def message_kernel(place_ref, got_ref, rates_ref, out_ref):
-    y, x, z2, w = digits(place_ref[0])
-    gaps = [8 * (x - i // 2) + 4 * (z2 - i % 2) for i in range(8)]
-    for part in range(CH // 128):
-        lanes = slice(part * 128, (part + 1) * 128)
-        decay = rates_ref[:, lanes] * (-float(TOK))
-
-        def faded(steps):
-            return jnp.exp(decay * jnp.maximum(steps, 0).astype(F32))
-
+def write_messages(index, own_ref, other_ref, rates_ref, out_ref):
+    y, x, z2, w = digits(index)
+    rows = pl.ds(pl.multiple_of(128 + x * 16, 16), 16)
+    decay = rates_ref[x] * (-float(TOK))
+    second = jnp.where(y == 1, 1.0, 0.0).astype(F32)
+
+    def faded(steps):
+        return jnp.exp(decay * jnp.maximum(steps, 0).astype(F32))
+
+    def when(condition):
+        return jnp.where(condition, 1.0, 0.0).astype(F32)
+
+    own_states = [own_ref[i, rows, :].astype(F32) for i in range(8)]
+    other_states = [other_ref[i, rows, :].astype(F32) * second for i in range(8)]
+    reach = [faded(wt - w + 3) for wt in range(4)]
+    step = [faded(wt - w - 1) * when(wt > w) for wt in range(4)]
+    for xt in range(4):
         before = jnp.zeros((MODES, 128), F32)
-        whole = jnp.zeros((MODES, 128), F32)
         own = jnp.zeros((MODES, 128), F32)
-        for i, gap in enumerate(gaps):
-            state = got_ref[i, 128 + part * 16 : 144 + part * 16, :].astype(F32)
-            before = before + jnp.where(gap > 0, 1.0, 0.0).astype(F32) * faded(gap - 4) * state
-            own = own + jnp.where(gap == 0, 1.0, 0.0).astype(F32) * state
-            whole = whole + faded(gap + 28) * state
-        for other in range(4):
-            reach = faded(other - w + 3)
-            same = reach * before + jnp.where(other > w, 1.0, 0.0).astype(F32) * faded(other - w - 1) * own
-            cross = reach * whole
-            out_ref[other, :, lanes] = jnp.where(y == 0, same, 0.0).astype(BF)
-            out_ref[4 + other, :, lanes] = jnp.where(y == 0, cross, same).astype(BF)
+        for i in range(8):
+            gap = 8 * (xt - i // 2) + 4 * (z2 - i % 2)
+            before = before + when(gap > 0) * faded(gap - 4) * own_states[i]
+            before = before + faded(gap + 28) * other_states[i]
+            own = own + when(gap == 0) * own_states[i]
+        for wt in range(4):
+            out_ref[xt * 4 + wt, 80:96, :] = (reach[wt] * before + step[wt] * own).astype(BF)
 
 
 def far_kernel(got_ref, coeff_ref, rates_ref, near_ref, gate_ref, gain_ref, gained_ref, square_ref):
     squares = jnp.zeros((TOK, 128), F32)
     for part in range(CH // 128):
         lanes = slice(part * 128, (part + 1) * 128)
-        state = got_ref[0, :, lanes].astype(F32)
-        for j in range(1, 8):
-            state = state + got_ref[j, :, lanes].astype(F32)
+        state = got_ref[part * 4, 80:96, :].astype(F32)
+        for j in range(1, 4):
+            state = state + got_ref[part * 4 + j, 80:96, :].astype(F32)
         tiles = expand(rates_ref[:, lanes], coeff_ref[:, lanes] * state, 1)
         gated = gate_ref[:, lanes] * (near_ref[:, lanes] + jnp.concatenate(tiles, 0))
         gained_ref[:, lanes] = gated * gain_ref[:, lanes]
@@ -218,10 +219,13 @@
         stats_ref[1:2, lanes] = total
 
 
-def far_attend_kernel(place_ref, q_ref, other_ref, mixed_ref, stats_ref, out_ref):
+def far_attend_kernel(
+    place_ref, q_ref, own_ref, other_ref, mixed_ref, stats_ref, rates_ref, out_ref
+):
     bias = jnp.where(digits(place_ref[0])[0] == 1, 0.0, NEG).astype(F32)
     keys = other_ref[:, :TOK, :].reshape(8 * TOK, HEAD)
-    values = other_ref[:, TOK:, :].reshape(8 * TOK, HEAD)
+    values = other_ref[:, TOK:128, :].reshape(8 * TOK, HEAD)
+    write_messages(place_ref[0], own_ref, other_ref, rates_ref, out_ref)
     which = lax.broadcasted_iota(jnp.int32, (16, 128), 0)
     for tile in range(16 * TOK // WIDE):
         lanes = slice(tile * WIDE, (tile + 1) * WIDE)
@@ -248,12 +252,12 @@
                 high[:, part],
                 jnp.where(which == 1, middle[:, part], jnp.where(which == 2, last[:, part], 0.0)),
             )
-            out_ref[place, TOK:, :] = stats.astype(BF)
+            out_ref[place, TOK:80, :] = stats.astype(BF)
 
 
 def merge_kernel(place_ref, got_ref, out_ref):
     odd = place_ref[0] % 2
-    levels = jnp.sum(got_ref[:, TOK:, :].astype(F32), 1)
+    levels = jnp.sum(got_ref[:, TOK:80, :].astype(F32), 1)
     levels = jnp.where(odd == 1, pltpu.roll(levels, TOK, 1), levels)
     weights = []
     for h in range(HEADS_DEV):
@@ -309,47 +313,45 @@
         [VMEM] * 5,
         20000000000,
     )(features, rim, feat_weight, rates, pairs)
-    queries, sent, coeff = lax.optimization_barrier((queries, sent, coeff))
+    quarters = jnp.transpose(rates.reshape(MODES, CH // 128, 128), (1, 0, 2))
+    queries, sent, coeff, quarters, skip, gain = lax.optimization_barrier(
+        (queries, sent, coeff, quarters, skip[None, :], norm_gain[None, :])
+    )
     got = exchange(sent, KV_GROUPS)
-
     product, got = lax.optimization_barrier((product, got))
-    (near,) = call(
-        near_kernel,
-        [((TOK, CH), F32)],
-        [VMEM] * 4,
-        2000000000,
-        [pltpu.VMEM((2 * TOK, CH), F32), pltpu.VMEM((TOK, CH), F32)],
-    )(product, coeff, rates, skip[None, :])
-    other = lax.ppermute(
-        got[:, :128], "context", [(s, s + devices // 2) for s in range(devices // 2)]
-    )
-    (messages,) = call(
-        message_kernel, [((8, MODES, CH), BF)], [SMEM, VMEM, VMEM], 1000000000
-    )(place, got, rates)
-    arrived = exchange(messages, STATE_GROUPS)
-
+
+    other = lax.ppermute(got, "context", [(s, s + devices // 2) for s in range(devices // 2)])
     mixed, stats = call(
         near_attend_kernel,
         [((HEAD, 16 * TOK), F32), ((8, 16 * TOK), F32)],
         [SMEM, VMEM, VMEM],
         200000000,
     )(place, queries, got)
+    (near,) = call(
+        near_kernel,
+        [((TOK, CH), F32)],
+        [VMEM] * 4,
+        200000000,
+        [pltpu.VMEM((2 * TOK, CH), F32), pltpu.VMEM((TOK, CH), F32)],
+    )(product, coeff, rates, skip)
+    near, other = lax.optimization_barrier((near, other))
+    (partial,) = call(
+        far_attend_kernel,
+        [((16, TOK + 32, HEAD), BF)],
+        [SMEM] + [VMEM] * 6,
+        20000000000,
+    )(place, queries, got, other, mixed, stats, quarters)
+    partial = exchange(partial, Q_GROUPS)
+
     gained, squares = call(
         far_kernel,
         [((TOK, CH), F32), ((8, 128), F32)],
         [VMEM] * 6,
         1000000000,
-    )(arrived, coeff, rates, near, gate, norm_gain[None, :])
+    )(partial, coeff, rates, near, gate, gain)
     squares = lax.all_to_all(squares, "dp", 0, 0, tiled=True)
-    (partial,) = call(
-        far_attend_kernel,
-        [((16, TOK + 16, HEAD), BF)],
-        [SMEM, VMEM, VMEM, VMEM, VMEM],
-        20000000000,
-    )(place, queries, other, mixed, stats)
-    partial = exchange(partial, Q_GROUPS)
+    (attn_out,) = call(merge_kernel, [((TOK, CH), BF)], [SMEM, VMEM], 1000000000)(place, partial)
     (hyena_out,) = call(norm_kernel, [((TOK, CH), BF)], [VMEM] * 2, 100000000)(squares, gained)
-    (attn_out,) = call(merge_kernel, [((TOK, CH), BF)], [SMEM, VMEM], 1000000000)(place, partial)
     return (hyena_out, attn_out)
 
 

time: 98 us -> 102 us (1.041)
  blocking collectives: 15.3 us -> 38.4 us
  starting transfers between devices: 47.1 us -> 37.8 us
  waiting for transfers between devices: 21.3 us -> 13.7 us
  Pallas kernels: 10.4 us -> 8.83 us
    all_to_all x1 -> x2, blocking collectives: 15.3 us -> 38.4 us  [exchange(): lax.all_to_all(value, 'context', 0, 0, axis_index_groups=groups, tiled=True)]
    all_to_all x3 -> x1, starting transfers between devices: 29.6 us -> 10.9 us  [exchange(): lax.all_to_all(value, 'context', 0, 0, axis_index_groups=groups, tiled=True)]
    all_to_all x3 -> x1, waiting for transfers between devices: 19 us -> 8.31 us  [exchange(): lax.all_to_all(value, 'context', 0, 0, axis_index_groups=groups, tiled=True)]
    all_to_all x1, starting transfers between devices: 5.31 us -> 14.6 us  [local(): squares = lax.all_to_all(squares, 'dp', 0, 0, tiled=True)]
    ppermute x1, waiting for transfers between devices: 0.01 us -> 1.71 us  [local(): lax.ppermute(got, 'context', [(s, s + devices // 2) for s in range(device...]
    pallas_call x3 -> x2, Pallas kernels: 4.55 us -> 2.98 us  [the longest x1 1.85 us: local(): call(far_attend_kernel, [((16, TOK + 32, HEAD), BF)], [SMEM] + [VMEM] * 6...]
    all_to_all x1, waiting for transfers between devices: 2.25 us -> 3.73 us  [local(): squares = lax.all_to_all(squares, 'dp', 0, 0, tiled=True)]
  transfers between devices with their start and end apart: 6 -> 4, of which waited for: 3 -> 3; matrix products, arithmetic and copies ran while one was open for 0% -> 0% of each run, Pallas kernels for 9% -> 5%
where the time goes in v5:
time: 102 us
  blocking collectives  38.4 us (38%)
  starting transfers between devices  37.8 us (37%)
  waiting for transfers between devices  13.7 us (13%)
  Pallas kernels  8.83 us (9%)
  local copies, waits for them, and re-layouts  1.65 us (2%)
    all_to_all x2, blocking collectives, exchange(): lax.all_to_all(value, 'context', 0, 0, axis_index_groups=groups, tiled=True)  38.4 us
    all_to_all x1, starting transfers between devices, local(): squares = lax.all_to_all(squares, 'dp', 0, 0, tiled=True)  14.6 us
    all_to_all x1, starting transfers between devices, exchange(): lax.all_to_all(value, 'context', 0, 0, axis_index_groups=groups, tiled=True)  10.9 us
    all_to_all x1, waiting for transfers between devices, exchange(): lax.all_to_all(value, 'context', 0, 0, axis_index_groups=groups, tiled=True)  8.31 us
    ppermute x1, starting transfers between devices, local(): lax.ppermute(got, 'context', [(s, s + devices // 2) for s in range(device...  7.46 us
    ppermute x1, starting transfers between devices, local(): lax.ppermute(features[:, TOK - (FEAT - 1):], 'context', [(s, s + 1) for s...  4.83 us
    all_to_all x1, waiting for transfers between devices, local(): squares = lax.all_to_all(squares, 'dp', 0, 0, tiled=True)  3.73 us
  transfers between devices with their start and end apart: 4, of which 3 were waited for; matrix products, arithmetic and copies ran while one was open for 0% of the time, Pallas kernels for 5%

profile of v5, /device:TPU:1, one launch (start us, length us, event | category | flops | bytes accessed | tf_op | source)
XLA Modules:
  0.0 101.6 jit_solution(12515398472588805802)
XLA Ops:
  0.6 0.0 copy-start.2
  0.6 0.8 slice.4
  1.4 4.8 %collective-permute-start = (bf16[3,2,512]{2,1,0:T(2,128)(2,1)S(1)}, bf16[3,2,512]{2,1,0:T(2,128)(2,1)S(1)}, u32[]{:S(2)}, u32[]{:S(2)}) collective-permute-start(bf16[3,2,512]{2,1,0:T(2,128)(2,1)S(1)} %slice.4), channel_id=1, source_target_pairs={{0,8},{8,16},{16,24},{24,32},{32,40},{40,48},{48,56},{56,64},{64,7... | collective-permute-start | bytes 18440 | tf_op jit(solution)/shard_map/ppermute | solution.py:287
  6.3 0.2 fusion
  6.5 0.1 pad_maximum_fusion
  6.6 0.0 copy-done.2
  6.6 0.8 shard_map.86
  7.4 0.0 copy-start
  7.4 0.0 copy-start.6
  7.4 0.0 copy-start.3
  7.4 10.9 %all-to-all-start = ((bf16[16,64,128]{2,1,0:T(8,128)(2,1)}), bf16[16,64,128]{2,1,0:T(8,128)(2,1)S(1)}, u32[]{:S(2)}, u32[]{:S(2)}) async-start(bf16[16,64,128]{2,1,0:T(8,128)(2,1)} %get-tuple-element.21), calls=%async_computation | async-start | bytes 524288 | tf_op jit(solution)/shard_map/all_to_all | solution.py:278
  18.3 0.0 copy-done
  18.3 0.0 copy-done.6
  18.3 0.0 copy-start.1
  18.4 0.0 collective-permute-done
  18.4 0.0 copy-done.3
  18.4 0.8 copy-done.1
  19.3 0.4 shard_map.87
  19.7 8.3 %all-to-all-done.q_ref = bf16[16,64,128]{2,1,0:T(8,128)(2,1)S(1)} async-done(((bf16[16,64,128]{2,1,0:T(8,128)(2,1)}), bf16[16,64,128]{2,1,0:T(8,128)(2,1)S(1)}, u32[]{:S(2)}, u32[]{:S(2)}) %all-to-all-start) | async-done | bytes 262176 | tf_op jit(solution)/shard_map/all_to_all | solution.py:278
  28.0 15.3 %all_to_all.26.own_ref = bf16[8,192,128]{2,1,0:T(8,128)(2,1)S(1)} all-to-all(bf16[8,192,128]{2,1,0:T(8,128)(2,1)S(1)} %get-tuple-element.26), channel_id=1, replica_groups={{0,32,64,96,128,160,192,224},{8,40,72,104,136,168,200,232},{16,48,80,11..., dimensions={0} | all-to-all | bytes 786432 | tf_op jit(solution)/shard_map/all_to_all | solution.py:278
  43.3 7.5 %collective-permute-start.1 = (bf16[8,192,128]{2,1,0:T(8,128)(2,1)S(1)}, bf16[8,192,128]{2,1,0:T(8,128)(2,1)S(1)}, u32[]{:S(2)}, u32[]{:S(2)}) collective-permute-start(bf16[8,192,128]{2,1,0:T(8,128)(2,1)S(1)} %all_to_all.26.own_ref), channel_id=1, source_target_pairs={{0,256},{8,264},{16,272},{24,280},{32,288},{40,296},{48,304},{56,3... | collective-permute-start | bytes 1179656 | tf_op jit(solution)/shard_map/ppermute | solution.py:323
  50.8 0.0 copy-start.4
  50.8 1.8 %shard_map.89 = (f32[128,1024]{1,0:T(8,128)S(1)}, f32[8,1024]{1,0:T(8,128)S(1)}) custom-call(s32[1]{0:T(128)} %bitcast.place_ref, bf16[16,64,128]{2,1,0:T(8,128)(2,1)S(1)} %all-to-all-done.q_ref, bf16[8,192,128]{2,1,0:T(8,128)(2,1)S(1)} %all_to_all.26.own_ref), custom_call_target="tpu_custom_call" | custom-call | flops 200000000 | bytes 1000 | tf_op jit(solution)/shard_map/pallas_call | solution.py:324
  52.6 0.0 copy-done.4
  52.6 1.1 %shard_map.88.near_ref = f32[64,512]{1,0:T(8,128)S(1)} custom-call(f32[64,512]{1,0:T(8,128)S(1)} %get-tuple-element.28.prod_ref, f32[16,512]{1,0:T(8,128)S(1)} %sqrt_multiply_fusion.coeff_ref, f32[16,512]{1,0:T(8,128)S(1)} %copy-done, f32[1,512]{1,0:T(1,128)S(1)} %bitcast.20), custom_call_target="tpu_custom_call" | custom-call | flops 200000000 | bytes 1000 | tf_op jit(solution)/shard_map/pallas_call | solution.py:330
  53.8 1.7 %collective-permute-done.1.other_ref = bf16[8,192,128]{2,1,0:T(8,128)(2,1)S(1)} collective-permute-done((bf16[8,192,128]{2,1,0:T(8,128)(2,1)S(1)}, bf16[8,192,128]{2,1,0:T(8,128)(2,1)S(1)}, u32[]{:S(2)}, u32[]{:S(2)}) %collective-permute-start.1) | collective-permute-done | bytes 393248 | tf_op jit(solution)/shard_map/ppermute | solution.py:323
  55.5 1.9 %shard_map.90 = bf16[16,96,128]{2,1,0:T(8,128)(2,1)S(1)} custom-call(s32[1]{0:T(128)} %bitcast.place_ref, bf16[16,64,128]{2,1,0:T(8,128)(2,1)S(1)} %all-to-all-done.q_ref, bf16[8,192,128]{2,1,0:T(8,128)(2,1)S(1)} %all_to_all.26.own_ref, bf16[8,192,128]{2,1,0:T(8,128)(2,1)S(1)} %collective-permute-done.1.other_ref, ...), custom_call_target="tpu_custom_call" | custom-call | flops 20000000000 | bytes 1000 | tf_op jit(solution)/shard_map/pallas_call | solution.py:338
  57.3 0.0 copy-start.5
  57.3 23.1 %all_to_all.27.got_ref = bf16[16,96,128]{2,1,0:T(8,128)(2,1)S(1)} all-to-all(bf16[16,96,128]{2,1,0:T(8,128)(2,1)S(1)} %shard_map.90), channel_id=1, replica_groups={{0,8,16,24,64,72,80,88,128,136,144,152,192,200,208,216},{32,40,48,56,96..., dimensions={0} | all-to-all | bytes 786432 | tf_op jit(solution)/shard_map/all_to_all | solution.py:278
  80.4 0.0 copy-done.5
  80.4 1.0 %shard_map.91 = (f32[64,512]{1,0:T(8,128)S(1)}, f32[8,128]{1,0:T(8,128)}) custom-call(bf16[16,96,128]{2,1,0:T(8,128)(2,1)S(1)} %all_to_all.27.got_ref, f32[16,512]{1,0:T(8,128)S(1)} %sqrt_multiply_fusion.coeff_ref, f32[16,512]{1,0:T(8,128)S(1)} %copy-done, f32[64,512]{1,0:T(8,128)S(1)} %shard_map.88.near_ref, f32[64,512]{1,0:T(8,128)S(1)} %get-tuple-element.36.gate_ref, ...), custom_call_target="tpu_custom_call" | custom-call | flops 1000000000 | bytes 1000 | tf_op jit(solution)/shard_map/pallas_call | solution.py:346
  81.5 14.6 %all-to-all-start.3 = ((f32[8,1,128]{2,1,0:T(1,128)}), f32[8,1,128]{2,1,0:T(1,128)S(1)}, u32[]{:S(2)}, u32[]{:S(2)}) async-start(f32[8,1,128]{2,1,0:T(1,128)} %bitcast.7), calls=%async_computation.3 | async-start | bytes 8192 | tf_op jit(solution)/shard_map/all_to_all | solution.py:352
  96.1 1.1 %shard_map.93 = bf16[64,512]{1,0:T(8,128)(2,1)} custom-call(s32[1]{0:T(128)} %bitcast.place_ref, bf16[16,96,128]{2,1,0:T(8,128)(2,1)S(1)} %all_to_all.27.got_ref), custom_call_target="tpu_custom_call" | custom-call | flops 1000000000 | bytes 1000 | tf_op jit(solution)/shard_map/pallas_call | solution.py:353
  97.1 3.7 %all-to-all-done.3 = f32[8,1,128]{2,1,0:T(1,128)S(1)} async-done(((f32[8,1,128]{2,1,0:T(1,128)}), f32[8,1,128]{2,1,0:T(1,128)S(1)}, u32[]{:S(2)}, u32[]{:S(2)}) %all-to-all-start.3) | async-done | bytes 4128 | tf_op jit(solution)/shard_map/all_to_all | solution.py:352
  100.9 0.7 shard_map.92
  (5 shorter events, 0.1 us)
Async XLA Ops:
  0.6 6.0 %copy-start.2 = (bf16[64,3,512]{2,0,1:T(8,128)(2,1)S(1)}, bf16[64,3,512]{2,0,1:T(8,128)(2,1)}, u32[]{:S(2)}) copy-start(bf16[64,3,512]{2,0,1:T(8,128)(2,1)} %param.13) | copy-start | bytes 589828
  1.4 17.0 %collective-permute-start = (bf16[3,2,512]{2,1,0:T(2,128)(2,1)S(1)}, bf16[3,2,512]{2,1,0:T(2,128)(2,1)S(1)}, u32[]{:S(2)}, u32[]{:S(2)}) collective-permute-start(bf16[3,2,512]{2,1,0:T(2,128)(2,1)S(1)} %slice.4), channel_id=1, source_target_pairs={{0,8},{8,16},{16,24},{24,32},{32,40},{40,48},{48,56},{56,64},{64,7... | collective-permute-start | bytes 18440 | tf_op jit(solution)/shard_map/ppermute | solution.py:287
  7.4 10.9 %copy-start = (f32[16,512]{1,0:T(8,128)S(1)}, f32[16,512]{1,0:T(8,128)}, u32[]{:S(2)}) copy-start(f32[16,512]{1,0:T(8,128)} %rates_ref.5) | copy-start | bytes 98308
  7.4 10.9 %copy-start.6 = (f32[16,512]{1,0:T(8,128)S(1)}, f32[16,512]{1,0:T(8,128)}, u32[]{:S(2)}) copy-start(f32[16,512]{1,0:T(8,128)} %param.10) | copy-start | bytes 98308
  7.4 11.0 %copy-start.3 = (f32[3,3,512]{2,1,0:T(4,128)S(1)}, f32[3,3,512]{2,1,0:T(4,128)}, u32[]{:S(2)}) copy-start(f32[3,3,512]{2,1,0:T(4,128)} %weight_ref.1) | copy-start | bytes 55300
  7.4 20.6 %all-to-all-start = ((bf16[16,64,128]{2,1,0:T(8,128)(2,1)}), bf16[16,64,128]{2,1,0:T(8,128)(2,1)S(1)}, u32[]{:S(2)}, u32[]{:S(2)}) async-start(bf16[16,64,128]{2,1,0:T(8,128)(2,1)} %get-tuple-element.21), calls=%async_computation | async-start | bytes 524288 | tf_op jit(solution)/shard_map/all_to_all | solution.py:278
  18.3 0.9 copy-start.1
  43.3 12.1 %collective-permute-start.1 = (bf16[8,192,128]{2,1,0:T(8,128)(2,1)S(1)}, bf16[8,192,128]{2,1,0:T(8,128)(2,1)S(1)}, u32[]{:S(2)}, u32[]{:S(2)}) collective-permute-start(bf16[8,192,128]{2,1,0:T(8,128)(2,1)S(1)} %all_to_all.26.own_ref), channel_id=1, source_target_pairs={{0,256},{8,264},{16,272},{24,280},{32,288},{40,296},{48,304},{56,3... | collective-permute-start | bytes 1179656 | tf_op jit(solution)/shard_map/ppermute | solution.py:323
  50.8 1.8 %copy-start.4 = (f32[512]{0:T(512)S(1)}, f32[512]{0:T(512)}, u32[]{:S(2)}) copy-start(f32[512]{0:T(512)} %param.9) | copy-start | bytes 6148
  57.3 23.1 %copy-start.5 = (f32[512]{0:T(512)S(1)}, f32[512]{0:T(512)}, u32[]{:S(2)}) copy-start(f32[512]{0:T(512)} %param.12) | copy-start | bytes 6148
  81.5 19.4 %all-to-all-start.3 = ((f32[8,1,128]{2,1,0:T(1,128)}), f32[8,1,128]{2,1,0:T(1,128)S(1)}, u32[]{:S(2)}, u32[]{:S(2)}) async-start(f32[8,1,128]{2,1,0:T(1,128)} %bitcast.7), calls=%async_computation.3 | async-start | bytes 8192 | tf_op jit(solution)/shard_map/all_to_all | solution.py:352

commit v6 on v5

--- a/solution.py
+++ b/solution.py
@@ -18,12 +18,13 @@
 CH = 512
 ROPE_BASE = 1000000.0
 NEG = -1e30
+PACK = 2 * TOK + MODES
 WIDE = 256
 BLOCKS = WIDE // TOK
 BF = jnp.bfloat16
 F32 = jnp.float32
 
-DIGITS = {"y": (2, 32), "x": (4, 8), "z2": (2, 4), "w": (4, 1)}
+DIGITS = {"y": (2, 32), "x": (4, 8), "v": (4, 2), "u": (2, 1)}
 
 
 def groups_over(*free):
@@ -38,8 +39,8 @@
     return [[base + step for step in places(free)] for base in places(fixed)]
 
 
-Q_GROUPS = groups_over("x", "w")
-KV_GROUPS = groups_over("x", "z2")
+Q_GROUPS = groups_over("x", "v")
+KV_GROUPS = groups_over("x", "u")
 
 VMEM = pl.BlockSpec(memory_space=pltpu.VMEM)
 SMEM = pl.BlockSpec(memory_space=pltpu.SMEM)
@@ -109,12 +110,14 @@
                 total = total * step[n : n + 1, :] + product[8 * a : 8 * a + 8, lanes]
             total = total * jnp.exp(-rates_ref[n : n + 1, lanes] * back)
             rows.append(jnp.sum(total, 0, keepdims=True))
-        state = jnp.concatenate(rows, 0).astype(BF)
-        for peer in range(8):
-            sent_ref[peer, 128 + part * 16 : 144 + part * 16, :] = state
-    for x in range(4):
-        for z2 in range(2):
-            sent_ref[x * 2 + z2, :128, :] = kv_ref[x]
+        sent_ref[part, : 2 * TOK, :] = kv_ref[part]
+        sent_ref[part, 2 * TOK :, :] = jnp.concatenate(rows, 0).astype(BF)
+
+
+def join_kernel(own_ref, other_ref, out_ref):
+    for peer in range(8):
+        out_ref[peer, :PACK, :] = own_ref[peer // 2]
+        out_ref[peer, PACK:, :] = other_ref[peer // 2]
 
 
 def near_kernel(prod_ref, coeff_ref, rates_ref, skip_ref, out_ref, padded, impulse):
@@ -131,32 +134,36 @@
         out_ref[:, lanes] = y
 
 
-def write_messages(index, own_ref, other_ref, rates_ref, out_ref):
-    y, x, z2, w = digits(index)
-    rows = pl.ds(pl.multiple_of(128 + x * 16, 16), 16)
+def write_messages(index, got_ref, rates_ref, out_ref):
+    y, x, v, u = digits(index)
     decay = rates_ref[x] * (-float(TOK))
     second = jnp.where(y == 1, 1.0, 0.0).astype(F32)
 
     def faded(steps):
         return jnp.exp(decay * jnp.maximum(steps, 0).astype(F32))
 
-    def when(condition):
-        return jnp.where(condition, 1.0, 0.0).astype(F32)
-
-    own_states = [own_ref[i, rows, :].astype(F32) for i in range(8)]
-    other_states = [other_ref[i, rows, :].astype(F32) * second for i in range(8)]
-    reach = [faded(wt - w + 3) for wt in range(4)]
-    step = [faded(wt - w - 1) * when(wt > w) for wt in range(4)]
+    own_states = [got_ref[i, 2 * TOK : PACK, :].astype(F32) for i in range(8)]
+    other_states = [got_ref[i, PACK + 2 * TOK :, :].astype(F32) * second for i in range(8)]
+    reach = [faded(2 * (vt - v) + 6) for vt in range(4)]
+    near_steps = [[2 * (vt - v) + u - us - 1 for us in range(2)] for vt in range(4)]
+    close = [
+        [faded(steps) * jnp.where(steps >= 0, 1.0, 0.0).astype(F32) for steps in pair]
+        for pair in near_steps
+    ]
+    before = {(dx, us): faded(8 * dx - 7 + u - us) for dx in range(1, 4) for us in range(2)}
+    across = {(dx, us): faded(8 * dx + 25 + u - us) for dx in range(-3, 4) for us in range(2)}
     for xt in range(4):
-        before = jnp.zeros((MODES, 128), F32)
-        own = jnp.zeros((MODES, 128), F32)
-        for i in range(8):
-            gap = 8 * (xt - i // 2) + 4 * (z2 - i % 2)
-            before = before + when(gap > 0) * faded(gap - 4) * own_states[i]
-            before = before + faded(gap + 28) * other_states[i]
-            own = own + when(gap == 0) * own_states[i]
-        for wt in range(4):
-            out_ref[xt * 4 + wt, 80:96, :] = (reach[wt] * before + step[wt] * own).astype(BF)
+        total = jnp.zeros((MODES, 128), F32)
+        for xs in range(4):
+            for us in range(2):
+                total = total + across[xt - xs, us] * other_states[xs * 2 + us]
+                if xs < xt:
+                    total = total + before[xt - xs, us] * own_states[xs * 2 + us]
+        for vt in range(4):
+            state = reach[vt] * total
+            for us in range(2):
+                state = state + close[vt][us] * own_states[xt * 2 + us]
+            out_ref[xt * 4 + vt, 80:96, :] = state.astype(BF)
 
 
 def far_kernel(got_ref, coeff_ref, rates_ref, near_ref, gate_ref, gain_ref, gained_ref, square_ref):
@@ -184,60 +191,36 @@
         out_ref[:, lanes] = (gained_ref[:, lanes] * factor).astype(BF)
 
 
-def attend(keys, values, query, mask):
-    scores = lax.dot_general(
-        keys, query, (((1,), (1,)), ((), ())), preferred_element_type=F32
-    ) * (1.0 / math.sqrt(HEAD))
-    scores = mask(scores)
-    top = jnp.max(scores, 0, keepdims=True)
-    weights = jnp.exp(scores - top)
-    total = jnp.sum(weights, 0, keepdims=True)
-    mixed = lax.dot_general(
-        values, weights.astype(BF), (((0,), (0,)), ((), ())), preferred_element_type=F32
-    )
-    return top, total, mixed
-
-
-def near_attend_kernel(place_ref, q_ref, own_ref, mixed_ref, stats_ref):
-    _, _, z2, w = digits(place_ref[0])
-    keys = own_ref[:, :TOK, :].reshape(8 * TOK, HEAD)
-    values = own_ref[:, TOK:128, :].reshape(8 * TOK, HEAD)
-    row = lax.broadcasted_iota(jnp.int32, (8 * TOK, 1), 0)
+def attend_kernel(place_ref, q_ref, got_ref, rates_ref, out_ref):
+    y, _, v, u = digits(place_ref[0])
+    write_messages(place_ref[0], got_ref, rates_ref, out_ref)
+    keys = jnp.concatenate(
+        [got_ref[:, first : first + TOK, :].reshape(8 * TOK, HEAD) for first in (0, PACK)], 0
+    )
+    values = jnp.concatenate(
+        [got_ref[:, first + TOK : first + 2 * TOK, :].reshape(8 * TOK, HEAD) for first in (0, PACK)], 0
+    )
+    row = lax.broadcasted_iota(jnp.int32, (16 * TOK, 1), 0)
     block = row // TOK
-    key_pos = ((block // 2) * 8 + (block % 2) * 4 + w) * TOK + row % TOK
+    key_pos = (((block // 2) % 4) * 8 + 2 * v + block % 2) * TOK + row % TOK
+    key_pos = jnp.where(block < 8, key_pos, jnp.where(y == 1, -1, 1 << 20))
+    which = lax.broadcasted_iota(jnp.int32, (16, 128), 0)
     for tile in range(16 * TOK // WIDE):
         query = q_ref[tile * BLOCKS : (tile + 1) * BLOCKS].reshape(WIDE, HEAD)
         lane = lax.broadcasted_iota(jnp.int32, (1, WIDE), 1) + tile * WIDE
         q_block = lane // TOK
-        q_pos = ((q_block // 4) * 8 + z2 * 4 + q_block % 4) * TOK + lane % TOK
-        top, total, mixed = attend(
-            keys, values, query, lambda s: jnp.where(key_pos <= q_pos, s, NEG)
+        q_pos = ((q_block // 4) * 8 + 2 * (q_block % 4) + u) * TOK + lane % TOK
+        scores = lax.dot_general(
+            keys, query, (((1,), (1,)), ((), ())), preferred_element_type=F32
+        ) * (1.0 / math.sqrt(HEAD))
+        scores = jnp.where(key_pos <= q_pos, scores, NEG)
+        top = jnp.max(scores, 0, keepdims=True)
+        weights = jnp.exp(scores - top)
+        total = jnp.sum(weights, 0, keepdims=True)
+        mixed = lax.dot_general(
+            values, weights.astype(BF), (((0,), (0,)), ((), ())), preferred_element_type=F32
         )
-        lanes = slice(tile * WIDE, (tile + 1) * WIDE)
-        mixed_ref[:, lanes] = mixed
-        stats_ref[0:1, lanes] = top
-        stats_ref[1:2, lanes] = total
-
-
-def far_attend_kernel(
-    place_ref, q_ref, own_ref, other_ref, mixed_ref, stats_ref, rates_ref, out_ref
-):
-    bias = jnp.where(digits(place_ref[0])[0] == 1, 0.0, NEG).astype(F32)
-    keys = other_ref[:, :TOK, :].reshape(8 * TOK, HEAD)
-    values = other_ref[:, TOK:128, :].reshape(8 * TOK, HEAD)
-    write_messages(place_ref[0], own_ref, other_ref, rates_ref, out_ref)
-    which = lax.broadcasted_iota(jnp.int32, (16, 128), 0)
-    for tile in range(16 * TOK // WIDE):
-        lanes = slice(tile * WIDE, (tile + 1) * WIDE)
-        query = q_ref[tile * BLOCKS : (tile + 1) * BLOCKS].reshape(WIDE, HEAD)
-        top_b, total_b, mixed_b = attend(keys, values, query, lambda s: s + bias)
-        top_a, total_a = stats_ref[0:1, lanes], stats_ref[1:2, lanes]
-        top = jnp.maximum(top_a, top_b)
-        scale_a, scale_b = jnp.exp(top_a - top), jnp.exp(top_b - top)
-        total = total_a * scale_a + total_b * scale_b
-        inverse = 1.0 / total
-        mixed = mixed_ref[:, lanes] * (scale_a * inverse) + mixed_b * (scale_b * inverse)
-        mixed = jnp.transpose(mixed).astype(BF)
+        mixed = jnp.transpose(mixed * (1.0 / total)).astype(BF)
         level = top + jnp.log(total)
         high = level.astype(BF).astype(F32)
         rest = level - high
@@ -256,7 +239,7 @@
 
 
 def merge_kernel(place_ref, got_ref, out_ref):
-    odd = place_ref[0] % 2
+    odd = digits(place_ref[0])[2] % 2
     levels = jnp.sum(got_ref[:, TOK:80, :].astype(F32), 1)
     levels = jnp.where(odd == 1, pltpu.roll(levels, TOK, 1), levels)
     weights = []
@@ -309,38 +292,30 @@
     rim = jnp.pad(rim.astype(F32), ((0, 0), (6, 0), (0, 0)))
     sent, gate, product = call(
         state_kernel,
-        [((8, 192, HEAD), BF), ((TOK, CH), F32), ((TOK, CH), F32)],
+        [((HEADS_DEV, PACK, HEAD), BF), ((TOK, CH), F32), ((TOK, CH), F32)],
         [VMEM] * 5,
         20000000000,
     )(features, rim, feat_weight, rates, pairs)
-    quarters = jnp.transpose(rates.reshape(MODES, CH // 128, 128), (1, 0, 2))
-    queries, sent, coeff, quarters, skip, gain = lax.optimization_barrier(
-        (queries, sent, coeff, quarters, skip[None, :], norm_gain[None, :])
-    )
-    got = exchange(sent, KV_GROUPS)
-    product, got = lax.optimization_barrier((product, got))
-
-    other = lax.ppermute(got, "context", [(s, s + devices // 2) for s in range(devices // 2)])
-    mixed, stats = call(
-        near_attend_kernel,
-        [((HEAD, 16 * TOK), F32), ((8, 16 * TOK), F32)],
-        [SMEM, VMEM, VMEM],
-        200000000,
-    )(place, queries, got)
+    other = lax.ppermute(sent, "context", [(s, s + devices // 2) for s in range(devices // 2)])
     (near,) = call(
         near_kernel,
         [((TOK, CH), F32)],
         [VMEM] * 4,
         200000000,
         [pltpu.VMEM((2 * TOK, CH), F32), pltpu.VMEM((TOK, CH), F32)],
-    )(product, coeff, rates, skip)
-    near, other = lax.optimization_barrier((near, other))
+    )(product, coeff, rates, skip[None, :])
+    quarters = jnp.transpose(rates.reshape(MODES, CH // 128, 128), (1, 0, 2))
+    (both,) = call(join_kernel, [((8, 2 * PACK, HEAD), BF)], [VMEM] * 2, 500000000)(sent, other)
+    queries, both, coeff, quarters, near, gain = lax.optimization_barrier(
+        (queries, both, coeff, quarters, near, norm_gain[None, :])
+    )
+    got = exchange(both, KV_GROUPS)
     (partial,) = call(
-        far_attend_kernel,
+        attend_kernel,
         [((16, TOK + 32, HEAD), BF)],
-        [SMEM] + [VMEM] * 6,
-        20000000000,
-    )(place, queries, got, other, mixed, stats, quarters)
+        [SMEM] + [VMEM] * 3,
+        4000000000,
+    )(place, queries, got, quarters)
     partial = exchange(partial, Q_GROUPS)
 
     gained, squares = call(

time: 102 us -> 85.2 us (0.84)
  waiting for transfers between devices: 13.7 us -> 4.58 us
  blocking collectives: 38.4 us -> 31.2 us
    all_to_all x1, waiting for transfers between devices: 8.31 us -> 0.59 us  [exchange(): lax.all_to_all(value, 'context', 0, 0, axis_index_groups=groups, tiled=True)]
    all_to_all x2, blocking collectives: 38.4 us -> 31.2 us  [exchange(): lax.all_to_all(value, 'context', 0, 0, axis_index_groups=groups, tiled=True)]
    all_to_all x1, starting transfers between devices: 14.6 us -> 13.2 us  [local(): squares = lax.all_to_all(squares, 'dp', 0, 0, tiled=True)]
    ppermute x1, waiting for transfers between devices: 1.71 us -> 0.25 us  [local(): lax.ppermute(sent, 'context', [(s, s + devices // 2) for s in range(devic...]
  transfers between devices with their start and end apart: 4 -> 4, of which waited for: 3 -> 3; matrix products, arithmetic and copies ran while one was open for 0% -> 0% of each run, Pallas kernels for 5% -> 4%
where the time goes in v6:
time: 85.2 us; the launch traced here: 84.7 us
  starting transfers between devices  37.3 us (44%)
  blocking collectives  31.2 us (37%)
  Pallas kernels  8.37 us (10%)
  waiting for transfers between devices  4.58 us (5%)
  local copies, waits for them, and re-layouts  2.19 us (3%)
    all_to_all x2, blocking collectives, exchange(): lax.all_to_all(value, 'context', 0, 0, axis_index_groups=groups, tiled=True)  31.2 us
    all_to_all x1, starting transfers between devices, local(): squares = lax.all_to_all(squares, 'dp', 0, 0, tiled=True)  13.2 us
    all_to_all x1, starting transfers between devices, exchange(): lax.all_to_all(value, 'context', 0, 0, axis_index_groups=groups, tiled=True)  11.8 us
    ppermute x1, starting transfers between devices, local(): lax.ppermute(sent, 'context', [(s, s + devices // 2) for s in range(devic...  7.46 us
    ppermute x1, starting transfers between devices, local(): lax.ppermute(features[:, TOK - (FEAT - 1):], 'context', [(s, s + 1) for s...  4.83 us
    all_to_all x1, waiting for transfers between devices, local(): squares = lax.all_to_all(squares, 'dp', 0, 0, tiled=True)  3.73 us
    pallas_call x1, Pallas kernels, local(): call(attend_kernel, [((16, TOK + 32, HEAD), BF)], [SMEM] + [VMEM] * 3, 40...  3.17 us
  transfers between devices with their start and end apart: 4, of which 3 were waited for; matrix products, arithmetic and copies ran while one was open for 0% of the time, Pallas kernels for 4%

profile of v6, /device:TPU:1, one launch (start us, length us, event | category | flops | bytes accessed | tf_op | source)
XLA Modules:
  0.0 84.7 jit_solution(5588023135820411364)
XLA Ops:
  0.6 0.0 copy-start.2
  0.6 0.8 slice.4
  1.4 4.8 %collective-permute-start = (bf16[3,2,512]{2,1,0:T(2,128)(2,1)S(1)}, bf16[3,2,512]{2,1,0:T(2,128)(2,1)S(1)}, u32[]{:S(2)}, u32[]{:S(2)}) collective-permute-start(bf16[3,2,512]{2,1,0:T(2,128)(2,1)S(1)} %slice.4), channel_id=1, source_target_pairs={{0,8},{8,16},{16,24},{24,32},{32,40},{40,48},{48,56},{56,64},{64,7... | collective-permute-start | bytes 18440 | tf_op jit(solution)/shard_map/ppermute | solution.py:270
  6.3 0.2 fusion
  6.5 0.1 pad_maximum_fusion
  6.6 0.0 copy-done.2
  6.6 0.8 shard_map.86
  7.4 0.0 copy-start
  7.4 0.0 copy-start.6
  7.4 0.0 copy-start.1
  7.4 11.8 %all-to-all-start = ((bf16[16,64,128]{2,1,0:T(8,128)(2,1)}), bf16[16,64,128]{2,1,0:T(8,128)(2,1)S(1)}, u32[]{:S(2)}, u32[]{:S(2)}) async-start(bf16[16,64,128]{2,1,0:T(8,128)(2,1)} %get-tuple-element.15), calls=%async_computation | async-start | bytes 524288 | tf_op jit(solution)/shard_map/all_to_all | solution.py:261
  19.2 0.0 copy-done
  19.2 0.0 copy-done.6
  19.3 0.0 copy-start.3
  19.3 0.0 collective-permute-done
  19.3 0.0 copy-done.1
  19.3 0.7 copy-done.3
  20.0 0.4 shard_map.87
  20.4 7.5 %collective-permute-start.1 = (bf16[4,144,128]{2,1,0:T(8,128)(2,1)S(1)}, bf16[4,144,128]{2,1,0:T(8,128)(2,1)S(1)}, u32[]{:S(2)}, u32[]{:S(2)}) collective-permute-start(bf16[4,144,128]{2,1,0:T(8,128)(2,1)S(1)} %get-tuple-element.17.own_ref), channel_id=1, source_target_pairs={{0,256},{8,264},{16,272},{24,280},{32,288},{40,296},{48,304},{56,3... | collective-permute-start | bytes 442376 | tf_op jit(solution)/shard_map/ppermute | solution.py:299
  27.9 0.0 copy-start.4
  27.9 0.7 copy-done.4
  28.6 1.1 %shard_map.89.near_ref = f32[64,512]{1,0:T(8,128)S(1)} custom-call(f32[64,512]{1,0:T(8,128)S(1)} %get-tuple-element.18.prod_ref, f32[16,512]{1,0:T(8,128)S(1)} %sqrt_multiply_fusion.coeff_ref, f32[16,512]{1,0:T(8,128)S(1)} %copy-done, f32[1,512]{1,0:T(1,128)S(1)} %bitcast.20), custom_call_target="tpu_custom_call" | custom-call | flops 200000000 | bytes 1000 | tf_op jit(solution)/shard_map/pallas_call | solution.py:300
  29.7 0.3 collective-permute-done.1.other_ref
  30.0 0.1 shard_map.88
  30.1 0.6 all-to-all-done.q_ref
  30.6 12.3 %all_to_all.26.got_ref = bf16[8,288,128]{2,1,0:T(8,128)(2,1)S(1)} all-to-all(bf16[8,288,128]{2,1,0:T(8,128)(2,1)S(1)} %shard_map.88), channel_id=1, replica_groups={{0,8,64,72,128,136,192,200},{16,24,80,88,144,152,208,216},{32,40,96,104..., dimensions={0} | all-to-all | bytes 1179648 | tf_op jit(solution)/shard_map/all_to_all | solution.py:261
  42.9 3.2 %shard_map.90 = bf16[16,96,128]{2,1,0:T(8,128)(2,1)S(1)} custom-call(s32[1]{0:T(128)} %bitcast.place_ref, bf16[16,64,128]{2,1,0:T(8,128)(2,1)S(1)} %all-to-all-done.q_ref, bf16[8,288,128]{2,1,0:T(8,128)(2,1)S(1)} %all_to_all.26.got_ref, f32[4,16,128]{2,1,0:T(8,128)S(1)} %bitcast_bitcast_fusion.rates_ref), custom_call_target="tpu_custom_call" | custom-call | flops 4000000000 | bytes 1000 | tf_op jit(solution)/shard_map/pallas_call | solution.py:313
  46.1 0.0 copy-start.5
  46.1 18.9 %all_to_all.27.got_ref = bf16[16,96,128]{2,1,0:T(8,128)(2,1)S(1)} all-to-all(bf16[16,96,128]{2,1,0:T(8,128)(2,1)S(1)} %shard_map.90), channel_id=1, replica_groups={{0,16,32,48,64,80,96,112,128,144,160,176,192,208,224,240},{8,24,40,56,7..., dimensions={0} | all-to-all | bytes 786432 | tf_op jit(solution)/shard_map/all_to_all | solution.py:261
  65.0 0.0 copy-done.5
  65.0 1.0 %shard_map.91 = (f32[64,512]{1,0:T(8,128)S(1)}, f32[8,128]{1,0:T(8,128)}) custom-call(bf16[16,96,128]{2,1,0:T(8,128)(2,1)S(1)} %all_to_all.27.got_ref, f32[16,512]{1,0:T(8,128)S(1)} %sqrt_multiply_fusion.coeff_ref, f32[16,512]{1,0:T(8,128)S(1)} %copy-done, f32[64,512]{1,0:T(8,128)S(1)} %shard_map.89.near_ref, f32[64,512]{1,0:T(8,128)S(1)} %get-tuple-element.24.gate_ref, ...), custom_call_target="tpu_custom_call" | custom-call | flops 1000000000 | bytes 1000 | tf_op jit(solution)/shard_map/pallas_call | solution.py:321
  66.0 13.2 %all-to-all-start.3 = ((f32[8,1,128]{2,1,0:T(1,128)}), f32[8,1,128]{2,1,0:T(1,128)S(1)}, u32[]{:S(2)}, u32[]{:S(2)}) async-start(f32[8,1,128]{2,1,0:T(1,128)} %bitcast.7), calls=%async_computation.3 | async-start | bytes 8192 | tf_op jit(solution)/shard_map/all_to_all | solution.py:327
  79.2 1.1 %shard_map.93 = bf16[64,512]{1,0:T(8,128)(2,1)} custom-call(s32[1]{0:T(128)} %bitcast.place_ref, bf16[16,96,128]{2,1,0:T(8,128)(2,1)S(1)} %all_to_all.27.got_ref), custom_call_target="tpu_custom_call" | custom-call | flops 1000000000 | bytes 1000 | tf_op jit(solution)/shard_map/pallas_call | solution.py:328
  80.3 3.7 %all-to-all-done.3 = f32[8,1,128]{2,1,0:T(1,128)S(1)} async-done(((f32[8,1,128]{2,1,0:T(1,128)}), f32[8,1,128]{2,1,0:T(1,128)S(1)}, u32[]{:S(2)}, u32[]{:S(2)}) %all-to-all-start.3) | async-done | bytes 4128 | tf_op jit(solution)/shard_map/all_to_all | solution.py:327
  84.0 0.7 shard_map.92
  (5 shorter events, 0.1 us)
Async XLA Ops:
  0.6 6.0 %copy-start.2 = (bf16[64,3,512]{2,0,1:T(8,128)(2,1)S(1)}, bf16[64,3,512]{2,0,1:T(8,128)(2,1)}, u32[]{:S(2)}) copy-start(bf16[64,3,512]{2,0,1:T(8,128)(2,1)} %param.13) | copy-start | bytes 589828
  1.4 17.9 %collective-permute-start = (bf16[3,2,512]{2,1,0:T(2,128)(2,1)S(1)}, bf16[3,2,512]{2,1,0:T(2,128)(2,1)S(1)}, u32[]{:S(2)}, u32[]{:S(2)}) collective-permute-start(bf16[3,2,512]{2,1,0:T(2,128)(2,1)S(1)} %slice.4), channel_id=1, source_target_pairs={{0,8},{8,16},{16,24},{24,32},{32,40},{40,48},{48,56},{56,64},{64,7... | collective-permute-start | bytes 18440 | tf_op jit(solution)/shard_map/ppermute | solution.py:270
  7.4 11.8 %copy-start = (f32[16,512]{1,0:T(8,128)S(1)}, f32[16,512]{1,0:T(8,128)}, u32[]{:S(2)}) copy-start(f32[16,512]{1,0:T(8,128)} %rates_ref.5) | copy-start | bytes 98308
  7.4 11.9 %copy-start.6 = (f32[16,512]{1,0:T(8,128)S(1)}, f32[16,512]{1,0:T(8,128)}, u32[]{:S(2)}) copy-start(f32[16,512]{1,0:T(8,128)} %param.10) | copy-start | bytes 98308
  7.4 11.9 %copy-start.1 = (bf16[64,3,512]{2,0,1:T(8,128)(2,1)S(1)}, bf16[64,3,512]{2,0,1:T(8,128)(2,1)}, u32[]{:S(2)}) copy-start(bf16[64,3,512]{2,0,1:T(8,128)(2,1)} %param.7) | copy-start | bytes 589828
  7.4 23.3 %all-to-all-start = ((bf16[16,64,128]{2,1,0:T(8,128)(2,1)}), bf16[16,64,128]{2,1,0:T(8,128)(2,1)S(1)}, u32[]{:S(2)}, u32[]{:S(2)}) async-start(bf16[16,64,128]{2,1,0:T(8,128)(2,1)} %get-tuple-element.15), calls=%async_computation | async-start | bytes 524288 | tf_op jit(solution)/shard_map/all_to_all | solution.py:261
  19.3 0.7 copy-start.3
  20.4 9.5 %collective-permute-start.1 = (bf16[4,144,128]{2,1,0:T(8,128)(2,1)S(1)}, bf16[4,144,128]{2,1,0:T(8,128)(2,1)S(1)}, u32[]{:S(2)}, u32[]{:S(2)}) collective-permute-start(bf16[4,144,128]{2,1,0:T(8,128)(2,1)S(1)} %get-tuple-element.17.own_ref), channel_id=1, source_target_pairs={{0,256},{8,264},{16,272},{24,280},{32,288},{40,296},{48,304},{56,3... | collective-permute-start | bytes 442376 | tf_op jit(solution)/shard_map/ppermute | solution.py:299
  27.9 0.7 copy-start.4
  46.1 18.9 %copy-start.5 = (f32[512]{0:T(512)S(1)}, f32[512]{0:T(512)}, u32[]{:S(2)}) copy-start(f32[512]{0:T(512)} %param.12) | copy-start | bytes 6148
  66.0 17.9 %all-to-all-start.3 = ((f32[8,1,128]{2,1,0:T(1,128)}), f32[8,1,128]{2,1,0:T(1,128)S(1)}, u32[]{:S(2)}, u32[]{:S(2)}) async-start(f32[8,1,128]{2,1,0:T(1,128)} %bitcast.7), calls=%async_computation.3 | async-start | bytes 8192 | tf_op jit(solution)/shard_map/all_to_all | solution.py:327

commit v7 on v6

--- a/solution.py
+++ b/solution.py
@@ -166,22 +166,6 @@
             out_ref[xt * 4 + vt, 80:96, :] = state.astype(BF)
 
 
-def far_kernel(got_ref, coeff_ref, rates_ref, near_ref, gate_ref, gain_ref, gained_ref, square_ref):
-    squares = jnp.zeros((TOK, 128), F32)
-    for part in range(CH // 128):
-        lanes = slice(part * 128, (part + 1) * 128)
-        state = got_ref[part * 4, 80:96, :].astype(F32)
-        for j in range(1, 4):
-            state = state + got_ref[part * 4 + j, 80:96, :].astype(F32)
-        tiles = expand(rates_ref[:, lanes], coeff_ref[:, lanes] * state, 1)
-        gated = gate_ref[:, lanes] * (near_ref[:, lanes] + jnp.concatenate(tiles, 0))
-        gained_ref[:, lanes] = gated * gain_ref[:, lanes]
-        squares = squares + gated * gated
-    total = jnp.broadcast_to(jnp.sum(squares, 1, keepdims=True), (TOK, 128))
-    total = jnp.concatenate([total, jnp.zeros((TOK, 128), F32)], 0)
-    square_ref[...] = jnp.transpose(total)[:8, :]
-
-
 def norm_kernel(square_ref, gained_ref, out_ref):
     total = jnp.sum(square_ref[...], 0, keepdims=True)
     total = jnp.transpose(jnp.broadcast_to(total, (128, 128)))[:TOK, :]
@@ -191,37 +175,46 @@
         out_ref[:, lanes] = (gained_ref[:, lanes] * factor).astype(BF)
 
 
+def attend(keys, values, query, mask):
+    scores = lax.dot_general(
+        keys, query, (((1,), (1,)), ((), ())), preferred_element_type=F32
+    ) * (math.log2(math.e) / math.sqrt(HEAD))
+    scores = mask(scores)
+    top = jnp.max(scores, 0, keepdims=True)
+    weights = jnp.exp2(scores - top)
+    total = jnp.sum(weights, 0, keepdims=True)
+    mixed = lax.dot_general(
+        values, weights.astype(BF), (((0,), (0,)), ((), ())), preferred_element_type=F32
+    )
+    return top, total, mixed
+
+
 def attend_kernel(place_ref, q_ref, got_ref, rates_ref, out_ref):
     y, _, v, u = digits(place_ref[0])
     write_messages(place_ref[0], got_ref, rates_ref, out_ref)
-    keys = jnp.concatenate(
-        [got_ref[:, first : first + TOK, :].reshape(8 * TOK, HEAD) for first in (0, PACK)], 0
-    )
-    values = jnp.concatenate(
-        [got_ref[:, first + TOK : first + 2 * TOK, :].reshape(8 * TOK, HEAD) for first in (0, PACK)], 0
-    )
-    row = lax.broadcasted_iota(jnp.int32, (16 * TOK, 1), 0)
+
+    def half(first):
+        keys = got_ref[:, first : first + TOK, :].reshape(8 * TOK, HEAD)
+        return keys, got_ref[:, first + TOK : first + 2 * TOK, :].reshape(8 * TOK, HEAD)
+
+    own, other = half(0), half(PACK)
+    row = lax.broadcasted_iota(jnp.int32, (8 * TOK, 1), 0)
     block = row // TOK
-    key_pos = (((block // 2) % 4) * 8 + 2 * v + block % 2) * TOK + row % TOK
-    key_pos = jnp.where(block < 8, key_pos, jnp.where(y == 1, -1, 1 << 20))
+    key_pos = ((block // 2) * 8 + 2 * v + block % 2) * TOK + row % TOK
     which = lax.broadcasted_iota(jnp.int32, (16, 128), 0)
-    for tile in range(16 * TOK // WIDE):
-        query = q_ref[tile * BLOCKS : (tile + 1) * BLOCKS].reshape(WIDE, HEAD)
+
+    def query_of(tile):
+        return q_ref[tile * BLOCKS : (tile + 1) * BLOCKS].reshape(WIDE, HEAD)
+
+    def own_part(tile):
         lane = lax.broadcasted_iota(jnp.int32, (1, WIDE), 1) + tile * WIDE
         q_block = lane // TOK
         q_pos = ((q_block // 4) * 8 + 2 * (q_block % 4) + u) * TOK + lane % TOK
-        scores = lax.dot_general(
-            keys, query, (((1,), (1,)), ((), ())), preferred_element_type=F32
-        ) * (1.0 / math.sqrt(HEAD))
-        scores = jnp.where(key_pos <= q_pos, scores, NEG)
-        top = jnp.max(scores, 0, keepdims=True)
-        weights = jnp.exp(scores - top)
-        total = jnp.sum(weights, 0, keepdims=True)
-        mixed = lax.dot_general(
-            values, weights.astype(BF), (((0,), (0,)), ((), ())), preferred_element_type=F32
-        )
-        mixed = jnp.transpose(mixed * (1.0 / total)).astype(BF)
-        level = top + jnp.log(total)
+        return attend(*own, query_of(tile), lambda s: jnp.where(key_pos <= q_pos, s, NEG))
+
+    def write(tile, top, total, mixed):
+        mixed = jnp.transpose(mixed).astype(BF)
+        level = top + jnp.log2(total)
         high = level.astype(BF).astype(F32)
         rest = level - high
         middle = rest.astype(BF).astype(F32)
@@ -237,15 +230,32 @@
             )
             out_ref[place, TOK:80, :] = stats.astype(BF)
 
-
-def merge_kernel(place_ref, got_ref, out_ref):
-    odd = digits(place_ref[0])[2] % 2
+    @pl.when(y == 0)
+    def _():
+        for tile in range(16 * TOK // WIDE):
+            top, total, mixed = own_part(tile)
+            write(tile, top, total, mixed * (1.0 / total))
+
+    @pl.when(y == 1)
+    def _():
+        for tile in range(16 * TOK // WIDE):
+            top_a, total_a, mixed_a = own_part(tile)
+            top_b, total_b, mixed_b = attend(*other, query_of(tile), lambda s: s)
+            top = jnp.maximum(top_a, top_b)
+            scale_a, scale_b = jnp.exp2(top_a - top), jnp.exp2(top_b - top)
+            total = total_a * scale_a + total_b * scale_b
+            inverse = 1.0 / total
+            write(tile, top, total, mixed_a * (scale_a * inverse) + mixed_b * (scale_b * inverse))
+
+
+def merge(index, got_ref, out_ref):
+    odd = digits(index)[2] % 2
     levels = jnp.sum(got_ref[:, TOK:80, :].astype(F32), 1)
     levels = jnp.where(odd == 1, pltpu.roll(levels, TOK, 1), levels)
     weights = []
     for h in range(HEADS_DEV):
         part = levels[h * 4 : (h + 1) * 4]
-        part = jnp.exp(part - jnp.max(part, 0, keepdims=True))
+        part = jnp.exp2(part - jnp.max(part, 0, keepdims=True))
         weights.append(part / jnp.sum(part, 0, keepdims=True))
     weights = jnp.concatenate(weights + [jnp.zeros((112, 128), F32)], 0)
     weights = jnp.transpose(weights)[:TOK, :]
@@ -255,6 +265,25 @@
             place = h * 4 + k
             total = total + weights[:, place : place + 1] * got_ref[place, :TOK, :].astype(F32)
         out_ref[:, h * HEAD : (h + 1) * HEAD] = total.astype(BF)
+
+
+def tail_kernel(
+    place_ref, got_ref, coeff_ref, rates_ref, near_ref, gate_ref, gain_ref, gained_ref, square_ref, out_ref
+):
+    squares = jnp.zeros((TOK, 128), F32)
+    for part in range(CH // 128):
+        lanes = slice(part * 128, (part + 1) * 128)
+        state = got_ref[part * 4, 80:96, :].astype(F32)
+        for j in range(1, 4):
+            state = state + got_ref[part * 4 + j, 80:96, :].astype(F32)
+        tiles = expand(rates_ref[:, lanes], coeff_ref[:, lanes] * state, 1)
+        gated = gate_ref[:, lanes] * (near_ref[:, lanes] + jnp.concatenate(tiles, 0))
+        gained_ref[:, lanes] = gated * gain_ref[:, lanes]
+        squares = squares + gated * gated
+    total = jnp.broadcast_to(jnp.sum(squares, 1, keepdims=True), (TOK, 128))
+    total = jnp.concatenate([total, jnp.zeros((TOK, 128), F32)], 0)
+    square_ref[...] = jnp.transpose(total)[:8, :]
+    merge(place_ref[0], got_ref, out_ref)
 
 
 def exchange(value, groups):
@@ -318,14 +347,13 @@
     )(place, queries, got, quarters)
     partial = exchange(partial, Q_GROUPS)
 
-    gained, squares = call(
-        far_kernel,
-        [((TOK, CH), F32), ((8, 128), F32)],
-        [VMEM] * 6,
+    gained, squares, attn_out = call(
+        tail_kernel,
+        [((TOK, CH), F32), ((8, 128), F32), ((TOK, CH), BF)],
+        [SMEM] + [VMEM] * 6,
         1000000000,
-    )(partial, coeff, rates, near, gate, gain)
+    )(place, partial, coeff, rates, near, gate, gain)
     squares = lax.all_to_all(squares, "dp", 0, 0, tiled=True)
-    (attn_out,) = call(merge_kernel, [((TOK, CH), BF)], [SMEM, VMEM], 1000000000)(place, partial)
     (hyena_out,) = call(norm_kernel, [((TOK, CH), BF)], [VMEM] * 2, 100000000)(squares, gained)
     return (hyena_out, attn_out)
 

time: 85.2 us -> 85.7 us (level)
  the two profiles are of different devices: /device:TPU:1 before, /device:TPU:32 now
where the time goes in v7:
time: 85.7 us; the launch traced here: 85.3 us
  blocking collectives  47 us (55%)
  starting transfers between devices  17.7 us (21%)
  waiting for transfers between devices  9.02 us (11%)
  Pallas kernels  8.23 us (10%)
  local copies, waits for them, and re-layouts  2.19 us (3%)
    all_to_all x2, blocking collectives, exchange(): lax.all_to_all(value, 'context', 0, 0, axis_index_groups=groups, tiled=True)  33.4 us
    all_to_all x1, blocking collectives, local(): squares = lax.all_to_all(squares, 'dp', 0, 0, tiled=True)  13.6 us
    all_to_all x1, starting transfers between devices, exchange(): lax.all_to_all(value, 'context', 0, 0, axis_index_groups=groups, tiled=True)  12.1 us
    ppermute x1, waiting for transfers between devices, local(): lax.ppermute(sent, 'context', [(s, s + devices // 2) for s in range(devic...  7.83 us
    ppermute x1, starting transfers between devices, local(): lax.ppermute(features[:, TOK - (FEAT - 1):], 'context', [(s, s + 1) for s...  4.28 us
    pallas_call x1, Pallas kernels, local(): call(attend_kernel, [((16, TOK + 32, HEAD), BF)], [SMEM] + [VMEM] * 3, 40...  3.8 us
  transfers between devices with their start and end apart: 3, of which 2 were waited for; matrix products, arithmetic and copies ran while one was open for 0% of the time, Pallas kernels for 3%

profile of v7, /device:TPU:32, one launch (start us, length us, event | category | flops | bytes accessed | tf_op | source)
XLA Modules:
  0.0 85.3 jit_solution(13632852328294659482)
XLA Ops:
  0.6 0.0 copy-start.2
  0.6 0.8 slice.4
  1.4 4.3 %collective-permute-start = (bf16[3,2,512]{2,1,0:T(2,128)(2,1)S(1)}, bf16[3,2,512]{2,1,0:T(2,128)(2,1)S(1)}, u32[]{:S(2)}, u32[]{:S(2)}) collective-permute-start(bf16[3,2,512]{2,1,0:T(2,128)(2,1)S(1)} %slice.4), channel_id=1, source_target_pairs={{0,8},{8,16},{16,24},{24,32},{32,40},{40,48},{48,56},{56,64},{64,7... | collective-permute-start | bytes 18440 | tf_op jit(solution)/shard_map/ppermute | solution.py:299
  5.8 0.2 fusion
  6.0 0.1 pad_maximum_fusion
  6.0 0.0 copy-done.2
  6.1 0.8 shard_map.86
  6.9 0.0 copy-start
  6.9 0.0 copy-start.6
  6.9 0.0 copy-start.1
  6.9 12.1 %all-to-all-start = ((bf16[16,64,128]{2,1,0:T(8,128)(2,1)}), bf16[16,64,128]{2,1,0:T(8,128)(2,1)S(1)}, u32[]{:S(2)}, u32[]{:S(2)}) async-start(bf16[16,64,128]{2,1,0:T(8,128)(2,1)} %get-tuple-element.16), calls=%async_computation | async-start | bytes 524288 | tf_op jit(solution)/shard_map/all_to_all | solution.py:290
  19.0 0.0 copy-done
  19.0 0.0 copy-done.6
  19.0 0.0 copy-start.3
  19.0 0.0 collective-permute-done
  19.1 0.0 copy-done.1
  19.1 0.7 copy-done.3
  19.8 0.4 shard_map.87
  20.2 1.3 %collective-permute-start.1 = (bf16[4,144,128]{2,1,0:T(8,128)(2,1)S(1)}, bf16[4,144,128]{2,1,0:T(8,128)(2,1)S(1)}, u32[]{:S(2)}, u32[]{:S(2)}) collective-permute-start(bf16[4,144,128]{2,1,0:T(8,128)(2,1)S(1)} %get-tuple-element.18.own_ref), channel_id=1, source_target_pairs={{0,256},{8,264},{16,272},{24,280},{32,288},{40,296},{48,304},{56,3... | collective-permute-start | bytes 442376 | tf_op jit(solution)/shard_map/ppermute | solution.py:328
  21.5 0.0 copy-start.4
  21.5 0.7 copy-done.4
  22.2 1.1 %shard_map.89.near_ref = f32[64,512]{1,0:T(8,128)S(1)} custom-call(f32[64,512]{1,0:T(8,128)S(1)} %get-tuple-element.19.prod_ref, f32[16,512]{1,0:T(8,128)S(1)} %sqrt_multiply_fusion.coeff_ref, f32[16,512]{1,0:T(8,128)S(1)} %copy-done, f32[1,512]{1,0:T(1,128)S(1)} %bitcast.21), custom_call_target="tpu_custom_call" | custom-call | flops 200000000 | bytes 1000 | tf_op jit(solution)/shard_map/pallas_call | solution.py:329
  23.3 7.8 %collective-permute-done.1.other_ref = bf16[4,144,128]{2,1,0:T(8,128)(2,1)S(1)} collective-permute-done((bf16[4,144,128]{2,1,0:T(8,128)(2,1)S(1)}, bf16[4,144,128]{2,1,0:T(8,128)(2,1)S(1)}, u32[]{:S(2)}, u32[]{:S(2)}) %collective-permute-start.1) | collective-permute-done | bytes 147488 | tf_op jit(solution)/shard_map/ppermute | solution.py:328
  31.1 0.1 shard_map.88
  31.2 1.2 %all-to-all-done.q_ref = bf16[16,64,128]{2,1,0:T(8,128)(2,1)S(1)} async-done(((bf16[16,64,128]{2,1,0:T(8,128)(2,1)}), bf16[16,64,128]{2,1,0:T(8,128)(2,1)S(1)}, u32[]{:S(2)}, u32[]{:S(2)}) %all-to-all-start) | async-done | bytes 262176 | tf_op jit(solution)/shard_map/all_to_all | solution.py:290
  32.4 13.4 %all_to_all.26.got_ref = bf16[8,288,128]{2,1,0:T(8,128)(2,1)S(1)} all-to-all(bf16[8,288,128]{2,1,0:T(8,128)(2,1)S(1)} %shard_map.88), channel_id=1, replica_groups={{0,8,64,72,128,136,192,200},{16,24,80,88,144,152,208,216},{32,40,96,104..., dimensions={0} | all-to-all | bytes 1179648 | tf_op jit(solution)/shard_map/all_to_all | solution.py:290
  45.8 3.8 %shard_map.90 = bf16[16,96,128]{2,1,0:T(8,128)(2,1)S(1)} custom-call(s32[1]{0:T(128)} %bitcast.place_ref, bf16[16,64,128]{2,1,0:T(8,128)(2,1)S(1)} %all-to-all-done.q_ref, bf16[8,288,128]{2,1,0:T(8,128)(2,1)S(1)} %all_to_all.26.got_ref, f32[4,16,128]{2,1,0:T(8,128)S(1)} %bitcast_bitcast_fusion.rates_ref), custom_call_target="tpu_custom_call" | custom-call | flops 4000000000 | bytes 1000 | tf_op jit(solution)/shard_map/pallas_call | solution.py:342
  49.6 0.0 copy-start.5
  49.6 20.0 %all_to_all.27.got_ref = bf16[16,96,128]{2,1,0:T(8,128)(2,1)S(1)} all-to-all(bf16[16,96,128]{2,1,0:T(8,128)(2,1)S(1)} %shard_map.90), channel_id=1, replica_groups={{0,16,32,48,64,80,96,112,128,144,160,176,192,208,224,240},{8,24,40,56,7..., dimensions={0} | all-to-all | bytes 786432 | tf_op jit(solution)/shard_map/all_to_all | solution.py:290
  69.7 0.0 copy-done.5
  69.7 1.3 %shard_map.91 = (f32[64,512]{1,0:T(8,128)S(1)}, f32[8,128]{1,0:T(8,128)S(1)}, bf16[64,512]{1,0:T(8,128)(2,1)}) custom-call(s32[1]{0:T(128)} %bitcast.place_ref, bf16[16,96,128]{2,1,0:T(8,128)(2,1)S(1)} %all_to_all.27.got_ref, f32[16,512]{1,0:T(8,128)S(1)} %sqrt_multiply_fusion.coeff_ref, f32[16,512]{1,0:T(8,128)S(1)} %copy-done, ...), custom_call_target="tpu_custom_call" | custom-call | flops 1000000000 | bytes 1000 | tf_op jit(solution)/shard_map/pallas_call | solution.py:350
  71.0 13.6 %all_to_all.28 = f32[8,1,128]{2,1,0:T(1,128)S(1)} all-to-all(f32[8,1,128]{2,1,0:T(1,128)S(1)} %bitcast.16), channel_id=1, replica_groups=mesh['context'=64,'dp'=8] {'dp'}, dimensions={0} | all-to-all | bytes 8192 | tf_op jit(solution)/shard_map/all_to_all | solution.py:356
  84.5 0.7 shard_map.92
  (5 shorter events, 0.1 us)
Async XLA Ops:
  0.6 5.4 %copy-start.2 = (bf16[64,3,512]{2,0,1:T(8,128)(2,1)S(1)}, bf16[64,3,512]{2,0,1:T(8,128)(2,1)}, u32[]{:S(2)}) copy-start(bf16[64,3,512]{2,0,1:T(8,128)(2,1)} %param.13) | copy-start | bytes 589828
  1.4 17.6 %collective-permute-start = (bf16[3,2,512]{2,1,0:T(2,128)(2,1)S(1)}, bf16[3,2,512]{2,1,0:T(2,128)(2,1)S(1)}, u32[]{:S(2)}, u32[]{:S(2)}) collective-permute-start(bf16[3,2,512]{2,1,0:T(2,128)(2,1)S(1)} %slice.4), channel_id=1, source_target_pairs={{0,8},{8,16},{16,24},{24,32},{32,40},{40,48},{48,56},{56,64},{64,7... | collective-permute-start | bytes 18440 | tf_op jit(solution)/shard_map/ppermute | solution.py:299
  6.9 12.1 %copy-start = (f32[16,512]{1,0:T(8,128)S(1)}, f32[16,512]{1,0:T(8,128)}, u32[]{:S(2)}) copy-start(f32[16,512]{1,0:T(8,128)} %rates_ref.5) | copy-start | bytes 98308
  6.9 12.1 %copy-start.6 = (f32[16,512]{1,0:T(8,128)S(1)}, f32[16,512]{1,0:T(8,128)}, u32[]{:S(2)}) copy-start(f32[16,512]{1,0:T(8,128)} %param.10) | copy-start | bytes 98308
  6.9 12.2 %copy-start.1 = (bf16[64,3,512]{2,0,1:T(8,128)(2,1)S(1)}, bf16[64,3,512]{2,0,1:T(8,128)(2,1)}, u32[]{:S(2)}) copy-start(bf16[64,3,512]{2,0,1:T(8,128)(2,1)} %param.7) | copy-start | bytes 589828
  6.9 25.5 %all-to-all-start = ((bf16[16,64,128]{2,1,0:T(8,128)(2,1)}), bf16[16,64,128]{2,1,0:T(8,128)(2,1)S(1)}, u32[]{:S(2)}, u32[]{:S(2)}) async-start(bf16[16,64,128]{2,1,0:T(8,128)(2,1)} %get-tuple-element.16), calls=%async_computation | async-start | bytes 524288 | tf_op jit(solution)/shard_map/all_to_all | solution.py:290
  19.0 0.7 copy-start.3
  20.2 10.9 %collective-permute-start.1 = (bf16[4,144,128]{2,1,0:T(8,128)(2,1)S(1)}, bf16[4,144,128]{2,1,0:T(8,128)(2,1)S(1)}, u32[]{:S(2)}, u32[]{:S(2)}) collective-permute-start(bf16[4,144,128]{2,1,0:T(8,128)(2,1)S(1)} %get-tuple-element.18.own_ref), channel_id=1, source_target_pairs={{0,256},{8,264},{16,272},{24,280},{32,288},{40,296},{48,304},{56,3... | collective-permute-start | bytes 442376 | tf_op jit(solution)/shard_map/ppermute | solution.py:328
  21.5 0.7 copy-start.4
  49.6 20.0 %copy-start.5 = (f32[512]{0:T(512)S(1)}, f32[512]{0:T(512)}, u32[]{:S(2)}) copy-start(f32[512]{0:T(512)} %param.12) | copy-start | bytes 6148

commit v8 on v7

--- a/solution.py
+++ b/solution.py
@@ -316,8 +316,6 @@
         [VMEM] * 3,
         1000000000,
     )(attn_in, cosine, sine)
-    queries = exchange(queries, Q_GROUPS)
-
     rim = jnp.pad(rim.astype(F32), ((0, 0), (6, 0), (0, 0)))
     sent, gate, product = call(
         state_kernel,
@@ -325,6 +323,8 @@
         [VMEM] * 5,
         20000000000,
     )(features, rim, feat_weight, rates, pairs)
+    sent, queries = lax.optimization_barrier((sent, queries))
+    queries = exchange(queries, Q_GROUPS)
     other = lax.ppermute(sent, "context", [(s, s + devices // 2) for s in range(devices // 2)])
     (near,) = call(
         near_kernel,
@@ -334,7 +334,7 @@
         [pltpu.VMEM((2 * TOK, CH), F32), pltpu.VMEM((TOK, CH), F32)],
     )(product, coeff, rates, skip[None, :])
     quarters = jnp.transpose(rates.reshape(MODES, CH // 128, 128), (1, 0, 2))
-    (both,) = call(join_kernel, [((8, 2 * PACK, HEAD), BF)], [VMEM] * 2, 500000000)(sent, other)
+    (both,) = call(join_kernel, [((8, 2 * PACK, HEAD), BF)], [VMEM] * 2, 50000000000)(sent, other)
     queries, both, coeff, quarters, near, gain = lax.optimization_barrier(
         (queries, both, coeff, quarters, near, norm_gain[None, :])
     )

time: 85.7 us -> 83.5 us (0.974)
  the two profiles are of different devices: /device:TPU:32 before, /device:TPU:1 now
where the time goes in v8:
time: 83.5 us; the launch traced here: 83 us
  blocking collectives  37.7 us (45%)
  starting transfers between devices  24 us (29%)
  waiting for transfers between devices  10.5 us (13%)
  Pallas kernels  6.6 us (8%)
  local copies, waits for them, and re-layouts  2.25 us (3%)
  other arithmetic  1.11 us (1%)
    all_to_all x2, blocking collectives, exchange(): lax.all_to_all(value, 'context', 0, 0, axis_index_groups=groups, tiled=True)  25.4 us
    ppermute x1, starting transfers between devices, local(): lax.ppermute(sent, 'context', [(s, s + devices // 2) for s in range(devic...  14.2 us
    all_to_all x1, blocking collectives, local(): squares = lax.all_to_all(squares, 'dp', 0, 0, tiled=True)  12.3 us
    all_to_all x1, waiting for transfers between devices, exchange(): lax.all_to_all(value, 'context', 0, 0, axis_index_groups=groups, tiled=True)  10.5 us
    all_to_all x1, starting transfers between devices, exchange(): lax.all_to_all(value, 'context', 0, 0, axis_index_groups=groups, tiled=True)  5 us
    ppermute x1, starting transfers between devices, local(): lax.ppermute(features[:, TOK - (FEAT - 1):], 'context', [(s, s + 1) for s...  4.83 us
    pallas_call x1, Pallas kernels, local(): call(attend_kernel, [((16, TOK + 32, HEAD), BF)], [SMEM] + [VMEM] * 3, 40...  2.17 us
  transfers between devices with their start and end apart: 3, of which 1 were waited for; matrix products, arithmetic and copies ran while one was open for 1% of the time, Pallas kernels for 2%

profile of v8, /device:TPU:1, one launch (start us, length us, event | category | flops | bytes accessed | tf_op | source)
XLA Modules:
  0.0 83.0 jit_solution(11072337394215931014)
XLA Ops:
  0.6 0.0 copy-start.2
  0.6 0.8 slice.4
  1.4 4.8 %collective-permute-start = (bf16[3,2,512]{2,1,0:T(2,128)(2,1)S(1)}, bf16[3,2,512]{2,1,0:T(2,128)(2,1)S(1)}, u32[]{:S(2)}, u32[]{:S(2)}) collective-permute-start(bf16[3,2,512]{2,1,0:T(2,128)(2,1)S(1)} %slice.4), channel_id=1, source_target_pairs={{0,8},{8,16},{16,24},{24,32},{32,40},{40,48},{48,56},{56,64},{64,7... | collective-permute-start | bytes 18440 | tf_op jit(solution)/shard_map/ppermute | solution.py:299
  6.3 0.8 sqrt_multiply_fusion.coeff_ref
  7.1 0.2 fusion
  7.3 0.1 pad_maximum_fusion
  7.4 0.0 copy-done.2
  7.4 0.0 copy-start.1
  7.4 0.0 copy-start.3
  7.4 0.8 shard_map.86
  8.2 0.0 copy-start
  8.2 0.0 collective-permute-done
  8.3 0.1 copy-done.1
  8.3 0.0 copy-done.3
  8.3 0.7 copy-done
  9.0 0.4 shard_map.87
  9.4 14.2 %collective-permute-start.1 = (bf16[4,144,128]{2,1,0:T(8,128)(2,1)S(1)}, bf16[4,144,128]{2,1,0:T(8,128)(2,1)S(1)}, u32[]{:S(2)}, u32[]{:S(2)}) collective-permute-start(bf16[4,144,128]{2,1,0:T(8,128)(2,1)S(1)} %get-tuple-element.22.own_ref), channel_id=1, source_target_pairs={{0,256},{8,264},{16,272},{24,280},{32,288},{40,296},{48,304},{56,3... | collective-permute-start | bytes 442376 | tf_op jit(solution)/shard_map/ppermute | solution.py:328
  23.6 5.0 %all-to-all-start = ((bf16[16,64,128]{2,1,0:T(8,128)(2,1)}), bf16[16,64,128]{2,1,0:T(8,128)(2,1)S(1)}, u32[]{:S(2)}, u32[]{:S(2)}) async-start(bf16[16,64,128]{2,1,0:T(8,128)(2,1)} %get-tuple-element.21), calls=%async_computation | async-start | bytes 524288 | tf_op jit(solution)/shard_map/all_to_all | solution.py:290
  28.6 0.0 copy-start.4
  28.6 0.7 copy-done.4
  29.3 1.1 %shard_map.89.near_ref = f32[64,512]{1,0:T(8,128)S(1)} custom-call(f32[64,512]{1,0:T(8,128)S(1)} %get-tuple-element.23.prod_ref, f32[16,512]{1,0:T(8,128)S(1)} %sqrt_multiply_fusion.coeff_ref, f32[16,512]{1,0:T(8,128)S(1)} %copy-done, f32[1,512]{1,0:T(1,128)S(1)} %bitcast.21), custom_call_target="tpu_custom_call" | custom-call | flops 200000000 | bytes 1000 | tf_op jit(solution)/shard_map/pallas_call | solution.py:329
  30.4 0.0 collective-permute-done.1.other_ref
  30.4 0.1 shard_map.88
  30.5 10.5 %all-to-all-done.q_ref = bf16[16,64,128]{2,1,0:T(8,128)(2,1)S(1)} async-done(((bf16[16,64,128]{2,1,0:T(8,128)(2,1)}), bf16[16,64,128]{2,1,0:T(8,128)(2,1)S(1)}, u32[]{:S(2)}, u32[]{:S(2)}) %all-to-all-start) | async-done | bytes 262176 | tf_op jit(solution)/shard_map/all_to_all | solution.py:290
  41.0 10.9 %all_to_all.26.got_ref = bf16[8,288,128]{2,1,0:T(8,128)(2,1)S(1)} all-to-all(bf16[8,288,128]{2,1,0:T(8,128)(2,1)S(1)} %shard_map.88), channel_id=1, replica_groups={{0,8,64,72,128,136,192,200},{16,24,80,88,144,152,208,216},{32,40,96,104..., dimensions={0} | all-to-all | bytes 1179648 | tf_op jit(solution)/shard_map/all_to_all | solution.py:290
  51.9 2.2 %shard_map.90 = bf16[16,96,128]{2,1,0:T(8,128)(2,1)S(1)} custom-call(s32[1]{0:T(128)} %bitcast.place_ref, bf16[16,64,128]{2,1,0:T(8,128)(2,1)S(1)} %all-to-all-done.q_ref, bf16[8,288,128]{2,1,0:T(8,128)(2,1)S(1)} %all_to_all.26.got_ref, f32[4,16,128]{2,1,0:T(8,128)S(1)} %bitcast_bitcast_fusion.rates_ref), custom_call_target="tpu_custom_call" | custom-call | flops 4000000000 | bytes 1000 | tf_op jit(solution)/shard_map/pallas_call | solution.py:342
  54.1 0.0 copy-start.5
  54.1 14.5 %all_to_all.27.got_ref = bf16[16,96,128]{2,1,0:T(8,128)(2,1)S(1)} all-to-all(bf16[16,96,128]{2,1,0:T(8,128)(2,1)S(1)} %shard_map.90), channel_id=1, replica_groups={{0,16,32,48,64,80,96,112,128,144,160,176,192,208,224,240},{8,24,40,56,7..., dimensions={0} | all-to-all | bytes 786432 | tf_op jit(solution)/shard_map/all_to_all | solution.py:290
  68.6 0.0 copy-done.5
  68.6 1.3 %shard_map.91 = (f32[64,512]{1,0:T(8,128)S(1)}, f32[8,128]{1,0:T(8,128)S(1)}, bf16[64,512]{1,0:T(8,128)(2,1)}) custom-call(s32[1]{0:T(128)} %bitcast.place_ref, bf16[16,96,128]{2,1,0:T(8,128)(2,1)S(1)} %all_to_all.27.got_ref, f32[16,512]{1,0:T(8,128)S(1)} %sqrt_multiply_fusion.coeff_ref, f32[16,512]{1,0:T(8,128)S(1)} %copy-done, ...), custom_call_target="tpu_custom_call" | custom-call | flops 1000000000 | bytes 1000 | tf_op jit(solution)/shard_map/pallas_call | solution.py:350
  69.9 12.3 %all_to_all.28 = f32[8,1,128]{2,1,0:T(1,128)S(1)} all-to-all(f32[8,1,128]{2,1,0:T(1,128)S(1)} %bitcast.16), channel_id=1, replica_groups=mesh['context'=64,'dp'=8] {'dp'}, dimensions={0} | all-to-all | bytes 8192 | tf_op jit(solution)/shard_map/all_to_all | solution.py:356
  82.2 0.7 shard_map.92
  (4 shorter events, 0.0 us)
Async XLA Ops:
  0.6 6.8 %copy-start.2 = (bf16[64,3,512]{2,0,1:T(8,128)(2,1)S(1)}, bf16[64,3,512]{2,0,1:T(8,128)(2,1)}, u32[]{:S(2)}) copy-start(bf16[64,3,512]{2,0,1:T(8,128)(2,1)} %param.13) | copy-start | bytes 589828
  1.4 6.8 %collective-permute-start = (bf16[3,2,512]{2,1,0:T(2,128)(2,1)S(1)}, bf16[3,2,512]{2,1,0:T(2,128)(2,1)S(1)}, u32[]{:S(2)}, u32[]{:S(2)}) collective-permute-start(bf16[3,2,512]{2,1,0:T(2,128)(2,1)S(1)} %slice.4), channel_id=1, source_target_pairs={{0,8},{8,16},{16,24},{24,32},{32,40},{40,48},{48,56},{56,64},{64,7... | collective-permute-start | bytes 18440 | tf_op jit(solution)/shard_map/ppermute | solution.py:299
  7.4 0.9 %copy-start.1 = (bf16[64,3,512]{2,0,1:T(8,128)(2,1)S(1)}, bf16[64,3,512]{2,0,1:T(8,128)(2,1)}, u32[]{:S(2)}) copy-start(bf16[64,3,512]{2,0,1:T(8,128)(2,1)} %param.7) | copy-start | bytes 589828
  7.4 0.9 %copy-start.3 = (f32[3,3,512]{2,1,0:T(4,128)S(1)}, f32[3,3,512]{2,1,0:T(4,128)}, u32[]{:S(2)}) copy-start(f32[3,3,512]{2,1,0:T(4,128)} %weight_ref.1) | copy-start | bytes 55300
  8.2 0.8 copy-start
  9.4 21.0 %collective-permute-start.1 = (bf16[4,144,128]{2,1,0:T(8,128)(2,1)S(1)}, bf16[4,144,128]{2,1,0:T(8,128)(2,1)S(1)}, u32[]{:S(2)}, u32[]{:S(2)}) collective-permute-start(bf16[4,144,128]{2,1,0:T(8,128)(2,1)S(1)} %get-tuple-element.22.own_ref), channel_id=1, source_target_pairs={{0,256},{8,264},{16,272},{24,280},{32,288},{40,296},{48,304},{56,3... | collective-permute-start | bytes 442376 | tf_op jit(solution)/shard_map/ppermute | solution.py:328
  23.6 17.4 %all-to-all-start = ((bf16[16,64,128]{2,1,0:T(8,128)(2,1)}), bf16[16,64,128]{2,1,0:T(8,128)(2,1)S(1)}, u32[]{:S(2)}, u32[]{:S(2)}) async-start(bf16[16,64,128]{2,1,0:T(8,128)(2,1)} %get-tuple-element.21), calls=%async_computation | async-start | bytes 524288 | tf_op jit(solution)/shard_map/all_to_all | solution.py:290
  28.6 0.7 copy-start.4
  54.1 14.5 %copy-start.5 = (f32[512]{0:T(512)S(1)}, f32[512]{0:T(512)}, u32[]{:S(2)}) copy-start(f32[512]{0:T(512)} %param.12) | copy-start | bytes 6148

commit v9 on v7

--- a/solution.py
+++ b/solution.py
@@ -72,23 +72,28 @@
     return tiles
 
 
-def rotate_kernel(attn_ref, cos_ref, sin_ref, q_ref, kv_ref):
+def rotated(x, cosine, sine):
+    x = x.astype(F32)
+    return (x * cosine + pltpu.roll(x, HEAD // 2, 1) * sine).astype(BF)
+
+
+def pair_kernel(attn_ref, cos_ref, sin_ref, kv_ref):
     cosine, sine = cos_ref[...], sin_ref[...]
-    for g in range(2):
-        x = attn_ref[g].astype(F32)
-        for h in range(HEADS_DEV):
-            part = x[:, h * HEAD : (h + 1) * HEAD]
-            turned = (part * cosine + pltpu.roll(part, HEAD // 2, 1) * sine).astype(BF)
-            if g == 0:
-                for w in range(4):
-                    q_ref[h * 4 + w] = turned
-            else:
-                kv_ref[h, :TOK, :] = turned
     for h in range(HEADS_DEV):
-        kv_ref[h, TOK:, :] = attn_ref[2, :, h * HEAD : (h + 1) * HEAD]
-
-
-def state_kernel(feat_ref, rim_ref, weight_ref, rates_ref, kv_ref, sent_ref, gate_ref, prod_ref):
+        lanes = slice(h * HEAD, (h + 1) * HEAD)
+        kv_ref[h, :TOK, :] = rotated(attn_ref[1, :, lanes], cosine, sine)
+        kv_ref[h, TOK:, :] = attn_ref[2, :, lanes]
+
+
+def query_kernel(attn_ref, cos_ref, sin_ref, q_ref):
+    cosine, sine = cos_ref[...], sin_ref[...]
+    for h in range(HEADS_DEV):
+        turned = rotated(attn_ref[0, :, h * HEAD : (h + 1) * HEAD], cosine, sine)
+        for v in range(4):
+            q_ref[h * 4 + v] = turned
+
+
+def state_kernel(feat_ref, rim_ref, weight_ref, rates_ref, state_ref, gate_ref, prod_ref):
     groups = []
     for g in range(3):
         x = jnp.concatenate([rim_ref[g], feat_ref[g].astype(F32)], 0)
@@ -110,14 +115,16 @@
                 total = total * step[n : n + 1, :] + product[8 * a : 8 * a + 8, lanes]
             total = total * jnp.exp(-rates_ref[n : n + 1, lanes] * back)
             rows.append(jnp.sum(total, 0, keepdims=True))
-        sent_ref[part, : 2 * TOK, :] = kv_ref[part]
-        sent_ref[part, 2 * TOK :, :] = jnp.concatenate(rows, 0).astype(BF)
-
-
-def join_kernel(own_ref, other_ref, out_ref):
+        state_ref[part] = jnp.concatenate(rows, 0).astype(BF)
+
+
+def join_kernel(pair_ref, state_ref, far_pair_ref, far_state_ref, out_ref):
     for peer in range(8):
-        out_ref[peer, :PACK, :] = own_ref[peer // 2]
-        out_ref[peer, PACK:, :] = other_ref[peer // 2]
+        head = peer // 2
+        out_ref[peer, : 2 * TOK, :] = pair_ref[head]
+        out_ref[peer, 2 * TOK : PACK, :] = state_ref[head]
+        out_ref[peer, PACK : PACK + 2 * TOK, :] = far_pair_ref[head]
+        out_ref[peer, PACK + 2 * TOK :, :] = far_state_ref[head]
 
 
 def near_kernel(prod_ref, coeff_ref, rates_ref, skip_ref, out_ref, padded, impulse):
@@ -310,31 +317,36 @@
     cosine = jnp.concatenate([cosine, cosine], 1)
     sine = jnp.concatenate([-sine, sine], 1)
 
-    queries, pairs = call(
-        rotate_kernel,
-        [((16, TOK, HEAD), BF), ((HEADS_DEV, 2 * TOK, HEAD), BF)],
-        [VMEM] * 3,
-        1000000000,
+    (pairs,) = call(
+        pair_kernel, [((HEADS_DEV, 2 * TOK, HEAD), BF)], [VMEM] * 3, 1000000000
     )(attn_in, cosine, sine)
+    pairs, cosine = lax.optimization_barrier((pairs, cosine))
+    (queries,) = call(
+        query_kernel, [((16, TOK, HEAD), BF)], [VMEM] * 3, 20000000000
+    )(attn_in, cosine, sine)
+    over_y = [(s, s + devices // 2) for s in range(devices // 2)]
+    far_pairs = lax.ppermute(pairs, "context", over_y)
     queries = exchange(queries, Q_GROUPS)
 
     rim = jnp.pad(rim.astype(F32), ((0, 0), (6, 0), (0, 0)))
-    sent, gate, product = call(
+    states, gate, product = call(
         state_kernel,
-        [((HEADS_DEV, PACK, HEAD), BF), ((TOK, CH), F32), ((TOK, CH), F32)],
-        [VMEM] * 5,
-        20000000000,
-    )(features, rim, feat_weight, rates, pairs)
-    other = lax.ppermute(sent, "context", [(s, s + devices // 2) for s in range(devices // 2)])
+        [((HEADS_DEV, MODES, HEAD), BF), ((TOK, CH), F32), ((TOK, CH), F32)],
+        [VMEM] * 4,
+        1000000,
+    )(features, rim, feat_weight, rates)
+    far_states = lax.ppermute(states, "context", over_y)
     (near,) = call(
         near_kernel,
         [((TOK, CH), F32)],
         [VMEM] * 4,
-        200000000,
+        1000000,
         [pltpu.VMEM((2 * TOK, CH), F32), pltpu.VMEM((TOK, CH), F32)],
     )(product, coeff, rates, skip[None, :])
     quarters = jnp.transpose(rates.reshape(MODES, CH // 128, 128), (1, 0, 2))
-    (both,) = call(join_kernel, [((8, 2 * PACK, HEAD), BF)], [VMEM] * 2, 500000000)(sent, other)
+    (both,) = call(join_kernel, [((8, 2 * PACK, HEAD), BF)], [VMEM] * 4, 50000000000)(
+        pairs, states, far_pairs, far_states
+    )
     queries, both, coeff, quarters, near, gain = lax.optimization_barrier(
         (queries, both, coeff, quarters, near, norm_gain[None, :])
     )

time: 85.7 us -> 84.2 us (0.982)
  the two profiles are of different devices: /device:TPU:32 before, /device:TPU:1 now
where the time goes in v9:
time: 84.2 us; the launch traced here: 83.7 us
  blocking collectives  40.9 us (49%)
  starting transfers between devices  25.4 us (30%)
  waiting for transfers between devices  7.38 us (9%)
  Pallas kernels  6.68 us (8%)
  local copies, waits for them, and re-layouts  2.19 us (3%)
  between operations  0.85 us (1%)
    all_to_all x2, blocking collectives, exchange(): lax.all_to_all(value, 'context', 0, 0, axis_index_groups=groups, tiled=True)  30.1 us
    all_to_all x1, starting transfers between devices, exchange(): lax.all_to_all(value, 'context', 0, 0, axis_index_groups=groups, tiled=True)  11.8 us
    all_to_all x1, blocking collectives, local(): squares = lax.all_to_all(squares, 'dp', 0, 0, tiled=True)  10.7 us
    ppermute x1, starting transfers between devices, local(): far_pairs = lax.ppermute(pairs, 'context', over_y)  7.46 us
    all_to_all x1, waiting for transfers between devices, exchange(): lax.all_to_all(value, 'context', 0, 0, axis_index_groups=groups, tiled=True)  7.37 us
    ppermute x1, starting transfers between devices, local(): lax.ppermute(features[:, TOK - (FEAT - 1):], 'context', [(s, s + 1) for s...  4.83 us
    pallas_call x1, Pallas kernels, local(): call(attend_kernel, [((16, TOK + 32, HEAD), BF)], [SMEM] + [VMEM] * 3, 40...  2.17 us
  transfers between devices with their start and end apart: 4, of which 1 were waited for; matrix products, arithmetic and copies ran while one was open for 0% of the time, Pallas kernels for 3%

profile of v9, /device:TPU:1, one launch (start us, length us, event | category | flops | bytes accessed | tf_op | source)
XLA Modules:
  0.0 83.7 jit_solution(2957661396160601370)
XLA Ops:
  0.6 0.0 copy-start.4
  0.6 0.8 slice.4
  1.4 4.8 %collective-permute-start = (bf16[3,2,512]{2,1,0:T(2,128)(2,1)S(1)}, bf16[3,2,512]{2,1,0:T(2,128)(2,1)S(1)}, u32[]{:S(2)}, u32[]{:S(2)}) collective-permute-start(bf16[3,2,512]{2,1,0:T(2,128)(2,1)S(1)} %slice.4), channel_id=1, source_target_pairs={{0,8},{8,16},{16,24},{24,32},{32,40},{40,48},{48,56},{56,64},{64,7... | collective-permute-start | bytes 18440 | tf_op jit(solution)/shard_map/ppermute | solution.py:306
  6.3 0.2 fusion
  6.5 0.1 pad_maximum_fusion
  6.6 0.0 copy-done.4
  6.6 0.1 shard_map.86.pair_ref
  6.7 7.5 %collective-permute-start.1 = (bf16[4,128,128]{2,1,0:T(8,128)(2,1)S(1)}, bf16[4,128,128]{2,1,0:T(8,128)(2,1)S(1)}, u32[]{:S(2)}, u32[]{:S(2)}) collective-permute-start(bf16[4,128,128]{2,1,0:T(8,128)(2,1)S(1)} %shard_map.86.pair_ref), channel_id=1, source_target_pairs={{0,256},{8,264},{16,272},{24,280},{32,288},{40,296},{48,304},{56,3... | collective-permute-start | bytes 393224 | tf_op jit(solution)/shard_map/ppermute | solution.py:328
  14.2 0.0 copy-start.1
  14.2 0.8 shard_map.87
  15.0 0.0 copy-start
  15.0 0.0 copy-start.6
  15.0 11.8 %all-to-all-start = ((bf16[16,64,128]{2,1,0:T(8,128)(2,1)}), bf16[16,64,128]{2,1,0:T(8,128)(2,1)S(1)}, u32[]{:S(2)}, u32[]{:S(2)}) async-start(bf16[16,64,128]{2,1,0:T(8,128)(2,1)} %shard_map.87), calls=%async_computation | async-start | bytes 524288 | tf_op jit(solution)/shard_map/all_to_all | solution.py:297
  26.8 0.0 copy-done
  26.8 0.0 copy-done.6
  26.9 0.0 copy-start.2
  26.9 0.0 collective-permute-done
  26.9 0.0 copy-done.1
  26.9 0.7 copy-done.2
  27.6 0.4 shard_map.88
  28.0 1.3 %collective-permute-start.2 = (bf16[4,16,128]{2,1,0:T(8,128)(2,1)S(1)}, bf16[4,16,128]{2,1,0:T(8,128)(2,1)S(1)}, u32[]{:S(2)}, u32[]{:S(2)}) collective-permute-start(bf16[4,16,128]{2,1,0:T(8,128)(2,1)S(1)} %get-tuple-element.18.state_ref), channel_id=1, source_target_pairs={{0,256},{8,264},{16,272},{24,280},{32,288},{40,296},{48,304},{56,3... | collective-permute-start | bytes 49160 | tf_op jit(solution)/shard_map/ppermute | solution.py:338
  29.3 0.0 copy-start.3
  29.3 0.7 copy-done.3
  30.0 1.1 %shard_map.90.near_ref = f32[64,512]{1,0:T(8,128)S(1)} custom-call(f32[64,512]{1,0:T(8,128)S(1)} %get-tuple-element.19.prod_ref, f32[16,512]{1,0:T(8,128)S(1)} %sqrt_multiply_fusion.coeff_ref, f32[16,512]{1,0:T(8,128)S(1)} %copy-done, f32[1,512]{1,0:T(1,128)S(1)} %bitcast.20), custom_call_target="tpu_custom_call" | custom-call | flops 1000000 | bytes 1000 | tf_op jit(solution)/shard_map/pallas_call | solution.py:339
  31.1 0.0 collective-permute-done.2.far_state_ref
  31.1 0.0 collective-permute-done.1.far_pair_ref
  31.2 0.1 shard_map.89
  31.2 7.4 %all-to-all-done.q_ref = bf16[16,64,128]{2,1,0:T(8,128)(2,1)S(1)} async-done(((bf16[16,64,128]{2,1,0:T(8,128)(2,1)}), bf16[16,64,128]{2,1,0:T(8,128)(2,1)S(1)}, u32[]{:S(2)}, u32[]{:S(2)}) %all-to-all-start) | async-done | bytes 262176 | tf_op jit(solution)/shard_map/all_to_all | solution.py:297
  38.6 12.0 %all_to_all.26.got_ref = bf16[8,288,128]{2,1,0:T(8,128)(2,1)S(1)} all-to-all(bf16[8,288,128]{2,1,0:T(8,128)(2,1)S(1)} %shard_map.89), channel_id=1, replica_groups={{0,8,64,72,128,136,192,200},{16,24,80,88,144,152,208,216},{32,40,96,104..., dimensions={0} | all-to-all | bytes 1179648 | tf_op jit(solution)/shard_map/all_to_all | solution.py:297
  50.6 2.2 %shard_map.91 = bf16[16,96,128]{2,1,0:T(8,128)(2,1)S(1)} custom-call(s32[1]{0:T(128)} %bitcast.place_ref, bf16[16,64,128]{2,1,0:T(8,128)(2,1)S(1)} %all-to-all-done.q_ref, bf16[8,288,128]{2,1,0:T(8,128)(2,1)S(1)} %all_to_all.26.got_ref, f32[4,16,128]{2,1,0:T(8,128)S(1)} %bitcast_bitcast_fusion.rates_ref), custom_call_target="tpu_custom_call" | custom-call | flops 4000000000 | bytes 1000 | tf_op jit(solution)/shard_map/pallas_call | solution.py:354
  52.8 0.0 copy-start.5
  52.8 18.2 %all_to_all.27.got_ref = bf16[16,96,128]{2,1,0:T(8,128)(2,1)S(1)} all-to-all(bf16[16,96,128]{2,1,0:T(8,128)(2,1)S(1)} %shard_map.91), channel_id=1, replica_groups={{0,16,32,48,64,80,96,112,128,144,160,176,192,208,224,240},{8,24,40,56,7..., dimensions={0} | all-to-all | bytes 786432 | tf_op jit(solution)/shard_map/all_to_all | solution.py:297
  70.9 0.0 copy-done.5
  70.9 1.3 %shard_map.92 = (f32[64,512]{1,0:T(8,128)S(1)}, f32[8,128]{1,0:T(8,128)S(1)}, bf16[64,512]{1,0:T(8,128)(2,1)}) custom-call(s32[1]{0:T(128)} %bitcast.place_ref, bf16[16,96,128]{2,1,0:T(8,128)(2,1)S(1)} %all_to_all.27.got_ref, f32[16,512]{1,0:T(8,128)S(1)} %sqrt_multiply_fusion.coeff_ref, f32[16,512]{1,0:T(8,128)S(1)} %copy-done, ...), custom_call_target="tpu_custom_call" | custom-call | flops 1000000000 | bytes 1000 | tf_op jit(solution)/shard_map/pallas_call | solution.py:362
  72.2 10.7 %all_to_all.28 = f32[8,1,128]{2,1,0:T(1,128)S(1)} all-to-all(f32[8,1,128]{2,1,0:T(1,128)S(1)} %bitcast.18), channel_id=1, replica_groups=mesh['context'=64,'dp'=8] {'dp'}, dimensions={0} | all-to-all | bytes 8192 | tf_op jit(solution)/shard_map/all_to_all | solution.py:368
  83.0 0.7 shard_map.93
  (5 shorter events, 0.1 us)
Async XLA Ops:
  0.6 6.0 %copy-start.4 = (bf16[64,3,512]{2,0,1:T(8,128)(2,1)S(1)}, bf16[64,3,512]{2,0,1:T(8,128)(2,1)}, u32[]{:S(2)}) copy-start(bf16[64,3,512]{2,0,1:T(8,128)(2,1)} %param.13) | copy-start | bytes 589828
  1.4 25.5 %collective-permute-start = (bf16[3,2,512]{2,1,0:T(2,128)(2,1)S(1)}, bf16[3,2,512]{2,1,0:T(2,128)(2,1)S(1)}, u32[]{:S(2)}, u32[]{:S(2)}) collective-permute-start(bf16[3,2,512]{2,1,0:T(2,128)(2,1)S(1)} %slice.4), channel_id=1, source_target_pairs={{0,8},{8,16},{16,24},{24,32},{32,40},{40,48},{48,56},{56,64},{64,7... | collective-permute-start | bytes 18440 | tf_op jit(solution)/shard_map/ppermute | solution.py:306
  6.7 24.4 %collective-permute-start.1 = (bf16[4,128,128]{2,1,0:T(8,128)(2,1)S(1)}, bf16[4,128,128]{2,1,0:T(8,128)(2,1)S(1)}, u32[]{:S(2)}, u32[]{:S(2)}) collective-permute-start(bf16[4,128,128]{2,1,0:T(8,128)(2,1)S(1)} %shard_map.86.pair_ref), channel_id=1, source_target_pairs={{0,256},{8,264},{16,272},{24,280},{32,288},{40,296},{48,304},{56,3... | collective-permute-start | bytes 393224 | tf_op jit(solution)/shard_map/ppermute | solution.py:328
  14.2 12.7 %copy-start.1 = (bf16[64,3,512]{2,0,1:T(8,128)(2,1)S(1)}, bf16[64,3,512]{2,0,1:T(8,128)(2,1)}, u32[]{:S(2)}) copy-start(bf16[64,3,512]{2,0,1:T(8,128)(2,1)} %param.7) | copy-start | bytes 589828
  15.0 11.8 %copy-start = (f32[16,512]{1,0:T(8,128)S(1)}, f32[16,512]{1,0:T(8,128)}, u32[]{:S(2)}) copy-start(f32[16,512]{1,0:T(8,128)} %rates_ref.5) | copy-start | bytes 98308
  15.0 11.8 %copy-start.6 = (f32[16,512]{1,0:T(8,128)S(1)}, f32[16,512]{1,0:T(8,128)}, u32[]{:S(2)}) copy-start(f32[16,512]{1,0:T(8,128)} %param.10) | copy-start | bytes 98308
  15.0 23.6 %all-to-all-start = ((bf16[16,64,128]{2,1,0:T(8,128)(2,1)}), bf16[16,64,128]{2,1,0:T(8,128)(2,1)S(1)}, u32[]{:S(2)}, u32[]{:S(2)}) async-start(bf16[16,64,128]{2,1,0:T(8,128)(2,1)} %shard_map.87), calls=%async_computation | async-start | bytes 524288 | tf_op jit(solution)/shard_map/all_to_all | solution.py:297
  26.9 0.7 copy-start.2
  28.0 3.1 %collective-permute-start.2 = (bf16[4,16,128]{2,1,0:T(8,128)(2,1)S(1)}, bf16[4,16,128]{2,1,0:T(8,128)(2,1)S(1)}, u32[]{:S(2)}, u32[]{:S(2)}) collective-permute-start(bf16[4,16,128]{2,1,0:T(8,128)(2,1)S(1)} %get-tuple-element.18.state_ref), channel_id=1, source_target_pairs={{0,256},{8,264},{16,272},{24,280},{32,288},{40,296},{48,304},{56,3... | collective-permute-start | bytes 49160 | tf_op jit(solution)/shard_map/ppermute | solution.py:338
  29.3 0.7 copy-start.3
  52.8 18.2 %copy-start.5 = (f32[512]{0:T(512)S(1)}, f32[512]{0:T(512)}, u32[]{:S(2)}) copy-start(f32[512]{0:T(512)} %param.12) | copy-start | bytes 6148

commit v10 on v7

--- a/solution.py
+++ b/solution.py
@@ -88,7 +88,7 @@
         kv_ref[h, TOK:, :] = attn_ref[2, :, h * HEAD : (h + 1) * HEAD]
 
 
-def state_kernel(feat_ref, rim_ref, weight_ref, rates_ref, kv_ref, sent_ref, gate_ref, prod_ref):
+def state_kernel(feat_ref, rim_ref, weight_ref, rates_ref, state_ref, gate_ref, prod_ref):
     groups = []
     for g in range(3):
         x = jnp.concatenate([rim_ref[g], feat_ref[g].astype(F32)], 0)
@@ -110,14 +110,16 @@
                 total = total * step[n : n + 1, :] + product[8 * a : 8 * a + 8, lanes]
             total = total * jnp.exp(-rates_ref[n : n + 1, lanes] * back)
             rows.append(jnp.sum(total, 0, keepdims=True))
-        sent_ref[part, : 2 * TOK, :] = kv_ref[part]
-        sent_ref[part, 2 * TOK :, :] = jnp.concatenate(rows, 0).astype(BF)
-
-
-def join_kernel(own_ref, other_ref, out_ref):
+        state_ref[part] = jnp.concatenate(rows, 0).astype(BF)
+
+
+def join_kernel(pair_ref, state_ref, far_pair_ref, far_state_ref, out_ref):
     for peer in range(8):
-        out_ref[peer, :PACK, :] = own_ref[peer // 2]
-        out_ref[peer, PACK:, :] = other_ref[peer // 2]
+        head = peer // 2
+        out_ref[peer, : 2 * TOK, :] = pair_ref[head]
+        out_ref[peer, 2 * TOK : PACK, :] = state_ref[head]
+        out_ref[peer, PACK : PACK + 2 * TOK, :] = far_pair_ref[head]
+        out_ref[peer, PACK + 2 * TOK :, :] = far_state_ref[head]
 
 
 def near_kernel(prod_ref, coeff_ref, rates_ref, skip_ref, out_ref, padded, impulse):
@@ -316,25 +318,29 @@
         [VMEM] * 3,
         1000000000,
     )(attn_in, cosine, sine)
+    over_y = [(s, s + devices // 2) for s in range(devices // 2)]
+    far_pairs = lax.ppermute(pairs, "context", over_y)
     queries = exchange(queries, Q_GROUPS)
 
     rim = jnp.pad(rim.astype(F32), ((0, 0), (6, 0), (0, 0)))
-    sent, gate, product = call(
+    states, gate, product = call(
         state_kernel,
-        [((HEADS_DEV, PACK, HEAD), BF), ((TOK, CH), F32), ((TOK, CH), F32)],
-        [VMEM] * 5,
-        20000000000,
-    )(features, rim, feat_weight, rates, pairs)
-    other = lax.ppermute(sent, "context", [(s, s + devices // 2) for s in range(devices // 2)])
+        [((HEADS_DEV, MODES, HEAD), BF), ((TOK, CH), F32), ((TOK, CH), F32)],
+        [VMEM] * 4,
+        1000000,
+    )(features, rim, feat_weight, rates)
+    far_states = lax.ppermute(states, "context", over_y)
     (near,) = call(
         near_kernel,
         [((TOK, CH), F32)],
         [VMEM] * 4,
-        200000000,
+        1000000,
         [pltpu.VMEM((2 * TOK, CH), F32), pltpu.VMEM((TOK, CH), F32)],
     )(product, coeff, rates, skip[None, :])
     quarters = jnp.transpose(rates.reshape(MODES, CH // 128, 128), (1, 0, 2))
-    (both,) = call(join_kernel, [((8, 2 * PACK, HEAD), BF)], [VMEM] * 2, 500000000)(sent, other)
+    (both,) = call(join_kernel, [((8, 2 * PACK, HEAD), BF)], [VMEM] * 4, 50000000000)(
+        pairs, states, far_pairs, far_states
+    )
     queries, both, coeff, quarters, near, gain = lax.optimization_barrier(
         (queries, both, coeff, quarters, near, norm_gain[None, :])
     )

time: 85.7 us -> 84.3 us (0.984)
  blocking collectives: 47 us -> 45.6 us
  starting transfers between devices: 17.7 us -> 19 us
  waiting for transfers between devices: 9.02 us -> 7.72 us
    all_to_all x1, blocking collectives: 13.6 us -> 12.1 us  [local(): squares = lax.all_to_all(squares, 'dp', 0, 0, tiled=True)]
    ppermute x1 -> x2, waiting for transfers between devices: 7.83 us -> 6.53 us  [the longest x1 6.53 us: local(): far_states = lax.ppermute(states, 'context', over_y)]
    ppermute x1 -> x2, starting transfers between devices: 1.29 us -> 2.58 us  [the longest x1 1.29 us: local(): far_pairs = lax.ppermute(pairs, 'context', over_y)]
  transfers between devices with their start and end apart: 3 -> 4, of which waited for: 2 -> 2; matrix products, arithmetic and copies ran while one was open for 0% -> 0% of each run, Pallas kernels for 3% -> 3%
where the time goes in v10:
time: 84.3 us; the launch traced here: 83.9 us
  blocking collectives  45.6 us (54%)
  starting transfers between devices  19 us (23%)
  Pallas kernels  8.23 us (10%)
  waiting for transfers between devices  7.72 us (9%)
  local copies, waits for them, and re-layouts  2.19 us (3%)
    all_to_all x2, blocking collectives, exchange(): lax.all_to_all(value, 'context', 0, 0, axis_index_groups=groups, tiled=True)  33.5 us
    all_to_all x1, blocking collectives, local(): squares = lax.all_to_all(squares, 'dp', 0, 0, tiled=True)  12.1 us
    all_to_all x1, starting transfers between devices, exchange(): lax.all_to_all(value, 'context', 0, 0, axis_index_groups=groups, tiled=True)  12.1 us
    ppermute x1, waiting for transfers between devices, local(): far_states = lax.ppermute(states, 'context', over_y)  6.53 us
    ppermute x1, starting transfers between devices, local(): lax.ppermute(features[:, TOK - (FEAT - 1):], 'context', [(s, s + 1) for s...  4.28 us
    pallas_call x1, Pallas kernels, local(): call(attend_kernel, [((16, TOK + 32, HEAD), BF)], [SMEM] + [VMEM] * 3, 40...  3.81 us
  transfers between devices with their start and end apart: 4, of which 2 were waited for; matrix products, arithmetic and copies ran while one was open for 0% of the time, Pallas kernels for 3%

profile of v10, /device:TPU:32, one launch (start us, length us, event | category | flops | bytes accessed | tf_op | source)
XLA Modules:
  0.0 83.9 jit_solution(481058528917890183)
XLA Ops:
  0.6 0.0 copy-start.4
  0.6 0.8 slice.4
  1.4 4.3 %collective-permute-start = (bf16[3,2,512]{2,1,0:T(2,128)(2,1)S(1)}, bf16[3,2,512]{2,1,0:T(2,128)(2,1)S(1)}, u32[]{:S(2)}, u32[]{:S(2)}) collective-permute-start(bf16[3,2,512]{2,1,0:T(2,128)(2,1)S(1)} %slice.4), channel_id=1, source_target_pairs={{0,8},{8,16},{16,24},{24,32},{32,40},{40,48},{48,56},{56,64},{64,7... | collective-permute-start | bytes 18440 | tf_op jit(solution)/shard_map/ppermute | solution.py:301
  5.8 0.2 fusion
  6.0 0.1 pad_maximum_fusion
  6.0 0.0 copy-done.4
  6.1 0.8 shard_map.86
  6.8 0.0 copy-start
  6.8 0.0 copy-start.6
  6.9 0.0 copy-start.1
  6.9 12.1 %all-to-all-start = ((bf16[16,64,128]{2,1,0:T(8,128)(2,1)}), bf16[16,64,128]{2,1,0:T(8,128)(2,1)S(1)}, u32[]{:S(2)}, u32[]{:S(2)}) async-start(bf16[16,64,128]{2,1,0:T(8,128)(2,1)} %get-tuple-element.16), calls=%async_computation | async-start | bytes 524288 | tf_op jit(solution)/shard_map/all_to_all | solution.py:292
  19.0 1.3 %collective-permute-start.1 = (bf16[4,128,128]{2,1,0:T(8,128)(2,1)S(1)}, bf16[4,128,128]{2,1,0:T(8,128)(2,1)S(1)}, u32[]{:S(2)}, u32[]{:S(2)}) collective-permute-start(bf16[4,128,128]{2,1,0:T(8,128)(2,1)S(1)} %get-tuple-element.17.pair_ref), channel_id=1, source_target_pairs={{0,256},{8,264},{16,272},{24,280},{32,288},{40,296},{48,304},{56,3... | collective-permute-start | bytes 393224 | tf_op jit(solution)/shard_map/ppermute | solution.py:322
  20.3 0.0 copy-done
  20.3 0.0 copy-done.6
  20.3 0.0 copy-start.2
  20.3 0.0 collective-permute-done
  20.4 0.0 copy-done.1
  20.4 0.7 copy-done.2
  21.1 0.4 shard_map.87
  21.5 1.3 %collective-permute-start.2 = (bf16[4,16,128]{2,1,0:T(8,128)(2,1)S(1)}, bf16[4,16,128]{2,1,0:T(8,128)(2,1)S(1)}, u32[]{:S(2)}, u32[]{:S(2)}) collective-permute-start(bf16[4,16,128]{2,1,0:T(8,128)(2,1)S(1)} %get-tuple-element.18.state_ref), channel_id=1, source_target_pairs={{0,256},{8,264},{16,272},{24,280},{32,288},{40,296},{48,304},{56,3... | collective-permute-start | bytes 49160 | tf_op jit(solution)/shard_map/ppermute | solution.py:332
  22.8 0.0 copy-start.3
  22.8 0.7 copy-done.3
  23.5 1.1 %shard_map.89.near_ref = f32[64,512]{1,0:T(8,128)S(1)} custom-call(f32[64,512]{1,0:T(8,128)S(1)} %get-tuple-element.19.prod_ref, f32[16,512]{1,0:T(8,128)S(1)} %sqrt_multiply_fusion.coeff_ref, f32[16,512]{1,0:T(8,128)S(1)} %copy-done, f32[1,512]{1,0:T(1,128)S(1)} %bitcast.20), custom_call_target="tpu_custom_call" | custom-call | flops 1000000 | bytes 1000 | tf_op jit(solution)/shard_map/pallas_call | solution.py:333
  24.6 6.5 %collective-permute-done.2.far_state_ref = bf16[4,16,128]{2,1,0:T(8,128)(2,1)S(1)} collective-permute-done((bf16[4,16,128]{2,1,0:T(8,128)(2,1)S(1)}, bf16[4,16,128]{2,1,0:T(8,128)(2,1)S(1)}, u32[]{:S(2)}, u32[]{:S(2)}) %collective-permute-start.2) | collective-permute-done | bytes 16416 | tf_op jit(solution)/shard_map/ppermute | solution.py:332
  31.1 0.0 collective-permute-done.1.far_pair_ref
  31.1 0.1 shard_map.88
  31.2 1.2 %all-to-all-done.q_ref = bf16[16,64,128]{2,1,0:T(8,128)(2,1)S(1)} async-done(((bf16[16,64,128]{2,1,0:T(8,128)(2,1)}), bf16[16,64,128]{2,1,0:T(8,128)(2,1)S(1)}, u32[]{:S(2)}, u32[]{:S(2)}) %all-to-all-start) | async-done | bytes 262176 | tf_op jit(solution)/shard_map/all_to_all | solution.py:292
  32.4 13.4 %all_to_all.26.got_ref = bf16[8,288,128]{2,1,0:T(8,128)(2,1)S(1)} all-to-all(bf16[8,288,128]{2,1,0:T(8,128)(2,1)S(1)} %shard_map.88), channel_id=1, replica_groups={{0,8,64,72,128,136,192,200},{16,24,80,88,144,152,208,216},{32,40,96,104..., dimensions={0} | all-to-all | bytes 1179648 | tf_op jit(solution)/shard_map/all_to_all | solution.py:292
  45.8 3.8 %shard_map.90 = bf16[16,96,128]{2,1,0:T(8,128)(2,1)S(1)} custom-call(s32[1]{0:T(128)} %bitcast.place_ref, bf16[16,64,128]{2,1,0:T(8,128)(2,1)S(1)} %all-to-all-done.q_ref, bf16[8,288,128]{2,1,0:T(8,128)(2,1)S(1)} %all_to_all.26.got_ref, f32[4,16,128]{2,1,0:T(8,128)S(1)} %bitcast_bitcast_fusion.rates_ref), custom_call_target="tpu_custom_call" | custom-call | flops 4000000000 | bytes 1000 | tf_op jit(solution)/shard_map/pallas_call | solution.py:348
  49.6 0.0 copy-start.5
  49.6 20.1 %all_to_all.27.got_ref = bf16[16,96,128]{2,1,0:T(8,128)(2,1)S(1)} all-to-all(bf16[16,96,128]{2,1,0:T(8,128)(2,1)S(1)} %shard_map.90), channel_id=1, replica_groups={{0,16,32,48,64,80,96,112,128,144,160,176,192,208,224,240},{8,24,40,56,7..., dimensions={0} | all-to-all | bytes 786432 | tf_op jit(solution)/shard_map/all_to_all | solution.py:292
  69.7 0.0 copy-done.5
  69.7 1.3 %shard_map.91 = (f32[64,512]{1,0:T(8,128)S(1)}, f32[8,128]{1,0:T(8,128)S(1)}, bf16[64,512]{1,0:T(8,128)(2,1)}) custom-call(s32[1]{0:T(128)} %bitcast.place_ref, bf16[16,96,128]{2,1,0:T(8,128)(2,1)S(1)} %all_to_all.27.got_ref, f32[16,512]{1,0:T(8,128)S(1)} %sqrt_multiply_fusion.coeff_ref, f32[16,512]{1,0:T(8,128)S(1)} %copy-done, ...), custom_call_target="tpu_custom_call" | custom-call | flops 1000000000 | bytes 1000 | tf_op jit(solution)/shard_map/pallas_call | solution.py:356
  71.0 12.1 %all_to_all.28 = f32[8,1,128]{2,1,0:T(1,128)S(1)} all-to-all(f32[8,1,128]{2,1,0:T(1,128)S(1)} %bitcast.18), channel_id=1, replica_groups=mesh['context'=64,'dp'=8] {'dp'}, dimensions={0} | all-to-all | bytes 8192 | tf_op jit(solution)/shard_map/all_to_all | solution.py:362
  83.1 0.7 shard_map.92
  (5 shorter events, 0.1 us)
Async XLA Ops:
  0.6 5.4 %copy-start.4 = (bf16[64,3,512]{2,0,1:T(8,128)(2,1)S(1)}, bf16[64,3,512]{2,0,1:T(8,128)(2,1)}, u32[]{:S(2)}) copy-start(bf16[64,3,512]{2,0,1:T(8,128)(2,1)} %param.13) | copy-start | bytes 589828
  1.4 18.9 %collective-permute-start = (bf16[3,2,512]{2,1,0:T(2,128)(2,1)S(1)}, bf16[3,2,512]{2,1,0:T(2,128)(2,1)S(1)}, u32[]{:S(2)}, u32[]{:S(2)}) collective-permute-start(bf16[3,2,512]{2,1,0:T(2,128)(2,1)S(1)} %slice.4), channel_id=1, source_target_pairs={{0,8},{8,16},{16,24},{24,32},{32,40},{40,48},{48,56},{56,64},{64,7... | collective-permute-start | bytes 18440 | tf_op jit(solution)/shard_map/ppermute | solution.py:301
  6.8 13.4 %copy-start = (f32[16,512]{1,0:T(8,128)S(1)}, f32[16,512]{1,0:T(8,128)}, u32[]{:S(2)}) copy-start(f32[16,512]{1,0:T(8,128)} %rates_ref.5) | copy-start | bytes 98308
  6.8 13.4 %copy-start.6 = (f32[16,512]{1,0:T(8,128)S(1)}, f32[16,512]{1,0:T(8,128)}, u32[]{:S(2)}) copy-start(f32[16,512]{1,0:T(8,128)} %param.10) | copy-start | bytes 98308
  6.9 13.5 %copy-start.1 = (bf16[64,3,512]{2,0,1:T(8,128)(2,1)S(1)}, bf16[64,3,512]{2,0,1:T(8,128)(2,1)}, u32[]{:S(2)}) copy-start(bf16[64,3,512]{2,0,1:T(8,128)(2,1)} %param.7) | copy-start | bytes 589828
  6.9 25.5 %all-to-all-start = ((bf16[16,64,128]{2,1,0:T(8,128)(2,1)}), bf16[16,64,128]{2,1,0:T(8,128)(2,1)S(1)}, u32[]{:S(2)}, u32[]{:S(2)}) async-start(bf16[16,64,128]{2,1,0:T(8,128)(2,1)} %get-tuple-element.16), calls=%async_computation | async-start | bytes 524288 | tf_op jit(solution)/shard_map/all_to_all | solution.py:292
  19.0 12.2 %collective-permute-start.1 = (bf16[4,128,128]{2,1,0:T(8,128)(2,1)S(1)}, bf16[4,128,128]{2,1,0:T(8,128)(2,1)S(1)}, u32[]{:S(2)}, u32[]{:S(2)}) collective-permute-start(bf16[4,128,128]{2,1,0:T(8,128)(2,1)S(1)} %get-tuple-element.17.pair_ref), channel_id=1, source_target_pairs={{0,256},{8,264},{16,272},{24,280},{32,288},{40,296},{48,304},{56,3... | collective-permute-start | bytes 393224 | tf_op jit(solution)/shard_map/ppermute | solution.py:322
  20.3 0.7 copy-start.2
  21.5 9.6 %collective-permute-start.2 = (bf16[4,16,128]{2,1,0:T(8,128)(2,1)S(1)}, bf16[4,16,128]{2,1,0:T(8,128)(2,1)S(1)}, u32[]{:S(2)}, u32[]{:S(2)}) collective-permute-start(bf16[4,16,128]{2,1,0:T(8,128)(2,1)S(1)} %get-tuple-element.18.state_ref), channel_id=1, source_target_pairs={{0,256},{8,264},{16,272},{24,280},{32,288},{40,296},{48,304},{56,3... | collective-permute-start | bytes 49160 | tf_op jit(solution)/shard_map/ppermute | solution.py:332
  22.8 0.7 copy-start.3
  49.6 20.1 %copy-start.5 = (f32[512]{0:T(512)S(1)}, f32[512]{0:T(512)}, u32[]{:S(2)}) copy-start(f32[512]{0:T(512)} %param.12) | copy-start | bytes 6148

commit v11 on v10

--- a/solution.py
+++ b/solution.py
@@ -19,7 +19,7 @@
 ROPE_BASE = 1000000.0
 NEG = -1e30
 PACK = 2 * TOK + MODES
-WIDE = 256
+WIDE = 512
 BLOCKS = WIDE // TOK
 BF = jnp.bfloat16
 F32 = jnp.float32
@@ -179,14 +179,14 @@
 
 def attend(keys, values, query, mask):
     scores = lax.dot_general(
-        keys, query, (((1,), (1,)), ((), ())), preferred_element_type=F32
+        query, keys, (((1,), (1,)), ((), ())), preferred_element_type=F32
     ) * (math.log2(math.e) / math.sqrt(HEAD))
     scores = mask(scores)
-    top = jnp.max(scores, 0, keepdims=True)
+    top = jnp.max(scores, 1, keepdims=True)
     weights = jnp.exp2(scores - top)
-    total = jnp.sum(weights, 0, keepdims=True)
+    total = jnp.sum(weights, 1, keepdims=True)
     mixed = lax.dot_general(
-        values, weights.astype(BF), (((0,), (0,)), ((), ())), preferred_element_type=F32
+        weights.astype(BF), values, (((1,), (0,)), ((), ())), preferred_element_type=F32
     )
     return top, total, mixed
 
@@ -200,37 +200,37 @@
         return keys, got_ref[:, first + TOK : first + 2 * TOK, :].reshape(8 * TOK, HEAD)
 
     own, other = half(0), half(PACK)
-    row = lax.broadcasted_iota(jnp.int32, (8 * TOK, 1), 0)
-    block = row // TOK
-    key_pos = ((block // 2) * 8 + 2 * v + block % 2) * TOK + row % TOK
+    lane = lax.broadcasted_iota(jnp.int32, (1, 8 * TOK), 1)
+    block = lane // TOK
+    key_pos = ((block // 2) * 8 + 2 * v + block % 2) * TOK + lane % TOK
     which = lax.broadcasted_iota(jnp.int32, (16, 128), 0)
 
     def query_of(tile):
         return q_ref[tile * BLOCKS : (tile + 1) * BLOCKS].reshape(WIDE, HEAD)
 
     def own_part(tile):
-        lane = lax.broadcasted_iota(jnp.int32, (1, WIDE), 1) + tile * WIDE
-        q_block = lane // TOK
-        q_pos = ((q_block // 4) * 8 + 2 * (q_block % 4) + u) * TOK + lane % TOK
+        row = lax.broadcasted_iota(jnp.int32, (WIDE, 1), 0) + tile * WIDE
+        q_block = row // TOK
+        q_pos = ((q_block // 4) * 8 + 2 * (q_block % 4) + u) * TOK + row % TOK
         return attend(*own, query_of(tile), lambda s: jnp.where(key_pos <= q_pos, s, NEG))
 
     def write(tile, top, total, mixed):
-        mixed = jnp.transpose(mixed).astype(BF)
-        level = top + jnp.log2(total)
-        high = level.astype(BF).astype(F32)
-        rest = level - high
-        middle = rest.astype(BF).astype(F32)
-        last = rest - middle
-        for b in range(BLOCKS):
-            place = tile * BLOCKS + b
-            out_ref[place, :TOK, :] = mixed[b * TOK : (b + 1) * TOK]
-            part = slice((b // 2) * 128, (b // 2) * 128 + 128)
+        mixed = mixed.astype(BF).reshape(BLOCKS, TOK, HEAD)
+        out_ref[tile * BLOCKS : (tile + 1) * BLOCKS, :TOK, :] = mixed
+        level = jnp.broadcast_to(top + jnp.log2(total), (WIDE, 128))
+        for pair in range(WIDE // 128):
+            row = jnp.transpose(level[pair * 128 : (pair + 1) * 128])[:1, :]
+            high = row.astype(BF).astype(F32)
+            rest = row - high
+            middle = rest.astype(BF).astype(F32)
+            last = rest - middle
             stats = jnp.where(
                 which == 0,
-                high[:, part],
-                jnp.where(which == 1, middle[:, part], jnp.where(which == 2, last[:, part], 0.0)),
-            )
-            out_ref[place, TOK:80, :] = stats.astype(BF)
+                high,
+                jnp.where(which == 1, middle, jnp.where(which == 2, last, 0.0)),
+            ).astype(BF)
+            for b in range(2):
+                out_ref[tile * BLOCKS + 2 * pair + b, TOK:80, :] = stats
 
     @pl.when(y == 0)
     def _():

time: 84.3 us -> 82.9 us (0.983)
  the two profiles are of different devices: /device:TPU:32 before, /device:TPU:1 now
where the time goes in v11:
time: 82.9 us; the launch traced here: 81.5 us
  blocking collectives  46.7 us (56%)
  starting transfers between devices  25.4 us (31%)
  Pallas kernels  6.05 us (7%)
  local copies, waits for them, and re-layouts  2.18 us (3%)
  between operations  0.83 us (1%)
    all_to_all x2, blocking collectives, exchange(): lax.all_to_all(value, 'context', 0, 0, axis_index_groups=groups, tiled=True)  33.4 us
    all_to_all x1, blocking collectives, local(): squares = lax.all_to_all(squares, 'dp', 0, 0, tiled=True)  13.3 us
    all_to_all x1, starting transfers between devices, exchange(): lax.all_to_all(value, 'context', 0, 0, axis_index_groups=groups, tiled=True)  11.8 us
    ppermute x1, starting transfers between devices, local(): far_pairs = lax.ppermute(pairs, 'context', over_y)  7.46 us
    ppermute x1, starting transfers between devices, local(): lax.ppermute(features[:, TOK - (FEAT - 1):], 'context', [(s, s + 1) for s...  4.83 us
  transfers between devices with their start and end apart: 4, of which 0 were waited for; matrix products, arithmetic and copies ran while one was open for 0% of the time, Pallas kernels for 3%

profile of v11, /device:TPU:1, one launch (start us, length us, event | category | flops | bytes accessed | tf_op | source)
XLA Modules:
  0.0 81.5 jit_solution(6750035308191288448)
XLA Ops:
  0.6 0.0 copy-start.4
  0.6 0.8 slice.4
  1.4 4.8 %collective-permute-start = (bf16[3,2,512]{2,1,0:T(2,128)(2,1)S(1)}, bf16[3,2,512]{2,1,0:T(2,128)(2,1)S(1)}, u32[]{:S(2)}, u32[]{:S(2)}) collective-permute-start(bf16[3,2,512]{2,1,0:T(2,128)(2,1)S(1)} %slice.4), channel_id=1, source_target_pairs={{0,8},{8,16},{16,24},{24,32},{32,40},{40,48},{48,56},{56,64},{64,7... | collective-permute-start | bytes 18440 | tf_op jit(solution)/shard_map/ppermute | solution.py:301
  6.3 0.2 fusion
  6.5 0.1 pad_maximum_fusion
  6.6 0.0 copy-done.4
  6.6 0.8 shard_map.86
  7.4 0.0 copy-start
  7.4 0.0 copy-start.6
  7.4 0.0 copy-start.1
  7.4 11.8 %all-to-all-start = ((bf16[16,64,128]{2,1,0:T(8,128)(2,1)}), bf16[16,64,128]{2,1,0:T(8,128)(2,1)S(1)}, u32[]{:S(2)}, u32[]{:S(2)}) async-start(bf16[16,64,128]{2,1,0:T(8,128)(2,1)} %get-tuple-element.16), calls=%async_computation | async-start | bytes 524288 | tf_op jit(solution)/shard_map/all_to_all | solution.py:292
  19.2 7.5 %collective-permute-start.1 = (bf16[4,128,128]{2,1,0:T(8,128)(2,1)S(1)}, bf16[4,128,128]{2,1,0:T(8,128)(2,1)S(1)}, u32[]{:S(2)}, u32[]{:S(2)}) collective-permute-start(bf16[4,128,128]{2,1,0:T(8,128)(2,1)S(1)} %get-tuple-element.17.pair_ref), channel_id=1, source_target_pairs={{0,256},{8,264},{16,272},{24,280},{32,288},{40,296},{48,304},{56,3... | collective-permute-start | bytes 393224 | tf_op jit(solution)/shard_map/ppermute | solution.py:322
  26.7 0.0 copy-done
  26.7 0.0 copy-done.6
  26.8 0.0 copy-start.2
  26.8 0.0 collective-permute-done
  26.8 0.0 copy-done.1
  26.8 0.7 copy-done.2
  27.5 0.4 shard_map.87
  27.9 1.3 %collective-permute-start.2 = (bf16[4,16,128]{2,1,0:T(8,128)(2,1)S(1)}, bf16[4,16,128]{2,1,0:T(8,128)(2,1)S(1)}, u32[]{:S(2)}, u32[]{:S(2)}) collective-permute-start(bf16[4,16,128]{2,1,0:T(8,128)(2,1)S(1)} %get-tuple-element.18.state_ref), channel_id=1, source_target_pairs={{0,256},{8,264},{16,272},{24,280},{32,288},{40,296},{48,304},{56,3... | collective-permute-start | bytes 49160 | tf_op jit(solution)/shard_map/ppermute | solution.py:332
  29.2 0.0 copy-start.3
  29.2 0.7 copy-done.3
  29.9 1.1 %shard_map.89.near_ref = f32[64,512]{1,0:T(8,128)S(1)} custom-call(f32[64,512]{1,0:T(8,128)S(1)} %get-tuple-element.19.prod_ref, f32[16,512]{1,0:T(8,128)S(1)} %sqrt_multiply_fusion.coeff_ref, f32[16,512]{1,0:T(8,128)S(1)} %copy-done, f32[1,512]{1,0:T(1,128)S(1)} %bitcast.20), custom_call_target="tpu_custom_call" | custom-call | flops 1000000 | bytes 1000 | tf_op jit(solution)/shard_map/pallas_call | solution.py:333
  31.0 0.0 collective-permute-done.2.far_state_ref
  31.0 0.0 collective-permute-done.1.far_pair_ref
  31.0 0.1 shard_map.88
  31.1 0.0 all-to-all-done.q_ref
  31.1 13.6 %all_to_all.26.got_ref = bf16[8,288,128]{2,1,0:T(8,128)(2,1)S(1)} all-to-all(bf16[8,288,128]{2,1,0:T(8,128)(2,1)S(1)} %shard_map.88), channel_id=1, replica_groups={{0,8,64,72,128,136,192,200},{16,24,80,88,144,152,208,216},{32,40,96,104..., dimensions={0} | all-to-all | bytes 1179648 | tf_op jit(solution)/shard_map/all_to_all | solution.py:292
  44.7 1.6 %shard_map.90 = bf16[16,96,128]{2,1,0:T(8,128)(2,1)S(1)} custom-call(s32[1]{0:T(128)} %bitcast.place_ref, bf16[16,64,128]{2,1,0:T(8,128)(2,1)S(1)} %all-to-all-done.q_ref, bf16[8,288,128]{2,1,0:T(8,128)(2,1)S(1)} %all_to_all.26.got_ref, f32[4,16,128]{2,1,0:T(8,128)S(1)} %bitcast_bitcast_fusion.rates_ref), custom_call_target="tpu_custom_call" | custom-call | flops 4000000000 | bytes 1000 | tf_op jit(solution)/shard_map/pallas_call | solution.py:348
  46.3 0.0 copy-start.5
  46.3 19.8 %all_to_all.27.got_ref = bf16[16,96,128]{2,1,0:T(8,128)(2,1)S(1)} all-to-all(bf16[16,96,128]{2,1,0:T(8,128)(2,1)S(1)} %shard_map.90), channel_id=1, replica_groups={{0,16,32,48,64,80,96,112,128,144,160,176,192,208,224,240},{8,24,40,56,7..., dimensions={0} | all-to-all | bytes 786432 | tf_op jit(solution)/shard_map/all_to_all | solution.py:292
  66.2 0.0 copy-done.5
  66.2 1.3 %shard_map.91 = (f32[64,512]{1,0:T(8,128)S(1)}, f32[8,128]{1,0:T(8,128)S(1)}, bf16[64,512]{1,0:T(8,128)(2,1)}) custom-call(s32[1]{0:T(128)} %bitcast.place_ref, bf16[16,96,128]{2,1,0:T(8,128)(2,1)S(1)} %all_to_all.27.got_ref, f32[16,512]{1,0:T(8,128)S(1)} %sqrt_multiply_fusion.coeff_ref, f32[16,512]{1,0:T(8,128)S(1)} %copy-done, ...), custom_call_target="tpu_custom_call" | custom-call | flops 1000000000 | bytes 1000 | tf_op jit(solution)/shard_map/pallas_call | solution.py:356
  67.5 13.3 %all_to_all.28 = f32[8,1,128]{2,1,0:T(1,128)S(1)} all-to-all(f32[8,1,128]{2,1,0:T(1,128)S(1)} %bitcast.18), channel_id=1, replica_groups=mesh['context'=64,'dp'=8] {'dp'}, dimensions={0} | all-to-all | bytes 8192 | tf_op jit(solution)/shard_map/all_to_all | solution.py:362
  80.8 0.7 shard_map.92
  (5 shorter events, 0.1 us)
Async XLA Ops:
  0.6 6.0 %copy-start.4 = (bf16[64,3,512]{2,0,1:T(8,128)(2,1)S(1)}, bf16[64,3,512]{2,0,1:T(8,128)(2,1)}, u32[]{:S(2)}) copy-start(bf16[64,3,512]{2,0,1:T(8,128)(2,1)} %param.13) | copy-start | bytes 589828
  1.4 25.3 %collective-permute-start = (bf16[3,2,512]{2,1,0:T(2,128)(2,1)S(1)}, bf16[3,2,512]{2,1,0:T(2,128)(2,1)S(1)}, u32[]{:S(2)}, u32[]{:S(2)}) collective-permute-start(bf16[3,2,512]{2,1,0:T(2,128)(2,1)S(1)} %slice.4), channel_id=1, source_target_pairs={{0,8},{8,16},{16,24},{24,32},{32,40},{40,48},{48,56},{56,64},{64,7... | collective-permute-start | bytes 18440 | tf_op jit(solution)/shard_map/ppermute | solution.py:301
  7.4 19.3 %copy-start = (f32[16,512]{1,0:T(8,128)S(1)}, f32[16,512]{1,0:T(8,128)}, u32[]{:S(2)}) copy-start(f32[16,512]{1,0:T(8,128)} %rates_ref.5) | copy-start | bytes 98308
  7.4 19.3 %copy-start.6 = (f32[16,512]{1,0:T(8,128)S(1)}, f32[16,512]{1,0:T(8,128)}, u32[]{:S(2)}) copy-start(f32[16,512]{1,0:T(8,128)} %param.10) | copy-start | bytes 98308
  7.4 19.4 %copy-start.1 = (bf16[64,3,512]{2,0,1:T(8,128)(2,1)S(1)}, bf16[64,3,512]{2,0,1:T(8,128)(2,1)}, u32[]{:S(2)}) copy-start(bf16[64,3,512]{2,0,1:T(8,128)(2,1)} %param.7) | copy-start | bytes 589828
  7.4 23.7 %all-to-all-start = ((bf16[16,64,128]{2,1,0:T(8,128)(2,1)}), bf16[16,64,128]{2,1,0:T(8,128)(2,1)S(1)}, u32[]{:S(2)}, u32[]{:S(2)}) async-start(bf16[16,64,128]{2,1,0:T(8,128)(2,1)} %get-tuple-element.16), calls=%async_computation | async-start | bytes 524288 | tf_op jit(solution)/shard_map/all_to_all | solution.py:292
  19.2 11.8 %collective-permute-start.1 = (bf16[4,128,128]{2,1,0:T(8,128)(2,1)S(1)}, bf16[4,128,128]{2,1,0:T(8,128)(2,1)S(1)}, u32[]{:S(2)}, u32[]{:S(2)}) collective-permute-start(bf16[4,128,128]{2,1,0:T(8,128)(2,1)S(1)} %get-tuple-element.17.pair_ref), channel_id=1, source_target_pairs={{0,256},{8,264},{16,272},{24,280},{32,288},{40,296},{48,304},{56,3... | collective-permute-start | bytes 393224 | tf_op jit(solution)/shard_map/ppermute | solution.py:322
  26.8 0.7 copy-start.2
  27.9 3.1 %collective-permute-start.2 = (bf16[4,16,128]{2,1,0:T(8,128)(2,1)S(1)}, bf16[4,16,128]{2,1,0:T(8,128)(2,1)S(1)}, u32[]{:S(2)}, u32[]{:S(2)}) collective-permute-start(bf16[4,16,128]{2,1,0:T(8,128)(2,1)S(1)} %get-tuple-element.18.state_ref), channel_id=1, source_target_pairs={{0,256},{8,264},{16,272},{24,280},{32,288},{40,296},{48,304},{56,3... | collective-permute-start | bytes 49160 | tf_op jit(solution)/shard_map/ppermute | solution.py:332
  29.2 0.7 copy-start.3
  46.3 19.8 %copy-start.5 = (f32[512]{0:T(512)S(1)}, f32[512]{0:T(512)}, u32[]{:S(2)}) copy-start(f32[512]{0:T(512)} %param.12) | copy-start | bytes 6148

commit v12 on v11

--- a/solution.py
+++ b/solution.py
@@ -24,7 +24,7 @@
 BF = jnp.bfloat16
 F32 = jnp.float32
 
-DIGITS = {"y": (2, 32), "x": (4, 8), "v": (4, 2), "u": (2, 1)}
+DIGITS = {"y": (2, 32), "s": (2, 16), "r": (2, 8), "v": (4, 2), "u": (2, 1)}
 
 
 def groups_over(*free):
@@ -39,8 +39,8 @@
     return [[base + step for step in places(free)] for base in places(fixed)]
 
 
-Q_GROUPS = groups_over("x", "v")
-KV_GROUPS = groups_over("x", "u")
+Q_GROUPS = groups_over("r", "v", "u")
+KV_GROUPS = groups_over("s", "r", "u")
 
 VMEM = pl.BlockSpec(memory_space=pltpu.VMEM)
 SMEM = pl.BlockSpec(memory_space=pltpu.SMEM)
@@ -62,6 +62,10 @@
     return [(index // step) % size for size, step in DIGITS.values()]
 
 
+def member(head, v):
+    return (head // 2) * 8 + v * 2 + head % 2
+
+
 def expand(rates, weights, start):
     ahead = (lax.broadcasted_iota(jnp.int32, (8, 128), 0) + start).astype(F32)
     bases = [jnp.exp(-rates[n : n + 1, :] * ahead) for n in range(MODES)]
@@ -80,8 +84,8 @@
             part = x[:, h * HEAD : (h + 1) * HEAD]
             turned = (part * cosine + pltpu.roll(part, HEAD // 2, 1) * sine).astype(BF)
             if g == 0:
-                for w in range(4):
-                    q_ref[h * 4 + w] = turned
+                for v in range(4):
+                    q_ref[member(h, v)] = turned
             else:
                 kv_ref[h, :TOK, :] = turned
     for h in range(HEADS_DEV):
@@ -115,7 +119,7 @@
 
 def join_kernel(pair_ref, state_ref, far_pair_ref, far_state_ref, out_ref):
     for peer in range(8):
-        head = peer // 2
+        head = peer % 4
         out_ref[peer, : 2 * TOK, :] = pair_ref[head]
         out_ref[peer, 2 * TOK : PACK, :] = state_ref[head]
         out_ref[peer, PACK : PACK + 2 * TOK, :] = far_pair_ref[head]
@@ -137,35 +141,41 @@
 
 
 def write_messages(index, got_ref, rates_ref, out_ref):
-    y, x, v, u = digits(index)
-    decay = rates_ref[x] * (-float(TOK))
-    second = jnp.where(y == 1, 1.0, 0.0).astype(F32)
+    y, s, r, v, u = digits(index)
+    decay = rates_ref[2 * r + u] * (-float(TOK))
 
     def faded(steps):
         return jnp.exp(decay * jnp.maximum(steps, 0).astype(F32))
 
+    def when(condition):
+        return jnp.where(condition, 1.0, 0.0).astype(F32)
+
+    second = when(y == 1)
     own_states = [got_ref[i, 2 * TOK : PACK, :].astype(F32) for i in range(8)]
     other_states = [got_ref[i, PACK + 2 * TOK :, :].astype(F32) * second for i in range(8)]
-    reach = [faded(2 * (vt - v) + 6) for vt in range(4)]
-    near_steps = [[2 * (vt - v) + u - us - 1 for us in range(2)] for vt in range(4)]
-    close = [
-        [faded(steps) * jnp.where(steps >= 0, 1.0, 0.0).astype(F32) for steps in pair]
-        for pair in near_steps
-    ]
-    before = {(dx, us): faded(8 * dx - 7 + u - us) for dx in range(1, 4) for us in range(2)}
-    across = {(dx, us): faded(8 * dx + 25 + u - us) for dx in range(-3, 4) for us in range(2)}
-    for xt in range(4):
-        total = jnp.zeros((MODES, 128), F32)
-        for xs in range(4):
+    reach, close = {}, {}
+    for vt in range(4):
+        for du in (-1, 0, 1):
+            steps = 2 * (vt - v) + du - 1
+            reach[vt, du] = faded(steps + 8)
+            close[vt, du] = faded(steps) * when(steps >= 0)
+    for rt in range(2):
+        before = [jnp.zeros((MODES, 128), F32) for _ in range(2)]
+        level = [jnp.zeros((MODES, 128), F32) for _ in range(2)]
+        for pair in range(4):
+            gap = 16 * (s - pair // 2) + 8 * (rt - pair % 2)
+            earlier = faded(gap - 8) * when(gap > 0)
+            across = faded(gap + 24)
             for us in range(2):
-                total = total + across[xt - xs, us] * other_states[xs * 2 + us]
-                if xs < xt:
-                    total = total + before[xt - xs, us] * own_states[xs * 2 + us]
+                i = pair * 2 + us
+                before[us] = before[us] + earlier * own_states[i] + across * other_states[i]
+                level[us] = level[us] + when(gap == 0) * own_states[i]
         for vt in range(4):
-            state = reach[vt] * total
-            for us in range(2):
-                state = state + close[vt][us] * own_states[xt * 2 + us]
-            out_ref[xt * 4 + vt, 80:96, :] = state.astype(BF)
+            for ut in range(2):
+                state = jnp.zeros((MODES, 128), F32)
+                for us in range(2):
+                    state = state + reach[vt, ut - us] * before[us] + close[vt, ut - us] * level[us]
+                out_ref[rt * 8 + vt * 2 + ut, 80:96, :] = state.astype(BF)
 
 
 def norm_kernel(square_ref, gained_ref, out_ref):
@@ -192,7 +202,7 @@
 
 
 def attend_kernel(place_ref, q_ref, got_ref, rates_ref, out_ref):
-    y, _, v, u = digits(place_ref[0])
+    y, s, _, v, _ = digits(place_ref[0])
     write_messages(place_ref[0], got_ref, rates_ref, out_ref)
 
     def half(first):
@@ -202,7 +212,7 @@
     own, other = half(0), half(PACK)
     lane = lax.broadcasted_iota(jnp.int32, (1, 8 * TOK), 1)
     block = lane // TOK
-    key_pos = ((block // 2) * 8 + 2 * v + block % 2) * TOK + lane % TOK
+    key_pos = ((block // 4) * 16 + ((block // 2) % 2) * 8 + 2 * v + block % 2) * TOK + lane % TOK
     which = lax.broadcasted_iota(jnp.int32, (16, 128), 0)
 
     def query_of(tile):
@@ -210,9 +220,8 @@
 
     def own_part(tile):
         row = lax.broadcasted_iota(jnp.int32, (WIDE, 1), 0) + tile * WIDE
-        q_block = row // TOK
-        q_pos = ((q_block // 4) * 8 + 2 * (q_block % 4) + u) * TOK + row % TOK
-        return attend(*own, query_of(tile), lambda s: jnp.where(key_pos <= q_pos, s, NEG))
+        q_pos = s * (16 * TOK) + row
+        return attend(*own, query_of(tile), lambda t: jnp.where(key_pos <= q_pos, t, NEG))
 
     def write(tile, top, total, mixed):
         mixed = mixed.astype(BF).reshape(BLOCKS, TOK, HEAD)
@@ -242,7 +251,7 @@
     def _():
         for tile in range(16 * TOK // WIDE):
             top_a, total_a, mixed_a = own_part(tile)
-            top_b, total_b, mixed_b = attend(*other, query_of(tile), lambda s: s)
+            top_b, total_b, mixed_b = attend(*other, query_of(tile), lambda t: t)
             top = jnp.maximum(top_a, top_b)
             scale_a, scale_b = jnp.exp2(top_a - top), jnp.exp2(top_b - top)
             total = total_a * scale_a + total_b * scale_b
@@ -251,12 +260,12 @@
 
 
 def merge(index, got_ref, out_ref):
-    odd = digits(index)[2] % 2
+    odd = index % 2
     levels = jnp.sum(got_ref[:, TOK:80, :].astype(F32), 1)
     levels = jnp.where(odd == 1, pltpu.roll(levels, TOK, 1), levels)
     weights = []
     for h in range(HEADS_DEV):
-        part = levels[h * 4 : (h + 1) * 4]
+        part = jnp.concatenate([levels[member(h, k) : member(h, k) + 1] for k in range(4)], 0)
         part = jnp.exp2(part - jnp.max(part, 0, keepdims=True))
         weights.append(part / jnp.sum(part, 0, keepdims=True))
     weights = jnp.concatenate(weights + [jnp.zeros((112, 128), F32)], 0)
@@ -265,7 +274,8 @@
         total = jnp.zeros((TOK, HEAD), F32)
         for k in range(4):
             place = h * 4 + k
-            total = total + weights[:, place : place + 1] * got_ref[place, :TOK, :].astype(F32)
+            got = got_ref[member(h, k), :TOK, :].astype(F32)
+            total = total + weights[:, place : place + 1] * got
         out_ref[:, h * HEAD : (h + 1) * HEAD] = total.astype(BF)
 
 
@@ -275,9 +285,9 @@
     squares = jnp.zeros((TOK, 128), F32)
     for part in range(CH // 128):
         lanes = slice(part * 128, (part + 1) * 128)
-        state = got_ref[part * 4, 80:96, :].astype(F32)
-        for j in range(1, 4):
-            state = state + got_ref[part * 4 + j, 80:96, :].astype(F32)
+        state = got_ref[member(part, 0), 80:96, :].astype(F32)
+        for v in range(1, 4):
+            state = state + got_ref[member(part, v), 80:96, :].astype(F32)
         tiles = expand(rates_ref[:, lanes], coeff_ref[:, lanes] * state, 1)
         gated = gate_ref[:, lanes] * (near_ref[:, lanes] + jnp.concatenate(tiles, 0))
         gained_ref[:, lanes] = gated * gain_ref[:, lanes]
@@ -328,7 +338,7 @@
         [((HEADS_DEV, MODES, HEAD), BF), ((TOK, CH), F32), ((TOK, CH), F32)],
         [VMEM] * 4,
         1000000,
-    )(features, rim, feat_weight, rates)
+    )(features, rim, jnp.pad(feat_weight, ((0, 0), (0, 5), (0, 0))), rates)
     far_states = lax.ppermute(states, "context", over_y)
     (near,) = call(
         near_kernel,

time: 82.9 us -> 76.1 us (0.918)
  blocking collectives: 46.7 us -> 42.6 us
  starting transfers between devices: 25.4 us -> 24 us
    all_to_all x2, blocking collectives: 33.4 us -> 28 us  [exchange(): lax.all_to_all(value, 'context', 0, 0, axis_index_groups=groups, tiled=True)]
    all_to_all x1, starting transfers between devices: 11.8 us -> 10.3 us  [exchange(): lax.all_to_all(value, 'context', 0, 0, axis_index_groups=groups, tiled=True)]
    all_to_all x1, blocking collectives: 13.3 us -> 14.6 us  [local(): squares = lax.all_to_all(squares, 'dp', 0, 0, tiled=True)]
where the time goes in v12:
time: 76.1 us; the launch traced here: 75.3 us
  blocking collectives  42.6 us (56%)
  starting transfers between devices  24 us (32%)
  Pallas kernels  6.01 us (8%)
  local copies, waits for them, and re-layouts  1.5 us (2%)
  between operations  0.85 us (1%)
    all_to_all x2, blocking collectives, exchange(): lax.all_to_all(value, 'context', 0, 0, axis_index_groups=groups, tiled=True)  28 us
    all_to_all x1, blocking collectives, local(): squares = lax.all_to_all(squares, 'dp', 0, 0, tiled=True)  14.6 us
    all_to_all x1, starting transfers between devices, exchange(): lax.all_to_all(value, 'context', 0, 0, axis_index_groups=groups, tiled=True)  10.3 us
    ppermute x1, starting transfers between devices, local(): far_pairs = lax.ppermute(pairs, 'context', over_y)  7.59 us
    ppermute x1, starting transfers between devices, local(): lax.ppermute(features[:, TOK - (FEAT - 1):], 'context', [(s, s + 1) for s...  4.83 us
    pallas_call x1, Pallas kernels, local(): call(attend_kernel, [((16, TOK + 32, HEAD), BF)], [SMEM] + [VMEM] * 3, 40...  1.58 us
  transfers between devices with their start and end apart: 4, of which 0 were waited for; matrix products, arithmetic and copies ran while one was open for 0% of the time, Pallas kernels for 3%

profile of v12, /device:TPU:1, one launch (start us, length us, event | category | flops | bytes accessed | tf_op | source)
XLA Modules:
  0.0 75.3 jit_solution(2302942595725068288)
XLA Ops:
  0.6 0.0 copy-start.3
  0.6 0.8 %slice.4 = bf16[3,2,512]{2,1,0:T(2,128)(2,1)S(1)} slice(bf16[3,64,512]{2,1,0:T(8,128)(2,1)} %bitcast.16), slice={[0:3], [62:64], [0:512]} | slice | bytes 12288 | tf_op jit(solution)/shard_map/slice | solution.py:312
  1.4 4.8 %collective-permute-start = (bf16[3,2,512]{2,1,0:T(2,128)(2,1)S(1)}, bf16[3,2,512]{2,1,0:T(2,128)(2,1)S(1)}, u32[]{:S(2)}, u32[]{:S(2)}) collective-permute-start(bf16[3,2,512]{2,1,0:T(2,128)(2,1)S(1)} %slice.4), channel_id=1, source_target_pairs={{0,8},{8,16},{16,24},{24,32},{32,40},{40,48},{48,56},{56,64},{64,7... | collective-permute-start | bytes 18440 | tf_op jit(solution)/shard_map/ppermute | solution.py:311
  6.3 0.2 fusion
  6.5 0.1 pad_maximum_fusion
  6.6 0.0 copy-done.3
  6.6 0.8 %shard_map.86 = (bf16[16,64,128]{2,1,0:T(8,128)(2,1)}, bf16[4,128,128]{2,1,0:T(8,128)(2,1)S(1)}) custom-call(bf16[3,64,512]{2,1,0:T(8,128)(2,1)S(1)} %bitcast.21, f32[64,128]{1,0:T(8,128)S(1)} %get-tuple-element.33.cos_ref, f32[64,128]{1,0:T(8,128)S(1)} %get-tuple-element.34.sin_ref), custom_call_target="tpu_custom_call" | custom-call | flops 1000000000 | bytes 1000 | tf_op jit(solution)/shard_map/pallas_call | solution.py:325
  7.4 0.0 copy-start
  7.4 0.0 copy-start.5
  7.4 0.0 copy-start.6
  7.4 10.3 %all-to-all-start = ((bf16[16,64,128]{2,1,0:T(8,128)(2,1)}), bf16[16,64,128]{2,1,0:T(8,128)(2,1)S(1)}, u32[]{:S(2)}, u32[]{:S(2)}) async-start(bf16[16,64,128]{2,1,0:T(8,128)(2,1)} %get-tuple-element.16), calls=%async_computation | async-start | bytes 524288 | tf_op jit(solution)/shard_map/all_to_all | solution.py:302
  17.7 0.0 copy-start.1
  17.7 7.6 %collective-permute-start.1 = (bf16[4,128,128]{2,1,0:T(8,128)(2,1)S(1)}, bf16[4,128,128]{2,1,0:T(8,128)(2,1)S(1)}, u32[]{:S(2)}, u32[]{:S(2)}) collective-permute-start(bf16[4,128,128]{2,1,0:T(8,128)(2,1)S(1)} %get-tuple-element.17.pair_ref), channel_id=1, source_target_pairs={{0,256},{8,264},{16,272},{24,280},{32,288},{40,296},{48,304},{56,3... | collective-permute-start | bytes 393224 | tf_op jit(solution)/shard_map/ppermute | solution.py:332
  25.3 0.0 copy-done
  25.3 0.0 copy-done.5
  25.4 0.0 copy-done.6
  25.4 0.0 collective-permute-done
  25.4 0.0 copy-done.1
  25.4 0.4 shard_map.87
  25.8 1.3 %collective-permute-start.2 = (bf16[4,16,128]{2,1,0:T(8,128)(2,1)S(1)}, bf16[4,16,128]{2,1,0:T(8,128)(2,1)S(1)}, u32[]{:S(2)}, u32[]{:S(2)}) collective-permute-start(bf16[4,16,128]{2,1,0:T(8,128)(2,1)S(1)} %get-tuple-element.18.state_ref), channel_id=1, source_target_pairs={{0,256},{8,264},{16,272},{24,280},{32,288},{40,296},{48,304},{56,3... | collective-permute-start | bytes 49160 | tf_op jit(solution)/shard_map/ppermute | solution.py:342
  27.2 0.0 copy-start.2
  27.2 0.7 copy-done.2
  27.8 1.1 %shard_map.89.near_ref = f32[64,512]{1,0:T(8,128)S(1)} custom-call(f32[64,512]{1,0:T(8,128)S(1)} %get-tuple-element.19.prod_ref, f32[16,512]{1,0:T(8,128)S(1)} %sqrt_multiply_fusion.coeff_ref, f32[16,512]{1,0:T(8,128)S(1)} %copy-done, f32[1,512]{1,0:T(1,128)S(1)} %bitcast.20), custom_call_target="tpu_custom_call" | custom-call | flops 1000000 | bytes 1000 | tf_op jit(solution)/shard_map/pallas_call | solution.py:343
  29.0 0.0 collective-permute-done.2.far_state_ref
  29.0 0.0 collective-permute-done.1.far_pair_ref
  29.0 0.1 shard_map.88
  29.1 0.0 all-to-all-done.q_ref
  29.1 13.3 %all_to_all.26.got_ref = bf16[8,288,128]{2,1,0:T(8,128)(2,1)S(1)} all-to-all(bf16[8,288,128]{2,1,0:T(8,128)(2,1)S(1)} %shard_map.88), channel_id=1, replica_groups={{0,8,64,72,128,136,192,200},{16,24,80,88,144,152,208,216},{32,40,96,104..., dimensions={0} | all-to-all | bytes 1179648 | tf_op jit(solution)/shard_map/all_to_all | solution.py:302
  42.4 1.6 %shard_map.90 = bf16[16,96,128]{2,1,0:T(8,128)(2,1)S(1)} custom-call(s32[1]{0:T(128)} %bitcast.place_ref, bf16[16,64,128]{2,1,0:T(8,128)(2,1)S(1)} %all-to-all-done.q_ref, bf16[8,288,128]{2,1,0:T(8,128)(2,1)S(1)} %all_to_all.26.got_ref, f32[4,16,128]{2,1,0:T(8,128)S(1)} %bitcast_bitcast_fusion.rates_ref), custom_call_target="tpu_custom_call" | custom-call | flops 4000000000 | bytes 1000 | tf_op jit(solution)/shard_map/pallas_call | solution.py:358
  44.0 0.0 copy-start.4
  44.0 14.7 %all_to_all.27.got_ref = bf16[16,96,128]{2,1,0:T(8,128)(2,1)S(1)} all-to-all(bf16[16,96,128]{2,1,0:T(8,128)(2,1)S(1)} %shard_map.90), channel_id=1, replica_groups={{0,8,16,24,32,40,48,56,64,72,80,88,96,104,112,120},{128,136,144,152,160..., dimensions={0} | all-to-all | bytes 786432 | tf_op jit(solution)/shard_map/all_to_all | solution.py:302
  58.7 0.0 copy-done.4
  58.7 1.3 %shard_map.91 = (f32[64,512]{1,0:T(8,128)S(1)}, f32[8,128]{1,0:T(8,128)S(1)}, bf16[64,512]{1,0:T(8,128)(2,1)}) custom-call(s32[1]{0:T(128)} %bitcast.place_ref, bf16[16,96,128]{2,1,0:T(8,128)(2,1)S(1)} %all_to_all.27.got_ref, f32[16,512]{1,0:T(8,128)S(1)} %sqrt_multiply_fusion.coeff_ref, f32[16,512]{1,0:T(8,128)S(1)} %copy-done, ...), custom_call_target="tpu_custom_call" | custom-call | flops 1000000000 | bytes 1000 | tf_op jit(solution)/shard_map/pallas_call | solution.py:366
  60.0 14.6 %all_to_all.28 = f32[8,1,128]{2,1,0:T(1,128)S(1)} all-to-all(f32[8,1,128]{2,1,0:T(1,128)S(1)} %bitcast.18), channel_id=1, replica_groups=mesh['context'=64,'dp'=8] {'dp'}, dimensions={0} | all-to-all | bytes 8192 | tf_op jit(solution)/shard_map/all_to_all | solution.py:372
  74.6 0.7 shard_map.92
  (6 shorter events, 0.1 us)
Async XLA Ops:
  0.6 6.0 %copy-start.3 = (bf16[64,3,512]{2,0,1:T(8,128)(2,1)S(1)}, bf16[64,3,512]{2,0,1:T(8,128)(2,1)}, u32[]{:S(2)}) copy-start(bf16[64,3,512]{2,0,1:T(8,128)(2,1)} %param.13) | copy-start | bytes 589828
  1.4 24.0 %collective-permute-start = (bf16[3,2,512]{2,1,0:T(2,128)(2,1)S(1)}, bf16[3,2,512]{2,1,0:T(2,128)(2,1)S(1)}, u32[]{:S(2)}, u32[]{:S(2)}) collective-permute-start(bf16[3,2,512]{2,1,0:T(2,128)(2,1)S(1)} %slice.4), channel_id=1, source_target_pairs={{0,8},{8,16},{16,24},{24,32},{32,40},{40,48},{48,56},{56,64},{64,7... | collective-permute-start | bytes 18440 | tf_op jit(solution)/shard_map/ppermute | solution.py:311
  7.4 17.9 %copy-start = (f32[16,512]{1,0:T(8,128)S(1)}, f32[16,512]{1,0:T(8,128)}, u32[]{:S(2)}) copy-start(f32[16,512]{1,0:T(8,128)} %rates_ref.5) | copy-start | bytes 98308
  7.4 17.9 %copy-start.5 = (f32[16,512]{1,0:T(8,128)S(1)}, f32[16,512]{1,0:T(8,128)}, u32[]{:S(2)}) copy-start(f32[16,512]{1,0:T(8,128)} %param.10) | copy-start | bytes 98308
  7.4 18.0 %copy-start.6 = (f32[3,3,512]{2,1,0:T(4,128)S(1)}, f32[3,3,512]{2,1,0:T(4,128)}, u32[]{:S(2)}) copy-start(f32[3,3,512]{2,1,0:T(4,128)} %param.8) | copy-start | bytes 55300
  7.4 21.7 %all-to-all-start = ((bf16[16,64,128]{2,1,0:T(8,128)(2,1)}), bf16[16,64,128]{2,1,0:T(8,128)(2,1)S(1)}, u32[]{:S(2)}, u32[]{:S(2)}) async-start(bf16[16,64,128]{2,1,0:T(8,128)(2,1)} %get-tuple-element.16), calls=%async_computation | async-start | bytes 524288 | tf_op jit(solution)/shard_map/all_to_all | solution.py:302
  17.7 7.7 %copy-start.1 = (bf16[64,3,512]{2,0,1:T(8,128)(2,1)S(1)}, bf16[64,3,512]{2,0,1:T(8,128)(2,1)}, u32[]{:S(2)}) copy-start(bf16[64,3,512]{2,0,1:T(8,128)(2,1)} %param.7) | copy-start | bytes 589828
  17.7 11.3 %collective-permute-start.1 = (bf16[4,128,128]{2,1,0:T(8,128)(2,1)S(1)}, bf16[4,128,128]{2,1,0:T(8,128)(2,1)S(1)}, u32[]{:S(2)}, u32[]{:S(2)}) collective-permute-start(bf16[4,128,128]{2,1,0:T(8,128)(2,1)S(1)} %get-tuple-element.17.pair_ref), channel_id=1, source_target_pairs={{0,256},{8,264},{16,272},{24,280},{32,288},{40,296},{48,304},{56,3... | collective-permute-start | bytes 393224 | tf_op jit(solution)/shard_map/ppermute | solution.py:332
  25.8 3.1 %collective-permute-start.2 = (bf16[4,16,128]{2,1,0:T(8,128)(2,1)S(1)}, bf16[4,16,128]{2,1,0:T(8,128)(2,1)S(1)}, u32[]{:S(2)}, u32[]{:S(2)}) collective-permute-start(bf16[4,16,128]{2,1,0:T(8,128)(2,1)S(1)} %get-tuple-element.18.state_ref), channel_id=1, source_target_pairs={{0,256},{8,264},{16,272},{24,280},{32,288},{40,296},{48,304},{56,3... | collective-permute-start | bytes 49160 | tf_op jit(solution)/shard_map/ppermute | solution.py:342
  27.2 0.7 copy-start.2
  44.0 14.7 %copy-start.4 = (f32[512]{0:T(512)S(1)}, f32[512]{0:T(512)}, u32[]{:S(2)}) copy-start(f32[512]{0:T(512)} %param.12) | copy-start | bytes 6148

commit v13 on v12

--- a/solution.py
+++ b/solution.py
@@ -76,20 +76,25 @@
     return tiles
 
 
-def rotate_kernel(attn_ref, cos_ref, sin_ref, q_ref, kv_ref):
+def rotated(x, cosine, sine):
+    x = x.astype(F32)
+    return (x * cosine + pltpu.roll(x, HEAD // 2, 1) * sine).astype(BF)
+
+
+def pair_kernel(attn_ref, cos_ref, sin_ref, kv_ref):
     cosine, sine = cos_ref[...], sin_ref[...]
-    for g in range(2):
-        x = attn_ref[g].astype(F32)
-        for h in range(HEADS_DEV):
-            part = x[:, h * HEAD : (h + 1) * HEAD]
-            turned = (part * cosine + pltpu.roll(part, HEAD // 2, 1) * sine).astype(BF)
-            if g == 0:
-                for v in range(4):
-                    q_ref[member(h, v)] = turned
-            else:
-                kv_ref[h, :TOK, :] = turned
     for h in range(HEADS_DEV):
-        kv_ref[h, TOK:, :] = attn_ref[2, :, h * HEAD : (h + 1) * HEAD]
+        lanes = slice(h * HEAD, (h + 1) * HEAD)
+        kv_ref[h, :TOK, :] = rotated(attn_ref[1, :, lanes], cosine, sine)
+        kv_ref[h, TOK:, :] = attn_ref[2, :, lanes]
+
+
+def query_kernel(attn_ref, cos_ref, sin_ref, q_ref):
+    cosine, sine = cos_ref[...], sin_ref[...]
+    for h in range(HEADS_DEV):
+        turned = rotated(attn_ref[0, :, h * HEAD : (h + 1) * HEAD], cosine, sine)
+        for v in range(4):
+            q_ref[member(h, v)] = turned
 
 
 def state_kernel(feat_ref, rim_ref, weight_ref, rates_ref, state_ref, gate_ref, prod_ref):
@@ -134,7 +139,7 @@
         rows = expand(rates_ref[:, lanes], coeff_ref[:, lanes], 0)
         for a in range(8):
             impulse[8 * a : 8 * a + 8, lanes] = rows[a]
-        y = skip_ref[:, lanes] * prod_ref[:, lanes]
+        y = skip_ref[:1, lanes] * prod_ref[:, lanes]
         for t in range(TOK):
             y = y + impulse[t : t + 1, lanes] * padded[TOK - t : 2 * TOK - t, lanes]
         out_ref[:, lanes] = y
@@ -322,11 +327,12 @@
     cosine = jnp.concatenate([cosine, cosine], 1)
     sine = jnp.concatenate([-sine, sine], 1)
 
-    queries, pairs = call(
-        rotate_kernel,
-        [((16, TOK, HEAD), BF), ((HEADS_DEV, 2 * TOK, HEAD), BF)],
-        [VMEM] * 3,
-        1000000000,
+    (pairs,) = call(
+        pair_kernel, [((HEADS_DEV, 2 * TOK, HEAD), BF)], [VMEM] * 3, 1000000000
+    )(attn_in, cosine, sine)
+    pairs, cosine = lax.optimization_barrier((pairs, cosine))
+    (queries,) = call(
+        query_kernel, [((16, TOK, HEAD), BF)], [VMEM] * 3, 20000000000
     )(attn_in, cosine, sine)
     over_y = [(s, s + devices // 2) for s in range(devices // 2)]
     far_pairs = lax.ppermute(pairs, "context", over_y)
@@ -346,7 +352,7 @@
         [VMEM] * 4,
         1000000,
         [pltpu.VMEM((2 * TOK, CH), F32), pltpu.VMEM((TOK, CH), F32)],
-    )(product, coeff, rates, skip[None, :])
+    )(product, coeff, rates, jnp.pad(skip[None, :], ((0, 7), (0, 0))))
     quarters = jnp.transpose(rates.reshape(MODES, CH // 128, 128), (1, 0, 2))
     (both,) = call(join_kernel, [((8, 2 * PACK, HEAD), BF)], [VMEM] * 4, 50000000000)(
         pairs, states, far_pairs, far_states

time: 76.1 us -> 76.7 us (level)
  waiting for transfers between devices: 0.01 us -> 3.92 us
  blocking collectives: 42.6 us -> 39.5 us
    all_to_all x1, waiting for transfers between devices: 0.01 us -> 3.91 us  [exchange(): lax.all_to_all(value, 'context', 0, 0, axis_index_groups=groups, tiled=True)]
    all_to_all x1, blocking collectives: 14.6 us -> 12.1 us  [local(): squares = lax.all_to_all(squares, 'dp', 0, 0, tiled=True)]
  transfers between devices with their start and end apart: 4 -> 4, of which waited for: 0 -> 1; matrix products, arithmetic and copies ran while one was open for 0% -> 0% of each run, Pallas kernels for 3% -> 3%
where the time goes in v13:
time: 76.7 us; the launch traced here: 76.2 us
  blocking collectives  39.5 us (51%)
  starting transfers between devices  23.9 us (31%)
  Pallas kernels  6.1 us (8%)
  waiting for transfers between devices  3.92 us (5%)
  local copies, waits for them, and re-layouts  1.66 us (2%)
  between operations  0.85 us (1%)
    all_to_all x2, blocking collectives, exchange(): lax.all_to_all(value, 'context', 0, 0, axis_index_groups=groups, tiled=True)  27.4 us
    all_to_all x1, blocking collectives, local(): squares = lax.all_to_all(squares, 'dp', 0, 0, tiled=True)  12.1 us
    all_to_all x1, starting transfers between devices, exchange(): lax.all_to_all(value, 'context', 0, 0, axis_index_groups=groups, tiled=True)  10.3 us
    ppermute x1, starting transfers between devices, local(): far_pairs = lax.ppermute(pairs, 'context', over_y)  7.46 us
    ppermute x1, starting transfers between devices, local(): lax.ppermute(features[:, TOK - (FEAT - 1):], 'context', [(s, s + 1) for s...  4.83 us
    all_to_all x1, waiting for transfers between devices, exchange(): lax.all_to_all(value, 'context', 0, 0, axis_index_groups=groups, tiled=True)  3.91 us
    pallas_call x1, Pallas kernels, local(): call(attend_kernel, [((16, TOK + 32, HEAD), BF)], [SMEM] + [VMEM] * 3, 40...  1.58 us
  transfers between devices with their start and end apart: 4, of which 1 were waited for; matrix products, arithmetic and copies ran while one was open for 0% of the time, Pallas kernels for 3%

profile of v13, /device:TPU:1, one launch (start us, length us, event | category | flops | bytes accessed | tf_op | source)
XLA Modules:
  0.0 76.2 jit_solution(9952416782737022573)
XLA Ops:
  0.6 0.0 copy-start.2
  0.6 0.8 %slice.4 = bf16[3,2,512]{2,1,0:T(2,128)(2,1)S(1)} slice(bf16[3,64,512]{2,1,0:T(8,128)(2,1)} %bitcast.16), slice={[0:3], [62:64], [0:512]} | slice | bytes 12288 | tf_op jit(solution)/shard_map/slice | solution.py:317
  1.4 4.8 %collective-permute-start = (bf16[3,2,512]{2,1,0:T(2,128)(2,1)S(1)}, bf16[3,2,512]{2,1,0:T(2,128)(2,1)S(1)}, u32[]{:S(2)}, u32[]{:S(2)}) collective-permute-start(bf16[3,2,512]{2,1,0:T(2,128)(2,1)S(1)} %slice.4), channel_id=1, source_target_pairs={{0,8},{8,16},{16,24},{24,32},{32,40},{40,48},{48,56},{56,64},{64,7... | collective-permute-start | bytes 18440 | tf_op jit(solution)/shard_map/ppermute | solution.py:316
  6.3 0.2 fusion
  6.5 0.1 pad_maximum_fusion
  6.6 0.0 copy-done.2
  6.6 0.1 shard_map.86.pair_ref
  6.7 7.5 %collective-permute-start.1 = (bf16[4,128,128]{2,1,0:T(8,128)(2,1)S(1)}, bf16[4,128,128]{2,1,0:T(8,128)(2,1)S(1)}, u32[]{:S(2)}, u32[]{:S(2)}) collective-permute-start(bf16[4,128,128]{2,1,0:T(8,128)(2,1)S(1)} %shard_map.86.pair_ref), channel_id=1, source_target_pairs={{0,256},{8,264},{16,272},{24,280},{32,288},{40,296},{48,304},{56,3... | collective-permute-start | bytes 393224 | tf_op jit(solution)/shard_map/ppermute | solution.py:338
  14.2 0.0 copy-start.5
  14.2 0.8 %shard_map.87 = bf16[16,64,128]{2,1,0:T(8,128)(2,1)} custom-call(bf16[3,64,512]{2,1,0:T(8,128)(2,1)S(1)} %bitcast.21, f32[64,128]{1,0:T(8,128)S(1)} %get-tuple-element.16.cos_ref, f32[64,128]{1,0:T(8,128)S(1)} %get-tuple-element.34.sin_ref), custom_call_target="tpu_custom_call" | custom-call | flops 20000000000 | bytes 1000 | tf_op jit(solution)/shard_map/pallas_call | solution.py:334
  15.0 0.0 copy-start
  15.0 0.0 copy-start.4
  15.0 0.0 copy-start.6
  15.0 10.3 %all-to-all-start = ((bf16[16,64,128]{2,1,0:T(8,128)(2,1)}), bf16[16,64,128]{2,1,0:T(8,128)(2,1)S(1)}, u32[]{:S(2)}, u32[]{:S(2)}) async-start(bf16[16,64,128]{2,1,0:T(8,128)(2,1)} %shard_map.87), calls=%async_computation | async-start | bytes 524288 | tf_op jit(solution)/shard_map/all_to_all | solution.py:307
  25.3 0.0 copy-done
  25.3 0.0 copy-done.4
  25.3 0.0 copy-start.1
  25.3 0.0 copy-done.5
  25.4 0.0 collective-permute-done
  25.4 0.8 %copy-done.1 = bf16[64,3,512]{2,0,1:T(8,128)(2,1)S(1)} copy-done((bf16[64,3,512]{2,0,1:T(8,128)(2,1)S(1)}, bf16[64,3,512]{2,0,1:T(8,128)(2,1)}, u32[]{:S(2)}) %copy-start.1) | copy-done | bytes 196632
  26.2 0.4 shard_map.88
  26.6 1.3 %collective-permute-start.2 = (bf16[4,16,128]{2,1,0:T(8,128)(2,1)S(1)}, bf16[4,16,128]{2,1,0:T(8,128)(2,1)S(1)}, u32[]{:S(2)}, u32[]{:S(2)}) collective-permute-start(bf16[4,16,128]{2,1,0:T(8,128)(2,1)S(1)} %get-tuple-element.18.state_ref), channel_id=1, source_target_pairs={{0,256},{8,264},{16,272},{24,280},{32,288},{40,296},{48,304},{56,3... | collective-permute-start | bytes 49160 | tf_op jit(solution)/shard_map/ppermute | solution.py:348
  27.9 0.0 copy-done.6
  28.0 1.1 %shard_map.90.near_ref = f32[64,512]{1,0:T(8,128)S(1)} custom-call(f32[64,512]{1,0:T(8,128)S(1)} %get-tuple-element.19.prod_ref, f32[16,512]{1,0:T(8,128)S(1)} %sqrt_multiply_fusion.coeff_ref, f32[16,512]{1,0:T(8,128)S(1)} %copy-done, f32[8,512]{1,0:T(8,128)S(1)} %pad.17.skip_ref), custom_call_target="tpu_custom_call" | custom-call | flops 1000000 | bytes 1000 | tf_op jit(solution)/shard_map/pallas_call | solution.py:349
  29.1 0.0 collective-permute-done.2.far_state_ref
  29.1 0.0 collective-permute-done.1.far_pair_ref
  29.1 0.1 shard_map.89
  29.2 3.9 %all-to-all-done.q_ref = bf16[16,64,128]{2,1,0:T(8,128)(2,1)S(1)} async-done(((bf16[16,64,128]{2,1,0:T(8,128)(2,1)}), bf16[16,64,128]{2,1,0:T(8,128)(2,1)S(1)}, u32[]{:S(2)}, u32[]{:S(2)}) %all-to-all-start) | async-done | bytes 262176 | tf_op jit(solution)/shard_map/all_to_all | solution.py:307
  33.1 13.7 %all_to_all.26.got_ref = bf16[8,288,128]{2,1,0:T(8,128)(2,1)S(1)} all-to-all(bf16[8,288,128]{2,1,0:T(8,128)(2,1)S(1)} %shard_map.89), channel_id=1, replica_groups={{0,8,64,72,128,136,192,200},{16,24,80,88,144,152,208,216},{32,40,96,104..., dimensions={0} | all-to-all | bytes 1179648 | tf_op jit(solution)/shard_map/all_to_all | solution.py:307
  46.8 1.6 %shard_map.91 = bf16[16,96,128]{2,1,0:T(8,128)(2,1)S(1)} custom-call(s32[1]{0:T(128)} %bitcast.place_ref, bf16[16,64,128]{2,1,0:T(8,128)(2,1)S(1)} %all-to-all-done.q_ref, bf16[8,288,128]{2,1,0:T(8,128)(2,1)S(1)} %all_to_all.26.got_ref, f32[4,16,128]{2,1,0:T(8,128)S(1)} %bitcast_bitcast_fusion.rates_ref), custom_call_target="tpu_custom_call" | custom-call | flops 4000000000 | bytes 1000 | tf_op jit(solution)/shard_map/pallas_call | solution.py:364
  48.4 0.0 copy-start.3
  48.4 13.7 %all_to_all.27.got_ref = bf16[16,96,128]{2,1,0:T(8,128)(2,1)S(1)} all-to-all(bf16[16,96,128]{2,1,0:T(8,128)(2,1)S(1)} %shard_map.91), channel_id=1, replica_groups={{0,8,16,24,32,40,48,56,64,72,80,88,96,104,112,120},{128,136,144,152,160..., dimensions={0} | all-to-all | bytes 786432 | tf_op jit(solution)/shard_map/all_to_all | solution.py:307
  62.1 0.0 copy-done.3
  62.1 1.3 %shard_map.92 = (f32[64,512]{1,0:T(8,128)S(1)}, f32[8,128]{1,0:T(8,128)S(1)}, bf16[64,512]{1,0:T(8,128)(2,1)}) custom-call(s32[1]{0:T(128)} %bitcast.place_ref, bf16[16,96,128]{2,1,0:T(8,128)(2,1)S(1)} %all_to_all.27.got_ref, f32[16,512]{1,0:T(8,128)S(1)} %sqrt_multiply_fusion.coeff_ref, f32[16,512]{1,0:T(8,128)S(1)} %copy-done, ...), custom_call_target="tpu_custom_call" | custom-call | flops 1000000000 | bytes 1000 | tf_op jit(solution)/shard_map/pallas_call | solution.py:372
  63.4 12.1 %all_to_all.28 = f32[8,1,128]{2,1,0:T(1,128)S(1)} all-to-all(f32[8,1,128]{2,1,0:T(1,128)S(1)} %bitcast.18), channel_id=1, replica_groups=mesh['context'=64,'dp'=8] {'dp'}, dimensions={0} | all-to-all | bytes 8192 | tf_op jit(solution)/shard_map/all_to_all | solution.py:378
  75.5 0.7 shard_map.93
  (7 shorter events, 0.1 us)
Async XLA Ops:
  0.6 6.0 %copy-start.2 = (bf16[64,3,512]{2,0,1:T(8,128)(2,1)S(1)}, bf16[64,3,512]{2,0,1:T(8,128)(2,1)}, u32[]{:S(2)}) copy-start(bf16[64,3,512]{2,0,1:T(8,128)(2,1)} %param.13) | copy-start | bytes 589828
  1.4 23.9 %collective-permute-start = (bf16[3,2,512]{2,1,0:T(2,128)(2,1)S(1)}, bf16[3,2,512]{2,1,0:T(2,128)(2,1)S(1)}, u32[]{:S(2)}, u32[]{:S(2)}) collective-permute-start(bf16[3,2,512]{2,1,0:T(2,128)(2,1)S(1)} %slice.4), channel_id=1, source_target_pairs={{0,8},{8,16},{16,24},{24,32},{32,40},{40,48},{48,56},{56,64},{64,7... | collective-permute-start | bytes 18440 | tf_op jit(solution)/shard_map/ppermute | solution.py:316
  6.7 22.4 %collective-permute-start.1 = (bf16[4,128,128]{2,1,0:T(8,128)(2,1)S(1)}, bf16[4,128,128]{2,1,0:T(8,128)(2,1)S(1)}, u32[]{:S(2)}, u32[]{:S(2)}) collective-permute-start(bf16[4,128,128]{2,1,0:T(8,128)(2,1)S(1)} %shard_map.86.pair_ref), channel_id=1, source_target_pairs={{0,256},{8,264},{16,272},{24,280},{32,288},{40,296},{48,304},{56,3... | collective-permute-start | bytes 393224 | tf_op jit(solution)/shard_map/ppermute | solution.py:338
  14.2 11.2 %copy-start.5 = (f32[3,3,512]{2,1,0:T(4,128)S(1)}, f32[3,3,512]{2,1,0:T(4,128)}, u32[]{:S(2)}) copy-start(f32[3,3,512]{2,1,0:T(4,128)} %param.8) | copy-start | bytes 55300
  15.0 10.3 %copy-start = (f32[16,512]{1,0:T(8,128)S(1)}, f32[16,512]{1,0:T(8,128)}, u32[]{:S(2)}) copy-start(f32[16,512]{1,0:T(8,128)} %rates_ref.5) | copy-start | bytes 98308
  15.0 10.3 %copy-start.4 = (f32[16,512]{1,0:T(8,128)S(1)}, f32[16,512]{1,0:T(8,128)}, u32[]{:S(2)}) copy-start(f32[16,512]{1,0:T(8,128)} %param.10) | copy-start | bytes 98308
  15.0 13.0 %copy-start.6 = (f32[512]{0:T(512)S(1)}, f32[512]{0:T(512)}, u32[]{:S(2)}) copy-start(f32[512]{0:T(512)} %param.9) | copy-start | bytes 6148
  15.0 18.1 %all-to-all-start = ((bf16[16,64,128]{2,1,0:T(8,128)(2,1)}), bf16[16,64,128]{2,1,0:T(8,128)(2,1)S(1)}, u32[]{:S(2)}, u32[]{:S(2)}) async-start(bf16[16,64,128]{2,1,0:T(8,128)(2,1)} %shard_map.87), calls=%async_computation | async-start | bytes 524288 | tf_op jit(solution)/shard_map/all_to_all | solution.py:307
  25.3 0.9 %copy-start.1 = (bf16[64,3,512]{2,0,1:T(8,128)(2,1)S(1)}, bf16[64,3,512]{2,0,1:T(8,128)(2,1)}, u32[]{:S(2)}) copy-start(bf16[64,3,512]{2,0,1:T(8,128)(2,1)} %param.7) | copy-start | bytes 589828
  26.6 2.5 %collective-permute-start.2 = (bf16[4,16,128]{2,1,0:T(8,128)(2,1)S(1)}, bf16[4,16,128]{2,1,0:T(8,128)(2,1)S(1)}, u32[]{:S(2)}, u32[]{:S(2)}) collective-permute-start(bf16[4,16,128]{2,1,0:T(8,128)(2,1)S(1)} %get-tuple-element.18.state_ref), channel_id=1, source_target_pairs={{0,256},{8,264},{16,272},{24,280},{32,288},{40,296},{48,304},{56,3... | collective-permute-start | bytes 49160 | tf_op jit(solution)/shard_map/ppermute | solution.py:348
  48.4 13.7 %copy-start.3 = (f32[512]{0:T(512)S(1)}, f32[512]{0:T(512)}, u32[]{:S(2)}) copy-start(f32[512]{0:T(512)} %param.12) | copy-start | bytes 6148

commit v14 on v12

--- a/solution.py
+++ b/solution.py
@@ -19,7 +19,7 @@
 ROPE_BASE = 1000000.0
 NEG = -1e30
 PACK = 2 * TOK + MODES
-WIDE = 512
+WIDE = 128
 BLOCKS = WIDE // TOK
 BF = jnp.bfloat16
 F32 = jnp.float32
@@ -134,7 +134,7 @@
         rows = expand(rates_ref[:, lanes], coeff_ref[:, lanes], 0)
         for a in range(8):
             impulse[8 * a : 8 * a + 8, lanes] = rows[a]
-        y = skip_ref[:, lanes] * prod_ref[:, lanes]
+        y = skip_ref[:1, lanes] * prod_ref[:, lanes]
         for t in range(TOK):
             y = y + impulse[t : t + 1, lanes] * padded[TOK - t : 2 * TOK - t, lanes]
         out_ref[:, lanes] = y
@@ -194,11 +194,10 @@
     scores = mask(scores)
     top = jnp.max(scores, 1, keepdims=True)
     weights = jnp.exp2(scores - top)
-    total = jnp.sum(weights, 1, keepdims=True)
     mixed = lax.dot_general(
         weights.astype(BF), values, (((1,), (0,)), ((), ())), preferred_element_type=F32
     )
-    return top, total, mixed
+    return top, mixed[:, HEAD:], mixed[:, :HEAD]
 
 
 def attend_kernel(place_ref, q_ref, got_ref, rates_ref, out_ref):
@@ -207,7 +206,8 @@
 
     def half(first):
         keys = got_ref[:, first : first + TOK, :].reshape(8 * TOK, HEAD)
-        return keys, got_ref[:, first + TOK : first + 2 * TOK, :].reshape(8 * TOK, HEAD)
+        values = got_ref[:, first + TOK : first + 2 * TOK, :].reshape(8 * TOK, HEAD)
+        return keys, jnp.concatenate([values, jnp.ones((8 * TOK, HEAD), BF)], 1)
 
     own, other = half(0), half(PACK)
     lane = lax.broadcasted_iota(jnp.int32, (1, 8 * TOK), 1)
@@ -346,7 +346,7 @@
         [VMEM] * 4,
         1000000,
         [pltpu.VMEM((2 * TOK, CH), F32), pltpu.VMEM((TOK, CH), F32)],
-    )(product, coeff, rates, skip[None, :])
+    )(product, coeff, rates, jnp.pad(skip[None, :], ((0, 7), (0, 0))))
     quarters = jnp.transpose(rates.reshape(MODES, CH // 128, 128), (1, 0, 2))
     (both,) = call(join_kernel, [((8, 2 * PACK, HEAD), BF)], [VMEM] * 4, 50000000000)(
         pairs, states, far_pairs, far_states

time: 76.1 us -> 75.8 us (level)
  no operation moved by 1% of the time
where the time goes in v14:
time: 75.8 us; the launch traced here: 75 us
  blocking collectives  42.6 us (56%)
  starting transfers between devices  24 us (32%)
  Pallas kernels  5.64 us (7%)
  local copies, waits for them, and re-layouts  1.5 us (2%)
  between operations  0.85 us (1%)
    all_to_all x2, blocking collectives, exchange(): lax.all_to_all(value, 'context', 0, 0, axis_index_groups=groups, tiled=True)  28 us
    all_to_all x1, blocking collectives, local(): squares = lax.all_to_all(squares, 'dp', 0, 0, tiled=True)  14.6 us
    all_to_all x1, starting transfers between devices, exchange(): lax.all_to_all(value, 'context', 0, 0, axis_index_groups=groups, tiled=True)  10.3 us
    ppermute x1, starting transfers between devices, local(): far_pairs = lax.ppermute(pairs, 'context', over_y)  7.59 us
    ppermute x1, starting transfers between devices, local(): lax.ppermute(features[:, TOK - (FEAT - 1):], 'context', [(s, s + 1) for s...  4.83 us
  transfers between devices with their start and end apart: 4, of which 0 were waited for; matrix products, arithmetic and copies ran while one was open for 0% of the time, Pallas kernels for 3%

profile of v14, /device:TPU:1, one launch (start us, length us, event | category | flops | bytes accessed | tf_op | source)
XLA Modules:
  0.0 75.0 jit_solution(6002729728550778907)
XLA Ops:
  0.6 0.0 copy-start.2
  0.6 0.8 %slice.4 = bf16[3,2,512]{2,1,0:T(2,128)(2,1)S(1)} slice(bf16[3,64,512]{2,1,0:T(8,128)(2,1)} %bitcast.16), slice={[0:3], [62:64], [0:512]} | slice | bytes 12288 | tf_op jit(solution)/shard_map/slice | solution.py:312
  1.4 4.8 %collective-permute-start = (bf16[3,2,512]{2,1,0:T(2,128)(2,1)S(1)}, bf16[3,2,512]{2,1,0:T(2,128)(2,1)S(1)}, u32[]{:S(2)}, u32[]{:S(2)}) collective-permute-start(bf16[3,2,512]{2,1,0:T(2,128)(2,1)S(1)} %slice.4), channel_id=1, source_target_pairs={{0,8},{8,16},{16,24},{24,32},{32,40},{40,48},{48,56},{56,64},{64,7... | collective-permute-start | bytes 18440 | tf_op jit(solution)/shard_map/ppermute | solution.py:311
  6.3 0.2 fusion
  6.5 0.1 pad_maximum_fusion
  6.6 0.0 copy-done.2
  6.6 0.8 %shard_map.86 = (bf16[16,64,128]{2,1,0:T(8,128)(2,1)}, bf16[4,128,128]{2,1,0:T(8,128)(2,1)S(1)}) custom-call(bf16[3,64,512]{2,1,0:T(8,128)(2,1)S(1)} %bitcast.20, f32[64,128]{1,0:T(8,128)S(1)} %get-tuple-element.33.cos_ref, f32[64,128]{1,0:T(8,128)S(1)} %get-tuple-element.34.sin_ref), custom_call_target="tpu_custom_call" | custom-call | flops 1000000000 | bytes 1000 | tf_op jit(solution)/shard_map/pallas_call | solution.py:325
  7.4 0.0 copy-start
  7.4 0.0 copy-start.4
  7.4 0.0 copy-start.5
  7.4 10.3 %all-to-all-start = ((bf16[16,64,128]{2,1,0:T(8,128)(2,1)}), bf16[16,64,128]{2,1,0:T(8,128)(2,1)S(1)}, u32[]{:S(2)}, u32[]{:S(2)}) async-start(bf16[16,64,128]{2,1,0:T(8,128)(2,1)} %get-tuple-element.16), calls=%async_computation | async-start | bytes 524288 | tf_op jit(solution)/shard_map/all_to_all | solution.py:302
  17.7 0.0 copy-start.1
  17.7 7.6 %collective-permute-start.1 = (bf16[4,128,128]{2,1,0:T(8,128)(2,1)S(1)}, bf16[4,128,128]{2,1,0:T(8,128)(2,1)S(1)}, u32[]{:S(2)}, u32[]{:S(2)}) collective-permute-start(bf16[4,128,128]{2,1,0:T(8,128)(2,1)S(1)} %get-tuple-element.17.pair_ref), channel_id=1, source_target_pairs={{0,256},{8,264},{16,272},{24,280},{32,288},{40,296},{48,304},{56,3... | collective-permute-start | bytes 393224 | tf_op jit(solution)/shard_map/ppermute | solution.py:332
  25.3 0.0 copy-done
  25.3 0.0 copy-done.4
  25.4 0.0 copy-done.5
  25.4 0.0 collective-permute-done
  25.4 0.0 copy-done.1
  25.4 0.4 shard_map.87
  25.8 1.3 %collective-permute-start.2 = (bf16[4,16,128]{2,1,0:T(8,128)(2,1)S(1)}, bf16[4,16,128]{2,1,0:T(8,128)(2,1)S(1)}, u32[]{:S(2)}, u32[]{:S(2)}) collective-permute-start(bf16[4,16,128]{2,1,0:T(8,128)(2,1)S(1)} %get-tuple-element.18.state_ref), channel_id=1, source_target_pairs={{0,256},{8,264},{16,272},{24,280},{32,288},{40,296},{48,304},{56,3... | collective-permute-start | bytes 49160 | tf_op jit(solution)/shard_map/ppermute | solution.py:342
  27.1 0.0 copy-start.6
  27.2 0.7 copy-done.6
  27.8 1.1 %shard_map.89.near_ref = f32[64,512]{1,0:T(8,128)S(1)} custom-call(f32[64,512]{1,0:T(8,128)S(1)} %get-tuple-element.19.prod_ref, f32[16,512]{1,0:T(8,128)S(1)} %sqrt_multiply_fusion.coeff_ref, f32[16,512]{1,0:T(8,128)S(1)} %copy-done, f32[8,512]{1,0:T(8,128)S(1)} %pad.17.skip_ref), custom_call_target="tpu_custom_call" | custom-call | flops 1000000 | bytes 1000 | tf_op jit(solution)/shard_map/pallas_call | solution.py:343
  29.0 0.0 collective-permute-done.2.far_state_ref
  29.0 0.0 collective-permute-done.1.far_pair_ref
  29.0 0.1 shard_map.88
  29.1 0.0 all-to-all-done.q_ref
  29.1 13.3 %all_to_all.26.got_ref = bf16[8,288,128]{2,1,0:T(8,128)(2,1)S(1)} all-to-all(bf16[8,288,128]{2,1,0:T(8,128)(2,1)S(1)} %shard_map.88), channel_id=1, replica_groups={{0,8,64,72,128,136,192,200},{16,24,80,88,144,152,208,216},{32,40,96,104..., dimensions={0} | all-to-all | bytes 1179648 | tf_op jit(solution)/shard_map/all_to_all | solution.py:302
  42.4 1.2 %shard_map.90 = bf16[16,96,128]{2,1,0:T(8,128)(2,1)S(1)} custom-call(s32[1]{0:T(128)} %bitcast.place_ref, bf16[16,64,128]{2,1,0:T(8,128)(2,1)S(1)} %all-to-all-done.q_ref, bf16[8,288,128]{2,1,0:T(8,128)(2,1)S(1)} %all_to_all.26.got_ref, f32[4,16,128]{2,1,0:T(8,128)S(1)} %bitcast_bitcast_fusion.rates_ref), custom_call_target="tpu_custom_call" | custom-call | flops 4000000000 | bytes 1000 | tf_op jit(solution)/shard_map/pallas_call | solution.py:358
  43.6 0.0 copy-start.3
  43.6 14.7 %all_to_all.27.got_ref = bf16[16,96,128]{2,1,0:T(8,128)(2,1)S(1)} all-to-all(bf16[16,96,128]{2,1,0:T(8,128)(2,1)S(1)} %shard_map.90), channel_id=1, replica_groups={{0,8,16,24,32,40,48,56,64,72,80,88,96,104,112,120},{128,136,144,152,160..., dimensions={0} | all-to-all | bytes 786432 | tf_op jit(solution)/shard_map/all_to_all | solution.py:302
  58.3 0.0 copy-done.3
  58.3 1.3 %shard_map.91 = (f32[64,512]{1,0:T(8,128)S(1)}, f32[8,128]{1,0:T(8,128)S(1)}, bf16[64,512]{1,0:T(8,128)(2,1)}) custom-call(s32[1]{0:T(128)} %bitcast.place_ref, bf16[16,96,128]{2,1,0:T(8,128)(2,1)S(1)} %all_to_all.27.got_ref, f32[16,512]{1,0:T(8,128)S(1)} %sqrt_multiply_fusion.coeff_ref, f32[16,512]{1,0:T(8,128)S(1)} %copy-done, ...), custom_call_target="tpu_custom_call" | custom-call | flops 1000000000 | bytes 1000 | tf_op jit(solution)/shard_map/pallas_call | solution.py:366
  59.6 14.6 %all_to_all.28 = f32[8,1,128]{2,1,0:T(1,128)S(1)} all-to-all(f32[8,1,128]{2,1,0:T(1,128)S(1)} %bitcast.18), channel_id=1, replica_groups=mesh['context'=64,'dp'=8] {'dp'}, dimensions={0} | all-to-all | bytes 8192 | tf_op jit(solution)/shard_map/all_to_all | solution.py:372
  74.2 0.7 shard_map.92
  (7 shorter events, 0.1 us)
Async XLA Ops:
  0.6 6.0 %copy-start.2 = (bf16[64,3,512]{2,0,1:T(8,128)(2,1)S(1)}, bf16[64,3,512]{2,0,1:T(8,128)(2,1)}, u32[]{:S(2)}) copy-start(bf16[64,3,512]{2,0,1:T(8,128)(2,1)} %param.13) | copy-start | bytes 589828
  1.4 24.0 %collective-permute-start = (bf16[3,2,512]{2,1,0:T(2,128)(2,1)S(1)}, bf16[3,2,512]{2,1,0:T(2,128)(2,1)S(1)}, u32[]{:S(2)}, u32[]{:S(2)}) collective-permute-start(bf16[3,2,512]{2,1,0:T(2,128)(2,1)S(1)} %slice.4), channel_id=1, source_target_pairs={{0,8},{8,16},{16,24},{24,32},{32,40},{40,48},{48,56},{56,64},{64,7... | collective-permute-start | bytes 18440 | tf_op jit(solution)/shard_map/ppermute | solution.py:311
  7.4 17.9 %copy-start = (f32[16,512]{1,0:T(8,128)S(1)}, f32[16,512]{1,0:T(8,128)}, u32[]{:S(2)}) copy-start(f32[16,512]{1,0:T(8,128)} %rates_ref.5) | copy-start | bytes 98308
  7.4 17.9 %copy-start.4 = (f32[16,512]{1,0:T(8,128)S(1)}, f32[16,512]{1,0:T(8,128)}, u32[]{:S(2)}) copy-start(f32[16,512]{1,0:T(8,128)} %param.10) | copy-start | bytes 98308
  7.4 18.0 %copy-start.5 = (f32[3,3,512]{2,1,0:T(4,128)S(1)}, f32[3,3,512]{2,1,0:T(4,128)}, u32[]{:S(2)}) copy-start(f32[3,3,512]{2,1,0:T(4,128)} %param.8) | copy-start | bytes 55300
  7.4 21.7 %all-to-all-start = ((bf16[16,64,128]{2,1,0:T(8,128)(2,1)}), bf16[16,64,128]{2,1,0:T(8,128)(2,1)S(1)}, u32[]{:S(2)}, u32[]{:S(2)}) async-start(bf16[16,64,128]{2,1,0:T(8,128)(2,1)} %get-tuple-element.16), calls=%async_computation | async-start | bytes 524288 | tf_op jit(solution)/shard_map/all_to_all | solution.py:302
  17.7 7.7 %copy-start.1 = (bf16[64,3,512]{2,0,1:T(8,128)(2,1)S(1)}, bf16[64,3,512]{2,0,1:T(8,128)(2,1)}, u32[]{:S(2)}) copy-start(bf16[64,3,512]{2,0,1:T(8,128)(2,1)} %param.7) | copy-start | bytes 589828
  17.7 11.3 %collective-permute-start.1 = (bf16[4,128,128]{2,1,0:T(8,128)(2,1)S(1)}, bf16[4,128,128]{2,1,0:T(8,128)(2,1)S(1)}, u32[]{:S(2)}, u32[]{:S(2)}) collective-permute-start(bf16[4,128,128]{2,1,0:T(8,128)(2,1)S(1)} %get-tuple-element.17.pair_ref), channel_id=1, source_target_pairs={{0,256},{8,264},{16,272},{24,280},{32,288},{40,296},{48,304},{56,3... | collective-permute-start | bytes 393224 | tf_op jit(solution)/shard_map/ppermute | solution.py:332
  25.8 3.1 %collective-permute-start.2 = (bf16[4,16,128]{2,1,0:T(8,128)(2,1)S(1)}, bf16[4,16,128]{2,1,0:T(8,128)(2,1)S(1)}, u32[]{:S(2)}, u32[]{:S(2)}) collective-permute-start(bf16[4,16,128]{2,1,0:T(8,128)(2,1)S(1)} %get-tuple-element.18.state_ref), channel_id=1, source_target_pairs={{0,256},{8,264},{16,272},{24,280},{32,288},{40,296},{48,304},{56,3... | collective-permute-start | bytes 49160 | tf_op jit(solution)/shard_map/ppermute | solution.py:342
  27.1 0.7 copy-start.6
  43.6 14.7 %copy-start.3 = (f32[512]{0:T(512)S(1)}, f32[512]{0:T(512)}, u32[]{:S(2)}) copy-start(f32[512]{0:T(512)} %param.12) | copy-start | bytes 6148

commit v15 on v14

--- a/solution.py
+++ b/solution.py
@@ -95,7 +95,7 @@
 def state_kernel(feat_ref, rim_ref, weight_ref, rates_ref, state_ref, gate_ref, prod_ref):
     groups = []
     for g in range(3):
-        x = jnp.concatenate([rim_ref[g], feat_ref[g].astype(F32)], 0)
+        x = jnp.concatenate([rim_ref[g].astype(F32)[8:], feat_ref[g].astype(F32)], 0)
         total = weight_ref[0, g : g + 1, :] * x[8 : 8 + TOK]
         for o in range(1, FEAT):
             total = total + weight_ref[o, g : g + 1, :] * x[8 - o : 8 - o + TOK]
@@ -309,7 +309,7 @@
     features = jnp.transpose(features, (1, 0, 2))
     attn_in = jnp.transpose(attn_in, (1, 0, 2))
     rim = lax.ppermute(
-        features[:, TOK - (FEAT - 1) :], "context", [(s, s + 1) for s in range(devices - 1)]
+        features[:, TOK - 16 :], "context", [(s, s + 1) for s in range(devices - 1)]
     )
 
     coeff = residues * jnp.sqrt(-jnp.expm1(-2.0 * rates))
@@ -332,7 +332,6 @@
     far_pairs = lax.ppermute(pairs, "context", over_y)
     queries = exchange(queries, Q_GROUPS)
 
-    rim = jnp.pad(rim.astype(F32), ((0, 0), (6, 0), (0, 0)))
     states, gate, product = call(
         state_kernel,
         [((HEADS_DEV, MODES, HEAD), BF), ((TOK, CH), F32), ((TOK, CH), F32)],

time: 75.8 us -> 75.7 us (level)
  no operation moved by 1% of the time
where the time goes in v15:
time: 75.7 us; the launch traced here: 74.9 us
  blocking collectives  42.6 us (56%)
  starting transfers between devices  23.9 us (32%)
  Pallas kernels  5.64 us (7%)
  local copies, waits for them, and re-layouts  1.55 us (2%)
  between operations  0.84 us (1%)
    all_to_all x2, blocking collectives, exchange(): lax.all_to_all(value, 'context', 0, 0, axis_index_groups=groups, tiled=True)  28 us
    all_to_all x1, blocking collectives, local(): squares = lax.all_to_all(squares, 'dp', 0, 0, tiled=True)  14.6 us
    all_to_all x1, starting transfers between devices, exchange(): lax.all_to_all(value, 'context', 0, 0, axis_index_groups=groups, tiled=True)  10.3 us
    ppermute x1, starting transfers between devices, local(): far_pairs = lax.ppermute(pairs, 'context', over_y)  7.46 us
    ppermute x1, starting transfers between devices, local(): lax.ppermute(features[:, TOK - 16:], 'context', [(s, s + 1) for s in rang...  4.82 us
  transfers between devices with their start and end apart: 4, of which 0 were waited for; matrix products, arithmetic and copies ran while one was open for 0% of the time, Pallas kernels for 3%

profile of v15, /device:TPU:1, one launch (start us, length us, event | category | flops | bytes accessed | tf_op | source)
XLA Modules:
  0.0 74.9 jit_solution(5121506854660043644)
XLA Ops:
  0.6 0.0 copy-start.2
  0.6 0.8 %slice.4 = bf16[3,16,512]{2,1,0:T(8,128)(2,1)S(1)} slice(bf16[3,64,512]{2,1,0:T(8,128)(2,1)} %bitcast.16), slice={[0:3], [48:64], [0:512]} | slice | bytes 98304 | tf_op jit(solution)/shard_map/slice | solution.py:312
  1.5 4.8 %collective-permute-start = (bf16[3,16,512]{2,1,0:T(8,128)(2,1)S(1)}, bf16[3,16,512]{2,1,0:T(8,128)(2,1)S(1)}, u32[]{:S(2)}, u32[]{:S(2)}) collective-permute-start(bf16[3,16,512]{2,1,0:T(8,128)(2,1)S(1)} %slice.4), channel_id=1, source_target_pairs={{0,8},{8,16},{16,24},{24,32},{32,40},{40,48},{48,56},{56,64},{64,7... | collective-permute-start | bytes 147464 | tf_op jit(solution)/shard_map/ppermute | solution.py:311
  6.3 0.2 fusion
  6.5 0.1 pad_maximum_fusion
  6.6 0.0 copy-done.2
  6.6 0.8 %shard_map.86 = (bf16[16,64,128]{2,1,0:T(8,128)(2,1)}, bf16[4,128,128]{2,1,0:T(8,128)(2,1)S(1)}) custom-call(bf16[3,64,512]{2,1,0:T(8,128)(2,1)S(1)} %bitcast.20, f32[64,128]{1,0:T(8,128)S(1)} %get-tuple-element.33.cos_ref, f32[64,128]{1,0:T(8,128)S(1)} %get-tuple-element.34.sin_ref), custom_call_target="tpu_custom_call" | custom-call | flops 1000000000 | bytes 1000 | tf_op jit(solution)/shard_map/pallas_call | solution.py:325
  7.4 0.0 copy-start
  7.4 0.0 copy-start.4
  7.4 0.0 copy-start.1
  7.4 10.3 %all-to-all-start = ((bf16[16,64,128]{2,1,0:T(8,128)(2,1)}), bf16[16,64,128]{2,1,0:T(8,128)(2,1)S(1)}, u32[]{:S(2)}, u32[]{:S(2)}) async-start(bf16[16,64,128]{2,1,0:T(8,128)(2,1)} %get-tuple-element.16), calls=%async_computation | async-start | bytes 524288 | tf_op jit(solution)/shard_map/all_to_all | solution.py:302
  17.7 0.0 copy-start.5
  17.8 7.5 %collective-permute-start.1 = (bf16[4,128,128]{2,1,0:T(8,128)(2,1)S(1)}, bf16[4,128,128]{2,1,0:T(8,128)(2,1)S(1)}, u32[]{:S(2)}, u32[]{:S(2)}) collective-permute-start(bf16[4,128,128]{2,1,0:T(8,128)(2,1)S(1)} %get-tuple-element.17.pair_ref), channel_id=1, source_target_pairs={{0,256},{8,264},{16,272},{24,280},{32,288},{40,296},{48,304},{56,3... | collective-permute-start | bytes 393224 | tf_op jit(solution)/shard_map/ppermute | solution.py:332
  25.2 0.0 copy-done
  25.2 0.0 copy-done.4
  25.3 0.0 copy-done.5
  25.3 0.0 collective-permute-done.rim_ref
  25.3 0.0 copy-done.1
  25.3 0.4 shard_map.87
  25.7 1.3 %collective-permute-start.2 = (bf16[4,16,128]{2,1,0:T(8,128)(2,1)S(1)}, bf16[4,16,128]{2,1,0:T(8,128)(2,1)S(1)}, u32[]{:S(2)}, u32[]{:S(2)}) collective-permute-start(bf16[4,16,128]{2,1,0:T(8,128)(2,1)S(1)} %get-tuple-element.18.state_ref), channel_id=1, source_target_pairs={{0,256},{8,264},{16,272},{24,280},{32,288},{40,296},{48,304},{56,3... | collective-permute-start | bytes 49160 | tf_op jit(solution)/shard_map/ppermute | solution.py:341
  27.0 0.0 copy-start.6
  27.1 0.7 copy-done.6
  27.7 1.1 %shard_map.89.near_ref = f32[64,512]{1,0:T(8,128)S(1)} custom-call(f32[64,512]{1,0:T(8,128)S(1)} %get-tuple-element.19.prod_ref, f32[16,512]{1,0:T(8,128)S(1)} %sqrt_multiply_fusion.coeff_ref, f32[16,512]{1,0:T(8,128)S(1)} %copy-done, f32[8,512]{1,0:T(8,128)S(1)} %pad.9.skip_ref), custom_call_target="tpu_custom_call" | custom-call | flops 1000000 | bytes 1000 | tf_op jit(solution)/shard_map/pallas_call | solution.py:342
  28.9 0.0 collective-permute-done.2.far_state_ref
  28.9 0.0 collective-permute-done.1.far_pair_ref
  28.9 0.1 shard_map.88
  29.0 0.0 all-to-all-done.q_ref
  29.0 13.3 %all_to_all.26.got_ref = bf16[8,288,128]{2,1,0:T(8,128)(2,1)S(1)} all-to-all(bf16[8,288,128]{2,1,0:T(8,128)(2,1)S(1)} %shard_map.88), channel_id=1, replica_groups={{0,8,64,72,128,136,192,200},{16,24,80,88,144,152,208,216},{32,40,96,104..., dimensions={0} | all-to-all | bytes 1179648 | tf_op jit(solution)/shard_map/all_to_all | solution.py:302
  42.3 1.2 %shard_map.90 = bf16[16,96,128]{2,1,0:T(8,128)(2,1)S(1)} custom-call(s32[1]{0:T(128)} %bitcast.place_ref, bf16[16,64,128]{2,1,0:T(8,128)(2,1)S(1)} %all-to-all-done.q_ref, bf16[8,288,128]{2,1,0:T(8,128)(2,1)S(1)} %all_to_all.26.got_ref, f32[4,16,128]{2,1,0:T(8,128)S(1)} %bitcast_bitcast_fusion.rates_ref), custom_call_target="tpu_custom_call" | custom-call | flops 4000000000 | bytes 1000 | tf_op jit(solution)/shard_map/pallas_call | solution.py:357
  43.5 0.0 copy-start.3
  43.5 14.7 %all_to_all.27.got_ref = bf16[16,96,128]{2,1,0:T(8,128)(2,1)S(1)} all-to-all(bf16[16,96,128]{2,1,0:T(8,128)(2,1)S(1)} %shard_map.90), channel_id=1, replica_groups={{0,8,16,24,32,40,48,56,64,72,80,88,96,104,112,120},{128,136,144,152,160..., dimensions={0} | all-to-all | bytes 786432 | tf_op jit(solution)/shard_map/all_to_all | solution.py:302
  58.2 0.0 copy-done.3
  58.2 1.3 %shard_map.91 = (f32[64,512]{1,0:T(8,128)S(1)}, f32[8,128]{1,0:T(8,128)S(1)}, bf16[64,512]{1,0:T(8,128)(2,1)}) custom-call(s32[1]{0:T(128)} %bitcast.place_ref, bf16[16,96,128]{2,1,0:T(8,128)(2,1)S(1)} %all_to_all.27.got_ref, f32[16,512]{1,0:T(8,128)S(1)} %sqrt_multiply_fusion.coeff_ref, f32[16,512]{1,0:T(8,128)S(1)} %copy-done, ...), custom_call_target="tpu_custom_call" | custom-call | flops 1000000000 | bytes 1000 | tf_op jit(solution)/shard_map/pallas_call | solution.py:365
  59.5 14.6 %all_to_all.28 = f32[8,1,128]{2,1,0:T(1,128)S(1)} all-to-all(f32[8,1,128]{2,1,0:T(1,128)S(1)} %bitcast.18), channel_id=1, replica_groups=mesh['context'=64,'dp'=8] {'dp'}, dimensions={0} | all-to-all | bytes 8192 | tf_op jit(solution)/shard_map/all_to_all | solution.py:371
  74.1 0.7 shard_map.92
  (6 shorter events, 0.1 us)
Async XLA Ops:
  0.6 6.0 %copy-start.2 = (bf16[64,3,512]{2,0,1:T(8,128)(2,1)S(1)}, bf16[64,3,512]{2,0,1:T(8,128)(2,1)}, u32[]{:S(2)}) copy-start(bf16[64,3,512]{2,0,1:T(8,128)(2,1)} %param.13) | copy-start | bytes 589828
  1.5 23.8 %collective-permute-start = (bf16[3,16,512]{2,1,0:T(8,128)(2,1)S(1)}, bf16[3,16,512]{2,1,0:T(8,128)(2,1)S(1)}, u32[]{:S(2)}, u32[]{:S(2)}) collective-permute-start(bf16[3,16,512]{2,1,0:T(8,128)(2,1)S(1)} %slice.4), channel_id=1, source_target_pairs={{0,8},{8,16},{16,24},{24,32},{32,40},{40,48},{48,56},{56,64},{64,7... | collective-permute-start | bytes 147464 | tf_op jit(solution)/shard_map/ppermute | solution.py:311
  7.4 17.8 %copy-start = (f32[16,512]{1,0:T(8,128)S(1)}, f32[16,512]{1,0:T(8,128)}, u32[]{:S(2)}) copy-start(f32[16,512]{1,0:T(8,128)} %rates_ref.5) | copy-start | bytes 98308
  7.4 17.8 %copy-start.4 = (f32[16,512]{1,0:T(8,128)S(1)}, f32[16,512]{1,0:T(8,128)}, u32[]{:S(2)}) copy-start(f32[16,512]{1,0:T(8,128)} %param.10) | copy-start | bytes 98308
  7.4 17.9 %copy-start.1 = (bf16[64,3,512]{2,0,1:T(8,128)(2,1)S(1)}, bf16[64,3,512]{2,0,1:T(8,128)(2,1)}, u32[]{:S(2)}) copy-start(bf16[64,3,512]{2,0,1:T(8,128)(2,1)} %param.7) | copy-start | bytes 589828
  7.4 21.5 %all-to-all-start = ((bf16[16,64,128]{2,1,0:T(8,128)(2,1)}), bf16[16,64,128]{2,1,0:T(8,128)(2,1)S(1)}, u32[]{:S(2)}, u32[]{:S(2)}) async-start(bf16[16,64,128]{2,1,0:T(8,128)(2,1)} %get-tuple-element.16), calls=%async_computation | async-start | bytes 524288 | tf_op jit(solution)/shard_map/all_to_all | solution.py:302
  17.7 7.5 %copy-start.5 = (f32[3,3,512]{2,1,0:T(4,128)S(1)}, f32[3,3,512]{2,1,0:T(4,128)}, u32[]{:S(2)}) copy-start(f32[3,3,512]{2,1,0:T(4,128)} %param.8) | copy-start | bytes 55300
  17.8 11.1 %collective-permute-start.1 = (bf16[4,128,128]{2,1,0:T(8,128)(2,1)S(1)}, bf16[4,128,128]{2,1,0:T(8,128)(2,1)S(1)}, u32[]{:S(2)}, u32[]{:S(2)}) collective-permute-start(bf16[4,128,128]{2,1,0:T(8,128)(2,1)S(1)} %get-tuple-element.17.pair_ref), channel_id=1, source_target_pairs={{0,256},{8,264},{16,272},{24,280},{32,288},{40,296},{48,304},{56,3... | collective-permute-start | bytes 393224 | tf_op jit(solution)/shard_map/ppermute | solution.py:332
  25.7 3.1 %collective-permute-start.2 = (bf16[4,16,128]{2,1,0:T(8,128)(2,1)S(1)}, bf16[4,16,128]{2,1,0:T(8,128)(2,1)S(1)}, u32[]{:S(2)}, u32[]{:S(2)}) collective-permute-start(bf16[4,16,128]{2,1,0:T(8,128)(2,1)S(1)} %get-tuple-element.18.state_ref), channel_id=1, source_target_pairs={{0,256},{8,264},{16,272},{24,280},{32,288},{40,296},{48,304},{56,3... | collective-permute-start | bytes 49160 | tf_op jit(solution)/shard_map/ppermute | solution.py:341
  27.0 0.7 copy-start.6
  43.5 14.7 %copy-start.3 = (f32[512]{0:T(512)S(1)}, f32[512]{0:T(512)}, u32[]{:S(2)}) copy-start(f32[512]{0:T(512)} %param.12) | copy-start | bytes 6148

commit v16 on v15

--- a/solution.py
+++ b/solution.py
@@ -4,6 +4,7 @@
 
 import jax
 import jax.numpy as jnp
+import numpy as np
 from jax import lax
 from jax.experimental import pallas as pl
 from jax.experimental.pallas import tpu as pltpu
@@ -313,12 +314,13 @@
     )
 
     coeff = residues * jnp.sqrt(-jnp.expm1(-2.0 * rates))
-    inverse = jnp.exp(
-        jnp.arange(HEAD // 2, dtype=F32) * (-2.0 * math.log(ROPE_BASE) / HEAD)
-    )
-    positions = (index * TOK + jnp.arange(TOK)).astype(F32)
-    angle = positions[:, None] * inverse[None, :]
-    cosine, sine = jnp.cos(angle), jnp.sin(angle)
+    steps = np.arange(TOK)[:, None] * ROPE_BASE ** (-2.0 * np.arange(HEAD // 2)[None, :] / HEAD)
+    inner_cos, inner_sin = np.cos(steps).astype(np.float32), np.sin(steps).astype(np.float32)
+    inverse = jnp.exp(jnp.arange(HEAD // 2, dtype=F32) * (-2.0 * math.log(ROPE_BASE) / HEAD))
+    start = (index * TOK).astype(F32) * inverse[None, :]
+    start_cos, start_sin = lax.optimization_barrier((jnp.cos(start), jnp.sin(start)))
+    cosine = start_cos * inner_cos - start_sin * inner_sin
+    sine = start_sin * inner_cos + start_cos * inner_sin
     cosine = jnp.concatenate([cosine, cosine], 1)
     sine = jnp.concatenate([-sine, sine], 1)
 

time: 75.7 us -> 75.8 us (level)
  no operation moved by 1% of the time
where the time goes in v16:
time: 75.8 us; the launch traced here: 74.9 us
  blocking collectives  42.6 us (56%)
  starting transfers between devices  24 us (32%)
  Pallas kernels  5.66 us (7%)
  local copies, waits for them, and re-layouts  1.53 us (2%)
  between operations  0.84 us (1%)
    all_to_all x2, blocking collectives, exchange(): lax.all_to_all(value, 'context', 0, 0, axis_index_groups=groups, tiled=True)  28 us
    all_to_all x1, blocking collectives, local(): squares = lax.all_to_all(squares, 'dp', 0, 0, tiled=True)  14.6 us
    all_to_all x1, starting transfers between devices, exchange(): lax.all_to_all(value, 'context', 0, 0, axis_index_groups=groups, tiled=True)  10.3 us
    ppermute x1, starting transfers between devices, local(): far_pairs = lax.ppermute(pairs, 'context', over_y)  7.46 us
    ppermute x1, starting transfers between devices, local(): lax.ppermute(features[:, TOK - 16:], 'context', [(s, s + 1) for s in rang...  4.95 us
  transfers between devices with their start and end apart: 4, of which 0 were waited for; matrix products, arithmetic and copies ran while one was open for 0% of the time, Pallas kernels for 3%

profile of v16, /device:TPU:1, one launch (start us, length us, event | category | flops | bytes accessed | tf_op | source)
XLA Modules:
  0.0 74.9 jit_solution(10746255401448389221)
XLA Ops:
  0.6 0.0 copy-start.5
  0.6 0.0 copy-start.6
  0.7 0.8 %slice.4 = bf16[3,16,512]{2,1,0:T(8,128)(2,1)S(1)} slice(bf16[3,64,512]{2,1,0:T(8,128)(2,1)} %bitcast.18), slice={[0:3], [48:64], [0:512]} | slice | bytes 98304 | tf_op jit(solution)/shard_map/slice | solution.py:313
  1.5 0.0 copy-start.2
  1.5 4.9 %collective-permute-start = (bf16[3,16,512]{2,1,0:T(8,128)(2,1)S(1)}, bf16[3,16,512]{2,1,0:T(8,128)(2,1)S(1)}, u32[]{:S(2)}, u32[]{:S(2)}) collective-permute-start(bf16[3,16,512]{2,1,0:T(8,128)(2,1)S(1)} %slice.4), channel_id=1, source_target_pairs={{0,8},{8,16},{16,24},{24,32},{32,40},{40,48},{48,56},{56,64},{64,7... | collective-permute-start | bytes 147464 | tf_op jit(solution)/shard_map/ppermute | solution.py:312
  6.4 0.1 fusion.1
  6.5 0.0 copy-done.5
  6.5 0.0 copy-done.6
  6.5 0.1 pad_maximum_fusion.cos_ref
  6.6 0.1 pad_maximum_fusion.1.sin_ref
  6.7 0.0 copy-done.2
  6.7 0.8 %shard_map.104 = (bf16[16,64,128]{2,1,0:T(8,128)(2,1)}, bf16[4,128,128]{2,1,0:T(8,128)(2,1)S(1)}) custom-call(bf16[3,64,512]{2,1,0:T(8,128)(2,1)S(1)} %bitcast.22, f32[64,128]{1,0:T(8,128)S(1)} %pad_maximum_fusion.cos_ref, f32[64,128]{1,0:T(8,128)S(1)} %pad_maximum_fusion.1.sin_ref), custom_call_target="tpu_custom_call" | custom-call | flops 1000000000 | bytes 1000 | tf_op jit(solution)/shard_map/pallas_call | solution.py:327
  7.5 0.0 copy-start
  7.5 0.0 copy-start.4
  7.5 0.0 copy-start.1
  7.5 10.3 %all-to-all-start = ((bf16[16,64,128]{2,1,0:T(8,128)(2,1)}), bf16[16,64,128]{2,1,0:T(8,128)(2,1)S(1)}, u32[]{:S(2)}, u32[]{:S(2)}) async-start(bf16[16,64,128]{2,1,0:T(8,128)(2,1)} %get-tuple-element.20), calls=%async_computation | async-start | bytes 524288 | tf_op jit(solution)/shard_map/all_to_all | solution.py:303
  17.8 0.0 copy-start.7
  17.8 7.5 %collective-permute-start.1 = (bf16[4,128,128]{2,1,0:T(8,128)(2,1)S(1)}, bf16[4,128,128]{2,1,0:T(8,128)(2,1)S(1)}, u32[]{:S(2)}, u32[]{:S(2)}) collective-permute-start(bf16[4,128,128]{2,1,0:T(8,128)(2,1)S(1)} %get-tuple-element.21.pair_ref), channel_id=1, source_target_pairs={{0,256},{8,264},{16,272},{24,280},{32,288},{40,296},{48,304},{56,3... | collective-permute-start | bytes 393224 | tf_op jit(solution)/shard_map/ppermute | solution.py:334
  25.3 0.0 copy-done
  25.3 0.0 copy-done.4
  25.3 0.0 copy-done.7
  25.4 0.0 collective-permute-done.rim_ref
  25.4 0.0 copy-done.1
  25.4 0.4 shard_map.105
  25.8 1.3 %collective-permute-start.2 = (bf16[4,16,128]{2,1,0:T(8,128)(2,1)S(1)}, bf16[4,16,128]{2,1,0:T(8,128)(2,1)S(1)}, u32[]{:S(2)}, u32[]{:S(2)}) collective-permute-start(bf16[4,16,128]{2,1,0:T(8,128)(2,1)S(1)} %get-tuple-element.22.state_ref), channel_id=1, source_target_pairs={{0,256},{8,264},{16,272},{24,280},{32,288},{40,296},{48,304},{56,3... | collective-permute-start | bytes 49160 | tf_op jit(solution)/shard_map/ppermute | solution.py:343
  27.1 0.0 copy-start.8
  27.1 0.7 copy-done.8
  27.8 1.1 %shard_map.107.near_ref = f32[64,512]{1,0:T(8,128)S(1)} custom-call(f32[64,512]{1,0:T(8,128)S(1)} %get-tuple-element.23.prod_ref, f32[16,512]{1,0:T(8,128)S(1)} %sqrt_multiply_fusion.coeff_ref, f32[16,512]{1,0:T(8,128)S(1)} %copy-done, f32[8,512]{1,0:T(8,128)S(1)} %pad.9.skip_ref), custom_call_target="tpu_custom_call" | custom-call | flops 1000000 | bytes 1000 | tf_op jit(solution)/shard_map/pallas_call | solution.py:344
  28.9 0.0 collective-permute-done.2.far_state_ref
  28.9 0.0 collective-permute-done.1.far_pair_ref
  28.9 0.1 shard_map.106
  29.0 0.0 all-to-all-done.q_ref
  29.0 13.3 %all_to_all.26.got_ref = bf16[8,288,128]{2,1,0:T(8,128)(2,1)S(1)} all-to-all(bf16[8,288,128]{2,1,0:T(8,128)(2,1)S(1)} %shard_map.106), channel_id=1, replica_groups={{0,8,64,72,128,136,192,200},{16,24,80,88,144,152,208,216},{32,40,96,104..., dimensions={0} | all-to-all | bytes 1179648 | tf_op jit(solution)/shard_map/all_to_all | solution.py:303
  42.4 1.2 %shard_map.108 = bf16[16,96,128]{2,1,0:T(8,128)(2,1)S(1)} custom-call(s32[1]{0:T(128)} %bitcast.place_ref, bf16[16,64,128]{2,1,0:T(8,128)(2,1)S(1)} %all-to-all-done.q_ref, bf16[8,288,128]{2,1,0:T(8,128)(2,1)S(1)} %all_to_all.26.got_ref, f32[4,16,128]{2,1,0:T(8,128)S(1)} %bitcast_bitcast_fusion.rates_ref), custom_call_target="tpu_custom_call" | custom-call | flops 4000000000 | bytes 1000 | tf_op jit(solution)/shard_map/pallas_call | solution.py:359
  43.6 0.0 copy-start.3
  43.6 14.7 %all_to_all.27.got_ref = bf16[16,96,128]{2,1,0:T(8,128)(2,1)S(1)} all-to-all(bf16[16,96,128]{2,1,0:T(8,128)(2,1)S(1)} %shard_map.108), channel_id=1, replica_groups={{0,8,16,24,32,40,48,56,64,72,80,88,96,104,112,120},{128,136,144,152,160..., dimensions={0} | all-to-all | bytes 786432 | tf_op jit(solution)/shard_map/all_to_all | solution.py:303
  58.2 0.0 copy-done.3
  58.2 1.3 %shard_map.109 = (f32[64,512]{1,0:T(8,128)S(1)}, f32[8,128]{1,0:T(8,128)S(1)}, bf16[64,512]{1,0:T(8,128)(2,1)}) custom-call(s32[1]{0:T(128)} %bitcast.place_ref, bf16[16,96,128]{2,1,0:T(8,128)(2,1)S(1)} %all_to_all.27.got_ref, f32[16,512]{1,0:T(8,128)S(1)} %sqrt_multiply_fusion.coeff_ref, f32[16,512]{1,0:T(8,128)S(1)} %copy-done, ...), custom_call_target="tpu_custom_call" | custom-call | flops 1000000000 | bytes 1000 | tf_op jit(solution)/shard_map/pallas_call | solution.py:367
  59.6 14.6 %all_to_all.28 = f32[8,1,128]{2,1,0:T(1,128)S(1)} all-to-all(f32[8,1,128]{2,1,0:T(1,128)S(1)} %bitcast.20), channel_id=1, replica_groups=mesh['context'=64,'dp'=8] {'dp'}, dimensions={0} | all-to-all | bytes 8192 | tf_op jit(solution)/shard_map/all_to_all | solution.py:373
  74.2 0.7 shard_map.110
  (5 shorter events, 0.1 us)
Async XLA Ops:
  0.6 5.9 %copy-start.5 = (f32[64,64]{1,0:T(8,128)S(1)}, f32[64,64]{1,0:T(8,128)}, u32[]{:S(2)}) copy-start(f32[64,64]{1,0:T(8,128)} %constant.20.clone) | copy-start | bytes 49156
  0.6 5.9 %copy-start.6 = (f32[64,64]{1,0:T(8,128)S(1)}, f32[64,64]{1,0:T(8,128)}, u32[]{:S(2)}) copy-start(f32[64,64]{1,0:T(8,128)} %constant.19.clone) | copy-start | bytes 49156
  1.5 5.2 %copy-start.2 = (bf16[64,3,512]{2,0,1:T(8,128)(2,1)S(1)}, bf16[64,3,512]{2,0,1:T(8,128)(2,1)}, u32[]{:S(2)}) copy-start(bf16[64,3,512]{2,0,1:T(8,128)(2,1)} %param.15) | copy-start | bytes 589828
  1.5 23.9 %collective-permute-start = (bf16[3,16,512]{2,1,0:T(8,128)(2,1)S(1)}, bf16[3,16,512]{2,1,0:T(8,128)(2,1)S(1)}, u32[]{:S(2)}, u32[]{:S(2)}) collective-permute-start(bf16[3,16,512]{2,1,0:T(8,128)(2,1)S(1)} %slice.4), channel_id=1, source_target_pairs={{0,8},{8,16},{16,24},{24,32},{32,40},{40,48},{48,56},{56,64},{64,7... | collective-permute-start | bytes 147464 | tf_op jit(solution)/shard_map/ppermute | solution.py:312
  7.5 17.8 %copy-start = (f32[16,512]{1,0:T(8,128)S(1)}, f32[16,512]{1,0:T(8,128)}, u32[]{:S(2)}) copy-start(f32[16,512]{1,0:T(8,128)} %rates_ref.5) | copy-start | bytes 98308
  7.5 17.8 %copy-start.4 = (f32[16,512]{1,0:T(8,128)S(1)}, f32[16,512]{1,0:T(8,128)}, u32[]{:S(2)}) copy-start(f32[16,512]{1,0:T(8,128)} %param.12) | copy-start | bytes 98308
  7.5 17.9 %copy-start.1 = (bf16[64,3,512]{2,0,1:T(8,128)(2,1)S(1)}, bf16[64,3,512]{2,0,1:T(8,128)(2,1)}, u32[]{:S(2)}) copy-start(bf16[64,3,512]{2,0,1:T(8,128)(2,1)} %param.9) | copy-start | bytes 589828
  7.5 21.5 %all-to-all-start = ((bf16[16,64,128]{2,1,0:T(8,128)(2,1)}), bf16[16,64,128]{2,1,0:T(8,128)(2,1)S(1)}, u32[]{:S(2)}, u32[]{:S(2)}) async-start(bf16[16,64,128]{2,1,0:T(8,128)(2,1)} %get-tuple-element.20), calls=%async_computation | async-start | bytes 524288 | tf_op jit(solution)/shard_map/all_to_all | solution.py:303
  17.8 7.5 %copy-start.7 = (f32[3,3,512]{2,1,0:T(4,128)S(1)}, f32[3,3,512]{2,1,0:T(4,128)}, u32[]{:S(2)}) copy-start(f32[3,3,512]{2,1,0:T(4,128)} %param.10) | copy-start | bytes 55300
  17.8 11.1 %collective-permute-start.1 = (bf16[4,128,128]{2,1,0:T(8,128)(2,1)S(1)}, bf16[4,128,128]{2,1,0:T(8,128)(2,1)S(1)}, u32[]{:S(2)}, u32[]{:S(2)}) collective-permute-start(bf16[4,128,128]{2,1,0:T(8,128)(2,1)S(1)} %get-tuple-element.21.pair_ref), channel_id=1, source_target_pairs={{0,256},{8,264},{16,272},{24,280},{32,288},{40,296},{48,304},{56,3... | collective-permute-start | bytes 393224 | tf_op jit(solution)/shard_map/ppermute | solution.py:334
  25.8 3.1 %collective-permute-start.2 = (bf16[4,16,128]{2,1,0:T(8,128)(2,1)S(1)}, bf16[4,16,128]{2,1,0:T(8,128)(2,1)S(1)}, u32[]{:S(2)}, u32[]{:S(2)}) collective-permute-start(bf16[4,16,128]{2,1,0:T(8,128)(2,1)S(1)} %get-tuple-element.22.state_ref), channel_id=1, source_target_pairs={{0,256},{8,264},{16,272},{24,280},{32,288},{40,296},{48,304},{56,3... | collective-permute-start | bytes 49160 | tf_op jit(solution)/shard_map/ppermute | solution.py:343
  27.1 0.7 copy-start.8
  43.6 14.7 %copy-start.3 = (f32[512]{0:T(512)S(1)}, f32[512]{0:T(512)}, u32[]{:S(2)}) copy-start(f32[512]{0:T(512)} %param.14) | copy-start | bytes 6148

commit v17 on v13

--- a/solution.py
+++ b/solution.py
@@ -19,7 +19,7 @@
 ROPE_BASE = 1000000.0
 NEG = -1e30
 PACK = 2 * TOK + MODES
-WIDE = 512
+WIDE = 128
 BLOCKS = WIDE // TOK
 BF = jnp.bfloat16
 F32 = jnp.float32
@@ -199,11 +199,10 @@
     scores = mask(scores)
     top = jnp.max(scores, 1, keepdims=True)
     weights = jnp.exp2(scores - top)
-    total = jnp.sum(weights, 1, keepdims=True)
     mixed = lax.dot_general(
         weights.astype(BF), values, (((1,), (0,)), ((), ())), preferred_element_type=F32
     )
-    return top, total, mixed
+    return top, mixed[:, HEAD:], mixed[:, :HEAD]
 
 
 def attend_kernel(place_ref, q_ref, got_ref, rates_ref, out_ref):
@@ -212,7 +211,8 @@
 
     def half(first):
         keys = got_ref[:, first : first + TOK, :].reshape(8 * TOK, HEAD)
-        return keys, got_ref[:, first + TOK : first + 2 * TOK, :].reshape(8 * TOK, HEAD)
+        values = got_ref[:, first + TOK : first + 2 * TOK, :].reshape(8 * TOK, HEAD)
+        return keys, jnp.concatenate([values, jnp.ones((8 * TOK, HEAD), BF)], 1)
 
     own, other = half(0), half(PACK)
     lane = lax.broadcasted_iota(jnp.int32, (1, 8 * TOK), 1)
@@ -327,12 +327,12 @@
     cosine = jnp.concatenate([cosine, cosine], 1)
     sine = jnp.concatenate([-sine, sine], 1)
 
+    (queries,) = call(query_kernel, [((16, TOK, HEAD), BF)], [VMEM] * 3, 1000000)(
+        attn_in, cosine, sine
+    )
+    queries, cosine = lax.optimization_barrier((queries, cosine))
     (pairs,) = call(
-        pair_kernel, [((HEADS_DEV, 2 * TOK, HEAD), BF)], [VMEM] * 3, 1000000000
-    )(attn_in, cosine, sine)
-    pairs, cosine = lax.optimization_barrier((pairs, cosine))
-    (queries,) = call(
-        query_kernel, [((16, TOK, HEAD), BF)], [VMEM] * 3, 20000000000
+        pair_kernel, [((HEADS_DEV, 2 * TOK, HEAD), BF)], [VMEM] * 3, 1000000
     )(attn_in, cosine, sine)
     over_y = [(s, s + devices // 2) for s in range(devices // 2)]
     far_pairs = lax.ppermute(pairs, "context", over_y)

time: 76.7 us -> 75.8 us (0.988)
  waiting for transfers between devices: 3.92 us -> 0.01 us
  blocking collectives: 39.5 us -> 42.6 us
    all_to_all x1, waiting for transfers between devices: 3.91 us -> 0.01 us  [exchange(): lax.all_to_all(value, 'context', 0, 0, axis_index_groups=groups, tiled=True)]
    all_to_all x1, blocking collectives: 12.1 us -> 14.6 us  [local(): squares = lax.all_to_all(squares, 'dp', 0, 0, tiled=True)]
  transfers between devices with their start and end apart: 4 -> 4, of which waited for: 1 -> 0; matrix products, arithmetic and copies ran while one was open for 0% -> 1% of each run, Pallas kernels for 3% -> 3%
where the time goes in v17:
time: 75.8 us; the launch traced here: 75 us
  blocking collectives  42.6 us (56%)
  starting transfers between devices  23.9 us (32%)
  Pallas kernels  5.75 us (8%)
  local copies, waits for them, and re-layouts  1.5 us (2%)
  between operations  0.86 us (1%)
    all_to_all x2, blocking collectives, exchange(): lax.all_to_all(value, 'context', 0, 0, axis_index_groups=groups, tiled=True)  28 us
    all_to_all x1, blocking collectives, local(): squares = lax.all_to_all(squares, 'dp', 0, 0, tiled=True)  14.6 us
    all_to_all x1, starting transfers between devices, exchange(): lax.all_to_all(value, 'context', 0, 0, axis_index_groups=groups, tiled=True)  10.2 us
    ppermute x1, starting transfers between devices, local(): far_pairs = lax.ppermute(pairs, 'context', over_y)  7.59 us
    ppermute x1, starting transfers between devices, local(): lax.ppermute(features[:, TOK - (FEAT - 1):], 'context', [(s, s + 1) for s...  4.83 us
  transfers between devices with their start and end apart: 4, of which 0 were waited for; matrix products, arithmetic and copies ran while one was open for 1% of the time, Pallas kernels for 3%

profile of v17, /device:TPU:1, one launch (start us, length us, event | category | flops | bytes accessed | tf_op | source)
XLA Modules:
  0.0 75.0 jit_solution(4397562814766482144)
XLA Ops:
  0.6 0.0 copy-start
  0.6 0.8 %slice.4 = bf16[3,2,512]{2,1,0:T(2,128)(2,1)S(1)} slice(bf16[3,64,512]{2,1,0:T(8,128)(2,1)} %bitcast.18), slice={[0:3], [62:64], [0:512]} | slice | bytes 12288 | tf_op jit(solution)/shard_map/slice | solution.py:317
  1.4 4.8 %collective-permute-start = (bf16[3,2,512]{2,1,0:T(2,128)(2,1)S(1)}, bf16[3,2,512]{2,1,0:T(2,128)(2,1)S(1)}, u32[]{:S(2)}, u32[]{:S(2)}) collective-permute-start(bf16[3,2,512]{2,1,0:T(2,128)(2,1)S(1)} %slice.4), channel_id=1, source_target_pairs={{0,8},{8,16},{16,24},{24,32},{32,40},{40,48},{48,56},{56,64},{64,7... | collective-permute-start | bytes 18440 | tf_op jit(solution)/shard_map/ppermute | solution.py:316
  6.3 0.2 fusion
  6.5 0.1 pad_maximum_fusion.cos_ref
  6.6 0.1 pad_maximum_fusion.1.sin_ref
  6.7 0.0 copy-done
  6.7 0.8 %shard_map.86 = bf16[16,64,128]{2,1,0:T(8,128)(2,1)} custom-call(bf16[3,64,512]{2,1,0:T(8,128)(2,1)S(1)} %bitcast.16, f32[64,128]{1,0:T(8,128)S(1)} %pad_maximum_fusion.cos_ref, f32[64,128]{1,0:T(8,128)S(1)} %pad_maximum_fusion.1.sin_ref), custom_call_target="tpu_custom_call" | custom-call | flops 1000000 | bytes 1000 | tf_op jit(solution)/shard_map/pallas_call | solution.py:330
  7.5 10.2 %all-to-all-start = ((bf16[16,64,128]{2,1,0:T(8,128)(2,1)}), bf16[16,64,128]{2,1,0:T(8,128)(2,1)S(1)}, u32[]{:S(2)}, u32[]{:S(2)}) async-start(bf16[16,64,128]{2,1,0:T(8,128)(2,1)} %shard_map.86), calls=%async_computation | async-start | bytes 524288 | tf_op jit(solution)/shard_map/all_to_all | solution.py:307
  17.6 0.0 copy-start.1
  17.6 0.0 copy-start.4
  17.7 0.0 copy-start.5
  17.7 0.1 shard_map.87.pair_ref
  17.8 0.0 copy-start.2
  17.8 7.6 %collective-permute-start.1 = (bf16[4,128,128]{2,1,0:T(8,128)(2,1)S(1)}, bf16[4,128,128]{2,1,0:T(8,128)(2,1)S(1)}, u32[]{:S(2)}, u32[]{:S(2)}) collective-permute-start(bf16[4,128,128]{2,1,0:T(8,128)(2,1)S(1)} %shard_map.87.pair_ref), channel_id=1, source_target_pairs={{0,256},{8,264},{16,272},{24,280},{32,288},{40,296},{48,304},{56,3... | collective-permute-start | bytes 393224 | tf_op jit(solution)/shard_map/ppermute | solution.py:338
  25.4 0.0 copy-done.1
  25.4 0.0 copy-done.4
  25.4 0.0 copy-done.5
  25.5 0.0 collective-permute-done
  25.5 0.0 copy-done.2
  25.5 0.4 shard_map.88
  25.9 1.3 %collective-permute-start.2 = (bf16[4,16,128]{2,1,0:T(8,128)(2,1)S(1)}, bf16[4,16,128]{2,1,0:T(8,128)(2,1)S(1)}, u32[]{:S(2)}, u32[]{:S(2)}) collective-permute-start(bf16[4,16,128]{2,1,0:T(8,128)(2,1)S(1)} %get-tuple-element.18.state_ref), channel_id=1, source_target_pairs={{0,256},{8,264},{16,272},{24,280},{32,288},{40,296},{48,304},{56,3... | collective-permute-start | bytes 49160 | tf_op jit(solution)/shard_map/ppermute | solution.py:348
  27.2 0.0 copy-start.6
  27.2 0.7 copy-done.6
  27.9 1.1 %shard_map.90.near_ref = f32[64,512]{1,0:T(8,128)S(1)} custom-call(f32[64,512]{1,0:T(8,128)S(1)} %get-tuple-element.19.prod_ref, f32[16,512]{1,0:T(8,128)S(1)} %sqrt_multiply_fusion.coeff_ref, f32[16,512]{1,0:T(8,128)S(1)} %copy-done.1, f32[8,512]{1,0:T(8,128)S(1)} %pad.17.skip_ref), custom_call_target="tpu_custom_call" | custom-call | flops 1000000 | bytes 1000 | tf_op jit(solution)/shard_map/pallas_call | solution.py:349
  29.0 0.0 collective-permute-done.2.far_state_ref
  29.0 0.0 collective-permute-done.1.far_pair_ref
  29.0 0.1 shard_map.89
  29.1 0.0 all-to-all-done.q_ref
  29.1 13.3 %all_to_all.26.got_ref = bf16[8,288,128]{2,1,0:T(8,128)(2,1)S(1)} all-to-all(bf16[8,288,128]{2,1,0:T(8,128)(2,1)S(1)} %shard_map.89), channel_id=1, replica_groups={{0,8,64,72,128,136,192,200},{16,24,80,88,144,152,208,216},{32,40,96,104..., dimensions={0} | all-to-all | bytes 1179648 | tf_op jit(solution)/shard_map/all_to_all | solution.py:307
  42.5 1.2 %shard_map.91 = bf16[16,96,128]{2,1,0:T(8,128)(2,1)S(1)} custom-call(s32[1]{0:T(128)} %bitcast.place_ref, bf16[16,64,128]{2,1,0:T(8,128)(2,1)S(1)} %all-to-all-done.q_ref, bf16[8,288,128]{2,1,0:T(8,128)(2,1)S(1)} %all_to_all.26.got_ref, f32[4,16,128]{2,1,0:T(8,128)S(1)} %bitcast_bitcast_fusion.rates_ref), custom_call_target="tpu_custom_call" | custom-call | flops 4000000000 | bytes 1000 | tf_op jit(solution)/shard_map/pallas_call | solution.py:364
  43.7 0.0 copy-start.3
  43.7 14.7 %all_to_all.27.got_ref = bf16[16,96,128]{2,1,0:T(8,128)(2,1)S(1)} all-to-all(bf16[16,96,128]{2,1,0:T(8,128)(2,1)S(1)} %shard_map.91), channel_id=1, replica_groups={{0,8,16,24,32,40,48,56,64,72,80,88,96,104,112,120},{128,136,144,152,160..., dimensions={0} | all-to-all | bytes 786432 | tf_op jit(solution)/shard_map/all_to_all | solution.py:307
  58.4 0.0 copy-done.3
  58.4 1.3 %shard_map.92 = (f32[64,512]{1,0:T(8,128)S(1)}, f32[8,128]{1,0:T(8,128)S(1)}, bf16[64,512]{1,0:T(8,128)(2,1)}) custom-call(s32[1]{0:T(128)} %bitcast.place_ref, bf16[16,96,128]{2,1,0:T(8,128)(2,1)S(1)} %all_to_all.27.got_ref, f32[16,512]{1,0:T(8,128)S(1)} %sqrt_multiply_fusion.coeff_ref, f32[16,512]{1,0:T(8,128)S(1)} %copy-done.1, ...), custom_call_target="tpu_custom_call" | custom-call | flops 1000000000 | bytes 1000 | tf_op jit(solution)/shard_map/pallas_call | solution.py:372
  59.7 14.6 %all_to_all.28 = f32[8,1,128]{2,1,0:T(1,128)S(1)} all-to-all(f32[8,1,128]{2,1,0:T(1,128)S(1)} %bitcast.20), channel_id=1, replica_groups=mesh['context'=64,'dp'=8] {'dp'}, dimensions={0} | all-to-all | bytes 8192 | tf_op jit(solution)/shard_map/all_to_all | solution.py:378
  74.3 0.7 shard_map.93
  (7 shorter events, 0.1 us)
Async XLA Ops:
  0.6 6.0 %copy-start = (bf16[64,3,512]{2,0,1:T(8,128)(2,1)S(1)}, bf16[64,3,512]{2,0,1:T(8,128)(2,1)}, u32[]{:S(2)}) copy-start(bf16[64,3,512]{2,0,1:T(8,128)(2,1)} %param.13) | copy-start | bytes 589828
  1.4 24.0 %collective-permute-start = (bf16[3,2,512]{2,1,0:T(2,128)(2,1)S(1)}, bf16[3,2,512]{2,1,0:T(2,128)(2,1)S(1)}, u32[]{:S(2)}, u32[]{:S(2)}) collective-permute-start(bf16[3,2,512]{2,1,0:T(2,128)(2,1)S(1)} %slice.4), channel_id=1, source_target_pairs={{0,8},{8,16},{16,24},{24,32},{32,40},{40,48},{48,56},{56,64},{64,7... | collective-permute-start | bytes 18440 | tf_op jit(solution)/shard_map/ppermute | solution.py:316
  7.5 21.7 %all-to-all-start = ((bf16[16,64,128]{2,1,0:T(8,128)(2,1)}), bf16[16,64,128]{2,1,0:T(8,128)(2,1)S(1)}, u32[]{:S(2)}, u32[]{:S(2)}) async-start(bf16[16,64,128]{2,1,0:T(8,128)(2,1)} %shard_map.86), calls=%async_computation | async-start | bytes 524288 | tf_op jit(solution)/shard_map/all_to_all | solution.py:307
  17.6 7.7 %copy-start.1 = (f32[16,512]{1,0:T(8,128)S(1)}, f32[16,512]{1,0:T(8,128)}, u32[]{:S(2)}) copy-start(f32[16,512]{1,0:T(8,128)} %rates_ref.5) | copy-start | bytes 98308
  17.6 7.7 %copy-start.4 = (f32[16,512]{1,0:T(8,128)S(1)}, f32[16,512]{1,0:T(8,128)}, u32[]{:S(2)}) copy-start(f32[16,512]{1,0:T(8,128)} %param.10) | copy-start | bytes 98308
  17.7 7.8 %copy-start.5 = (f32[3,3,512]{2,1,0:T(4,128)S(1)}, f32[3,3,512]{2,1,0:T(4,128)}, u32[]{:S(2)}) copy-start(f32[3,3,512]{2,1,0:T(4,128)} %param.8) | copy-start | bytes 55300
  17.8 7.7 %copy-start.2 = (bf16[64,3,512]{2,0,1:T(8,128)(2,1)S(1)}, bf16[64,3,512]{2,0,1:T(8,128)(2,1)}, u32[]{:S(2)}) copy-start(bf16[64,3,512]{2,0,1:T(8,128)(2,1)} %param.7) | copy-start | bytes 589828
  17.8 11.3 %collective-permute-start.1 = (bf16[4,128,128]{2,1,0:T(8,128)(2,1)S(1)}, bf16[4,128,128]{2,1,0:T(8,128)(2,1)S(1)}, u32[]{:S(2)}, u32[]{:S(2)}) collective-permute-start(bf16[4,128,128]{2,1,0:T(8,128)(2,1)S(1)} %shard_map.87.pair_ref), channel_id=1, source_target_pairs={{0,256},{8,264},{16,272},{24,280},{32,288},{40,296},{48,304},{56,3... | collective-permute-start | bytes 393224 | tf_op jit(solution)/shard_map/ppermute | solution.py:338
  25.9 3.1 %collective-permute-start.2 = (bf16[4,16,128]{2,1,0:T(8,128)(2,1)S(1)}, bf16[4,16,128]{2,1,0:T(8,128)(2,1)S(1)}, u32[]{:S(2)}, u32[]{:S(2)}) collective-permute-start(bf16[4,16,128]{2,1,0:T(8,128)(2,1)S(1)} %get-tuple-element.18.state_ref), channel_id=1, source_target_pairs={{0,256},{8,264},{16,272},{24,280},{32,288},{40,296},{48,304},{56,3... | collective-permute-start | bytes 49160 | tf_op jit(solution)/shard_map/ppermute | solution.py:348
  27.2 0.7 copy-start.6
  43.7 14.7 %copy-start.3 = (f32[512]{0:T(512)S(1)}, f32[512]{0:T(512)}, u32[]{:S(2)}) copy-start(f32[512]{0:T(512)} %param.12) | copy-start | bytes 6148
